TPU v7x, 32 devices: a whole 2x2x4 slice. The times are simulated.
32 devices in a mesh: gx: 8 (over y, x, core), gy: 4 (over z).
Axes of the slice: x: 2, y: 2, z: 4, core: 2. Of those that a mesh axis runs over, the one named last changes fastest.
Arguments:
- amplitude: bfloat16 [128, 128, 128], P('gx', 'gy'), may hold values from -6 to 6
- conv_first: bfloat16 [16, 1, 3, 3, 3], replicated, may hold values from -1.25 to 1.25
- conv_second: bfloat16 [16, 16, 3, 3, 3], replicated, may hold values from -0.4375 to 0.4375
- conv_third: bfloat16 [16, 16, 3, 3, 3], replicated, may hold values from -0.4375 to 0.4375
- conv_last: bfloat16 [1, 16, 3, 3, 3], replicated, may hold values from -0.875 to 0.875
Outputs:
- fault: bfloat16 [128, 128, 128], P('gx', 'gy')
- shift_field: float32 [128, 128, 128], P(('gx', 'gy'))
All inputs are finite; a program needn't handle non-finite values.
Results may differ from a plain program's by a relative error of at most 0.0064.
Values may be sent and summed in bfloat16 or wider, within the bound.
No kernel may reach another device: no remote copies, remote signals or barrier semaphores. Data moves between devices by JAX's collectives and lax.ppermute only.
A program may use at most 192 MiB of HBM per device.

v0:
```python
import jax
import jax.numpy as jnp
from jax import lax
from jax.sharding import PartitionSpec as P

ITERS = 3


MU_DIAG = 0.05
ETA_TIME = 0.5


def extended(block, sides, width):
    for axis, dim in sides:
        count = lax.axis_size(axis)
        forward = [(i, i + 1) for i in range(count - 1)]
        backward = [(target, source) for source, target in forward]
        low = lax.ppermute(
            lax.slice_in_dim(block, block.shape[dim] - width, None, axis=dim), axis, forward
        )
        high = lax.ppermute(lax.slice_in_dim(block, 0, width, axis=dim), axis, backward)
        block = jnp.concatenate([low, block, high], axis=dim)
    return block


def smooth(values):
    values = 0.25 * values[:-2] + 0.5 * values[1:-1] + 0.25 * values[2:]
    values = 0.25 * values[:, :-2] + 0.5 * values[:, 1:-1] + 0.25 * values[:, 2:]
    return 0.25 * values[:, :, :-2] + 0.5 * values[:, :, 1:-1] + 0.25 * values[:, :, 2:]


def slopes(widened):
    field = widened.astype(jnp.float32)
    grad_x = (field[2:, 1:-1, 1:-1] - field[:-2, 1:-1, 1:-1]) * 0.5
    grad_y = (field[1:-1, 2:, 1:-1] - field[1:-1, :-2, 1:-1]) * 0.5
    grad_t = (field[1:-1, 1:-1, 2:] - field[1:-1, 1:-1, :-2]) * 0.5
    tensor_xt = smooth(grad_x * grad_t)
    tensor_yt = smooth(grad_y * grad_t)
    tensor_tt = smooth(grad_t * grad_t)
    tensor_xx = smooth(grad_x * grad_x)
    tensor_yy = smooth(grad_y * grad_y)
    denominator = tensor_tt + 0.25 * (tensor_xx + tensor_yy) + 0.05
    return (-tensor_xt / denominator, -tensor_yt / denominator)


def harmonic(centre, neighbour):
    return 2.0 * centre * neighbour / (centre + neighbour)


def assemble(fields_wide):
    weight_wide = fields_wide[0]
    slope_x_wide = fields_wide[1]
    slope_y_wide = fields_wide[2]
    centre = weight_wide[1:-1, 1:-1]
    upper_x = harmonic(centre, weight_wide[2:, 1:-1])
    lower_x = harmonic(centre, weight_wide[:-2, 1:-1])
    upper_y = harmonic(centre, weight_wide[1:-1, 2:])
    lower_y = harmonic(centre, weight_wide[1:-1, :-2])
    own_x = slope_x_wide[1:-1, 1:-1]
    own_y = slope_y_wide[1:-1, 1:-1]
    right_side = 0.5 * (
        lower_x * (own_x + slope_x_wide[:-2, 1:-1])
        - upper_x * (own_x + slope_x_wide[2:, 1:-1])
        + lower_y * (own_y + slope_y_wide[1:-1, :-2])
        - upper_y * (own_y + slope_y_wide[1:-1, 2:])
    )
    samples = centre.shape[2]
    positions = jnp.arange(samples, dtype=jnp.int32)
    time_count = (
        jnp.where(positions > 0, 1.0, 0.0) + jnp.where(positions < samples - 1, 1.0, 0.0)
    ).astype(jnp.float32)
    diagonal = MU_DIAG + ETA_TIME * time_count + upper_x + lower_x + upper_y + lower_y
    return (right_side, diagonal, (upper_x, lower_x, upper_y, lower_y), time_count)


def apply_operator(search_wide, couplings, time_count):
    upper_x, lower_x, upper_y, lower_y = couplings
    centre = search_wide[1:-1, 1:-1]
    time_wide = jnp.pad(centre, ((0, 0), (0, 0), (1, 1)))
    result = (MU_DIAG + ETA_TIME * time_count) * centre - ETA_TIME * (
        time_wide[:, :, 2:] + time_wide[:, :, :-2]
    )
    result = (
        result
        + upper_x * (centre - search_wide[2:, 1:-1])
        + lower_x * (centre - search_wide[:-2, 1:-1])
    )
    result = (
        result
        + upper_y * (centre - search_wide[1:-1, 2:])
        + lower_y * (centre - search_wide[1:-1, :-2])
    )
    return result


def valid_conv(widened, weight):
    result = lax.conv_general_dilated(
        widened[None],
        weight,
        (1, 1, 1),
        ((0, 0), (0, 0), (1, 1)),
        dimension_numbers=("NCDHW", "OIDHW", "NCDHW"),
        preferred_element_type=jnp.float32,
    )
    return result[0]


def convolve_tile(activation, weight):
    widened = extended(activation, (("gx", 1), ("gy", 2)), 1)
    return valid_conv(widened, weight)


def resid_product(residual, precond):
    return lax.psum(jnp.sum(residual * precond), ("gx", "gy"))


def solve(right_side, diagonal, operate):
    inverse = 1.0 / diagonal
    shift_field = jnp.zeros_like(right_side)
    residual = right_side
    precond = residual * inverse
    search = precond
    rz_now = resid_product(residual, precond)
    for iteration in range(ITERS):
        image = operate(search)
        step_size = rz_now / lax.psum(jnp.sum(search * image), ("gx", "gy"))
        shift_field = shift_field + step_size * search
        if iteration + 1 < ITERS:
            residual = residual - step_size * image
            precond = residual * inverse
            rz_next = resid_product(residual, precond)
            search = precond + rz_next / rz_now * search
            rz_now = rz_next
    return shift_field


def on_device(amplitude, conv_first, conv_second, conv_third, conv_last):
    activation = amplitude[None]
    for weight in (conv_first, conv_second, conv_third):
        activation = jax.nn.relu(convolve_tile(activation, weight)).astype(jnp.bfloat16)
    logit = convolve_tile(activation, conv_last)[0]
    fault = jax.nn.sigmoid(logit).astype(jnp.bfloat16)
    amp_rows, fault_rows = (
        lax.all_to_all(amplitude, "gy", split_axis=0, concat_axis=1, tiled=True),
        lax.all_to_all(fault, "gy", split_axis=0, concat_axis=1, tiled=True),
    )
    amp_wide = extended(amp_rows, ((("gx", "gy"), 0),), 2)
    amp_wide = jnp.pad(amp_wide, ((0, 0), (2, 2), (2, 2)))
    slope_x, slope_y = slopes(amp_wide)
    fields = jnp.stack([1.0 - 0.9 * fault_rows.astype(jnp.float32), slope_x, slope_y])
    fields_wide = extended(fields.astype(jnp.bfloat16), ((("gx", "gy"), 1),), 1).astype(
        fields.dtype
    )
    fields_wide = jnp.pad(fields_wide, ((0, 0), (0, 0), (1, 1), (0, 0)))
    right_side, diagonal, couplings, time_count = assemble(fields_wide)

    def operate_rows(search):
        search_wide = extended(search.astype(jnp.bfloat16), ((("gx", "gy"), 0),), 1).astype(
            search.dtype
        )
        search_wide = jnp.pad(search_wide, ((0, 0), (1, 1), (0, 0)))
        return apply_operator(search_wide, couplings, time_count)

    shift_field = solve(right_side, diagonal, operate_rows)
    return (fault, shift_field)


def solution(mesh):
    return jax.shard_map(
        on_device,
        mesh=mesh,
        in_specs=(P("gx", "gy", None), P(), P(), P(), P()),
        out_specs=(P("gx", "gy", None), P(("gx", "gy"), None, None)),
        check_vma=False,
    )
```

profile of v0, /device:TPU:0, one launch (start us, length us, event | category | flops | bytes accessed | tf_op | source)
XLA Modules:
  0.0 994.1 jit_solution(11331260720444143176)
XLA Ops:
  21.0 10.0 %copy.105 = bf16[1,18,34,8,19]{3,0,4,2,1:T(2,128)(2,1)} copy(bf16[1,18,34,8,19]{2,4,3,1,0:T(8,128)(2,1)S(1)} %fusion.37) | data formatting | bytes 372096 | tf_op jit(solution)/shard_map/conv_general_dilated | solution.py:97
  31.0 62.0 %maximum_convert_fusion.2 = bf16[16,32,8,17,16]{4,2,3,1,0:T(8,128)(2,1)} fusion(bf16[1,18,34,8,19]{3,0,4,2,1:T(2,128)(2,1)} %copy.105, pred[8,17]{0,1:T(8,128)(4,1)S(1)} %copy-done.12, bf16[16,1,3,3,3]{0,4,3,2,1:T(4,128)(2,1)S(1)} %copy-done.15), kind=kOutput, calls=%fused_computation.6 | convolution fusion | flops 63504384 | bytes 2415272 | tf_op jit(solution)/shard_map/conv_general_dilated | solution.py:97
  93.0 18.4 %copy.107 = bf16[16,32,8,17,16]{1,4,3,2,0:T(8,128)(2,1)} copy(bf16[16,32,8,17,16]{4,2,3,1,0:T(8,128)(2,1)} %maximum_convert_fusion.2) | data formatting | bytes 4456448 | tf_op jit(solution)/shard_map/convert_element_type | solution.py:140
  143.9 9.3 copy.108
  157.2 9.4 copy.109
  190.9 17.4 %maximum_bitcast_fusion = bf16[16,18,34,1,128]{2,0,4,1,3:T(8,128)(2,1)} fusion(bf16[16,18,1,128]{2,0,3,1:T(8,128)(2,1)} %copy.111, bf16[16,1,32,128]{2,0,3,1:T(8,128)(2,1)S(1)} %collective-permute-done.5, bf16[16,16,32,128]{2,0,3,1:T(8,128)(2,1)} %slice_bitcast_fusion.2, bf16[16,1,32,128]{2,0,3,1:T(8,128)(2,1)S(1)} %collective-permute-done.4, ...), kind=kLoop, calls=%fused_computation.29 | loop fusion | flops 12533760 | bytes 5013504 | tf_op jit(solution)/shard_map/broadcast_in_dim | solution.py:98
  208.3 9.9 pad.42
  218.2 27.9 %copy.113 = bf16[16,18,34,1,8,17]{0,4,5,2,1,3:T(8,128)(2,1)} copy(bf16[16,18,34,1,8,17]{2,0,5,4,1,3:T(8,128)(2,1)} %bitcast.81) | data formatting | bytes 5326848 | tf_op jit(solution)/shard_map/conv_general_dilated | solution.py:97
  248.5 46.8 %maximum_convert_fusion.1 = bf16[16,32,8,17,16]{4,2,3,1,0:T(8,128)(2,1)} fusion(pred[8,17]{0,1:T(8,128)(4,1)S(1)} %copy-done.12, bf16[16,16,3,3,3]{1,0,4,3,2:T(8,128)(2,1)S(1)} %copy-done, bf16[16,18,34,1,7,2]{0,4,5,2,1,3:T(8,128)(2,1)S(1)} %slice.481, bf16[16,18,34,1,8,17]{0,4,5,2,1,3:T(8,128)(2,1)} %copy.113), kind=kOutput, calls=%fused_computation.5 | convolution fusion | flops 974865408 | bytes 5179784 | tf_op jit(solution)/shard_map/conv_general_dilated | solution.py:97
  295.3 18.3 %copy.114 = bf16[16,32,8,17,16]{1,4,3,2,0:T(8,128)(2,1)} copy(bf16[16,32,8,17,16]{4,2,3,1,0:T(8,128)(2,1)} %maximum_convert_fusion.1) | data formatting | bytes 4456448 | tf_op jit(solution)/shard_map/convert_element_type | solution.py:140
  323.5 12.2 %collective-permute-start.8 = (bf16[16,1,32,128]{2,0,3,1:T(8,128)(2,1)S(1)}, bf16[16,1,32,128]{2,0,3,1:T(8,128)(2,1)S(1)}, u32[]{:S(2)}, u32[]{:S(2)}) collective-permute-start(bf16[16,1,32,128]{2,0,3,1:T(8,128)(2,1)S(1)} %get-tuple-element.42), channel_id=1, source_target_pairs={{0,4},{4,8},{8,12},{12,16},{16,20},{20,24},{24,28},{1,5},{5,9},{9,... | collective-permute-start | bytes 393224 | tf_op jit(solution)/shard_map/ppermute | solution.py:18
  354.5 9.3 copy.115
  366.1 9.4 copy.116
  392.8 17.4 %maximum_bitcast_fusion.1 = bf16[16,18,34,1,128]{2,0,4,1,3:T(8,128)(2,1)} fusion(bf16[16,18,1,128]{2,0,3,1:T(8,128)(2,1)} %copy.118, bf16[16,1,32,128]{2,0,3,1:T(8,128)(2,1)S(1)} %collective-permute-done.9, bf16[16,16,32,128]{2,0,3,1:T(8,128)(2,1)} %slice_bitcast_fusion.1, bf16[16,1,32,128]{2,0,3,1:T(8,128)(2,1)S(1)} %collective-permute-done.8, ...), kind=kLoop, calls=%fused_computation.31 | loop fusion | flops 12533760 | bytes 5013504 | tf_op jit(solution)/shard_map/broadcast_in_dim | solution.py:98
  410.2 9.9 pad.44
  420.2 28.0 %copy.120 = bf16[16,18,34,1,8,17]{0,4,5,2,1,3:T(8,128)(2,1)} copy(bf16[16,18,34,1,8,17]{2,0,5,4,1,3:T(8,128)(2,1)} %bitcast.82) | data formatting | bytes 5326848 | tf_op jit(solution)/shard_map/conv_general_dilated | solution.py:97
  450.5 47.1 %maximum_convert_fusion = bf16[16,32,8,17,16]{4,2,3,1,0:T(8,128)(2,1)} fusion(pred[8,17]{0,1:T(8,128)(4,1)S(1)} %copy-done.12, bf16[16,16,3,3,3]{1,0,4,3,2:T(8,128)(2,1)S(1)} %copy-done.14, bf16[16,18,34,1,7,2]{0,4,5,2,1,3:T(8,128)(2,1)S(1)} %slice.487, bf16[16,18,34,1,8,17]{0,4,5,2,1,3:T(8,128)(2,1)} %copy.120), kind=kOutput, calls=%fused_computation.4 | convolution fusion | flops 974865408 | bytes 5179784 | tf_op jit(solution)/shard_map/conv_general_dilated | solution.py:97
  497.6 18.3 %copy.121 = bf16[16,32,8,17,16]{1,4,3,2,0:T(8,128)(2,1)} copy(bf16[16,32,8,17,16]{4,2,3,1,0:T(8,128)(2,1)} %maximum_convert_fusion) | data formatting | bytes 4456448 | tf_op jit(solution)/shard_map/convert_element_type | solution.py:140
  515.9 8.7 slice_bitcast_fusion
  552.0 9.4 copy.122
  565.7 9.4 copy.123
  592.6 17.5 %maximum_bitcast_fusion.2 = bf16[16,18,34,1,128]{2,0,4,1,3:T(8,128)(2,1)} fusion(bf16[16,18,1,128]{2,0,3,1:T(8,128)(2,1)} %copy.125, bf16[16,1,32,128]{2,0,3,1:T(8,128)(2,1)S(1)} %collective-permute-done.13, bf16[16,16,32,128]{2,0,3,1:T(8,128)(2,1)} %slice_bitcast_fusion, bf16[16,1,32,128]{2,0,3,1:T(8,128)(2,1)S(1)} %collective-permute-done.12, ...), kind=kLoop, calls=%fused_computation.33 | loop fusion | flops 12533760 | bytes 5013504 | tf_op jit(solution)/shard_map/broadcast_in_dim | solution.py:98
  610.1 10.0 %pad.46 = bf16[16,18,34,1,136]{2,0,4,1,3:T(8,128)(2,1)} pad(bf16[16,18,34,1,128]{2,0,4,1,3:T(8,128)(2,1)} %maximum_bitcast_fusion.2, bf16[]{:T(256)} %constant.13.clone.1), padding=0_0x0_0x0_0x0_0x1_7 | pad | bytes 5170178 | tf_op jit(solution)/shard_map/broadcast_in_dim | solution.py:98
  620.0 28.0 %copy.127 = bf16[16,18,34,1,8,17]{0,4,5,2,1,3:T(8,128)(2,1)} copy(bf16[16,18,34,1,8,17]{2,0,5,4,1,3:T(8,128)(2,1)} %bitcast.80) | data formatting | bytes 5326848 | tf_op jit(solution)/shard_map/conv_general_dilated | solution.py:97
  650.4 43.8 %fusion.13 = f32[16,32,8,17,1]{4,2,3,1,0:T(8,128)} fusion(bf16[16,18,34,1,7,2]{0,4,5,2,1,3:T(8,128)(2,1)S(1)} %slice.493, bf16[16,18,34,1,8,17]{0,4,5,2,1,3:T(8,128)(2,1)} %copy.127, bf16[1,16,3,3,3]{1,4,3,2,0:T(4,128)(2,1)S(1)} %copy-done.16), kind=kOutput, calls=%fused_computation.15 | convolution fusion | flops 69092352 | bytes 3216992 | tf_op jit(solution)/shard_map/conv_general_dilated | solution.py:97
  694.3 21.8 %copy.129 = f32[16,32,8,17,1]{1,2,4,3,0:T(8,128)S(1)} copy(f32[16,32,8,17,1]{4,2,3,1,0:T(8,128)} %fusion.13) | data formatting | bytes 557056 | tf_op jit(solution)/shard_map/conv_general_dilated | solution.py:97
  742.4 11.3 %collective-permute-done.21 = bf16[1,128,128]{2,1,0:T(8,128)(2,1)S(1)} collective-permute-done((bf16[1,128,128]{2,1,0:T(8,128)(2,1)S(1)}, bf16[1,128,128]{2,1,0:T(8,128)(2,1)S(1)}, u32[]{:S(2)}, u32[]{:S(2)}) %collective-permute-start.21) | collective-permute-done | bytes 32800 | tf_op jit(solution)/shard_map/ppermute | solution.py:21
  754.7 44.1 %all-reduce.8 = (f32[]{:T(128)}, f32[]{:T(128)}) all-reduce(f32[]{:T(128)} %get-tuple-element.11, f32[]{:T(128)} %get-tuple-element.10), channel_id=1, replica_groups=mesh['gx'=8,'gy'=4] {'gx','gy'}, use_global_device_ids=true, to_apply=%region_1.2 | all-reduce | flops 2 | bytes 16 | tf_op jit(solution)/shard_map/psum | solution.py:114
  800.8 40.6 %psum.44 = f32[]{:T(128)} all-reduce(f32[]{:T(128)} %get-tuple-element.20), channel_id=1, replica_groups=mesh['gx'=8,'gy'=4] {'gx','gy'}, use_global_device_ids=true, to_apply=%region_5.6 | all-reduce | flops 1 | bytes 8 | tf_op jit(solution)/shard_map/psum | solution.py:114
  851.4 43.9 %psum.45 = f32[]{:T(128)} all-reduce(f32[]{:T(128)} %get-tuple-element.16), channel_id=1, replica_groups=mesh['gx'=8,'gy'=4] {'gx','gy'}, use_global_device_ids=true, to_apply=%region_7.8 | all-reduce | flops 1 | bytes 8 | tf_op jit(solution)/shard_map/psum | solution.py:126
  897.3 40.6 %psum.46 = f32[]{:T(128)} all-reduce(f32[]{:T(128)} %multiply_reduce_fusion), channel_id=1, replica_groups=mesh['gx'=8,'gy'=4] {'gx','gy'}, use_global_device_ids=true, to_apply=%region_9.10 | all-reduce | flops 1 | bytes 8 | tf_op jit(solution)/shard_map/psum | solution.py:114
  947.9 43.9 %psum.47 = f32[]{:T(128)} all-reduce(f32[]{:T(128)} %fusion.88), channel_id=1, replica_groups=mesh['gx'=8,'gy'=4] {'gx','gy'}, use_global_device_ids=true, to_apply=%region_11.12 | all-reduce | flops 1 | bytes 8 | tf_op jit(solution)/shard_map/psum | solution.py:126
  (163 shorter events, 232.1 us)
Async XLA Ops:
  0.6 247.9 %copy-start = (bf16[16,16,3,3,3]{1,0,4,3,2:T(8,128)(2,1)S(1)}, bf16[16,16,3,3,3]{1,0,4,3,2:T(8,128)(2,1)}, u32[]{:S(2)}) copy-start(bf16[16,16,3,3,3]{1,0,4,3,2:T(8,128)(2,1)} %param.7) | copy-start | bytes 41476
  1.4 3.7 collective-permute-start
  3.8 5.2 collective-permute-start.1
  9.7 4.8 collective-permute-start.2
  13.2 5.6 collective-permute-start.3
  121.2 8.6 collective-permute-start.4
  124.1 5.7 collective-permute-start.5
  125.4 42.4 %all-to-all-start.1 = ((bf16[16,32,128]{2,1,0:T(8,128)(2,1)}), bf16[16,32,128]{2,1,0:T(8,128)(2,1)S(1)}, u32[]{:S(2)}, u32[]{:S(2)}) async-start(bf16[16,32,128]{2,1,0:T(8,128)(2,1)} %param.5), calls=%async_computation.1 | async-start | bytes 262144 | tf_op jit(solution)/shard_map/all_to_all | solution.py:144
  153.3 22.4 %collective-permute-start.6 = (bf16[16,18,1,128]{3,0,2,1:T(8,128)(2,1)S(1)}, bf16[16,18,1,128]{3,0,2,1:T(8,128)(2,1)S(1)}, u32[]{:S(2)}, u32[]{:S(2)}) collective-permute-start(bf16[16,18,1,128]{3,0,2,1:T(8,128)(2,1)S(1)} %copy.108), channel_id=1, source_target_pairs={{0,1},{1,2},{2,3},{4,5},{5,6},{6,7},{8,9},{9,10},{10,11},{12,13},{... | collective-permute-start | bytes 221192 | tf_op jit(solution)/shard_map/ppermute | solution.py:18
  166.6 16.7 %collective-permute-start.7 = (bf16[16,18,1,128]{3,0,2,1:T(8,128)(2,1)S(1)}, bf16[16,18,1,128]{3,0,2,1:T(8,128)(2,1)S(1)}, u32[]{:S(2)}, u32[]{:S(2)}) collective-permute-start(bf16[16,18,1,128]{3,0,2,1:T(8,128)(2,1)S(1)} %copy.109), channel_id=1, source_target_pairs={{1,0},{2,1},{3,2},{5,4},{6,5},{7,6},{9,8},{10,9},{11,10},{13,12},{... | collective-permute-start | bytes 221192 | tf_op jit(solution)/shard_map/ppermute | solution.py:21
  169.2 167.8 %collective-permute-start.16 = (bf16[2,128,128]{2,1,0:T(8,128)(2,1)}, bf16[2,128,128]{2,1,0:T(8,128)(2,1)}, u32[]{:S(2)}, u32[]{:S(2)}) collective-permute-start(bf16[2,128,128]{2,1,0:T(8,128)(2,1)} %bitcast.31), channel_id=1, source_target_pairs={{0,1},{1,2},{2,3},{3,4},{4,5},{5,6},{6,7},{7,8},{8,9},{9,10},{10,1... | collective-permute-start | bytes 196616 | tf_op jit(solution)/shard_map/ppermute | solution.py:18
  174.4 162.7 %collective-permute-start.17 = (bf16[2,128,128]{2,1,0:T(8,128)(2,1)}, bf16[2,128,128]{2,1,0:T(8,128)(2,1)}, u32[]{:S(2)}, u32[]{:S(2)}) collective-permute-start(bf16[2,128,128]{2,1,0:T(8,128)(2,1)} %bitcast.33), channel_id=1, source_target_pairs={{1,0},{2,1},{3,2},{4,3},{5,4},{6,5},{7,6},{8,7},{9,8},{10,9},{11,1... | collective-permute-start | bytes 196616 | tf_op jit(solution)/shard_map/ppermute | solution.py:21
  323.5 20.1 %collective-permute-start.8 = (bf16[16,1,32,128]{2,0,3,1:T(8,128)(2,1)S(1)}, bf16[16,1,32,128]{2,0,3,1:T(8,128)(2,1)S(1)}, u32[]{:S(2)}, u32[]{:S(2)}) collective-permute-start(bf16[16,1,32,128]{2,0,3,1:T(8,128)(2,1)S(1)} %get-tuple-element.42), channel_id=1, source_target_pairs={{0,4},{4,8},{8,12},{12,16},{16,20},{20,24},{24,28},{1,5},{5,9},{9,... | collective-permute-start | bytes 393224 | tf_op jit(solution)/shard_map/ppermute | solution.py:18
  335.7 7.9 collective-permute-start.9
  363.9 13.8 %collective-permute-start.10 = (bf16[16,18,1,128]{3,0,2,1:T(8,128)(2,1)S(1)}, bf16[16,18,1,128]{3,0,2,1:T(8,128)(2,1)S(1)}, u32[]{:S(2)}, u32[]{:S(2)}) collective-permute-start(bf16[16,18,1,128]{3,0,2,1:T(8,128)(2,1)S(1)} %copy.115), channel_id=1, source_target_pairs={{0,1},{1,2},{2,3},{4,5},{5,6},{6,7},{8,9},{9,10},{10,11},{12,13},{... | collective-permute-start | bytes 221192 | tf_op jit(solution)/shard_map/ppermute | solution.py:18
  375.4 9.8 collective-permute-start.11
  420.2 30.4 %copy-start.14 = (bf16[16,16,3,3,3]{1,0,4,3,2:T(8,128)(2,1)S(1)}, bf16[16,16,3,3,3]{1,0,4,3,2:T(8,128)(2,1)}, u32[]{:S(2)}) copy-start(bf16[16,16,3,3,3]{1,0,4,3,2:T(8,128)(2,1)} %param.8) | copy-start | bytes 41476
  526.0 10.8 %collective-permute-start.12 = (bf16[16,1,32,128]{2,0,3,1:T(8,128)(2,1)S(1)}, bf16[16,1,32,128]{2,0,3,1:T(8,128)(2,1)S(1)}, u32[]{:S(2)}, u32[]{:S(2)}) collective-permute-start(bf16[16,1,32,128]{2,0,3,1:T(8,128)(2,1)S(1)} %get-tuple-element.40), channel_id=1, source_target_pairs={{0,4},{4,8},{8,12},{12,16},{16,20},{20,24},{24,28},{1,5},{5,9},{9,... | collective-permute-start | bytes 393224 | tf_op jit(solution)/shard_map/ppermute | solution.py:18
  534.1 3.8 collective-permute-start.13
  561.4 15.9 %collective-permute-start.14 = (bf16[16,18,1,128]{3,0,2,1:T(8,128)(2,1)S(1)}, bf16[16,18,1,128]{3,0,2,1:T(8,128)(2,1)S(1)}, u32[]{:S(2)}, u32[]{:S(2)}) collective-permute-start(bf16[16,18,1,128]{3,0,2,1:T(8,128)(2,1)S(1)} %copy.122), channel_id=1, source_target_pairs={{0,1},{1,2},{2,3},{4,5},{5,6},{6,7},{8,9},{9,10},{10,11},{12,13},{... | collective-permute-start | bytes 221192 | tf_op jit(solution)/shard_map/ppermute | solution.py:18
  575.1 10.1 %collective-permute-start.15 = (bf16[16,18,1,128]{3,0,2,1:T(8,128)(2,1)S(1)}, bf16[16,18,1,128]{3,0,2,1:T(8,128)(2,1)S(1)}, u32[]{:S(2)}, u32[]{:S(2)}) collective-permute-start(bf16[16,18,1,128]{3,0,2,1:T(8,128)(2,1)S(1)} %copy.123), channel_id=1, source_target_pairs={{1,0},{2,1},{3,2},{5,4},{6,5},{7,6},{9,8},{10,9},{11,10},{13,12},{... | collective-permute-start | bytes 221192 | tf_op jit(solution)/shard_map/ppermute | solution.py:21
  694.3 34.0 %copy-start.8 = (bf16[1,4,128,128]{3,2,1,0:T(8,128)(2,1)S(1)}, bf16[1,4,128,128]{3,2,1,0:T(8,128)(2,1)}, u32[]{:S(2)}) copy-start(bf16[1,4,128,128]{3,2,1,0:T(8,128)(2,1)} %get-tuple-element.32) | copy-start | bytes 393220
  717.7 10.5 %all-to-all-start = ((bf16[16,32,128]{2,1,0:T(8,128)(2,1)}), bf16[16,32,128]{2,1,0:T(8,128)(2,1)S(1)}, u32[]{:S(2)}, u32[]{:S(2)}) async-start(bf16[16,32,128]{2,1,0:T(8,128)(2,1)} %copy.134), calls=%async_computation | async-start | bytes 262144 | tf_op jit(solution)/shard_map/all_to_all | solution.py:145
  728.3 5.4 collective-permute-start.18
  731.5 6.5 collective-permute-start.19
  738.2 255.6 %copy-start.1 = (bf16[16,16,3,3,3]{1,0,4,3,2:T(8,128)(2,1)S(1)}, bf16[16,16,3,3,3]{1,0,4,3,2:T(8,128)(2,1)}, u32[]{:S(2)}) copy-start(bf16[16,16,3,3,3]{1,0,4,3,2:T(8,128)(2,1)} %param.7) | copy-start | bytes 41476
  738.7 3.7 collective-permute-start.20
  740.8 12.8 %collective-permute-start.21 = (bf16[1,128,128]{2,1,0:T(8,128)(2,1)S(1)}, bf16[1,128,128]{2,1,0:T(8,128)(2,1)S(1)}, u32[]{:S(2)}, u32[]{:S(2)}) collective-permute-start(bf16[1,128,128]{2,1,0:T(8,128)(2,1)S(1)} %get-tuple-element.63), channel_id=1, source_target_pairs={{1,0},{2,1},{3,2},{4,3},{5,4},{6,5},{7,6},{8,7},{9,8},{10,9},{11,1... | collective-permute-start | bytes 98312 | tf_op jit(solution)/shard_map/ppermute | solution.py:21
  842.7 3.4 collective-permute-start.22
  844.5 5.8 collective-permute-start.23
  939.2 3.4 collective-permute-start.24
  941.1 5.8 collective-permute-start.25
  (15 other events, 301.9 us)
where the time goes:
time: 1010 us; the launch traced here: 994 us
  local copies, waits for them, and re-layouts  368 us (36%)
  blocking collectives  213 us (21%)
  matrix products  200 us (20%)
  other arithmetic  84.8 us (8%)
  starting transfers between devices  79.4 us (8%)
  waiting for transfers between devices  40.5 us (4%)
    conv_general_dilated x4, matrix products, valid_conv(): lax.conv_general_dilated(widened[None], weight, (1, 1, 1), ((0, 0), (0, 0...  200 us
    psum x3, blocking collectives, resid_product(): return lax.psum(jnp.sum(residual * precond), ('gx', 'gy'))  125 us
    conv_general_dilated x10, local copies, waits for them, and re-layouts, valid_conv(): lax.conv_general_dilated(widened[None], weight, (1, 1, 1), ((0, 0), (0, 0...  123 us
    psum x2, blocking collectives, solve(): step_size = rz_now / lax.psum(jnp.sum(search * image), ('gx', 'gy'))  87.8 us
    convert_element_type x6, local copies, waits for them, and re-layouts, on_device(): jax.nn.relu(convolve_tile(activation, weight)).astype(jnp.bfloat16)  80.7 us
    slice x14, local copies, waits for them, and re-layouts, extended(): lax.slice_in_dim(block, block.shape[dim] - width, None, axis=dim)  58.2 us
    ppermute x13, starting transfers between devices, extended(): lax.ppermute(lax.slice_in_dim(block, block.shape[dim] - width, None, axis...  53.5 us
    broadcast_in_dim x4, other arithmetic, valid_conv(): widened[None]  53.2 us
  transfers between devices with their start and end apart: 28, of which 13 were waited for; matrix products, arithmetic and copies ran while one was open for 23% of the time, Pallas kernels for 0%

commit v1 on v0

v1 whole, which is shorter than its diff:
```python
import functools

import jax
import jax.numpy as jnp
from jax import lax
from jax.experimental import pallas as pl
from jax.experimental.pallas import tpu as pltpu
from jax.sharding import PartitionSpec as P

MU_DIAG = 0.05
ETA_TIME = 0.5

TX, NT, H = 16, 128, 8
CH = 16
XW = TX + 2 * H
BLK = 256
SUB = 16
PAD = SUB + NT + SUB

F32 = jnp.float32
BF16 = jnp.bfloat16


def iota(shape, dim):
    return lax.broadcasted_iota(jnp.int32, shape, dim)


def prep_kernel(w_ref, w1_ref, w2_ref, w3_ref, w4_ref):
    spread = jnp.where(iota((CH, BLK), 1) % CH == iota((CH, BLK), 0), 1.0, 0.0).astype(BF16)
    tiled = jnp.dot(w_ref[...], spread, preferred_element_type=F32)
    out_pos = iota((CH, BLK), 1) // CH
    for layer, ref in ((0, w2_ref), (1, w3_ref)):
        for dy in range(3):
            for dt in range(3):
                rows = [
                    tiled[(layer * 27 + dx * 9 + dy * 3 + dt) * CH :][:CH] for dx in range(3)
                ]
                for xi in range(16):
                    band = jnp.zeros((CH, BLK), F32)
                    for dx in range(3):
                        band = jnp.where(out_pos == xi - dx, rows[dx], band)
                    ref[dy * 3 + dt, xi * CH : (xi + 1) * CH, :] = band.astype(BF16)
    base = 2 * 27 * CH
    first = tiled[base : base + 32]
    last = tiled[base + 32 : base + 64]
    in_pos = iota((XW, BLK), 0)
    lane_pos = iota((XW, BLK), 1) // CH
    for dt in range(3):
        for yi in range(4):
            for yo in range(2):
                for blk in range(2):
                    band = jnp.zeros((XW, BLK), F32)
                    dy = yi - yo
                    if 0 <= dy <= 2:
                        for dx in range(3):
                            tap = dx * 9 + dy * 3 + dt
                            band = jnp.where(
                                in_pos - 14 * blk - lane_pos == dx, first[tap : tap + 1], band
                            )
                    w1_ref[
                        dt * 128 + yi * XW : dt * 128 + (yi + 1) * XW,
                        yo * 512 + blk * BLK : yo * 512 + (blk + 1) * BLK,
                    ] = band.astype(BF16)
    for dy in range(3):
        for dt in range(3):
            for blk in range(2):
                band = jnp.zeros((XW, BLK), F32)
                for dx in range(3):
                    tap = dx * 9 + dy * 3 + dt
                    band = jnp.where(
                        14 * blk + lane_pos + 4 - in_pos == dx, last[tap : tap + 1], band
                    )
                band = jnp.where(lane_pos < 14 - 2 * blk, band, 0.0)
                row = (dy * 3 + dt) * XW
                w4_ref[row : row + XW, blk * BLK : (blk + 1) * BLK] = band.astype(BF16)


def main_kernel(
    grid_x,
    grid_y,
    ty,
    pos_ref,
    amp_ref,
    xlow_ref,
    xhigh_ref,
    ylow_ref,
    yhigh_ref,
    w1_ref,
    w2_ref,
    w3_ref,
    w4_ref,
    fault_ref,
    waves_ref,
    mom_ref,
    raw,
    amp,
    act1,
    act2,
    act3,
    part,
    logit,
    prod,
    slope,
    weight,
    face,
    flux,
    inv,
    wave,
    stage,
):
    x0 = pos_ref[0]
    y0 = pos_ref[1]
    yw = ty + 2 * H
    nf = ty + 8
    dot = functools.partial(jnp.dot, preferred_element_type=F32)

    def dot_nt(a, b):
        return lax.dot_general(a, b, (((1,), (1,)), ((), ())), preferred_element_type=F32)

    def inside_y(y):
        at = y0 + y
        return jnp.where((at >= 0) & (at < grid_y), 1.0, 0.0).astype(F32)

    def lane_mask(start):
        masks = []
        for blk in range(2):
            at = x0 + start + 14 * blk + iota((1, BLK), 1) // CH
            masks.append(jnp.where((at >= 0) & (at < grid_x), 1.0, 0.0).astype(F32))
        return masks

    for x in range(XW):
        row = x * yw
        if x < H:
            mid = xlow_ref[x]
        elif x < H + TX:
            mid = amp_ref[x - H]
        else:
            mid = xhigh_ref[x - H - TX]
        raw[row + H : row + H + ty, :] = mid.astype(F32)
        raw[row : row + H, :] = ylow_ref[x].astype(F32)
        raw[row + H + ty : row + yw, :] = yhigh_ref[x].astype(F32)

    def turn(y, carry):
        amp[y] = raw[pl.ds(y, XW, stride=yw), :]
        return carry

    lax.fori_loop(0, yw, turn, 0)
    amp[yw] = jnp.zeros((XW, NT), F32)
    amp[yw + 1] = jnp.zeros((XW, NT), F32)

    tiled_row = iota((NT, NT), 0)
    natural = tiled_row // SUB + (tiled_row % SUB) * 8
    to_tiles = jnp.concatenate(
        [
            jnp.where(iota((NT, NT), 1) == natural + dt - 1, 1.0, 0.0).astype(BF16)
            for dt in range(3)
        ],
        axis=0,
    )
    from_tiles = jnp.concatenate(
        [
            jnp.where(iota((NT, NT), 1) + dt - 1 == natural, 1.0, 0.0).astype(BF16)
            for dt in range(3)
        ],
        axis=0,
    )
    sub_row = iota((SUB, BLK), 0)

    def put(act, y, blk, values):
        act[y, blk, SUB : SUB + NT, :] = values.astype(BF16)
        before = jnp.where(sub_row == 0, 0.0, pltpu.roll(values[NT - SUB :], 1, 0))
        after = jnp.where(sub_row == SUB - 1, 0.0, pltpu.roll(values[:SUB], SUB - 1, 0))
        act[y, blk, 0:SUB, :] = before.astype(BF16)
        act[y, blk, SUB + NT :, :] = after.astype(BF16)

    mask1 = lane_mask(-7)

    def first(step, carry):
        pieces = []
        for half in range(2):
            y = step * 4 + half * 2
            rows = amp[pl.ds(y, 4)].reshape(4 * XW, NT).astype(BF16)
            turned = dot_nt(to_tiles, rows).astype(BF16)
            pieces.append(
                jnp.concatenate([turned[:NT], turned[NT : 2 * NT], turned[2 * NT :]], axis=1)
            )
        result = dot(jnp.concatenate(pieces, axis=0), w1_ref[...])
        for half in range(2):
            for yo in range(2):
                y = step * 4 + half * 2 + yo
                ok = inside_y(y - 7)
                for blk in range(2):
                    lane = yo * 512 + blk * BLK
                    values = result[half * NT : (half + 1) * NT, lane : lane + BLK]
                    put(act1, y, blk, jnp.maximum(values, 0.0) * (mask1[blk] * ok))
        return carry

    lax.fori_loop(0, yw // 4, first, 0)

    def layer(source, w_ref, y, count):
        taps = []
        for dy in range(3):
            for dt in range(3):
                part_in = source[pl.ds(y + dy, count), :, SUB * dt : SUB * dt + NT, :]
                taps.append(part_in.reshape(count * 2 * NT, BLK))
        return dot(jnp.concatenate(taps, axis=1), w_ref[...].reshape(9 * BLK, BLK))

    mask2 = lane_mask(-6)
    lane_half = iota((NT, 128), 1)

    def second(step, carry):
        y = step * 4
        result = layer(act1, w2_ref, y, 4)
        for row in range(4):
            ok = inside_y(y + row - 6)
            low = result[row * 2 * NT : row * 2 * NT + NT]
            high = result[row * 2 * NT + NT : (row + 1) * 2 * NT]
            moved = jnp.where(lane_half >= 96, pltpu.roll(high[:, :128], 96, 1), low[:, 128:])
            low = jnp.concatenate([low[:, :128], moved], axis=1)
            put(act2, y + row, 0, jnp.maximum(low, 0.0) * (mask2[0] * ok))
            put(act2, y + row, 1, jnp.maximum(high, 0.0) * (mask2[1] * ok))
        return carry

    lax.fori_loop(0, (ty + 12) // 4, second, 0)

    mask3 = lane_mask(-5)

    def third(step, carry):
        y = step * 3
        result = layer(act2, w3_ref, y, 3)
        for row in range(3):
            ok = inside_y(y + row - 5)
            for blk in range(2):
                at = (row * 2 + blk) * NT
                values = jnp.maximum(result[at : at + NT], 0.0) * (mask3[blk] * ok)
                act3[y + row, :, blk * BLK : (blk + 1) * BLK] = values.astype(BF16)
        return carry

    lax.fori_loop(0, (ty + 10) // 3, third, 0)

    def fourth(y, carry):
        part[y] = dot_nt(w4_ref[...], act3[y])
        return carry

    lax.fori_loop(0, ty + 10, fourth, 0)

    def order(step, carry):
        sums = []
        for row in range(4):
            y = step * 4 + row
            total = part[y, 0:96] + part[y + 1, 96:192] + part[y + 2, 192:288]
            sums.append(
                jnp.concatenate([total[0:32], total[32:64], total[64:96]], axis=1)
            )
        sums = jnp.concatenate(sums, axis=0)
        high = sums.astype(BF16)
        low = (sums - high.astype(F32)).astype(BF16)
        both = dot(jnp.concatenate([high, low], axis=0), from_tiles)
        values = both[: 4 * XW] + both[4 * XW :]
        prob = (1.0 / (1.0 + jnp.exp(-values))).astype(BF16).astype(F32)
        for row in range(4):
            logit[step * 4 + row] = prob[row * XW : (row + 1) * XW]
        return carry

    lax.fori_loop(0, nf // 4, order, 0)

    lane = iota((XW, NT), 1)
    first_lane = lane == 0
    last_lane = lane == NT - 1

    def up_x(v):
        return pltpu.roll(v, XW - 1, 0)

    def down_x(v):
        return pltpu.roll(v, 1, 0)

    def up_t(v, edge=0.0):
        return jnp.where(last_lane, edge, pltpu.roll(v, NT - 1, 1))

    def down_t(v, edge=0.0):
        return jnp.where(first_lane, edge, pltpu.roll(v, 1, 1))

    def smooth_xt(v, edge=0.0):
        v = 0.5 * v + 0.25 * (up_t(v, edge) + down_t(v, edge))
        return 0.5 * v + 0.25 * (up_x(v) + down_x(v))

    def products(i, carry):
        here = amp[i + 3]
        grad_x = 0.5 * (up_x(here) - down_x(here))
        grad_y = 0.5 * (amp[i + 4] - amp[i + 2])
        grad_t = 0.5 * (up_t(here) - down_t(here))
        prod[0, i] = smooth_xt(grad_x * grad_t)
        prod[1, i] = smooth_xt(grad_y * grad_t)
        energy = grad_t * grad_t + 0.25 * (grad_x * grad_x + grad_y * grad_y)
        prod[2, i] = smooth_xt(energy, 0.25 * here * here)
        return carry

    lax.fori_loop(0, ty + 10, products, 0)

    at_x = x0 - H + iota((XW, NT), 0)
    mask_x = jnp.where((at_x >= 0) & (at_x < grid_x), 1.0, 0.0).astype(F32)

    def fields(k, carry):
        sums = []
        for which in range(3):
            sums.append(
                0.5 * prod[which, k + 1] + 0.25 * (prod[which, k] + prod[which, k + 2])
            )
        scale = -1.0 / (sums[2] + 0.05)
        slope[0, k] = sums[0] * scale
        slope[1, k] = sums[1] * scale
        raw_weight = 1.0 - 0.9 * logit[k]
        weight[0, k] = raw_weight
        weight[1, k] = raw_weight * (mask_x * inside_y(k - 4))
        return carry

    lax.fori_loop(0, nf, fields, 0)

    def faces(k, carry):
        raw_weight = weight[0, k]
        masked = weight[1, k]
        face_x = 2.0 * masked * up_x(masked) / (raw_weight + up_x(raw_weight))
        face_y = 2.0 * masked * weight[1, k + 1] / (raw_weight + weight[0, k + 1])
        slope_x = slope[0, k]
        face[0, k] = face_x
        face[1, k] = face_y
        flux[0, k] = 0.5 * face_x * (slope_x + up_x(slope_x))
        flux[1, k] = 0.5 * face_y * (slope[1, k] + slope[1, k + 1])
        return carry

    lax.fori_loop(0, nf - 1, faces, 0)

    time_part = MU_DIAG + ETA_TIME * (
        jnp.where(first_lane, 0.0, 1.0) + jnp.where(last_lane, 0.0, 1.0)
    )
    own = slice(H, H + TX)

    def owned(k):
        return jnp.where((k >= 4) & (k < 4 + ty), 1.0, 0.0).astype(F32)

    def start(k, total):
        flux_x = flux[0, k]
        face_x = face[0, k]
        right = down_x(flux_x) - flux_x + flux[1, k - 1] - flux[1, k]
        inverse = 1.0 / (time_part + face_x + down_x(face_x) + face[1, k] + face[1, k - 1])
        first_wave = right * inverse
        inv[k] = inverse
        wave[0, k] = first_wave
        return total + owned(k) * (right * first_wave)[own]

    zero = jnp.zeros((TX, NT), F32)
    b0 = lax.fori_loop(1, nf - 1, start, zero)

    def apply(which, k):
        here = wave[which, k]
        face_x = face[0, k]
        flow = face_x * (here - up_x(here))
        image = time_part * here - ETA_TIME * (up_t(here) + down_t(here))
        image = image + flow - down_x(flow)
        image = image + face[1, k] * (here - wave[which, k + 1])
        return here, image + face[1, k - 1] * (here - wave[which, k - 1])

    def advance(which):
        def body(k, totals):
            here, image = apply(which, k)
            after = here - image * inv[k]
            wave[which + 1, k] = after
            ok = owned(k)
            return (
                totals[0] + ok * (here * image)[own],
                totals[1] + ok * (after * image)[own],
            )

        return body

    a0, a1 = lax.fori_loop(2, nf - 2, advance(0), (zero, zero))
    a2, a3 = lax.fori_loop(3, nf - 3, advance(1), (zero, zero))

    def finish(k, total):
        here, image = apply(2, k)
        return total + (here * image)[own]

    a4 = lax.fori_loop(4, nf - 4, finish, zero)

    sums = [jnp.sum(v, axis=0, keepdims=True) for v in (b0, a0, a1, a2, a3, a4)]
    mom_ref[...] = jnp.concatenate(sums + [jnp.zeros((2, NT), F32)], axis=0)

    def own_cells(source, put_x):
        def body(y, carry):
            stage[pl.ds(y, TX, stride=ty), :] = source(y)[own]
            return carry

        lax.fori_loop(0, ty, body, 0)
        for x in range(TX):
            put_x(x, stage[x * ty : (x + 1) * ty, :].astype(BF16))

    def put_fault(x, values):
        fault_ref[x] = values

    own_cells(lambda y: logit[y + 4], put_fault)
    rows = waves_ref.shape[2]
    for which in range(3):

        def put_wave(x, values, which=which):
            waves_ref[x // rows, which, x % rows] = values

        own_cells(lambda y, which=which: wave[which, y + 4], put_wave)


def combine_kernel(ty, mom_ref, waves_ref, out_ref):
    moments = jnp.sum(jnp.sum(mom_ref[...], axis=0), axis=1, keepdims=True)
    b0, a0, a1, a2, a3, a4 = [
        jnp.broadcast_to(moments[i : i + 1], (1, NT)) for i in range(6)
    ]
    a0, a1, a2, a3, a4 = [v / b0 for v in (a0, a1, a2, a3, a4)]
    l21 = a1 / a0
    l31 = a2 / a0
    d2 = jnp.maximum(a2 - l21 * a1, 1e-7 * a2 + 1e-30)
    l32 = (a3 - l21 * a2) / d2
    d3 = jnp.maximum(a4 - l31 * a2 - l32 * l32 * d2, 1e-7 * a4 + 1e-30)
    y2 = (1.0 - a0) - l21
    y3 = (1.0 - a0 - a1) - l31 - l32 * y2
    c3 = y3 / d3
    c2 = y2 / d2 - l32 * c3
    c1 = 1.0 / a0 - l21 * c2 - l31 * c3
    for block in range(waves_ref.shape[0]):
        for x in range(waves_ref.shape[2]):
            w0, w1, w2 = [waves_ref[block, which, x].astype(F32) for which in range(3)]
            out_ref[x, block * ty : (block + 1) * ty, :] = c1 * w0 + c2 * w1 + c3 * w2


def vmem(count):
    return [pl.BlockSpec(memory_space=pltpu.VMEM)] * count


def on_device(amplitude, conv_first, conv_second, conv_third, conv_last):
    n_gx, n_gy = lax.axis_size("gx"), lax.axis_size("gy")
    ty = amplitude.shape[1]
    grid_x, grid_y = n_gx * TX, n_gy * ty
    assert amplitude.shape == (TX, ty, NT)

    def shift(values, axis, count, step):
        pairs = [(i, i + step) for i in range(count) if 0 <= i + step < count]
        return lax.ppermute(values, axis, pairs)

    xlow = shift(amplitude[TX - H :], "gx", n_gx, 1)
    xhigh = shift(amplitude[:H], "gx", n_gx, -1)
    ylow = shift(
        jnp.concatenate([xlow[:, ty - H :], amplitude[:, ty - H :], xhigh[:, ty - H :]]),
        "gy",
        n_gy,
        1,
    )
    yhigh = shift(
        jnp.concatenate([xlow[:, :H], amplitude[:, :H], xhigh[:, :H]]), "gy", n_gy, -1
    )

    def by_tap(weight):
        return jnp.transpose(weight.reshape(weight.shape[0], -1, 27), (2, 1, 0))

    small = jnp.concatenate(
        [
            by_tap(conv_second).reshape(27 * CH, CH),
            by_tap(conv_third).reshape(27 * CH, CH),
            by_tap(conv_first).reshape(27, CH),
            jnp.zeros((5, CH), BF16),
            conv_last.reshape(CH, 27).T,
            jnp.zeros((5, CH), BF16),
        ],
        axis=0,
    )
    w1, w2, w3, w4 = pl.pallas_call(
        prep_kernel,
        out_shape=[
            jax.ShapeDtypeStruct((3 * 4 * XW, 4 * BLK), BF16),
            jax.ShapeDtypeStruct((9, BLK, BLK), BF16),
            jax.ShapeDtypeStruct((9, BLK, BLK), BF16),
            jax.ShapeDtypeStruct((9 * XW, 2 * BLK), BF16),
        ],
        in_specs=vmem(1),
        out_specs=vmem(4),
        compiler_params=pltpu.CompilerParams(vmem_limit_bytes=32 * 2**20),
        cost_estimate=pl.CostEstimate(flops=10**7, bytes_accessed=4 * 10**6, transcendentals=0),
        name="band_weights",
    )(small)

    position = jnp.stack([lax.axis_index("gx") * TX, lax.axis_index("gy") * ty])
    yw, nf = ty + 2 * H, ty + 8
    scratch = [
        pltpu.VMEM((XW * yw, NT), F32),
        pltpu.VMEM((yw + 2, XW, NT), F32),
        pltpu.VMEM((yw, 2, PAD, BLK), BF16),
        pltpu.VMEM((ty + 12, 2, PAD, BLK), BF16),
        pltpu.VMEM((ty + 10, NT, 2 * BLK), BF16),
        pltpu.VMEM((ty + 10, 9 * XW, NT), F32),
        pltpu.VMEM((nf, XW, NT), F32),
        pltpu.VMEM((3, ty + 10, XW, NT), F32),
        pltpu.VMEM((2, nf, XW, NT), F32),
        pltpu.VMEM((2, nf, XW, NT), F32),
        pltpu.VMEM((2, nf, XW, NT), F32),
        pltpu.VMEM((2, nf, XW, NT), F32),
        pltpu.VMEM((nf, XW, NT), F32),
        pltpu.VMEM((3, nf, XW, NT), F32),
        pltpu.VMEM((TX * ty, NT), F32),
    ]
    fault, waves, moments = pl.pallas_call(
        functools.partial(main_kernel, grid_x, grid_y, ty),
        out_shape=[
            jax.ShapeDtypeStruct((TX, ty, NT), BF16),
            jax.ShapeDtypeStruct((n_gy, 3, TX // n_gy, ty, NT), BF16),
            jax.ShapeDtypeStruct((8, NT), F32),
        ],
        in_specs=[pl.BlockSpec(memory_space=pltpu.SMEM)] + vmem(9),
        out_specs=vmem(3),
        scratch_shapes=scratch,
        compiler_params=pltpu.CompilerParams(vmem_limit_bytes=58 * 2**20),
        cost_estimate=pl.CostEstimate(
            flops=3 * 10**10, bytes_accessed=10**7, transcendentals=10**6
        ),
        name="fault_and_waves",
    )(position, amplitude, xlow, xhigh, ylow, yhigh, w1, w2, w3, w4)

    everyone = jnp.broadcast_to(moments[None], (n_gx * n_gy, 8, NT))
    moments = lax.all_to_all(everyone, ("gx", "gy"), split_axis=0, concat_axis=0, tiled=True)
    waves = lax.all_to_all(waves, "gy", split_axis=0, concat_axis=0, tiled=True)
    shift_field = pl.pallas_call(
        functools.partial(combine_kernel, ty),
        out_shape=jax.ShapeDtypeStruct((TX // n_gy, grid_y, NT), F32),
        in_specs=vmem(2),
        out_specs=pl.BlockSpec(memory_space=pltpu.VMEM),
        compiler_params=pltpu.CompilerParams(vmem_limit_bytes=16 * 2**20),
        name="combine_waves",
    )(moments, waves)
    return (fault, shift_field)


def solution(mesh):
    return jax.shard_map(
        on_device,
        mesh=mesh,
        in_specs=(P("gx", "gy", None), P(), P(), P(), P()),
        out_specs=(P("gx", "gy", None), P(("gx", "gy"), None, None)),
        check_vma=False,
    )
```

time: 1010 us -> 131 us (0.13); the launches traced: 994 us -> 130 us
  local copies, waits for them, and re-layouts: 368 us -> 10.2 us
  matrix products: 200 us -> 0 us
  blocking collectives: 213 us -> 27.2 us
  other arithmetic: 84.8 us -> 0.62 us
  Pallas kernels: 0 us -> 75.8 us
  starting transfers between devices: 79.4 us -> 10.6 us
  waiting for transfers between devices: 40.5 us -> 4.82 us
    psum x5 -> x0, blocking collectives: 213 us -> none  [the longest x3 125 us: resid_product(): return lax.psum(jnp.sum(residual * precond), ('gx', 'gy'))]
    conv_general_dilated x4 -> x0, matrix products: 200 us -> none  [valid_conv(): lax.conv_general_dilated(widened[None], weight, (1, 1, 1), ((0, 0), (0, 0...]
    conv_general_dilated x10 -> x0, local copies, waits for them, and re-layouts: 123 us -> none  [valid_conv(): lax.conv_general_dilated(widened[None], weight, (1, 1, 1), ((0, 0), (0, 0...]
    slice x20 -> x4, local copies, waits for them, and re-layouts: 86.3 us -> 1.68 us  [the longest x1 0.88 us: on_device(): xhigh = shift(amplitude[:H], 'gx', n_gx, -1)]
    convert_element_type x6 -> x0, local copies, waits for them, and re-layouts: 80.7 us -> none  [on_device(): jax.nn.relu(convolve_tile(activation, weight)).astype(jnp.bfloat16)]
    pallas_call x0 -> x3, Pallas kernels: none -> 75.8 us  [the longest x1 73.9 us: on_device(): pl.pallas_call(functools.partial(main_kernel, grid_x, grid_y, ty), out_sh...]
    ppermute x26 -> x4, starting transfers between devices: 70.5 us -> 10.6 us  [shift(): return lax.ppermute(values, axis, pairs)]
    broadcast_in_dim x4 -> x0, other arithmetic: 53.2 us -> none  [valid_conv(): widened[None]]
  transfers between devices with their start and end apart: 28 -> 4, of which waited for: 13 -> 2; matrix products, arithmetic and copies ran while one was open for 23% -> 4% of each run, Pallas kernels for 0% -> 1%
where the time goes in v1:
time: 131 us; the launch traced here: 130 us
  Pallas kernels  75.8 us (58%)
  blocking collectives  27.2 us (21%)
  starting transfers between devices  10.6 us (8%)
  local copies, waits for them, and re-layouts  10.2 us (8%)
  waiting for transfers between devices  4.82 us (4%)
    pallas_call x1, Pallas kernels, on_device(): pl.pallas_call(functools.partial(main_kernel, grid_x, grid_y, ty), out_sh...  73.9 us
    all_to_all x1, blocking collectives, on_device(): waves = lax.all_to_all(waves, 'gy', split_axis=0, concat_axis=0, tiled=True)  14.7 us
    all_to_all x1, blocking collectives, on_device(): lax.all_to_all(everyone, ('gx', 'gy'), split_axis=0, concat_axis=0, tiled...  12.5 us
    ppermute x4, starting transfers between devices, shift(): return lax.ppermute(values, axis, pairs)  10.6 us
    ppermute x4, waiting for transfers between devices, shift(): return lax.ppermute(values, axis, pairs)  4.82 us
    unnamed x16, local copies, waits for them, and re-layouts  4.27 us
  transfers between devices with their start and end apart: 4, of which 2 were waited for; matrix products, arithmetic and copies ran while one was open for 4% of the time, Pallas kernels for 1%

profile of v1, /device:TPU:0, one launch (start us, length us, event | category | flops | bytes accessed | tf_op | source)
XLA Modules:
  0.0 130.0 jit_solution(2056749869395508467)
XLA Ops:
  0.6 0.9 fusion.1
  1.5 1.3 collective-permute-start.1
  2.8 3.0 %collective-permute-start = (bf16[8,32,128]{2,1,0:T(8,128)(2,1)S(1)}, bf16[8,32,128]{2,1,0:T(8,128)(2,1)S(1)}, u32[]{:S(2)}, u32[]{:S(2)}) collective-permute-start(bf16[8,32,128]{2,1,0:T(8,128)(2,1)S(1)} %get-tuple-element.19), channel_id=1, source_target_pairs={{0,4},{4,8},{8,12},{12,16},{16,20},{20,24},{24,28},{1,5},{5,9},{9,... | collective-permute-start | bytes 196616 | tf_op jit(solution)/shard_map/ppermute | solution.py:444
  5.9 0.8 fusion
  6.6 0.7 reshape.30
  7.4 0.7 reshape.32
  8.1 1.0 copy.25
  9.1 1.0 copy.26
  10.1 0.1 concatenate.11.w_ref
  10.2 1.0 band_weights.1
  11.3 0.0 copy-start
  11.3 1.0 copy-done
  12.3 1.0 copy-done.1
  13.3 0.9 copy-done.2
  14.2 0.7 copy-done.3
  14.9 0.0 collective-permute-done.1.xhigh_ref
  14.9 0.0 collective-permute-done.xlow_ref
  15.0 0.0 copy-start.5
  15.0 4.9 %collective-permute-start.2 = (bf16[32,8,128]{2,1,0:T(8,128)(2,1)S(1)}, bf16[32,8,128]{2,1,0:T(8,128)(2,1)S(1)}, u32[]{:S(2)}, u32[]{:S(2)}) collective-permute-start(bf16[32,8,128]{2,1,0:T(8,128)(2,1)S(1)} %pad_maximum_fusion), channel_id=1, source_target_pairs={{0,1},{1,2},{2,3},{4,5},{5,6},{6,7},{8,9},{9,10},{10,11},{12,13},{... | collective-permute-start | bytes 196616 | tf_op jit(solution)/shard_map/ppermute | solution.py:444
  20.0 1.3 collective-permute-start.3
  21.3 0.6 pad_add_fusion.pos_ref
  21.9 0.4 collective-permute-done.2.ylow_ref
  22.3 4.4 %collective-permute-done.3.yhigh_ref = bf16[32,8,128]{2,1,0:T(8,128)(2,1)S(1)} collective-permute-done((bf16[32,8,128]{2,1,0:T(8,128)(2,1)S(1)}, bf16[32,8,128]{2,1,0:T(8,128)(2,1)S(1)}, u32[]{:S(2)}, u32[]{:S(2)}) %collective-permute-start.3) | collective-permute-done | bytes 65568 | tf_op jit(solution)/shard_map/ppermute | solution.py:444
  26.7 0.0 copy-done.4
  26.7 0.0 copy-done.5
  26.7 0.0 copy-done.6
  26.7 0.6 copy-done.7
  27.3 73.9 %fault_and_waves.1 = (bf16[16,32,128]{2,1,0:T(8,128)(2,1)}, bf16[4,3,4,32,128]{4,3,2,1,0:T(8,128)(2,1)}, f32[8,128]{1,0:T(8,128)}) custom-call(s32[2]{0:T(128)} %pad_add_fusion.pos_ref, bf16[16,32,128]{2,1,0:T(8,128)(2,1)} %amp_ref.1, bf16[8,32,128]{2,1,0:T(8,128)(2,1)} %copy-done.5, bf16[8,32,128]{2,1,0:T(8,128)(2,1)} %copy-done.4, ...), custom_call_target="tpu_custom_call" | custom-call | flops 30000001024 | bytes 10000000 | tf_op jit(solution)/shard_map/fault_and_waves/pallas_call | solution.py:506
  101.1 0.7 broadcast_in_dim.2
  101.8 12.5 %all_to_all.10.mom_ref = f32[32,8,128]{2,1,0:T(8,128)S(1)} all-to-all(f32[32,8,128]{2,1,0:T(8,128)S(1)} %broadcast_in_dim.2), channel_id=1, replica_groups=mesh['gx'=8,'gy'=4] {'gx','gy'}, dimensions={0} | all-to-all | bytes 262144 | tf_op jit(solution)/shard_map/all_to_all | solution.py:524
  114.3 14.7 %all_to_all.11.waves_ref = bf16[4,3,4,32,128]{4,3,2,1,0:T(8,128)(2,1)S(1)} all-to-all(bf16[4,3,4,32,128]{4,3,2,1,0:T(8,128)(2,1)} %get-tuple-element.15), channel_id=1, replica_groups=mesh['gx'=8,'gy'=4] {'gy'}, dimensions={0} | all-to-all | bytes 786432 | tf_op jit(solution)/shard_map/all_to_all | solution.py:525
  129.0 0.9 combine_waves.1
  (11 shorter events, 0.0 us)
Async XLA Ops:
  1.5 13.4 %collective-permute-start.1 = (bf16[8,32,128]{2,1,0:T(8,128)(2,1)S(1)}, bf16[8,32,128]{2,1,0:T(8,128)(2,1)S(1)}, u32[]{:S(2)}, u32[]{:S(2)}) collective-permute-start(bf16[8,32,128]{2,1,0:T(8,128)(2,1)S(1)} %get-tuple-element.18), channel_id=1, source_target_pairs={{4,0},{8,4},{12,8},{16,12},{20,16},{24,20},{28,24},{5,1},{9,5},{13... | collective-permute-start | bytes 196616 | tf_op jit(solution)/shard_map/ppermute | solution.py:444
  2.8 12.1 %collective-permute-start = (bf16[8,32,128]{2,1,0:T(8,128)(2,1)S(1)}, bf16[8,32,128]{2,1,0:T(8,128)(2,1)S(1)}, u32[]{:S(2)}, u32[]{:S(2)}) collective-permute-start(bf16[8,32,128]{2,1,0:T(8,128)(2,1)S(1)} %get-tuple-element.19), channel_id=1, source_target_pairs={{0,4},{4,8},{8,12},{12,16},{16,20},{20,24},{24,28},{1,5},{5,9},{9,... | collective-permute-start | bytes 196616 | tf_op jit(solution)/shard_map/ppermute | solution.py:444
  11.3 1.0 copy-start
  12.3 1.0 copy-start.1
  13.3 0.9 copy-start.2
  14.2 0.7 copy-start.3
  14.9 11.7 %copy-start.4 = (bf16[8,32,128]{2,1,0:T(8,128)(2,1)}, bf16[8,32,128]{2,1,0:T(8,128)(2,1)S(1)}, u32[]{:S(2)}) copy-start(bf16[8,32,128]{2,1,0:T(8,128)(2,1)S(1)} %collective-permute-done.1.xhigh_ref) | copy-start | bytes 196612
  15.0 11.7 %copy-start.5 = (bf16[8,32,128]{2,1,0:T(8,128)(2,1)}, bf16[8,32,128]{2,1,0:T(8,128)(2,1)S(1)}, u32[]{:S(2)}) copy-start(bf16[8,32,128]{2,1,0:T(8,128)(2,1)S(1)} %collective-permute-done.xlow_ref) | copy-start | bytes 196612
  15.0 7.3 %collective-permute-start.2 = (bf16[32,8,128]{2,1,0:T(8,128)(2,1)S(1)}, bf16[32,8,128]{2,1,0:T(8,128)(2,1)S(1)}, u32[]{:S(2)}, u32[]{:S(2)}) collective-permute-start(bf16[32,8,128]{2,1,0:T(8,128)(2,1)S(1)} %pad_maximum_fusion), channel_id=1, source_target_pairs={{0,1},{1,2},{2,3},{4,5},{5,6},{6,7},{8,9},{9,10},{10,11},{12,13},{... | collective-permute-start | bytes 196616 | tf_op jit(solution)/shard_map/ppermute | solution.py:444
  20.0 6.7 %collective-permute-start.3 = (bf16[32,8,128]{2,1,0:T(8,128)(2,1)S(1)}, bf16[32,8,128]{2,1,0:T(8,128)(2,1)S(1)}, u32[]{:S(2)}, u32[]{:S(2)}) collective-permute-start(bf16[32,8,128]{2,1,0:T(8,128)(2,1)S(1)} %pad_maximum_fusion.1), channel_id=1, source_target_pairs={{1,0},{2,1},{3,2},{5,4},{6,5},{7,6},{9,8},{10,9},{11,10},{13,12},{... | collective-permute-start | bytes 196616 | tf_op jit(solution)/shard_map/ppermute | solution.py:444
  22.3 4.4 %copy-start.6 = (bf16[32,8,128]{2,1,0:T(8,128)(2,1)}, bf16[32,8,128]{2,1,0:T(8,128)(2,1)S(1)}, u32[]{:S(2)}) copy-start(bf16[32,8,128]{2,1,0:T(8,128)(2,1)S(1)} %collective-permute-done.2.ylow_ref) | copy-start | bytes 196612
  26.7 0.6 copy-start.7

commit v2 on v1

v2 whole, which is shorter than its diff:
```python
import functools

import jax
import jax.numpy as jnp
from jax import lax
from jax.experimental import pallas as pl
from jax.experimental.pallas import tpu as pltpu
from jax.sharding import PartitionSpec as P

MU_DIAG = 0.05
ETA_TIME = 0.5

TX, NT, H = 16, 128, 8
CH = 16
XW = TX + 2 * H
FX = TX + 8
RX = 4
BLK = 256
SUB = 16
PAD = SUB + NT + SUB

F32 = jnp.float32
BF16 = jnp.bfloat16


def iota(shape, dim):
    return lax.broadcasted_iota(jnp.int32, shape, dim)


def dot_nt(a, b):
    return lax.dot_general(a, b, (((1,), (1,)), ((), ())), preferred_element_type=F32)


def prep_kernel(first_ref, second_ref, third_ref, last_ref, after_ref, w1_ref, w2_ref, w3_ref, w4_ref):
    del after_ref
    spread = jnp.where(iota((CH, BLK), 1) % CH == iota((CH, BLK), 0), 1.0, 0.0).astype(BF16)
    unit = jnp.where(iota((BLK, BLK), 1) == iota((BLK, BLK), 0), 1.0, 0.0).astype(BF16)
    in_pos = iota((CH, BLK), 1) // CH
    for source, ref in ((second_ref, w2_ref), (third_ref, w3_ref)):
        tiled = jnp.dot(source[...], spread, preferred_element_type=F32)
        for dy in range(3):
            for dt in range(3):
                rows = [tiled[(dx * 9 + dy * 3 + dt) * CH :][:CH] for dx in range(3)]
                bands = []
                for xo in range(16):
                    band = jnp.zeros((CH, BLK), F32)
                    for dx in range(3):
                        band = jnp.where(in_pos == xo + dx, rows[dx], band)
                    bands.append(band.astype(BF16))
                turned = dot_nt(unit, jnp.concatenate(bands, axis=0))
                ref[dy * 3 + dt] = turned.astype(BF16)

    def taps(ref):
        found = {}
        for dx in range(3):
            for dy in range(3):
                piece = ref[0, dx, dy].astype(BF16)
                tiled = jnp.dot(piece, spread, preferred_element_type=F32)
                for dt in range(3):
                    found[dx, dy, dt] = tiled[dt : dt + 1]
        return found

    first, last = taps(first_ref), taps(last_ref)
    row_pos = iota((XW, BLK), 0)
    lane_pos = iota((XW, BLK), 1) // CH
    for dt in range(3):
        for yi in range(4):
            for yo in range(2):
                for blk in range(2):
                    band = jnp.zeros((XW, BLK), F32)
                    dy = yi - yo
                    if 0 <= dy <= 2:
                        for dx in range(3):
                            band = jnp.where(
                                row_pos - 14 * blk - lane_pos == dx, first[dx, dy, dt], band
                            )
                    w1_ref[
                        dt * 128 + yi * XW : dt * 128 + (yi + 1) * XW,
                        yo * 512 + blk * BLK : yo * 512 + (blk + 1) * BLK,
                    ] = band.astype(BF16)
    row_pos = iota((FX, BLK), 0)
    lane_pos = iota((FX, BLK), 1) // CH
    for blk in range(2):
        pieces = []
        for dy in range(3):
            for dt in range(3):
                band = jnp.zeros((FX, BLK), F32)
                for dx in range(3):
                    band = jnp.where(14 * blk + lane_pos - row_pos == dx, last[dx, dy, dt], band)
                pieces.append(jnp.where(lane_pos < 14 - 2 * blk, band, 0.0))
        pieces = jnp.concatenate(pieces, axis=0)
        w4_ref[:, blk * BLK : (blk + 1) * BLK] = pieces.astype(BF16)


def main_kernel(
    grid_x,
    grid_y,
    ty,
    amp_ref,
    xlow_ref,
    xhigh_ref,
    ylow_ref,
    yhigh_ref,
    w1_ref,
    w2_ref,
    w3_ref,
    w4_ref,
    *refs,
):
    n_gy = grid_y // ty
    fault_ref, mom_ref = refs[:2]
    waves_refs = refs[2 : 2 + n_gy]
    (raw, amp, act1, act2, act3, part, prob, prod, slope, weight, face, flux, inv, wave) = refs[
        2 + n_gy :
    ]
    place_y = lax.axis_index("gy")
    x0 = lax.axis_index("gx") * TX
    y0 = place_y * ty
    yw = ty + 2 * H
    dot = functools.partial(jnp.dot, preferred_element_type=F32)

    def inside_y(y):
        at = y0 + y
        return jnp.where((at >= 0) & (at < grid_y), 1.0, 0.0).astype(F32)

    def lane_mask(start):
        masks = []
        for blk in range(2):
            at = x0 + start + 14 * blk + iota((1, BLK), 1) // CH
            masks.append(jnp.where((at >= 0) & (at < grid_x), 1.0, 0.0).astype(F32))
        return masks

    for x in range(XW):
        row = x * yw
        if x < H:
            mid = xlow_ref[x]
        elif x < H + TX:
            mid = amp_ref[x - H]
        else:
            mid = xhigh_ref[x - H - TX]
        raw[row + H : row + H + ty, :] = mid.astype(F32)
        raw[row : row + H, :] = ylow_ref[x].astype(F32)
        raw[row + H + ty : row + yw, :] = yhigh_ref[x].astype(F32)

    def turn(y, carry):
        amp[y] = raw[pl.ds(y, XW, stride=yw), :]
        return carry

    lax.fori_loop(0, yw, turn, 0, unroll=8)
    amp[yw] = jnp.zeros((XW, NT), F32)
    amp[yw + 1] = jnp.zeros((XW, NT), F32)

    tiled_row = iota((NT, NT), 0)
    natural = tiled_row // SUB + (tiled_row % SUB) * 8
    to_tiles = jnp.concatenate(
        [
            jnp.where(iota((NT, NT), 1) == natural + dt - 1, 1.0, 0.0).astype(BF16)
            for dt in range(3)
        ],
        axis=0,
    )
    from_tiles = jnp.concatenate(
        [
            jnp.where(iota((NT, NT), 1) + dt - 1 == natural, 1.0, 0.0).astype(BF16)
            for dt in range(3)
        ],
        axis=0,
    )
    sub_row = iota((SUB, BLK), 0)

    def put(act, y, blk, values):
        act[y, blk, SUB : SUB + NT, :] = values.astype(BF16)
        before = jnp.where(sub_row == 0, 0.0, pltpu.roll(values[NT - SUB :], 1, 0))
        after = jnp.where(sub_row == SUB - 1, 0.0, pltpu.roll(values[:SUB], SUB - 1, 0))
        act[y, blk, 0:SUB, :] = before.astype(BF16)
        act[y, blk, SUB + NT :, :] = after.astype(BF16)

    mask1 = lane_mask(-7)

    def first(step, carry):
        pieces = []
        for half in range(2):
            y = step * 4 + half * 2
            rows = amp[pl.ds(y, 4)].reshape(4 * XW, NT).astype(BF16)
            turned = dot_nt(to_tiles, rows).astype(BF16)
            pieces.append(
                jnp.concatenate([turned[:NT], turned[NT : 2 * NT], turned[2 * NT :]], axis=1)
            )
        result = dot(jnp.concatenate(pieces, axis=0), w1_ref[...])
        for half in range(2):
            for yo in range(2):
                y = step * 4 + half * 2 + yo
                ok = inside_y(y - 7)
                for blk in range(2):
                    lane = yo * 512 + blk * BLK
                    values = result[half * NT : (half + 1) * NT, lane : lane + BLK]
                    put(act1, y, blk, jnp.maximum(values, 0.0) * (mask1[blk] * ok))
        return carry

    lax.fori_loop(0, yw // 4, first, 0)

    def layer(source, w_ref, y, count):
        taps = []
        for dy in range(3):
            for dt in range(3):
                part_in = source[pl.ds(y + dy, count), :, SUB * dt : SUB * dt + NT, :]
                taps.append(part_in.reshape(count * 2 * NT, BLK))
        return dot(jnp.concatenate(taps, axis=1), w_ref[...].reshape(9 * BLK, BLK))

    mask2 = lane_mask(-6)
    lane_half = iota((NT, 128), 1)

    def second(step, carry):
        y = step * 4
        result = layer(act1, w2_ref, y, 4)
        for row in range(4):
            ok = inside_y(y + row - 6)
            low = result[row * 2 * NT : row * 2 * NT + NT]
            high = result[row * 2 * NT + NT : (row + 1) * 2 * NT]
            moved = jnp.where(lane_half >= 96, pltpu.roll(high[:, :128], 96, 1), low[:, 128:])
            low = jnp.concatenate([low[:, :128], moved], axis=1)
            put(act2, y + row, 0, jnp.maximum(low, 0.0) * (mask2[0] * ok))
            put(act2, y + row, 1, jnp.maximum(high, 0.0) * (mask2[1] * ok))
        return carry

    lax.fori_loop(0, (ty + 12) // 4, second, 0)

    mask3 = lane_mask(-5)

    def third(step, carry):
        y = step * 3
        result = layer(act2, w3_ref, y, 3)
        for row in range(3):
            ok = inside_y(y + row - 5)
            for blk in range(2):
                at = (row * 2 + blk) * NT
                values = jnp.maximum(result[at : at + NT], 0.0) * (mask3[blk] * ok)
                act3[y + row, :, blk * BLK : (blk + 1) * BLK] = values.astype(BF16)
        return carry

    lax.fori_loop(0, (ty + 10) // 3, third, 0)

    def fourth(step, carry):
        y = step * 3
        result = dot_nt(w4_ref[...], act3[pl.ds(y, 3)].reshape(3 * NT, 2 * BLK))
        for row in range(3):
            part[y + row] = result[:, row * NT : (row + 1) * NT]
        return carry

    lax.fori_loop(0, (ty + 10) // 3, fourth, 0)

    for x in range(FX):
        prob[x * yw : x * yw + H, :] = jnp.zeros((H, NT), F32)
        prob[(x + 1) * yw - H : (x + 1) * yw, :] = jnp.zeros((H, NT), F32)

    def order(step, carry):
        sums = []
        for row in range(8):
            y = step * 8 + row
            total = (
                part[y, 0 : 3 * FX] + part[y + 1, 3 * FX : 6 * FX] + part[y + 2, 6 * FX : 9 * FX]
            )
            sums.append(jnp.concatenate([total[i * FX : (i + 1) * FX] for i in range(3)], axis=1))
        sums = jnp.concatenate(sums, axis=0)
        high = sums.astype(BF16)
        low = (sums - high.astype(F32)).astype(BF16)
        both = dot(jnp.concatenate([high, low], axis=0), from_tiles)
        values = both[: 8 * FX] + both[8 * FX :]
        values = (1.0 / (1.0 + jnp.exp(-values))).astype(BF16).astype(F32)
        for row in range(8):
            prob[pl.ds(step * 8 + row + 4, FX, stride=yw), :] = values[row * FX : (row + 1) * FX]
        return carry

    lax.fori_loop(0, (ty + 8) // 8, order, 0)

    block = (RX, yw, NT)
    lane = iota(block, 2)
    first_lane = lane == 0
    last_lane = lane == NT - 1

    def up_y(v):
        return pltpu.roll(v, yw - 1, 1)

    def down_y(v):
        return pltpu.roll(v, 1, 1)

    def up_t(v, edge=0.0):
        return jnp.where(last_lane, edge, pltpu.roll(v, NT - 1, 2))

    def down_t(v, edge=0.0):
        return jnp.where(first_lane, edge, pltpu.roll(v, 1, 2))

    def smooth_yt(v, edge=0.0):
        v = 0.5 * v + 0.25 * (up_t(v, edge) + down_t(v, edge))
        return 0.5 * v + 0.25 * (up_y(v) + down_y(v))

    def amp_rows(x):
        return raw[pl.ds(pl.multiple_of(x * yw, 8), RX * yw), :].reshape(block)

    def products(step, carry):
        k = step * RX
        here = amp_rows(k + 3)
        grad_x = 0.5 * (amp_rows(k + 4) - amp_rows(k + 2))
        grad_y = 0.5 * (up_y(here) - down_y(here))
        grad_t = 0.5 * (up_t(here) - down_t(here))
        at = pl.ds(k, RX)
        prod[0, at] = smooth_yt(grad_x * grad_t)
        prod[1, at] = smooth_yt(grad_y * grad_t)
        energy = grad_t * grad_t + 0.25 * (grad_x * grad_x + grad_y * grad_y)
        prod[2, at] = smooth_yt(energy, 0.25 * here * here)
        return carry

    lax.fori_loop(0, (FX + 2 + RX - 1) // RX, products, 0)

    at_y = y0 - H + iota(block, 1)
    mask_y = (at_y >= 0) & (at_y < grid_y)

    def fields(step, carry):
        k = step * RX
        at = pl.ds(k + 1, RX)
        sums = []
        for which in range(3):
            before, here, after = [prod[which, pl.ds(k + i, RX)] for i in range(3)]
            sums.append(0.5 * here + 0.25 * (before + after))
        scale = -1.0 / (sums[2] + 0.05)
        slope[0, at] = sums[0] * scale
        slope[1, at] = sums[1] * scale
        rows = prob[pl.ds(pl.multiple_of(k * yw, 8), RX * yw), :].reshape(block)
        raw_weight = 1.0 - 0.9 * rows
        at_x = x0 - 4 + k + iota(block, 0)
        weight[0, at] = raw_weight
        weight[1, at] = jnp.where(mask_y & (at_x >= 0) & (at_x < grid_x), raw_weight, 0.0)
        return carry

    lax.fori_loop(0, FX // RX, fields, 0)
    for which in range(2):
        slope[which, FX + 1] = jnp.zeros((yw, NT), F32)
        weight[which, FX + 1] = jnp.full((yw, NT), 1.0 - which, F32)
        face[which, 0] = jnp.zeros((yw, NT), F32)
        flux[which, 0] = jnp.zeros((yw, NT), F32)

    def faces(step, carry):
        k = step * RX + 1
        at, after = pl.ds(k, RX), pl.ds(k + 1, RX)
        raw_weight = weight[0, at]
        masked = weight[1, at]
        face_x = 2.0 * masked * weight[1, after] / (raw_weight + weight[0, after])
        face_y = 2.0 * masked * up_y(masked) / (raw_weight + up_y(raw_weight))
        slope_y = slope[1, at]
        face[0, at] = face_x
        face[1, at] = face_y
        flux[0, at] = 0.5 * face_x * (slope[0, at] + slope[0, after])
        flux[1, at] = 0.5 * face_y * (slope_y + up_y(slope_y))
        return carry

    lax.fori_loop(0, FX // RX, faces, 0)

    time_part = MU_DIAG + ETA_TIME * (
        jnp.where(first_lane, 0.0, 1.0) + jnp.where(last_lane, 0.0, 1.0)
    )

    def owned(total, k, values):
        for row in range(RX):
            ok = (k + row >= 5) & (k + row < 5 + TX)
            total = total + jnp.where(ok, values[row, H : H + ty], 0.0)
        return total

    def start(step, total):
        k = step * RX + 1
        at, before = pl.ds(k, RX), pl.ds(k - 1, RX)
        flux_y = flux[1, at]
        face_y = face[1, at]
        right = flux[0, before] - flux[0, at] + down_y(flux_y) - flux_y
        inverse = 1.0 / (time_part + face[0, at] + face[0, before] + face_y + down_y(face_y))
        first_wave = right * inverse
        inv[at] = inverse
        wave[0, at] = first_wave
        return owned(total, k, right * first_wave)

    zero = jnp.zeros((ty, NT), F32)
    b0 = lax.fori_loop(0, FX // RX, start, zero)

    def apply(which, k):
        at, before, after = [pl.ds(k + i, RX) for i in (0, -1, 1)]
        here = wave[which, at]
        flow = face[1, at] * (here - up_y(here))
        image = time_part * here - ETA_TIME * (up_t(here) + down_t(here))
        image = image + flow - down_y(flow)
        image = image + face[0, at] * (here - wave[which, after])
        return here, image + face[0, before] * (here - wave[which, before])

    def advance(which):
        def body(step, totals):
            k = step * RX + 3
            here, image = apply(which, k)
            at = pl.ds(k, RX)
            after = here - image * inv[at]
            wave[which + 1, at] = after
            return owned(totals[0], k, here * image), owned(totals[1], k, after * image)

        return body

    steps = (FX - 4) // RX
    a0, a1 = lax.fori_loop(0, steps, advance(0), (zero, zero))
    a2, a3 = lax.fori_loop(0, steps, advance(1), (zero, zero))

    def finish(step, total):
        k = step * RX + 5
        here, image = apply(2, k)
        return owned(total, k, here * image)

    a4 = lax.fori_loop(0, TX // RX, finish, zero)

    sums = [jnp.sum(v, axis=0, keepdims=True) for v in (b0, a0, a1, a2, a3, a4)]
    mom_ref[...] = jnp.concatenate(sums + [jnp.zeros((2, NT), F32)], axis=0)

    for x in range(TX):
        fault_ref[x] = prob[(x + 4) * yw + H : (x + 4) * yw + H + ty, :].astype(BF16)
    rows = TX // n_gy
    for place, ref in enumerate(waves_refs):
        to = lax.rem(place_y + place, n_gy) * rows + 5
        for which in range(3):
            for row in range(rows):
                ref[which, row] = wave[which, to + row, H : H + ty, :].astype(BF16)


def combine_kernel(n_gy, ty, mom_ref, *refs):
    waves_refs, out_ref = refs[:n_gy], refs[n_gy]
    place_y = lax.axis_index("gy")
    moments = jnp.sum(jnp.sum(mom_ref[...], axis=0), axis=1, keepdims=True)
    b0, a0, a1, a2, a3, a4 = [
        jnp.broadcast_to(moments[i : i + 1], (1, NT)) for i in range(6)
    ]
    a0, a1, a2, a3, a4 = [v / b0 for v in (a0, a1, a2, a3, a4)]
    l21 = a1 / a0
    l31 = a2 / a0
    d2 = jnp.maximum(a2 - l21 * a1, 1e-7 * a2 + 1e-30)
    l32 = (a3 - l21 * a2) / d2
    d3 = jnp.maximum(a4 - l31 * a2 - l32 * l32 * d2, 1e-7 * a4 + 1e-30)
    y2 = (1.0 - a0) - l21
    y3 = (1.0 - a0 - a1) - l31 - l32 * y2
    c3 = y3 / d3
    c2 = y2 / d2 - l32 * c3
    c1 = 1.0 / a0 - l21 * c2 - l31 * c3
    for place, ref in enumerate(waves_refs):
        source = lax.rem(place_y - place + n_gy, n_gy)
        at = pl.ds(pl.multiple_of(source * ty, 8), ty)
        for x in range(ref.shape[1]):
            w0, w1, w2 = [ref[which, x].astype(F32) for which in range(3)]
            out_ref[x, at, :] = c1 * w0 + c2 * w1 + c3 * w2


def vmem(count):
    return [pl.BlockSpec(memory_space=pltpu.VMEM)] * count


def on_device(amplitude, conv_first, conv_second, conv_third, conv_last):
    n_gx, n_gy = lax.axis_size("gx"), lax.axis_size("gy")
    ty = amplitude.shape[1]
    grid_x, grid_y = n_gx * TX, n_gy * ty
    assert amplitude.shape == (TX, ty, NT)

    def shift(values, axis, count, step):
        pairs = [(i, i + step) for i in range(count) if 0 <= i + step < count]
        return lax.ppermute(values, axis, pairs)

    xlow = shift(amplitude[TX - H :], "gx", n_gx, 1)
    xhigh = shift(amplitude[:H], "gx", n_gx, -1)
    ylow = shift(
        jnp.concatenate([xlow[:, ty - H :], amplitude[:, ty - H :], xhigh[:, ty - H :]]),
        "gy",
        n_gy,
        1,
    )
    yhigh = shift(
        jnp.concatenate([xlow[:, :H], amplitude[:, :H], xhigh[:, :H]]), "gy", n_gy, -1
    )

    def taps_first(weight):
        return jnp.transpose(weight, (2, 3, 4, 0, 1))

    w1, w2, w3, w4 = pl.pallas_call(
        prep_kernel,
        out_shape=[
            jax.ShapeDtypeStruct((3 * 4 * XW, 4 * BLK), BF16),
            jax.ShapeDtypeStruct((9, BLK, BLK), BF16),
            jax.ShapeDtypeStruct((9, BLK, BLK), BF16),
            jax.ShapeDtypeStruct((9 * FX, 2 * BLK), BF16),
        ],
        in_specs=vmem(4) + [pl.BlockSpec(memory_space=pl.ANY)],
        out_specs=vmem(4),
        compiler_params=pltpu.CompilerParams(vmem_limit_bytes=16 * 2**20),
        cost_estimate=pl.CostEstimate(flops=10**9, bytes_accessed=10**7, transcendentals=0),
        name="band_weights",
    )(
        jnp.transpose(conv_first, (1, 2, 3, 4, 0)),
        taps_first(conv_second).reshape(27 * CH, CH),
        taps_first(conv_third).reshape(27 * CH, CH),
        jnp.transpose(conv_last, (0, 2, 3, 4, 1)),
        xlow,
    )

    yw, nf = ty + 2 * H, FX + 2
    scratch = [
        pltpu.VMEM(((XW + 2) * yw, NT), F32),
        pltpu.VMEM((yw + 2, XW, NT), F32),
        pltpu.VMEM((yw, 2, PAD, BLK), BF16),
        pltpu.VMEM((ty + 12, 2, PAD, BLK), BF16),
        pltpu.VMEM((ty + 10, NT, 2 * BLK), BF16),
        pltpu.VMEM((ty + 10, 9 * FX, NT), F32),
        pltpu.VMEM((FX * yw, NT), F32),
        pltpu.VMEM((3, FX + 4, yw, NT), F32),
        pltpu.VMEM((2, nf, yw, NT), F32),
        pltpu.VMEM((2, nf, yw, NT), F32),
        pltpu.VMEM((2, nf, yw, NT), F32),
        pltpu.VMEM((2, nf, yw, NT), F32),
        pltpu.VMEM((nf, yw, NT), F32),
        pltpu.VMEM((3, nf, yw, NT), F32),
    ]
    rows = TX // n_gy
    fault, moments, *waves = pl.pallas_call(
        functools.partial(main_kernel, grid_x, grid_y, ty),
        out_shape=[
            jax.ShapeDtypeStruct((TX, ty, NT), BF16),
            jax.ShapeDtypeStruct((8, NT), F32),
        ]
        + [jax.ShapeDtypeStruct((3, rows, ty, NT), BF16)] * n_gy,
        in_specs=vmem(9),
        out_specs=vmem(2 + n_gy),
        scratch_shapes=scratch,
        compiler_params=pltpu.CompilerParams(vmem_limit_bytes=48 * 2**20),
        cost_estimate=pl.CostEstimate(
            flops=3 * 10**10, bytes_accessed=10**7, transcendentals=10**6
        ),
        name="fault_and_waves",
    )(amplitude, xlow, xhigh, ylow, yhigh, w1, w2, w3, w4)

    arrived = [waves[0]]
    for place in range(1, n_gy):
        pairs = [(i, (i + place) % n_gy) for i in range(n_gy)]
        arrived.append(lax.ppermute(waves[place], "gy", pairs))
    moments = lax.all_gather(moments, ("gx", "gy"), axis=0, tiled=False)
    shift_field = pl.pallas_call(
        functools.partial(combine_kernel, n_gy, ty),
        out_shape=jax.ShapeDtypeStruct((rows, grid_y, NT), F32),
        in_specs=vmem(1 + n_gy),
        out_specs=pl.BlockSpec(memory_space=pltpu.VMEM),
        compiler_params=pltpu.CompilerParams(vmem_limit_bytes=16 * 2**20),
        name="combine_waves",
    )(moments, *arrived)
    return (fault, shift_field)


def solution(mesh):
    return jax.shard_map(
        on_device,
        mesh=mesh,
        in_specs=(P("gx", "gy", None), P(), P(), P(), P()),
        out_specs=(P("gx", "gy", None), P(("gx", "gy"), None, None)),
        check_vma=False,
    )
```

time: 131 us -> 144 us (1.099)
  blocking collectives: 27.2 us -> 66.4 us
  Pallas kernels: 75.8 us -> 53.6 us
  starting transfers between devices: 10.6 us -> 16.9 us
  local copies, waits for them, and re-layouts: 10.2 us -> 4.87 us
  waiting for transfers between devices: 4.82 us -> 0.31 us
    all_gather x0 -> x1, blocking collectives: none -> 66.4 us  [on_device(): moments = lax.all_gather(moments, ('gx', 'gy'), axis=0, tiled=False)]
    all_to_all x2 -> x0, blocking collectives: 27.2 us -> none  [the longest x1 14.7 us: on_device(): waves = lax.all_to_all(waves, 'gy', split_axis=0, concat_axis=0, tiled=True)]
    pallas_call x1, Pallas kernels: 73.9 us -> 50.8 us  [on_device(): pl.pallas_call(functools.partial(main_kernel, grid_x, grid_y, ty), out_sh...]
    ppermute x0 -> x3, starting transfers between devices: none -> 6.37 us  [on_device(): arrived.append(lax.ppermute(waves[place], 'gy', pairs))]
    ppermute x4, waiting for transfers between devices: 4.82 us -> 0.3 us  [shift(): return lax.ppermute(values, axis, pairs)]
    reshape x4 -> x0, local copies, waits for them, and re-layouts: 3.44 us -> none  [the longest x1 1.01 us: on_device(): by_tap(conv_third).reshape(27 * CH, CH)]
    unnamed x16 -> x10, local copies, waits for them, and re-layouts: 4.27 us -> 3.19 us
  transfers between devices with their start and end apart: 4 -> 7, of which waited for: 2 -> 2; matrix products, arithmetic and copies ran while one was open for 4% -> 1% of each run, Pallas kernels for 1% -> 1%
where the time goes in v2:
time: 144 us; the launch traced here: 143 us
  blocking collectives  66.4 us (46%)
  Pallas kernels  53.6 us (37%)
  starting transfers between devices  16.9 us (12%)
  local copies, waits for them, and re-layouts  4.87 us (3%)
    all_gather x1, blocking collectives, on_device(): moments = lax.all_gather(moments, ('gx', 'gy'), axis=0, tiled=False)  66.4 us
    pallas_call x1, Pallas kernels, on_device(): pl.pallas_call(functools.partial(main_kernel, grid_x, grid_y, ty), out_sh...  50.8 us
    ppermute x4, starting transfers between devices, shift(): return lax.ppermute(values, axis, pairs)  10.5 us
    ppermute x3, starting transfers between devices, on_device(): arrived.append(lax.ppermute(waves[place], 'gy', pairs))  6.37 us
    unnamed x10, local copies, waits for them, and re-layouts  3.19 us
  transfers between devices with their start and end apart: 7, of which 2 were waited for; matrix products, arithmetic and copies ran while one was open for 1% of the time, Pallas kernels for 1%

profile of v2, /device:TPU:0, one launch (start us, length us, event | category | flops | bytes accessed | tf_op | source)
XLA Modules:
  0.0 142.8 jit_solution(15066598091048346485)
XLA Ops:
  0.6 0.9 fusion.1
  1.5 1.3 collective-permute-start.1
  2.8 3.0 %collective-permute-start = (bf16[8,32,128]{2,1,0:T(8,128)(2,1)S(1)}, bf16[8,32,128]{2,1,0:T(8,128)(2,1)S(1)}, u32[]{:S(2)}, u32[]{:S(2)}) collective-permute-start(bf16[8,32,128]{2,1,0:T(8,128)(2,1)S(1)} %get-tuple-element.25), channel_id=1, source_target_pairs={{0,4},{4,8},{8,12},{12,16},{16,20},{20,24},{24,28},{1,5},{5,9},{9,... | collective-permute-start | bytes 196616 | tf_op jit(solution)/shard_map/ppermute | solution.py:465
  5.9 0.8 fusion
  6.6 0.0 collective-permute-done.1.xhigh_ref
  6.7 0.1 collective-permute-done.after_ref.xlow_ref
  6.8 4.9 %collective-permute-start.2 = (bf16[32,8,128]{2,1,0:T(8,128)(2,1)S(1)}, bf16[32,8,128]{2,1,0:T(8,128)(2,1)S(1)}, u32[]{:S(2)}, u32[]{:S(2)}) collective-permute-start(bf16[32,8,128]{2,1,0:T(8,128)(2,1)S(1)} %pad_maximum_fusion), channel_id=1, source_target_pairs={{0,1},{1,2},{2,3},{4,5},{5,6},{6,7},{8,9},{9,10},{10,11},{12,13},{... | collective-permute-start | bytes 196616 | tf_op jit(solution)/shard_map/ppermute | solution.py:465
  11.7 1.3 collective-permute-start.3
  13.0 0.0 copy-start.1
  13.0 0.9 copy-done.1
  13.9 0.0 copy-start.2
  13.9 0.9 copy-done.2
  14.8 0.0 copy-start.3
  14.8 0.7 copy-done.3
  15.5 0.0 copy-start.4
  15.5 0.7 copy-done.4
  16.2 0.0 copy-start
  16.2 1.8 %band_weights.1 = (bf16[384,1024]{1,0:T(8,128)(2,1)S(1)}, bf16[9,256,256]{2,1,0:T(8,128)(2,1)S(1)}, bf16[9,256,256]{2,1,0:T(8,128)(2,1)S(1)}, bf16[216,512]{1,0:T(8,128)(2,1)S(1)}) custom-call(bf16[1,3,3,3,16]{4,3,2,1,0:T(4,128)(2,1)S(1)} %bitcast.12, bf16[432,16]{1,0:T(8,128)(2,1)S(1)} %bitcast.10, bf16[432,16]{1,0:T(8,128)(2,1)S(1)} %bitcast.11, ...), custom_call_target="tpu_custom_call" | custom-call | flops 1000000000 | bytes 10000000 | tf_op jit(solution)/shard_map/band_weights/pallas_call | solution.py:482
  18.1 0.0 collective-permute-done.2.ylow_ref
  18.1 0.2 collective-permute-done.3.yhigh_ref
  18.3 0.0 copy-done
  18.3 50.8 %fault_and_waves.1 = (bf16[16,32,128]{2,1,0:T(8,128)(2,1)}, f32[8,128]{1,0:T(8,128)S(1)}, bf16[3,4,32,128]{3,2,1,0:T(8,128)(2,1)S(1)}, bf16[3,4,32,128]{3,2,1,0:...) custom-call(bf16[16,32,128]{2,1,0:T(8,128)(2,1)S(1)} %copy-done, ...), custom_call_target="tpu_custom_call" | custom-call | flops 30000001024 | bytes 10000000 | tf_op jit(solution)/shard_map/fault_and_waves/pallas_call | solution.py:521
  69.1 2.4 %collective-permute-start.4 = (bf16[3,4,32,128]{3,2,1,0:T(8,128)(2,1)S(1)}, bf16[3,4,32,128]{3,2,1,0:T(8,128)(2,1)S(1)}, u32[]{:S(2)}, u32[]{:S(2)}) collective-permute-start(bf16[3,4,32,128]{3,2,1,0:T(8,128)(2,1)S(1)} %get-tuple-element.19), channel_id=1, source_target_pairs={{0,1},{1,2},{2,3},{3,0},{4,5},{5,6},{6,7},{7,4},{8,9},{9,10},{10,1... | collective-permute-start | bytes 294920 | tf_op jit(solution)/shard_map/ppermute | solution.py:541
  71.5 2.6 %collective-permute-start.5 = (bf16[3,4,32,128]{3,2,1,0:T(8,128)(2,1)S(1)}, bf16[3,4,32,128]{3,2,1,0:T(8,128)(2,1)S(1)}, u32[]{:S(2)}, u32[]{:S(2)}) collective-permute-start(bf16[3,4,32,128]{3,2,1,0:T(8,128)(2,1)S(1)} %get-tuple-element.20), channel_id=1, source_target_pairs={{0,2},{1,3},{2,0},{3,1},{4,6},{5,7},{6,4},{7,5},{8,10},{9,11},{10,... | collective-permute-start | bytes 294920 | tf_op jit(solution)/shard_map/ppermute | solution.py:541
  74.1 1.3 collective-permute-start.6
  75.5 66.4 %all-gather = f32[256,128]{1,0:T(8,128)S(1)} all-gather(f32[8,128]{1,0:T(8,128)S(1)} %get-tuple-element.17), channel_id=2, replica_groups=mesh['gx'=8,'gy'=4] {'gx','gy'}, dimensions={0}, use_global_device_ids=true | all-gather | bytes 135168 | tf_op jit(solution)/shard_map/all_gather | solution.py:542
  141.9 0.0 collective-permute-done.4.refs_1_
  141.9 0.0 collective-permute-done.5.refs_2_
  141.9 0.0 collective-permute-done.6.refs_3_
  141.9 0.9 combine_waves.1
  (4 shorter events, 0.0 us)
Async XLA Ops:
  1.5 5.1 %collective-permute-start.1 = (bf16[8,32,128]{2,1,0:T(8,128)(2,1)S(1)}, bf16[8,32,128]{2,1,0:T(8,128)(2,1)S(1)}, u32[]{:S(2)}, u32[]{:S(2)}) collective-permute-start(bf16[8,32,128]{2,1,0:T(8,128)(2,1)S(1)} %get-tuple-element.24), channel_id=1, source_target_pairs={{4,0},{8,4},{12,8},{16,12},{20,16},{24,20},{28,24},{5,1},{9,5},{13... | collective-permute-start | bytes 196616 | tf_op jit(solution)/shard_map/ppermute | solution.py:465
  2.8 3.9 %collective-permute-start = (bf16[8,32,128]{2,1,0:T(8,128)(2,1)S(1)}, bf16[8,32,128]{2,1,0:T(8,128)(2,1)S(1)}, u32[]{:S(2)}, u32[]{:S(2)}) collective-permute-start(bf16[8,32,128]{2,1,0:T(8,128)(2,1)S(1)} %get-tuple-element.25), channel_id=1, source_target_pairs={{0,4},{4,8},{8,12},{12,16},{16,20},{20,24},{24,28},{1,5},{5,9},{9,... | collective-permute-start | bytes 196616 | tf_op jit(solution)/shard_map/ppermute | solution.py:465
  6.8 11.3 %collective-permute-start.2 = (bf16[32,8,128]{2,1,0:T(8,128)(2,1)S(1)}, bf16[32,8,128]{2,1,0:T(8,128)(2,1)S(1)}, u32[]{:S(2)}, u32[]{:S(2)}) collective-permute-start(bf16[32,8,128]{2,1,0:T(8,128)(2,1)S(1)} %pad_maximum_fusion), channel_id=1, source_target_pairs={{0,1},{1,2},{2,3},{4,5},{5,6},{6,7},{8,9},{9,10},{10,11},{12,13},{... | collective-permute-start | bytes 196616 | tf_op jit(solution)/shard_map/ppermute | solution.py:465
  11.7 6.6 %collective-permute-start.3 = (bf16[32,8,128]{2,1,0:T(8,128)(2,1)S(1)}, bf16[32,8,128]{2,1,0:T(8,128)(2,1)S(1)}, u32[]{:S(2)}, u32[]{:S(2)}) collective-permute-start(bf16[32,8,128]{2,1,0:T(8,128)(2,1)S(1)} %pad_maximum_fusion.1), channel_id=1, source_target_pairs={{1,0},{2,1},{3,2},{5,4},{6,5},{7,6},{9,8},{10,9},{11,10},{13,12},{... | collective-permute-start | bytes 196616 | tf_op jit(solution)/shard_map/ppermute | solution.py:465
  13.0 0.9 copy-start.1
  13.9 0.9 copy-start.2
  14.8 0.7 copy-start.3
  15.5 0.7 copy-start.4
  16.2 2.1 %copy-start = (bf16[16,32,128]{2,1,0:T(8,128)(2,1)S(1)}, bf16[16,32,128]{2,1,0:T(8,128)(2,1)}, u32[]{:S(2)}) copy-start(bf16[16,32,128]{2,1,0:T(8,128)(2,1)} %amp_ref.1) | copy-start | bytes 393220
  69.1 72.8 %collective-permute-start.4 = (bf16[3,4,32,128]{3,2,1,0:T(8,128)(2,1)S(1)}, bf16[3,4,32,128]{3,2,1,0:T(8,128)(2,1)S(1)}, u32[]{:S(2)}, u32[]{:S(2)}) collective-permute-start(bf16[3,4,32,128]{3,2,1,0:T(8,128)(2,1)S(1)} %get-tuple-element.19), channel_id=1, source_target_pairs={{0,1},{1,2},{2,3},{3,0},{4,5},{5,6},{6,7},{7,4},{8,9},{9,10},{10,1... | collective-permute-start | bytes 294920 | tf_op jit(solution)/shard_map/ppermute | solution.py:541
  71.5 70.4 %collective-permute-start.5 = (bf16[3,4,32,128]{3,2,1,0:T(8,128)(2,1)S(1)}, bf16[3,4,32,128]{3,2,1,0:T(8,128)(2,1)S(1)}, u32[]{:S(2)}, u32[]{:S(2)}) collective-permute-start(bf16[3,4,32,128]{3,2,1,0:T(8,128)(2,1)S(1)} %get-tuple-element.20), channel_id=1, source_target_pairs={{0,2},{1,3},{2,0},{3,1},{4,6},{5,7},{6,4},{7,5},{8,10},{9,11},{10,... | collective-permute-start | bytes 294920 | tf_op jit(solution)/shard_map/ppermute | solution.py:541
  74.1 67.8 %collective-permute-start.6 = (bf16[3,4,32,128]{3,2,1,0:T(8,128)(2,1)S(1)}, bf16[3,4,32,128]{3,2,1,0:T(8,128)(2,1)S(1)}, u32[]{:S(2)}, u32[]{:S(2)}) collective-permute-start(bf16[3,4,32,128]{3,2,1,0:T(8,128)(2,1)S(1)} %get-tuple-element.21), channel_id=1, source_target_pairs={{0,3},{1,0},{2,1},{3,2},{4,7},{5,4},{6,5},{7,6},{8,11},{9,8},{10,9... | collective-permute-start | bytes 294920 | tf_op jit(solution)/shard_map/ppermute | solution.py:541

commit v3 on v2

--- a/solution.py
+++ b/solution.py
@@ -15,6 +15,7 @@
 XW = TX + 2 * H
 FX = TX + 8
 RX = 4
+SECOND, THIRD = 11, 14
 BLK = 256
 SUB = 16
 PAD = SUB + NT + SUB
@@ -27,12 +28,39 @@
     return lax.broadcasted_iota(jnp.int32, shape, dim)
 
 
+def groups(rows):
+    count = -(-rows // 5)
+    ends = [rows * i // count for i in range(count + 1)]
+    return [(a, b - a) for a, b in zip(ends, ends[1:])]
+
+
 def dot_nt(a, b):
     return lax.dot_general(a, b, (((1,), (1,)), ((), ())), preferred_element_type=F32)
 
 
-def prep_kernel(first_ref, second_ref, third_ref, last_ref, after_ref, w1_ref, w2_ref, w3_ref, w4_ref):
+def prep_kernel(
+    first_in,
+    second_in,
+    third_in,
+    last_in,
+    after_ref,
+    w1_ref,
+    w2_ref,
+    w3_ref,
+    w4_ref,
+    first_ref,
+    second_ref,
+    third_ref,
+    last_ref,
+    sems,
+):
     del after_ref
+    pairs = ((second_in, second_ref), (third_in, third_ref), (first_in, first_ref), (last_in, last_ref))
+    copies = [pltpu.make_async_copy(a, b, sems.at[i]) for i, (a, b) in enumerate(pairs)]
+    for copy in copies:
+        copy.start()
+    for copy in copies:
+        copy.wait()
     spread = jnp.where(iota((CH, BLK), 1) % CH == iota((CH, BLK), 0), 1.0, 0.0).astype(BF16)
     unit = jnp.where(iota((BLK, BLK), 1) == iota((BLK, BLK), 0), 1.0, 0.0).astype(BF16)
     in_pos = iota((CH, BLK), 1) // CH
@@ -197,7 +225,7 @@
                     put(act1, y, blk, jnp.maximum(values, 0.0) * (mask1[blk] * ok))
         return carry
 
-    lax.fori_loop(0, yw // 4, first, 0)
+    lax.fori_loop(0, yw // 4, first, 0, unroll=2)
 
     def layer(source, w_ref, y, count):
         taps = []
@@ -211,34 +239,36 @@
     lane_half = iota((NT, 128), 1)
 
     def second(step, carry):
-        y = step * 4
-        result = layer(act1, w2_ref, y, 4)
-        for row in range(4):
-            ok = inside_y(y + row - 6)
-            low = result[row * 2 * NT : row * 2 * NT + NT]
-            high = result[row * 2 * NT + NT : (row + 1) * 2 * NT]
-            moved = jnp.where(lane_half >= 96, pltpu.roll(high[:, :128], 96, 1), low[:, 128:])
-            low = jnp.concatenate([low[:, :128], moved], axis=1)
-            put(act2, y + row, 0, jnp.maximum(low, 0.0) * (mask2[0] * ok))
-            put(act2, y + row, 1, jnp.maximum(high, 0.0) * (mask2[1] * ok))
-        return carry
-
-    lax.fori_loop(0, (ty + 12) // 4, second, 0)
+        for begin, count in groups(SECOND):
+            y = step * SECOND + begin
+            result = layer(act1, w2_ref, y, count)
+            for row in range(count):
+                ok = inside_y(y + row - 6)
+                low = result[row * 2 * NT : row * 2 * NT + NT]
+                high = result[row * 2 * NT + NT : (row + 1) * 2 * NT]
+                moved = jnp.where(lane_half >= 96, pltpu.roll(high[:, :128], 96, 1), low[:, 128:])
+                low = jnp.concatenate([low[:, :128], moved], axis=1)
+                put(act2, y + row, 0, jnp.maximum(low, 0.0) * (mask2[0] * ok))
+                put(act2, y + row, 1, jnp.maximum(high, 0.0) * (mask2[1] * ok))
+        return carry
+
+    lax.fori_loop(0, (ty + 12) // SECOND, second, 0)
 
     mask3 = lane_mask(-5)
 
     def third(step, carry):
-        y = step * 3
-        result = layer(act2, w3_ref, y, 3)
-        for row in range(3):
-            ok = inside_y(y + row - 5)
-            for blk in range(2):
-                at = (row * 2 + blk) * NT
-                values = jnp.maximum(result[at : at + NT], 0.0) * (mask3[blk] * ok)
-                act3[y + row, :, blk * BLK : (blk + 1) * BLK] = values.astype(BF16)
-        return carry
-
-    lax.fori_loop(0, (ty + 10) // 3, third, 0)
+        for begin, count in groups(THIRD):
+            y = step * THIRD + begin
+            result = layer(act2, w3_ref, y, count)
+            for row in range(count):
+                ok = inside_y(y + row - 5)
+                for blk in range(2):
+                    at = (row * 2 + blk) * NT
+                    values = jnp.maximum(result[at : at + NT], 0.0) * (mask3[blk] * ok)
+                    act3[y + row, :, blk * BLK : (blk + 1) * BLK] = values.astype(BF16)
+        return carry
+
+    lax.fori_loop(0, (ty + 10) // THIRD, third, 0)
 
     def fourth(step, carry):
         y = step * 3
@@ -247,7 +277,7 @@
             part[y + row] = result[:, row * NT : (row + 1) * NT]
         return carry
 
-    lax.fori_loop(0, (ty + 10) // 3, fourth, 0)
+    lax.fori_loop(0, (ty + 10) // 3, fourth, 0, unroll=7)
 
     for x in range(FX):
         prob[x * yw : x * yw + H, :] = jnp.zeros((H, NT), F32)
@@ -487,8 +517,15 @@
             jax.ShapeDtypeStruct((9, BLK, BLK), BF16),
             jax.ShapeDtypeStruct((9 * FX, 2 * BLK), BF16),
         ],
-        in_specs=vmem(4) + [pl.BlockSpec(memory_space=pl.ANY)],
+        in_specs=[pl.BlockSpec(memory_space=pltpu.HBM)] * 4 + [pl.BlockSpec(memory_space=pl.ANY)],
         out_specs=vmem(4),
+        scratch_shapes=[
+            pltpu.VMEM((1, 3, 3, 3, CH), BF16),
+            pltpu.VMEM((27 * CH, CH), BF16),
+            pltpu.VMEM((27 * CH, CH), BF16),
+            pltpu.VMEM((1, 3, 3, 3, CH), BF16),
+            pltpu.SemaphoreType.DMA((4,)),
+        ],
         compiler_params=pltpu.CompilerParams(vmem_limit_bytes=16 * 2**20),
         cost_estimate=pl.CostEstimate(flops=10**9, bytes_accessed=10**7, transcendentals=0),
         name="band_weights",
@@ -539,7 +576,8 @@
     for place in range(1, n_gy):
         pairs = [(i, (i + place) % n_gy) for i in range(n_gy)]
         arrived.append(lax.ppermute(waves[place], "gy", pairs))
-    moments = lax.all_gather(moments, ("gx", "gy"), axis=0, tiled=False)
+    everyone = jnp.broadcast_to(moments[None], (n_gx * n_gy, 8, NT))
+    moments = lax.all_to_all(everyone, ("gx", "gy"), split_axis=0, concat_axis=0, tiled=True)
     shift_field = pl.pallas_call(
         functools.partial(combine_kernel, n_gy, ty),
         out_shape=jax.ShapeDtypeStruct((rows, grid_y, NT), F32),

time: 144 us -> 87.8 us (0.61)
  blocking collectives: 66.4 us -> 0 us
  starting transfers between devices: 16.9 us -> 26.2 us
  waiting for transfers between devices: 0.31 us -> 7.68 us
  Pallas kernels: 53.6 us -> 47.1 us
    all_gather x1 -> x0, blocking collectives: 66.4 us -> none  [on_device(): moments = lax.all_gather(moments, ('gx', 'gy'), axis=0, tiled=False)]
    all_to_all x0 -> x1, starting transfers between devices: none -> 10 us  [on_device(): lax.all_to_all(everyone, ('gx', 'gy'), split_axis=0, concat_axis=0, tiled...]
    ppermute x3, waiting for transfers between devices: 0.01 us -> 7.59 us  [on_device(): arrived.append(lax.ppermute(waves[place], 'gy', pairs))]
    pallas_call x1, Pallas kernels: 50.8 us -> 44 us  [on_device(): pl.pallas_call(functools.partial(main_kernel, grid_x, grid_y, ty), out_sh...]
  transfers between devices with their start and end apart: 7 -> 8, of which waited for: 2 -> 3; matrix products, arithmetic and copies ran while one was open for 1% -> 1% of each run, Pallas kernels for 1% -> 2%
where the time goes in v3:
time: 87.8 us; the launch traced here: 87.3 us
  Pallas kernels  47.1 us (54%)
  starting transfers between devices  26.2 us (30%)
  waiting for transfers between devices  7.68 us (9%)
  local copies, waits for them, and re-layouts  5.53 us (6%)
    pallas_call x1, Pallas kernels, on_device(): pl.pallas_call(functools.partial(main_kernel, grid_x, grid_y, ty), out_sh...  44 us
    ppermute x4, starting transfers between devices, shift(): return lax.ppermute(values, axis, pairs)  10.5 us
    all_to_all x1, starting transfers between devices, on_device(): lax.all_to_all(everyone, ('gx', 'gy'), split_axis=0, concat_axis=0, tiled...  10 us
    ppermute x3, waiting for transfers between devices, on_device(): arrived.append(lax.ppermute(waves[place], 'gy', pairs))  7.59 us
    ppermute x3, starting transfers between devices, on_device(): arrived.append(lax.ppermute(waves[place], 'gy', pairs))  5.65 us
    unnamed x10, local copies, waits for them, and re-layouts  3.19 us
    pallas_call x1, Pallas kernels, on_device(): pl.pallas_call(prep_kernel, out_shape=[jax.ShapeDtypeStruct((3 * 4 * XW,...  2.16 us
  transfers between devices with their start and end apart: 8, of which 3 were waited for; matrix products, arithmetic and copies ran while one was open for 1% of the time, Pallas kernels for 2%

profile of v3, /device:TPU:0, one launch (start us, length us, event | category | flops | bytes accessed | tf_op | source)
XLA Modules:
  0.0 87.3 jit_solution(13953041460265567584)
XLA Ops:
  0.6 0.9 %fusion.1 = (bf16[8,32,128]{2,1,0:T(8,128)(2,1)S(1)}, bf16[8,32,128]{2,1,0:T(8,128)(2,1)S(1)}) fusion(bf16[16,32,128]{2,1,0:T(8,128)(2,1)} %amp_ref.1), kind=kLoop, calls=%fused_computation.3 | loop fusion | bytes 262144 | tf_op jit(solution)/shard_map/slice | solution.py:498
  1.5 1.3 %collective-permute-start.1 = (bf16[8,32,128]{2,1,0:T(8,128)(2,1)S(1)}, bf16[8,32,128]{2,1,0:T(8,128)(2,1)S(1)}, u32[]{:S(2)}, u32[]{:S(2)}) collective-permute-start(bf16[8,32,128]{2,1,0:T(8,128)(2,1)S(1)} %get-tuple-element.24), channel_id=1, source_target_pairs={{4,0},{8,4},{12,8},{16,12},{20,16},{24,20},{28,24},{5,1},{9,5},{13... | collective-permute-start | bytes 196616 | tf_op jit(solution)/shard_map/ppermute | solution.py:495
  2.8 3.0 %collective-permute-start = (bf16[8,32,128]{2,1,0:T(8,128)(2,1)S(1)}, bf16[8,32,128]{2,1,0:T(8,128)(2,1)S(1)}, u32[]{:S(2)}, u32[]{:S(2)}) collective-permute-start(bf16[8,32,128]{2,1,0:T(8,128)(2,1)S(1)} %get-tuple-element.25), channel_id=1, source_target_pairs={{0,4},{4,8},{8,12},{12,16},{16,20},{20,24},{24,28},{1,5},{5,9},{9,... | collective-permute-start | bytes 196616 | tf_op jit(solution)/shard_map/ppermute | solution.py:495
  5.9 0.8 fusion
  6.6 0.0 collective-permute-done.1.xhigh_ref
  6.7 0.1 collective-permute-done.after_ref.xlow_ref
  6.8 4.9 %collective-permute-start.2 = (bf16[32,8,128]{2,1,0:T(8,128)(2,1)S(1)}, bf16[32,8,128]{2,1,0:T(8,128)(2,1)S(1)}, u32[]{:S(2)}, u32[]{:S(2)}) collective-permute-start(bf16[32,8,128]{2,1,0:T(8,128)(2,1)S(1)} %pad_maximum_fusion), channel_id=1, source_target_pairs={{0,1},{1,2},{2,3},{4,5},{5,6},{6,7},{8,9},{9,10},{10,11},{12,13},{... | collective-permute-start | bytes 196616 | tf_op jit(solution)/shard_map/ppermute | solution.py:495
  11.7 1.3 %collective-permute-start.3 = (bf16[32,8,128]{2,1,0:T(8,128)(2,1)S(1)}, bf16[32,8,128]{2,1,0:T(8,128)(2,1)S(1)}, u32[]{:S(2)}, u32[]{:S(2)}) collective-permute-start(bf16[32,8,128]{2,1,0:T(8,128)(2,1)S(1)} %pad_maximum_fusion.1), channel_id=1, source_target_pairs={{1,0},{2,1},{3,2},{5,4},{6,5},{7,6},{9,8},{10,9},{11,10},{13,12},{... | collective-permute-start | bytes 196616 | tf_op jit(solution)/shard_map/ppermute | solution.py:495
  13.0 0.0 copy-start.1
  13.0 0.9 %copy-done.1 = bf16[16,16,3,3,3]{1,0,4,3,2:T(8,128)(2,1)S(1)} copy-done((bf16[16,16,3,3,3]{1,0,4,3,2:T(8,128)(2,1)S(1)}, bf16[16,16,3,3,3]{1,0,4,3,2:T(8,128)(2,1)}, u32[]{:S(2)}) %copy-start.1) | copy-done | bytes 13848
  13.9 0.0 copy-start.2
  13.9 0.9 %copy-done.2 = bf16[16,16,3,3,3]{1,0,4,3,2:T(8,128)(2,1)S(1)} copy-done((bf16[16,16,3,3,3]{1,0,4,3,2:T(8,128)(2,1)S(1)}, bf16[16,16,3,3,3]{1,0,4,3,2:T(8,128)(2,1)}, u32[]{:S(2)}) %copy-start.2) | copy-done | bytes 13848
  14.8 0.0 copy-start.3
  14.8 0.7 copy-done.3
  15.5 0.0 copy-start.4
  15.5 0.7 copy-done.4
  16.2 0.0 copy-start
  16.2 2.2 %band_weights.1 = (bf16[384,1024]{1,0:T(8,128)(2,1)S(1)}, bf16[9,256,256]{2,1,0:T(8,128)(2,1)S(1)}, bf16[9,256,256]{2,1,0:T(8,128)(2,1)S(1)}, bf16[216,512]{1,0:T(8,128)(2,1)S(1)}) custom-call(bf16[1,3,3,3,16]{4,3,2,1,0:T(4,128)(2,1)S(1)} %bitcast.10, bf16[432,16]{1,0:T(8,128)(2,1)S(1)} %bitcast.8, bf16[432,16]{1,0:T(8,128)(2,1)S(1)} %bitcast.9, ...), custom_call_target="tpu_custom_call" | custom-call | flops 1000000000 | bytes 10000000 | tf_op jit(solution)/shard_map/band_weights/pallas_call | solution.py:512
  18.4 0.0 collective-permute-done.2.ylow_ref
  18.4 0.0 collective-permute-done.3.yhigh_ref
  18.4 0.0 copy-done
  18.4 44.0 %fault_and_waves.1 = (bf16[16,32,128]{2,1,0:T(8,128)(2,1)}, f32[8,128]{1,0:T(8,128)S(1)}, bf16[3,4,32,128]{3,2,1,0:T(8,128)(2,1)S(1)}, bf16[3,4,32,128]{3,2,1,0:...) custom-call(bf16[16,32,128]{2,1,0:T(8,128)(2,1)S(1)} %copy-done, ...), custom_call_target="tpu_custom_call" | custom-call | flops 30000001024 | bytes 10000000 | tf_op jit(solution)/shard_map/fault_and_waves/pallas_call | solution.py:558
  62.4 0.7 broadcast_in_dim.2
  63.1 10.0 %all-to-all-start = ((f32[32,8,128]{2,1,0:T(8,128)}), f32[32,8,128]{2,1,0:T(8,128)S(1)}, u32[]{:S(2)}, u32[]{:S(2)}) async-start(f32[32,8,128]{2,1,0:T(8,128)} %broadcast_in_dim.2), calls=%async_computation | async-start | bytes 262144 | tf_op jit(solution)/shard_map/all_to_all | solution.py:580
  73.1 1.8 %collective-permute-start.4 = (bf16[3,4,32,128]{3,2,1,0:T(8,128)(2,1)S(1)}, bf16[3,4,32,128]{3,2,1,0:T(8,128)(2,1)S(1)}, u32[]{:S(2)}, u32[]{:S(2)}) collective-permute-start(bf16[3,4,32,128]{3,2,1,0:T(8,128)(2,1)S(1)} %get-tuple-element.19), channel_id=1, source_target_pairs={{0,1},{1,2},{2,3},{3,0},{4,5},{5,6},{6,7},{7,4},{8,9},{9,10},{10,1... | collective-permute-start | bytes 294920 | tf_op jit(solution)/shard_map/ppermute | solution.py:578
  75.0 2.4 %collective-permute-start.5 = (bf16[3,4,32,128]{3,2,1,0:T(8,128)(2,1)S(1)}, bf16[3,4,32,128]{3,2,1,0:T(8,128)(2,1)S(1)}, u32[]{:S(2)}, u32[]{:S(2)}) collective-permute-start(bf16[3,4,32,128]{3,2,1,0:T(8,128)(2,1)S(1)} %get-tuple-element.20), channel_id=1, source_target_pairs={{0,2},{1,3},{2,0},{3,1},{4,6},{5,7},{6,4},{7,5},{8,10},{9,11},{10,... | collective-permute-start | bytes 294920 | tf_op jit(solution)/shard_map/ppermute | solution.py:578
  77.4 1.4 %collective-permute-start.6 = (bf16[3,4,32,128]{3,2,1,0:T(8,128)(2,1)S(1)}, bf16[3,4,32,128]{3,2,1,0:T(8,128)(2,1)S(1)}, u32[]{:S(2)}, u32[]{:S(2)}) collective-permute-start(bf16[3,4,32,128]{3,2,1,0:T(8,128)(2,1)S(1)} %get-tuple-element.21), channel_id=1, source_target_pairs={{0,3},{1,0},{2,1},{3,2},{4,7},{5,4},{6,5},{7,6},{8,11},{9,8},{10,9... | collective-permute-start | bytes 294920 | tf_op jit(solution)/shard_map/ppermute | solution.py:578
  78.8 3.7 %collective-permute-done.4.refs_1_ = bf16[3,4,32,128]{3,2,1,0:T(8,128)(2,1)S(1)} collective-permute-done((bf16[3,4,32,128]{3,2,1,0:T(8,128)(2,1)S(1)}, bf16[3,4,32,128]{3,2,1,0:T(8,128)(2,1)S(1)}, u32[]{:S(2)}, u32[]{:S(2)}) %collective-permute-start.4) | collective-permute-done | bytes 98336 | tf_op jit(solution)/shard_map/ppermute | solution.py:578
  82.5 3.8 %collective-permute-done.5.refs_2_ = bf16[3,4,32,128]{3,2,1,0:T(8,128)(2,1)S(1)} collective-permute-done((bf16[3,4,32,128]{3,2,1,0:T(8,128)(2,1)S(1)}, bf16[3,4,32,128]{3,2,1,0:T(8,128)(2,1)S(1)}, u32[]{:S(2)}, u32[]{:S(2)}) %collective-permute-start.5) | collective-permute-done | bytes 98336 | tf_op jit(solution)/shard_map/ppermute | solution.py:578
  86.4 0.0 collective-permute-done.6.refs_3_
  86.4 0.0 all-to-all-done.mom_ref
  86.4 0.9 %combine_waves.1 = f32[4,128,128]{2,1,0:T(8,128)} custom-call(f32[32,8,128]{2,1,0:T(8,128)S(1)} %all-to-all-done.mom_ref, bf16[3,4,32,128]{3,2,1,0:T(8,128)(2,1)S(1)} %get-tuple-element.18.refs_0_, bf16[3,4,32,128]{3,2,1,0:T(8,128)(2,1)S(1)} %collective-permute-done.4.refs_1_, bf16[3,4,32,128]{3,2,1,0:T(8,128)(2,1)S(1)} %collective-permute-done.5.refs_2_, ...), custom_call_target="tpu_custom_call" | custom-call | tf_op jit(solution)/shard_map/combine_waves/pallas_call | solution.py:581
  (4 shorter events, 0.0 us)
Async XLA Ops:
  1.5 5.1 %collective-permute-start.1 = (bf16[8,32,128]{2,1,0:T(8,128)(2,1)S(1)}, bf16[8,32,128]{2,1,0:T(8,128)(2,1)S(1)}, u32[]{:S(2)}, u32[]{:S(2)}) collective-permute-start(bf16[8,32,128]{2,1,0:T(8,128)(2,1)S(1)} %get-tuple-element.24), channel_id=1, source_target_pairs={{4,0},{8,4},{12,8},{16,12},{20,16},{24,20},{28,24},{5,1},{9,5},{13... | collective-permute-start | bytes 196616 | tf_op jit(solution)/shard_map/ppermute | solution.py:495
  2.8 3.9 %collective-permute-start = (bf16[8,32,128]{2,1,0:T(8,128)(2,1)S(1)}, bf16[8,32,128]{2,1,0:T(8,128)(2,1)S(1)}, u32[]{:S(2)}, u32[]{:S(2)}) collective-permute-start(bf16[8,32,128]{2,1,0:T(8,128)(2,1)S(1)} %get-tuple-element.25), channel_id=1, source_target_pairs={{0,4},{4,8},{8,12},{12,16},{16,20},{20,24},{24,28},{1,5},{5,9},{9,... | collective-permute-start | bytes 196616 | tf_op jit(solution)/shard_map/ppermute | solution.py:495
  6.8 11.6 %collective-permute-start.2 = (bf16[32,8,128]{2,1,0:T(8,128)(2,1)S(1)}, bf16[32,8,128]{2,1,0:T(8,128)(2,1)S(1)}, u32[]{:S(2)}, u32[]{:S(2)}) collective-permute-start(bf16[32,8,128]{2,1,0:T(8,128)(2,1)S(1)} %pad_maximum_fusion), channel_id=1, source_target_pairs={{0,1},{1,2},{2,3},{4,5},{5,6},{6,7},{8,9},{9,10},{10,11},{12,13},{... | collective-permute-start | bytes 196616 | tf_op jit(solution)/shard_map/ppermute | solution.py:495
  11.7 6.7 %collective-permute-start.3 = (bf16[32,8,128]{2,1,0:T(8,128)(2,1)S(1)}, bf16[32,8,128]{2,1,0:T(8,128)(2,1)S(1)}, u32[]{:S(2)}, u32[]{:S(2)}) collective-permute-start(bf16[32,8,128]{2,1,0:T(8,128)(2,1)S(1)} %pad_maximum_fusion.1), channel_id=1, source_target_pairs={{1,0},{2,1},{3,2},{5,4},{6,5},{7,6},{9,8},{10,9},{11,10},{13,12},{... | collective-permute-start | bytes 196616 | tf_op jit(solution)/shard_map/ppermute | solution.py:495
  13.0 0.9 %copy-start.1 = (bf16[16,16,3,3,3]{1,0,4,3,2:T(8,128)(2,1)S(1)}, bf16[16,16,3,3,3]{1,0,4,3,2:T(8,128)(2,1)}, u32[]{:S(2)}) copy-start(bf16[16,16,3,3,3]{1,0,4,3,2:T(8,128)(2,1)} %param.7) | copy-start | bytes 41476
  13.9 0.9 %copy-start.2 = (bf16[16,16,3,3,3]{1,0,4,3,2:T(8,128)(2,1)S(1)}, bf16[16,16,3,3,3]{1,0,4,3,2:T(8,128)(2,1)}, u32[]{:S(2)}) copy-start(bf16[16,16,3,3,3]{1,0,4,3,2:T(8,128)(2,1)} %param.8) | copy-start | bytes 41476
  14.8 0.7 copy-start.3
  15.5 0.7 copy-start.4
  16.2 2.2 %copy-start = (bf16[16,32,128]{2,1,0:T(8,128)(2,1)S(1)}, bf16[16,32,128]{2,1,0:T(8,128)(2,1)}, u32[]{:S(2)}) copy-start(bf16[16,32,128]{2,1,0:T(8,128)(2,1)} %amp_ref.1) | copy-start | bytes 393220
  63.1 23.3 %all-to-all-start = ((f32[32,8,128]{2,1,0:T(8,128)}), f32[32,8,128]{2,1,0:T(8,128)S(1)}, u32[]{:S(2)}, u32[]{:S(2)}) async-start(f32[32,8,128]{2,1,0:T(8,128)} %broadcast_in_dim.2), calls=%async_computation | async-start | bytes 262144 | tf_op jit(solution)/shard_map/all_to_all | solution.py:580
  73.1 9.4 %collective-permute-start.4 = (bf16[3,4,32,128]{3,2,1,0:T(8,128)(2,1)S(1)}, bf16[3,4,32,128]{3,2,1,0:T(8,128)(2,1)S(1)}, u32[]{:S(2)}, u32[]{:S(2)}) collective-permute-start(bf16[3,4,32,128]{3,2,1,0:T(8,128)(2,1)S(1)} %get-tuple-element.19), channel_id=1, source_target_pairs={{0,1},{1,2},{2,3},{3,0},{4,5},{5,6},{6,7},{7,4},{8,9},{9,10},{10,1... | collective-permute-start | bytes 294920 | tf_op jit(solution)/shard_map/ppermute | solution.py:578
  75.0 11.4 %collective-permute-start.5 = (bf16[3,4,32,128]{3,2,1,0:T(8,128)(2,1)S(1)}, bf16[3,4,32,128]{3,2,1,0:T(8,128)(2,1)S(1)}, u32[]{:S(2)}, u32[]{:S(2)}) collective-permute-start(bf16[3,4,32,128]{3,2,1,0:T(8,128)(2,1)S(1)} %get-tuple-element.20), channel_id=1, source_target_pairs={{0,2},{1,3},{2,0},{3,1},{4,6},{5,7},{6,4},{7,5},{8,10},{9,11},{10,... | collective-permute-start | bytes 294920 | tf_op jit(solution)/shard_map/ppermute | solution.py:578
  77.4 9.0 %collective-permute-start.6 = (bf16[3,4,32,128]{3,2,1,0:T(8,128)(2,1)S(1)}, bf16[3,4,32,128]{3,2,1,0:T(8,128)(2,1)S(1)}, u32[]{:S(2)}, u32[]{:S(2)}) collective-permute-start(bf16[3,4,32,128]{3,2,1,0:T(8,128)(2,1)S(1)} %get-tuple-element.21), channel_id=1, source_target_pairs={{0,3},{1,0},{2,1},{3,2},{4,7},{5,4},{6,5},{7,6},{8,11},{9,8},{10,9... | collective-permute-start | bytes 294920 | tf_op jit(solution)/shard_map/ppermute | solution.py:578

commit v4 on v3

--- a/solution.py
+++ b/solution.py
@@ -120,7 +120,28 @@
         w4_ref[:, blk * BLK : (blk + 1) * BLK] = pieces.astype(BF16)
 
 
-def main_kernel(
+def plane_shifts(yw):
+    block = (RX, yw, NT)
+    lane = iota(block, 2)
+    first_lane = lane == 0
+    last_lane = lane == NT - 1
+
+    def up_y(v):
+        return pltpu.roll(v, yw - 1, 1)
+
+    def down_y(v):
+        return pltpu.roll(v, 1, 1)
+
+    def up_t(v, edge=0.0):
+        return jnp.where(last_lane, edge, pltpu.roll(v, NT - 1, 2))
+
+    def down_t(v, edge=0.0):
+        return jnp.where(first_lane, edge, pltpu.roll(v, 1, 2))
+
+    return block, up_y, down_y, up_t, down_t
+
+
+def net_kernel(
     grid_x,
     grid_y,
     ty,
@@ -133,17 +154,19 @@
     w2_ref,
     w3_ref,
     w4_ref,
-    *refs,
+    fault_ref,
+    prob,
+    slope,
+    raw,
+    amp,
+    act1,
+    act2,
+    act3,
+    part,
+    prod,
 ):
-    n_gy = grid_y // ty
-    fault_ref, mom_ref = refs[:2]
-    waves_refs = refs[2 : 2 + n_gy]
-    (raw, amp, act1, act2, act3, part, prob, prod, slope, weight, face, flux, inv, wave) = refs[
-        2 + n_gy :
-    ]
-    place_y = lax.axis_index("gy")
     x0 = lax.axis_index("gx") * TX
-    y0 = place_y * ty
+    y0 = lax.axis_index("gy") * ty
     yw = ty + 2 * H
     dot = functools.partial(jnp.dot, preferred_element_type=F32)
 
@@ -235,10 +258,45 @@
                 taps.append(part_in.reshape(count * 2 * NT, BLK))
         return dot(jnp.concatenate(taps, axis=1), w_ref[...].reshape(9 * BLK, BLK))
 
+    block, up_y, down_y, up_t, down_t = plane_shifts(yw)
+
+    def smooth_yt(v, edge=0.0):
+        v = 0.5 * v + 0.25 * (up_t(v, edge) + down_t(v, edge))
+        return 0.5 * v + 0.25 * (up_y(v) + down_y(v))
+
+    def amp_rows(x):
+        return raw[pl.ds(pl.multiple_of(x * yw, 8), RX * yw), :].reshape(block)
+
+    def products(k):
+        here = amp_rows(k + 3)
+        grad_x = 0.5 * (amp_rows(k + 4) - amp_rows(k + 2))
+        grad_y = 0.5 * (up_y(here) - down_y(here))
+        grad_t = 0.5 * (up_t(here) - down_t(here))
+        at = pl.ds(k, RX)
+        prod[0, at] = smooth_yt(grad_x * grad_t)
+        prod[1, at] = smooth_yt(grad_y * grad_t)
+        energy = grad_t * grad_t + 0.25 * (grad_x * grad_x + grad_y * grad_y)
+        prod[2, at] = smooth_yt(energy, 0.25 * here * here)
+
+    def slopes(k):
+        at = pl.ds(k + 1, RX)
+        sums = []
+        for which in range(3):
+            before, here, after = [prod[which, pl.ds(k + i, RX)] for i in range(3)]
+            sums.append(0.5 * here + 0.25 * (before + after))
+        scale = -1.0 / (sums[2] + 0.05)
+        slope[0, at] = sums[0] * scale
+        slope[1, at] = sums[1] * scale
+
     mask2 = lane_mask(-6)
     lane_half = iota((NT, 128), 1)
+    steps2, steps3 = (ty + 12) // SECOND, (ty + 10) // THIRD
+    blocks2 = -(-(FX // RX + 1) // steps2)
+    blocks3 = -(-(FX // RX) // steps3)
 
     def second(step, carry):
+        for i in range(blocks2):
+            products(jnp.minimum((step * blocks2 + i) * RX, FX))
         for begin, count in groups(SECOND):
             y = step * SECOND + begin
             result = layer(act1, w2_ref, y, count)
@@ -252,11 +310,13 @@
                 put(act2, y + row, 1, jnp.maximum(high, 0.0) * (mask2[1] * ok))
         return carry
 
-    lax.fori_loop(0, (ty + 12) // SECOND, second, 0)
+    lax.fori_loop(0, steps2, second, 0)
 
     mask3 = lane_mask(-5)
 
     def third(step, carry):
+        for i in range(blocks3):
+            slopes(jnp.minimum((step * blocks3 + i) * RX, FX - RX))
         for begin, count in groups(THIRD):
             y = step * THIRD + begin
             result = layer(act2, w3_ref, y, count)
@@ -268,7 +328,7 @@
                     act3[y + row, :, blk * BLK : (blk + 1) * BLK] = values.astype(BF16)
         return carry
 
-    lax.fori_loop(0, (ty + 10) // THIRD, third, 0)
+    lax.fori_loop(0, steps3, third, 0)
 
     def fourth(step, carry):
         y = step * 3
@@ -303,58 +363,52 @@
 
     lax.fori_loop(0, (ty + 8) // 8, order, 0)
 
-    block = (RX, yw, NT)
+    for which in range(2):
+        slope[which, FX + 1] = jnp.zeros((yw, NT), F32)
+    for x in range(TX):
+        fault_ref[x] = prob[(x + 4) * yw + H : (x + 4) * yw + H + ty, :].astype(BF16)
+
+
+def owned(total, k, values, ty):
+    for row in range(RX):
+        ok = (k + row >= 5) & (k + row < 5 + TX)
+        total = total + jnp.where(ok, values[row, H : H + ty], 0.0)
+    return total
+
+
+def image_of(wave, face, k, shifts):
+    block, up_y, down_y, up_t, down_t = shifts
+    at, before, after = [pl.ds(k + i, RX) for i in (0, -1, 1)]
+    here = wave[at]
+    flow = face[1, at] * (here - up_y(here))
+    image = time_part(block) * here - ETA_TIME * (up_t(here) + down_t(here))
+    image = image + flow - down_y(flow)
+    image = image + face[0, at] * (here - wave[after])
+    return here, image + face[0, before] * (here - wave[before])
+
+
+def time_part(block):
     lane = iota(block, 2)
-    first_lane = lane == 0
-    last_lane = lane == NT - 1
-
-    def up_y(v):
-        return pltpu.roll(v, yw - 1, 1)
-
-    def down_y(v):
-        return pltpu.roll(v, 1, 1)
-
-    def up_t(v, edge=0.0):
-        return jnp.where(last_lane, edge, pltpu.roll(v, NT - 1, 2))
-
-    def down_t(v, edge=0.0):
-        return jnp.where(first_lane, edge, pltpu.roll(v, 1, 2))
-
-    def smooth_yt(v, edge=0.0):
-        v = 0.5 * v + 0.25 * (up_t(v, edge) + down_t(v, edge))
-        return 0.5 * v + 0.25 * (up_y(v) + down_y(v))
-
-    def amp_rows(x):
-        return raw[pl.ds(pl.multiple_of(x * yw, 8), RX * yw), :].reshape(block)
-
-    def products(step, carry):
-        k = step * RX
-        here = amp_rows(k + 3)
-        grad_x = 0.5 * (amp_rows(k + 4) - amp_rows(k + 2))
-        grad_y = 0.5 * (up_y(here) - down_y(here))
-        grad_t = 0.5 * (up_t(here) - down_t(here))
-        at = pl.ds(k, RX)
-        prod[0, at] = smooth_yt(grad_x * grad_t)
-        prod[1, at] = smooth_yt(grad_y * grad_t)
-        energy = grad_t * grad_t + 0.25 * (grad_x * grad_x + grad_y * grad_y)
-        prod[2, at] = smooth_yt(energy, 0.25 * here * here)
-        return carry
-
-    lax.fori_loop(0, (FX + 2 + RX - 1) // RX, products, 0)
-
+    count = jnp.where(lane == 0, 0.0, 1.0) + jnp.where(lane == NT - 1, 0.0, 1.0)
+    return MU_DIAG + ETA_TIME * count
+
+
+def waves_kernel(grid_x, grid_y, ty, prob, slope, mom_ref, face, wave2, *refs):
+    n_gy = grid_y // ty
+    waves_refs = refs[:n_gy]
+    weight, flux, inv, wave0, wave1 = refs[n_gy:]
+    place_y = lax.axis_index("gy")
+    x0 = lax.axis_index("gx") * TX
+    y0 = place_y * ty
+    yw = ty + 2 * H
+    shifts = plane_shifts(yw)
+    block, up_y, down_y, up_t, down_t = shifts
     at_y = y0 - H + iota(block, 1)
     mask_y = (at_y >= 0) & (at_y < grid_y)
 
-    def fields(step, carry):
+    def weights(step, carry):
         k = step * RX
         at = pl.ds(k + 1, RX)
-        sums = []
-        for which in range(3):
-            before, here, after = [prod[which, pl.ds(k + i, RX)] for i in range(3)]
-            sums.append(0.5 * here + 0.25 * (before + after))
-        scale = -1.0 / (sums[2] + 0.05)
-        slope[0, at] = sums[0] * scale
-        slope[1, at] = sums[1] * scale
         rows = prob[pl.ds(pl.multiple_of(k * yw, 8), RX * yw), :].reshape(block)
         raw_weight = 1.0 - 0.9 * rows
         at_x = x0 - 4 + k + iota(block, 0)
@@ -362,9 +416,8 @@
         weight[1, at] = jnp.where(mask_y & (at_x >= 0) & (at_x < grid_x), raw_weight, 0.0)
         return carry
 
-    lax.fori_loop(0, FX // RX, fields, 0)
+    lax.fori_loop(0, FX // RX, weights, 0)
     for which in range(2):
-        slope[which, FX + 1] = jnp.zeros((yw, NT), F32)
         weight[which, FX + 1] = jnp.full((yw, NT), 1.0 - which, F32)
         face[which, 0] = jnp.zeros((yw, NT), F32)
         flux[which, 0] = jnp.zeros((yw, NT), F32)
@@ -385,73 +438,62 @@
 
     lax.fori_loop(0, FX // RX, faces, 0)
 
-    time_part = MU_DIAG + ETA_TIME * (
-        jnp.where(first_lane, 0.0, 1.0) + jnp.where(last_lane, 0.0, 1.0)
-    )
-
-    def owned(total, k, values):
-        for row in range(RX):
-            ok = (k + row >= 5) & (k + row < 5 + TX)
-            total = total + jnp.where(ok, values[row, H : H + ty], 0.0)
-        return total
-
     def start(step, total):
         k = step * RX + 1
         at, before = pl.ds(k, RX), pl.ds(k - 1, RX)
         flux_y = flux[1, at]
         face_y = face[1, at]
         right = flux[0, before] - flux[0, at] + down_y(flux_y) - flux_y
-        inverse = 1.0 / (time_part + face[0, at] + face[0, before] + face_y + down_y(face_y))
+        inverse = 1.0 / (time_part(block) + face[0, at] + face[0, before] + face_y + down_y(face_y))
         first_wave = right * inverse
         inv[at] = inverse
-        wave[0, at] = first_wave
-        return owned(total, k, right * first_wave)
+        wave0[at] = first_wave
+        return owned(total, k, right * first_wave, ty)
 
     zero = jnp.zeros((ty, NT), F32)
     b0 = lax.fori_loop(0, FX // RX, start, zero)
 
-    def apply(which, k):
-        at, before, after = [pl.ds(k + i, RX) for i in (0, -1, 1)]
-        here = wave[which, at]
-        flow = face[1, at] * (here - up_y(here))
-        image = time_part * here - ETA_TIME * (up_t(here) + down_t(here))
-        image = image + flow - down_y(flow)
-        image = image + face[0, at] * (here - wave[which, after])
-        return here, image + face[0, before] * (here - wave[which, before])
-
-    def advance(which):
+    def advance(source, target):
         def body(step, totals):
             k = step * RX + 3
-            here, image = apply(which, k)
+            here, image = image_of(source, face, k, shifts)
             at = pl.ds(k, RX)
             after = here - image * inv[at]
-            wave[which + 1, at] = after
-            return owned(totals[0], k, here * image), owned(totals[1], k, after * image)
+            target[at] = after
+            return (
+                owned(totals[0], k, here * image, ty),
+                owned(totals[1], k, after * image, ty),
+            )
 
         return body
 
     steps = (FX - 4) // RX
-    a0, a1 = lax.fori_loop(0, steps, advance(0), (zero, zero))
-    a2, a3 = lax.fori_loop(0, steps, advance(1), (zero, zero))
-
-    def finish(step, total):
-        k = step * RX + 5
-        here, image = apply(2, k)
-        return owned(total, k, here * image)
-
-    a4 = lax.fori_loop(0, TX // RX, finish, zero)
-
-    sums = [jnp.sum(v, axis=0, keepdims=True) for v in (b0, a0, a1, a2, a3, a4)]
-    mom_ref[...] = jnp.concatenate(sums + [jnp.zeros((2, NT), F32)], axis=0)
-
-    for x in range(TX):
-        fault_ref[x] = prob[(x + 4) * yw + H : (x + 4) * yw + H + ty, :].astype(BF16)
+    a0, a1 = lax.fori_loop(0, steps, advance(wave0, wave1), (zero, zero))
+    a2, a3 = lax.fori_loop(0, steps, advance(wave1, wave2), (zero, zero))
+    sums = [jnp.sum(v, axis=0, keepdims=True) for v in (b0, a0, a1, a2, a3)]
+    mom_ref[...] = jnp.concatenate(sums + [jnp.zeros((3, NT), F32)], axis=0)
+
     rows = TX // n_gy
     for place, ref in enumerate(waves_refs):
         to = lax.rem(place_y + place, n_gy) * rows + 5
-        for which in range(3):
+        for which, wave in enumerate((wave0, wave1, wave2)):
             for row in range(rows):
-                ref[which, row] = wave[which, to + row, H : H + ty, :].astype(BF16)
+                ref[which, row] = wave[to + row, H : H + ty, :].astype(BF16)
+
+
+def last_kernel(ty, mom_ref, face, wave2, out_ref):
+    shifts = plane_shifts(ty + 2 * H)
+
+    def finish(step, total):
+        k = step * RX + 5
+        here, image = image_of(wave2, face, k, shifts)
+        return owned(total, k, here * image, ty)
+
+    total = lax.fori_loop(0, TX // RX, finish, jnp.zeros((ty, NT), F32))
+    a4 = jnp.sum(total, axis=0, keepdims=True)
+    values = jnp.where(iota((8, NT), 0) == 5, a4, mom_ref[...])
+    for device in range(out_ref.shape[0]):
+        out_ref[device] = values
 
 
 def combine_kernel(n_gy, ty, mom_ref, *refs):
@@ -538,45 +580,68 @@
     )
 
     yw, nf = ty + 2 * H, FX + 2
-    scratch = [
-        pltpu.VMEM(((XW + 2) * yw, NT), F32),
-        pltpu.VMEM((yw + 2, XW, NT), F32),
-        pltpu.VMEM((yw, 2, PAD, BLK), BF16),
-        pltpu.VMEM((ty + 12, 2, PAD, BLK), BF16),
-        pltpu.VMEM((ty + 10, NT, 2 * BLK), BF16),
-        pltpu.VMEM((ty + 10, 9 * FX, NT), F32),
-        pltpu.VMEM((FX * yw, NT), F32),
-        pltpu.VMEM((3, FX + 4, yw, NT), F32),
-        pltpu.VMEM((2, nf, yw, NT), F32),
-        pltpu.VMEM((2, nf, yw, NT), F32),
-        pltpu.VMEM((2, nf, yw, NT), F32),
-        pltpu.VMEM((2, nf, yw, NT), F32),
-        pltpu.VMEM((nf, yw, NT), F32),
-        pltpu.VMEM((3, nf, yw, NT), F32),
-    ]
-    rows = TX // n_gy
-    fault, moments, *waves = pl.pallas_call(
-        functools.partial(main_kernel, grid_x, grid_y, ty),
+    fault, prob, slope = pl.pallas_call(
+        functools.partial(net_kernel, grid_x, grid_y, ty),
         out_shape=[
             jax.ShapeDtypeStruct((TX, ty, NT), BF16),
-            jax.ShapeDtypeStruct((8, NT), F32),
-        ]
-        + [jax.ShapeDtypeStruct((3, rows, ty, NT), BF16)] * n_gy,
+            jax.ShapeDtypeStruct((FX * yw, NT), F32),
+            jax.ShapeDtypeStruct((2, nf, yw, NT), F32),
+        ],
         in_specs=vmem(9),
-        out_specs=vmem(2 + n_gy),
-        scratch_shapes=scratch,
-        compiler_params=pltpu.CompilerParams(vmem_limit_bytes=48 * 2**20),
+        out_specs=vmem(3),
+        scratch_shapes=[
+            pltpu.VMEM(((XW + 2) * yw, NT), F32),
+            pltpu.VMEM((yw + 2, XW, NT), F32),
+            pltpu.VMEM((yw, 2, PAD, BLK), BF16),
+            pltpu.VMEM((ty + 12, 2, PAD, BLK), BF16),
+            pltpu.VMEM((ty + 10, NT, 2 * BLK), BF16),
+            pltpu.VMEM((ty + 10, 9 * FX, NT), F32),
+            pltpu.VMEM((3, FX + 4, yw, NT), F32),
+        ],
+        compiler_params=pltpu.CompilerParams(vmem_limit_bytes=46 * 2**20),
         cost_estimate=pl.CostEstimate(
             flops=3 * 10**10, bytes_accessed=10**7, transcendentals=10**6
         ),
-        name="fault_and_waves",
+        name="fault_net",
     )(amplitude, xlow, xhigh, ylow, yhigh, w1, w2, w3, w4)
+
+    rows = TX // n_gy
+    moments, face, wave2, *waves = pl.pallas_call(
+        functools.partial(waves_kernel, grid_x, grid_y, ty),
+        out_shape=[
+            jax.ShapeDtypeStruct((8, NT), F32),
+            jax.ShapeDtypeStruct((2, nf, yw, NT), F32),
+            jax.ShapeDtypeStruct((nf, yw, NT), F32),
+        ]
+        + [jax.ShapeDtypeStruct((3, rows, ty, NT), BF16)] * n_gy,
+        in_specs=vmem(2),
+        out_specs=vmem(3 + n_gy),
+        scratch_shapes=[
+            pltpu.VMEM((2, nf, yw, NT), F32),
+            pltpu.VMEM((2, nf, yw, NT), F32),
+            pltpu.VMEM((nf, yw, NT), F32),
+            pltpu.VMEM((nf, yw, NT), F32),
+            pltpu.VMEM((nf, yw, NT), F32),
+        ],
+        compiler_params=pltpu.CompilerParams(vmem_limit_bytes=24 * 2**20),
+        cost_estimate=pl.CostEstimate(flops=10**8, bytes_accessed=10**7, transcendentals=0),
+        name="solver_waves",
+    )(prob, slope)
+
+    everyone = pl.pallas_call(
+        functools.partial(last_kernel, ty),
+        out_shape=jax.ShapeDtypeStruct((n_gx * n_gy, 8, NT), F32),
+        in_specs=vmem(3),
+        out_specs=pl.BlockSpec(memory_space=pltpu.VMEM),
+        compiler_params=pltpu.CompilerParams(vmem_limit_bytes=16 * 2**20),
+        cost_estimate=pl.CostEstimate(flops=10**9, bytes_accessed=10**8, transcendentals=0),
+        name="last_moment",
+    )(moments, face, wave2)
 
     arrived = [waves[0]]
     for place in range(1, n_gy):
         pairs = [(i, (i + place) % n_gy) for i in range(n_gy)]
         arrived.append(lax.ppermute(waves[place], "gy", pairs))
-    everyone = jnp.broadcast_to(moments[None], (n_gx * n_gy, 8, NT))
     moments = lax.all_to_all(everyone, ("gx", "gy"), split_axis=0, concat_axis=0, tiled=True)
     shift_field = pl.pallas_call(
         functools.partial(combine_kernel, n_gy, ty),

time: 87.8 us -> 85.4 us (0.973)
  Pallas kernels: 47.1 us -> 45.3 us
    pallas_call x1 -> x3, Pallas kernels: 44 us -> 42.2 us  [the longest x1 38.7 us: on_device(): pl.pallas_call(functools.partial(net_kernel, grid_x, grid_y, ty), out_sha...]
  transfers between devices with their start and end apart: 8 -> 8, of which waited for: 3 -> 3; matrix products, arithmetic and copies ran while one was open for 1% -> 1% of each run, Pallas kernels for 2% -> 3%
where the time goes in v4:
time: 85.4 us; the launch traced here: 84.9 us
  Pallas kernels  45.3 us (53%)
  starting transfers between devices  26.2 us (31%)
  waiting for transfers between devices  7.68 us (9%)
  local copies, waits for them, and re-layouts  4.87 us (6%)
    pallas_call x1, Pallas kernels, on_device(): pl.pallas_call(functools.partial(net_kernel, grid_x, grid_y, ty), out_sha...  38.7 us
    ppermute x4, starting transfers between devices, shift(): return lax.ppermute(values, axis, pairs)  10.5 us
    all_to_all x1, starting transfers between devices, on_device(): lax.all_to_all(everyone, ('gx', 'gy'), split_axis=0, concat_axis=0, tiled...  10 us
    ppermute x3, waiting for transfers between devices, on_device(): arrived.append(lax.ppermute(waves[place], 'gy', pairs))  7.59 us
    ppermute x3, starting transfers between devices, on_device(): arrived.append(lax.ppermute(waves[place], 'gy', pairs))  5.65 us
    unnamed x10, local copies, waits for them, and re-layouts  3.19 us
    pallas_call x1, Pallas kernels, on_device(): pl.pallas_call(functools.partial(waves_kernel, grid_x, grid_y, ty), out_s...  2.39 us
    pallas_call x1, Pallas kernels, on_device(): pl.pallas_call(prep_kernel, out_shape=[jax.ShapeDtypeStruct((3 * 4 * XW,...  2.16 us
  transfers between devices with their start and end apart: 8, of which 3 were waited for; matrix products, arithmetic and copies ran while one was open for 1% of the time, Pallas kernels for 3%

profile of v4, /device:TPU:0, one launch (start us, length us, event | category | flops | bytes accessed | tf_op | source)
XLA Modules:
  0.0 84.9 jit_solution(14070877012141649700)
XLA Ops:
  0.6 0.9 %fusion.1 = (bf16[8,32,128]{2,1,0:T(8,128)(2,1)S(1)}, bf16[8,32,128]{2,1,0:T(8,128)(2,1)S(1)}) fusion(bf16[16,32,128]{2,1,0:T(8,128)(2,1)} %amp_ref.1), kind=kLoop, calls=%fused_computation.3 | loop fusion | bytes 262144 | tf_op jit(solution)/shard_map/slice | solution.py:540
  1.5 1.3 %collective-permute-start.1 = (bf16[8,32,128]{2,1,0:T(8,128)(2,1)S(1)}, bf16[8,32,128]{2,1,0:T(8,128)(2,1)S(1)}, u32[]{:S(2)}, u32[]{:S(2)}) collective-permute-start(bf16[8,32,128]{2,1,0:T(8,128)(2,1)S(1)} %get-tuple-element.32), channel_id=1, source_target_pairs={{4,0},{8,4},{12,8},{16,12},{20,16},{24,20},{28,24},{5,1},{9,5},{13... | collective-permute-start | bytes 196616 | tf_op jit(solution)/shard_map/ppermute | solution.py:537
  2.8 3.0 %collective-permute-start = (bf16[8,32,128]{2,1,0:T(8,128)(2,1)S(1)}, bf16[8,32,128]{2,1,0:T(8,128)(2,1)S(1)}, u32[]{:S(2)}, u32[]{:S(2)}) collective-permute-start(bf16[8,32,128]{2,1,0:T(8,128)(2,1)S(1)} %get-tuple-element.33), channel_id=1, source_target_pairs={{0,4},{4,8},{8,12},{12,16},{16,20},{20,24},{24,28},{1,5},{5,9},{9,... | collective-permute-start | bytes 196616 | tf_op jit(solution)/shard_map/ppermute | solution.py:537
  5.9 0.8 fusion
  6.6 0.0 collective-permute-done.1.xhigh_ref
  6.7 0.1 collective-permute-done.after_ref.xlow_ref
  6.8 4.9 %collective-permute-start.2 = (bf16[32,8,128]{2,1,0:T(8,128)(2,1)S(1)}, bf16[32,8,128]{2,1,0:T(8,128)(2,1)S(1)}, u32[]{:S(2)}, u32[]{:S(2)}) collective-permute-start(bf16[32,8,128]{2,1,0:T(8,128)(2,1)S(1)} %pad_maximum_fusion), channel_id=1, source_target_pairs={{0,1},{1,2},{2,3},{4,5},{5,6},{6,7},{8,9},{9,10},{10,11},{12,13},{... | collective-permute-start | bytes 196616 | tf_op jit(solution)/shard_map/ppermute | solution.py:537
  11.7 1.3 %collective-permute-start.3 = (bf16[32,8,128]{2,1,0:T(8,128)(2,1)S(1)}, bf16[32,8,128]{2,1,0:T(8,128)(2,1)S(1)}, u32[]{:S(2)}, u32[]{:S(2)}) collective-permute-start(bf16[32,8,128]{2,1,0:T(8,128)(2,1)S(1)} %pad_maximum_fusion.1), channel_id=1, source_target_pairs={{1,0},{2,1},{3,2},{5,4},{6,5},{7,6},{9,8},{10,9},{11,10},{13,12},{... | collective-permute-start | bytes 196616 | tf_op jit(solution)/shard_map/ppermute | solution.py:537
  13.0 0.0 copy-start.1
  13.0 0.9 %copy-done.1 = bf16[16,16,3,3,3]{1,0,4,3,2:T(8,128)(2,1)S(1)} copy-done((bf16[16,16,3,3,3]{1,0,4,3,2:T(8,128)(2,1)S(1)}, bf16[16,16,3,3,3]{1,0,4,3,2:T(8,128)(2,1)}, u32[]{:S(2)}) %copy-start.1) | copy-done | bytes 13848
  13.9 0.0 copy-start.2
  13.9 0.9 %copy-done.2 = bf16[16,16,3,3,3]{1,0,4,3,2:T(8,128)(2,1)S(1)} copy-done((bf16[16,16,3,3,3]{1,0,4,3,2:T(8,128)(2,1)S(1)}, bf16[16,16,3,3,3]{1,0,4,3,2:T(8,128)(2,1)}, u32[]{:S(2)}) %copy-start.2) | copy-done | bytes 13848
  14.8 0.0 copy-start.3
  14.8 0.7 copy-done.3
  15.5 0.0 copy-start.4
  15.5 0.7 copy-done.4
  16.2 2.2 %band_weights.1 = (bf16[384,1024]{1,0:T(8,128)(2,1)S(1)}, bf16[9,256,256]{2,1,0:T(8,128)(2,1)S(1)}, bf16[9,256,256]{2,1,0:T(8,128)(2,1)S(1)}, bf16[216,512]{1,0:T(8,128)(2,1)S(1)}) custom-call(bf16[1,3,3,3,16]{4,3,2,1,0:T(4,128)(2,1)S(1)} %bitcast.10, bf16[432,16]{1,0:T(8,128)(2,1)S(1)} %bitcast.8, bf16[432,16]{1,0:T(8,128)(2,1)S(1)} %bitcast.9, ...), custom_call_target="tpu_custom_call" | custom-call | flops 1000000000 | bytes 10000000 | tf_op jit(solution)/shard_map/band_weights/pallas_call | solution.py:554
  18.4 0.0 collective-permute-done.2.ylow_ref
  18.4 0.0 collective-permute-done.3.yhigh_ref
  18.4 0.0 copy-done
  18.4 38.7 %fault_net.1 = (bf16[16,32,128]{2,1,0:T(8,128)(2,1)}, f32[1152,128]{1,0:T(8,128)S(1)}, f32[2,26,48,128]{3,2,1,0:T(8,128)S(1)}) custom-call(bf16[16,32,128]{2,1,0:T(8,128)(2,1)S(1)} %copy-done, bf16[8,32,128]{2,1,0:T(8,128)(2,1)S(1)} %collective-permute-done.after_ref.xlow_ref, bf16[8,32,128]{2,1,0:T(8,128)(2,1)S(1)} %collective-permute-done.1.xhigh_ref, ...), custom_call_target="tpu_custom_call" | custom-call | flops 30000001024 | bytes 10000000 | tf_op jit(solution)/shard_map/fault_net/pallas_call | solution.py:583
  57.1 2.4 %solver_waves.1 = (f32[8,128]{1,0:T(8,128)S(1)}, f32[2,26,48,128]{3,2,1,0:T(8,128)S(1)}, f32[26,48,128]{2,1,0:T(8,128)S(1)}, bf16[3,4,32,128]{3,2,1,0:T(8,128)(2...) custom-call(f32[1152,128]{1,0:T(8,128)S(1)} %get-tuple-element.21.pr, ...), custom_call_target="tpu_custom_call" | custom-call | flops 100000000 | bytes 10000000 | tf_op jit(solution)/shard_map/solver_waves/pallas_call | solution.py:609
  59.5 1.1 %last_moment.1 = f32[32,8,128]{2,1,0:T(8,128)} custom-call(f32[8,128]{1,0:T(8,128)S(1)} %get-tuple-element.23.mom_ref, f32[2,26,48,128]{3,2,1,0:T(8,128)S(1)} %get-tuple-element.24.face, f32[26,48,128]{2,1,0:T(8,128)S(1)} %get-tuple-element.25.wave2), custom_call_target="tpu_custom_call" | custom-call | flops 1000000000 | bytes 100000000 | tf_op jit(solution)/shard_map/last_moment/pallas_call | solution.py:631
  60.7 10.0 %all-to-all-start = ((f32[32,8,128]{2,1,0:T(8,128)}), f32[32,8,128]{2,1,0:T(8,128)S(1)}, u32[]{:S(2)}, u32[]{:S(2)}) async-start(f32[32,8,128]{2,1,0:T(8,128)} %last_moment.1), calls=%async_computation | async-start | bytes 262144 | tf_op jit(solution)/shard_map/all_to_all | solution.py:645
  70.7 1.8 %collective-permute-start.4 = (bf16[3,4,32,128]{3,2,1,0:T(8,128)(2,1)S(1)}, bf16[3,4,32,128]{3,2,1,0:T(8,128)(2,1)S(1)}, u32[]{:S(2)}, u32[]{:S(2)}) collective-permute-start(bf16[3,4,32,128]{3,2,1,0:T(8,128)(2,1)S(1)} %get-tuple-element.27), channel_id=1, source_target_pairs={{0,1},{1,2},{2,3},{3,0},{4,5},{5,6},{6,7},{7,4},{8,9},{9,10},{10,1... | collective-permute-start | bytes 294920 | tf_op jit(solution)/shard_map/ppermute | solution.py:644
  72.5 2.4 %collective-permute-start.5 = (bf16[3,4,32,128]{3,2,1,0:T(8,128)(2,1)S(1)}, bf16[3,4,32,128]{3,2,1,0:T(8,128)(2,1)S(1)}, u32[]{:S(2)}, u32[]{:S(2)}) collective-permute-start(bf16[3,4,32,128]{3,2,1,0:T(8,128)(2,1)S(1)} %get-tuple-element.28), channel_id=1, source_target_pairs={{0,2},{1,3},{2,0},{3,1},{4,6},{5,7},{6,4},{7,5},{8,10},{9,11},{10,... | collective-permute-start | bytes 294920 | tf_op jit(solution)/shard_map/ppermute | solution.py:644
  74.9 1.4 %collective-permute-start.6 = (bf16[3,4,32,128]{3,2,1,0:T(8,128)(2,1)S(1)}, bf16[3,4,32,128]{3,2,1,0:T(8,128)(2,1)S(1)}, u32[]{:S(2)}, u32[]{:S(2)}) collective-permute-start(bf16[3,4,32,128]{3,2,1,0:T(8,128)(2,1)S(1)} %get-tuple-element.29), channel_id=1, source_target_pairs={{0,3},{1,0},{2,1},{3,2},{4,7},{5,4},{6,5},{7,6},{8,11},{9,8},{10,9... | collective-permute-start | bytes 294920 | tf_op jit(solution)/shard_map/ppermute | solution.py:644
  76.3 3.7 %collective-permute-done.4.refs_1_ = bf16[3,4,32,128]{3,2,1,0:T(8,128)(2,1)S(1)} collective-permute-done((bf16[3,4,32,128]{3,2,1,0:T(8,128)(2,1)S(1)}, bf16[3,4,32,128]{3,2,1,0:T(8,128)(2,1)S(1)}, u32[]{:S(2)}, u32[]{:S(2)}) %collective-permute-start.4) | collective-permute-done | bytes 98336 | tf_op jit(solution)/shard_map/ppermute | solution.py:644
  80.1 3.8 %collective-permute-done.5.refs_2_ = bf16[3,4,32,128]{3,2,1,0:T(8,128)(2,1)S(1)} collective-permute-done((bf16[3,4,32,128]{3,2,1,0:T(8,128)(2,1)S(1)}, bf16[3,4,32,128]{3,2,1,0:T(8,128)(2,1)S(1)}, u32[]{:S(2)}, u32[]{:S(2)}) %collective-permute-start.5) | collective-permute-done | bytes 98336 | tf_op jit(solution)/shard_map/ppermute | solution.py:644
  83.9 0.0 collective-permute-done.6.refs_3_
  83.9 0.0 all-to-all-done.mom_ref
  83.9 0.9 %combine_waves.1 = f32[4,128,128]{2,1,0:T(8,128)} custom-call(f32[32,8,128]{2,1,0:T(8,128)S(1)} %all-to-all-done.mom_ref, bf16[3,4,32,128]{3,2,1,0:T(8,128)(2,1)S(1)} %get-tuple-element.26.refs_0_, bf16[3,4,32,128]{3,2,1,0:T(8,128)(2,1)S(1)} %collective-permute-done.4.refs_1_, bf16[3,4,32,128]{3,2,1,0:T(8,128)(2,1)S(1)} %collective-permute-done.5.refs_2_, ...), custom_call_target="tpu_custom_call" | custom-call | tf_op jit(solution)/shard_map/combine_waves/pallas_call | solution.py:646
  (5 shorter events, 0.0 us)
Async XLA Ops:
  1.5 5.1 %collective-permute-start.1 = (bf16[8,32,128]{2,1,0:T(8,128)(2,1)S(1)}, bf16[8,32,128]{2,1,0:T(8,128)(2,1)S(1)}, u32[]{:S(2)}, u32[]{:S(2)}) collective-permute-start(bf16[8,32,128]{2,1,0:T(8,128)(2,1)S(1)} %get-tuple-element.32), channel_id=1, source_target_pairs={{4,0},{8,4},{12,8},{16,12},{20,16},{24,20},{28,24},{5,1},{9,5},{13... | collective-permute-start | bytes 196616 | tf_op jit(solution)/shard_map/ppermute | solution.py:537
  2.8 3.9 %collective-permute-start = (bf16[8,32,128]{2,1,0:T(8,128)(2,1)S(1)}, bf16[8,32,128]{2,1,0:T(8,128)(2,1)S(1)}, u32[]{:S(2)}, u32[]{:S(2)}) collective-permute-start(bf16[8,32,128]{2,1,0:T(8,128)(2,1)S(1)} %get-tuple-element.33), channel_id=1, source_target_pairs={{0,4},{4,8},{8,12},{12,16},{16,20},{20,24},{24,28},{1,5},{5,9},{9,... | collective-permute-start | bytes 196616 | tf_op jit(solution)/shard_map/ppermute | solution.py:537
  6.8 11.6 %collective-permute-start.2 = (bf16[32,8,128]{2,1,0:T(8,128)(2,1)S(1)}, bf16[32,8,128]{2,1,0:T(8,128)(2,1)S(1)}, u32[]{:S(2)}, u32[]{:S(2)}) collective-permute-start(bf16[32,8,128]{2,1,0:T(8,128)(2,1)S(1)} %pad_maximum_fusion), channel_id=1, source_target_pairs={{0,1},{1,2},{2,3},{4,5},{5,6},{6,7},{8,9},{9,10},{10,11},{12,13},{... | collective-permute-start | bytes 196616 | tf_op jit(solution)/shard_map/ppermute | solution.py:537
  11.7 6.7 %collective-permute-start.3 = (bf16[32,8,128]{2,1,0:T(8,128)(2,1)S(1)}, bf16[32,8,128]{2,1,0:T(8,128)(2,1)S(1)}, u32[]{:S(2)}, u32[]{:S(2)}) collective-permute-start(bf16[32,8,128]{2,1,0:T(8,128)(2,1)S(1)} %pad_maximum_fusion.1), channel_id=1, source_target_pairs={{1,0},{2,1},{3,2},{5,4},{6,5},{7,6},{9,8},{10,9},{11,10},{13,12},{... | collective-permute-start | bytes 196616 | tf_op jit(solution)/shard_map/ppermute | solution.py:537
  13.0 0.9 %copy-start.1 = (bf16[16,16,3,3,3]{1,0,4,3,2:T(8,128)(2,1)S(1)}, bf16[16,16,3,3,3]{1,0,4,3,2:T(8,128)(2,1)}, u32[]{:S(2)}) copy-start(bf16[16,16,3,3,3]{1,0,4,3,2:T(8,128)(2,1)} %param.7) | copy-start | bytes 41476
  13.9 0.9 %copy-start.2 = (bf16[16,16,3,3,3]{1,0,4,3,2:T(8,128)(2,1)S(1)}, bf16[16,16,3,3,3]{1,0,4,3,2:T(8,128)(2,1)}, u32[]{:S(2)}) copy-start(bf16[16,16,3,3,3]{1,0,4,3,2:T(8,128)(2,1)} %param.8) | copy-start | bytes 41476
  14.8 0.7 copy-start.3
  15.5 0.7 copy-start.4
  16.2 2.2 %copy-start = (bf16[16,32,128]{2,1,0:T(8,128)(2,1)S(1)}, bf16[16,32,128]{2,1,0:T(8,128)(2,1)}, u32[]{:S(2)}) copy-start(bf16[16,32,128]{2,1,0:T(8,128)(2,1)} %amp_ref.1) | copy-start | bytes 393220
  60.7 23.3 %all-to-all-start = ((f32[32,8,128]{2,1,0:T(8,128)}), f32[32,8,128]{2,1,0:T(8,128)S(1)}, u32[]{:S(2)}, u32[]{:S(2)}) async-start(f32[32,8,128]{2,1,0:T(8,128)} %last_moment.1), calls=%async_computation | async-start | bytes 262144 | tf_op jit(solution)/shard_map/all_to_all | solution.py:645
  70.7 9.4 %collective-permute-start.4 = (bf16[3,4,32,128]{3,2,1,0:T(8,128)(2,1)S(1)}, bf16[3,4,32,128]{3,2,1,0:T(8,128)(2,1)S(1)}, u32[]{:S(2)}, u32[]{:S(2)}) collective-permute-start(bf16[3,4,32,128]{3,2,1,0:T(8,128)(2,1)S(1)} %get-tuple-element.27), channel_id=1, source_target_pairs={{0,1},{1,2},{2,3},{3,0},{4,5},{5,6},{6,7},{7,4},{8,9},{9,10},{10,1... | collective-permute-start | bytes 294920 | tf_op jit(solution)/shard_map/ppermute | solution.py:644
  72.5 11.4 %collective-permute-start.5 = (bf16[3,4,32,128]{3,2,1,0:T(8,128)(2,1)S(1)}, bf16[3,4,32,128]{3,2,1,0:T(8,128)(2,1)S(1)}, u32[]{:S(2)}, u32[]{:S(2)}) collective-permute-start(bf16[3,4,32,128]{3,2,1,0:T(8,128)(2,1)S(1)} %get-tuple-element.28), channel_id=1, source_target_pairs={{0,2},{1,3},{2,0},{3,1},{4,6},{5,7},{6,4},{7,5},{8,10},{9,11},{10,... | collective-permute-start | bytes 294920 | tf_op jit(solution)/shard_map/ppermute | solution.py:644
  74.9 9.0 %collective-permute-start.6 = (bf16[3,4,32,128]{3,2,1,0:T(8,128)(2,1)S(1)}, bf16[3,4,32,128]{3,2,1,0:T(8,128)(2,1)S(1)}, u32[]{:S(2)}, u32[]{:S(2)}) collective-permute-start(bf16[3,4,32,128]{3,2,1,0:T(8,128)(2,1)S(1)} %get-tuple-element.29), channel_id=1, source_target_pairs={{0,3},{1,0},{2,1},{3,2},{4,7},{5,4},{6,5},{7,6},{8,11},{9,8},{10,9... | collective-permute-start | bytes 294920 | tf_op jit(solution)/shard_map/ppermute | solution.py:644

commit v5 on v4

--- a/solution.py
+++ b/solution.py
@@ -15,10 +15,12 @@
 XW = TX + 2 * H
 FX = TX + 8
 RX = 4
-SECOND, THIRD = 11, 14
+FIRST, SECOND, THIRD = 4, 11, 11
+GROUP = 2
 BLK = 256
+EDGE = 7
 SUB = 16
-PAD = SUB + NT + SUB
+PAIRS = NT // 2
 
 F32 = jnp.float32
 BF16 = jnp.bfloat16
@@ -26,12 +28,6 @@
 
 def iota(shape, dim):
     return lax.broadcasted_iota(jnp.int32, shape, dim)
-
-
-def groups(rows):
-    count = -(-rows // 5)
-    ends = [rows * i // count for i in range(count + 1)]
-    return [(a, b - a) for a, b in zip(ends, ends[1:])]
 
 
 def dot_nt(a, b):
@@ -63,20 +59,24 @@
         copy.wait()
     spread = jnp.where(iota((CH, BLK), 1) % CH == iota((CH, BLK), 0), 1.0, 0.0).astype(BF16)
     unit = jnp.where(iota((BLK, BLK), 1) == iota((BLK, BLK), 0), 1.0, 0.0).astype(BF16)
-    in_pos = iota((CH, BLK), 1) // CH
+    cell = iota((CH, BLK), 1) // CH
+    inputs = input_cells()
     for source, ref in ((second_ref, w2_ref), (third_ref, w3_ref)):
         tiled = jnp.dot(source[...], spread, preferred_element_type=F32)
-        for dy in range(3):
-            for dt in range(3):
-                rows = [tiled[(dx * 9 + dy * 3 + dt) * CH :][:CH] for dx in range(3)]
-                bands = []
-                for xo in range(16):
-                    band = jnp.zeros((CH, BLK), F32)
-                    for dx in range(3):
-                        band = jnp.where(in_pos == xo + dx, rows[dx], band)
-                    bands.append(band.astype(BF16))
-                turned = dot_nt(unit, jnp.concatenate(bands, axis=0))
-                ref[dy * 3 + dt] = turned.astype(BF16)
+        for tile in range(6):
+            bands = []
+            for yo in range(2):
+                for to in range(2):
+                    for xo in range(4):
+                        band = jnp.zeros((CH, BLK), F32)
+                        for at, (y, t, x) in enumerate(inputs[tile]):
+                            dx, dy, dt = x - xo + 1, y - yo + 1, t - to + 1
+                            if min(dx, dy, dt) >= 0 and max(dx, dy, dt) <= 2:
+                                tap = tiled[(dx * 9 + dy * 3 + dt) * CH :][:CH]
+                                band = jnp.where(cell == at, tap, band)
+                        bands.append(band.astype(BF16))
+            turned = dot_nt(unit, jnp.concatenate(bands, axis=0))
+            ref[tile * BLK : (tile + 1) * BLK, :] = turned.astype(BF16)
 
     def taps(ref):
         found = {}
@@ -89,35 +89,65 @@
         return found
 
     first, last = taps(first_ref), taps(last_ref)
-    row_pos = iota((XW, BLK), 0)
-    lane_pos = iota((XW, BLK), 1) // CH
-    for dt in range(3):
+    row_x = iota((XW, BLK), 0)
+    lane = iota((XW, BLK), 1)
+    lane_yt, lane_x = lane // 64, lane // CH % 4
+    offset_x = []
+    for blk in range(EDGE):
+        offset_x.append(row_x - 1 - 4 * blk - lane_x)
+    edge = jnp.where(lane_x == 0, row_x - 29, jnp.where(lane_x == 3, row_x, -1))
+    offset_x.append(edge)
+    masks = [[offset_x[blk] == dx for dx in range(3)] for blk in range(EDGE + 1)]
+    for j in range(4):
         for yi in range(4):
-            for yo in range(2):
-                for blk in range(2):
-                    band = jnp.zeros((XW, BLK), F32)
-                    dy = yi - yo
-                    if 0 <= dy <= 2:
-                        for dx in range(3):
-                            band = jnp.where(
-                                row_pos - 14 * blk - lane_pos == dx, first[dx, dy, dt], band
+            row = (j * 4 + yi) * XW
+            columns = []
+            for dx in range(3):
+                value = jnp.zeros((1, BLK), F32)
+                for yo in range(2):
+                    for to in range(2):
+                        dy, dt = yi - yo, j - to
+                        if 0 <= dy <= 2 and 0 <= dt <= 2:
+                            value = jnp.where(
+                                lane_yt[:1] == yo * 2 + to, first[dx, dy, dt], value
                             )
-                    w1_ref[
-                        dt * 128 + yi * XW : dt * 128 + (yi + 1) * XW,
-                        yo * 512 + blk * BLK : yo * 512 + (blk + 1) * BLK,
-                    ] = band.astype(BF16)
-    row_pos = iota((FX, BLK), 0)
-    lane_pos = iota((FX, BLK), 1) // CH
-    for blk in range(2):
-        pieces = []
-        for dy in range(3):
-            for dt in range(3):
+                columns.append(value)
+            for blk in range(EDGE + 1):
+                band = jnp.zeros((XW, BLK), F32)
+                for dx in range(3):
+                    band = jnp.where(masks[blk][dx], columns[dx], band)
+                w1_ref[row : row + XW, blk * BLK : (blk + 1) * BLK] = band.astype(BF16)
+    row_x = iota((FX, BLK), 0)
+    lane_x = iota((FX, BLK), 1) // CH % 4
+    for blk in range(EDGE):
+        masks = [4 * blk + lane_x - 1 - row_x == dx for dx in range(3)]
+        bands = []
+        for yi in range(4):
+            for j in range(4):
                 band = jnp.zeros((FX, BLK), F32)
                 for dx in range(3):
-                    band = jnp.where(14 * blk + lane_pos - row_pos == dx, last[dx, dy, dt], band)
-                pieces.append(jnp.where(lane_pos < 14 - 2 * blk, band, 0.0))
-        pieces = jnp.concatenate(pieces, axis=0)
-        w4_ref[:, blk * BLK : (blk + 1) * BLK] = pieces.astype(BF16)
+                    value = jnp.zeros((1, BLK), F32)
+                    for y in range(2):
+                        for t in range(2):
+                            dy, dt = y + 2 - yi, t + 2 - j
+                            if 0 <= dy <= 2 and 0 <= dt <= 2:
+                                value = jnp.where(
+                                    lane_yt[:1] == y * 2 + t, last[dx, dy, dt], value
+                                )
+                    band = jnp.where(masks[dx], value, band)
+                bands.append(band)
+        w4_ref[:, blk * BLK : (blk + 1) * BLK] = jnp.concatenate(bands, axis=0).astype(BF16)
+
+
+def input_cells():
+    tiles = []
+    for times in ((0, 1), (-1, 2)):
+        for rows in ((0, 1), (-1, 2)):
+            tiles.append([(y, t, x) for y in rows for t in times for x in range(4)])
+    for rows in ((0, 1), (-1, 2)):
+        side = [(0, 4), (-1, 4), (-1, -1), (0, -1), (1, 4), (2, 4), (2, -1), (1, -1)]
+        tiles.append([(y, t, x) for y in rows for t, x in side])
+    return tiles
 
 
 def plane_shifts(yw):
@@ -161,25 +191,14 @@
     amp,
     act1,
     act2,
-    act3,
     part,
     prod,
 ):
     x0 = lax.axis_index("gx") * TX
     y0 = lax.axis_index("gy") * ty
     yw = ty + 2 * H
+    pairs1, pairs2 = yw // 2, ty // 2 + 6
     dot = functools.partial(jnp.dot, preferred_element_type=F32)
-
-    def inside_y(y):
-        at = y0 + y
-        return jnp.where((at >= 0) & (at < grid_y), 1.0, 0.0).astype(F32)
-
-    def lane_mask(start):
-        masks = []
-        for blk in range(2):
-            at = x0 + start + 14 * blk + iota((1, BLK), 1) // CH
-            masks.append(jnp.where((at >= 0) & (at < grid_x), 1.0, 0.0).astype(F32))
-        return masks
 
     for x in range(XW):
         row = x * yw
@@ -194,69 +213,109 @@
         raw[row + H + ty : row + yw, :] = yhigh_ref[x].astype(F32)
 
     def turn(y, carry):
-        amp[y] = raw[pl.ds(y, XW, stride=yw), :]
+        amp[y + 1] = raw[pl.ds(y, XW, stride=yw), :].astype(BF16)
         return carry
 
     lax.fori_loop(0, yw, turn, 0, unroll=8)
-    amp[yw] = jnp.zeros((XW, NT), F32)
-    amp[yw + 1] = jnp.zeros((XW, NT), F32)
-
-    tiled_row = iota((NT, NT), 0)
-    natural = tiled_row // SUB + (tiled_row % SUB) * 8
-    to_tiles = jnp.concatenate(
-        [
-            jnp.where(iota((NT, NT), 1) == natural + dt - 1, 1.0, 0.0).astype(BF16)
-            for dt in range(3)
-        ],
-        axis=0,
-    )
-    from_tiles = jnp.concatenate(
-        [
-            jnp.where(iota((NT, NT), 1) + dt - 1 == natural, 1.0, 0.0).astype(BF16)
-            for dt in range(3)
-        ],
-        axis=0,
-    )
-    sub_row = iota((SUB, BLK), 0)
-
-    def put(act, y, blk, values):
-        act[y, blk, SUB : SUB + NT, :] = values.astype(BF16)
-        before = jnp.where(sub_row == 0, 0.0, pltpu.roll(values[NT - SUB :], 1, 0))
-        after = jnp.where(sub_row == SUB - 1, 0.0, pltpu.roll(values[:SUB], SUB - 1, 0))
-        act[y, blk, 0:SUB, :] = before.astype(BF16)
-        act[y, blk, SUB + NT :, :] = after.astype(BF16)
-
-    mask1 = lane_mask(-7)
+    amp[0] = jnp.zeros((XW, NT), BF16)
+    amp[yw + 1] = jnp.zeros((XW, NT), BF16)
+
+    def pair_of(row):
+        return row // SUB + (row % SUB) * 4
+
+    at_row = iota((4 * PAIRS, NT), 0)
+    to_pairs = jnp.where(
+        iota((4 * PAIRS, NT), 1) == 2 * pair_of(at_row % PAIRS) - 1 + at_row // PAIRS, 1.0, 0.0
+    ).astype(BF16)
+    at_row = iota((4 * NT, 2 * NT), 0)
+    at_lane = iota((4 * NT, 2 * NT), 1)
+    from_pairs = jnp.where(
+        (at_lane % NT == 2 * pair_of(at_row % PAIRS) - 1 + at_row // NT)
+        & (at_lane // NT == at_row % NT // PAIRS),
+        1.0,
+        0.0,
+    ).astype(BF16)
+
+    def lane_masks(blocks):
+        slot = iota((1, BLK), 1) // CH % 4
+        masks = []
+        for blk in range(blocks):
+            if blk < EDGE:
+                at = x0 - 6 + 4 * blk + slot
+            else:
+                at = x0 + jnp.where(slot == 0, 22, -7)
+            masks.append((at >= 0) & (at < grid_x))
+        return masks
+
+    second_row = iota((1, BLK), 1) >= 128
+
+    def scale(mask, y):
+        at = y0 + y + jnp.where(second_row, 1, 0)
+        return jnp.where(mask & (at >= 0) & (at < grid_y), 1.0, 0.0)
+
+    sub_row = iota((SUB, 128), 0)
+    early = iota((PAIRS, 128), 1) < 64
+    slot = iota((PAIRS, 128), 1) // CH % 4
+
+    def put(act, pair, blk, values):
+        act[0, pair, blk] = values.astype(BF16)
+        for half in range(2):
+            turned = pltpu.roll(values[:, half * 128 : (half + 1) * 128], 64, 1)
+            head = jnp.where(sub_row == 0, 0.0, pltpu.roll(turned[PAIRS - SUB :], 1, 0))
+            tail = jnp.where(sub_row == SUB - 1, 0.0, pltpu.roll(turned[:SUB], SUB - 1, 0))
+            before = jnp.concatenate([head, turned[: PAIRS - SUB]], axis=0)
+            after = jnp.concatenate([turned[SUB:], tail], axis=0)
+            both = jnp.where(early, before, after)
+            act[1, pair, blk, :, half * 128 : (half + 1) * 128] = both.astype(BF16)
+
+    def put_sides(act, pair, blocks):
+        for blk in range(EDGE):
+            left, right = (blk - 1) % blocks, (blk + 1) % blocks
+            for half in range(2):
+                at = slice(half * 128, (half + 1) * 128)
+                here = jnp.where(
+                    slot == 0,
+                    act[0, pair, right, :, at].astype(F32),
+                    act[0, pair, left, :, at].astype(F32),
+                )
+                near = jnp.where(
+                    slot == 1,
+                    pltpu.roll(act[1, pair, right, :, at].astype(F32), CH, 1),
+                    pltpu.roll(act[1, pair, left, :, at].astype(F32), 128 - CH, 1),
+                )
+                mixed = jnp.where((slot == 0) | (slot == 3), here, near)
+                act[2, pair, blk, :, at] = mixed.astype(BF16)
+
+    mask1 = lane_masks(EDGE + 1)
 
     def first(step, carry):
         pieces = []
-        for half in range(2):
-            y = step * 4 + half * 2
-            rows = amp[pl.ds(y, 4)].reshape(4 * XW, NT).astype(BF16)
-            turned = dot_nt(to_tiles, rows).astype(BF16)
+        for i in range(FIRST):
+            rows = amp[pl.ds((step * FIRST + i) * 2, 4)].reshape(4 * XW, NT)
+            turned = dot_nt(to_pairs, rows).astype(BF16)
             pieces.append(
-                jnp.concatenate([turned[:NT], turned[NT : 2 * NT], turned[2 * NT :]], axis=1)
+                jnp.concatenate([turned[j * PAIRS : (j + 1) * PAIRS] for j in range(4)], axis=1)
             )
         result = dot(jnp.concatenate(pieces, axis=0), w1_ref[...])
-        for half in range(2):
-            for yo in range(2):
-                y = step * 4 + half * 2 + yo
-                ok = inside_y(y - 7)
-                for blk in range(2):
-                    lane = yo * 512 + blk * BLK
-                    values = result[half * NT : (half + 1) * NT, lane : lane + BLK]
-                    put(act1, y, blk, jnp.maximum(values, 0.0) * (mask1[blk] * ok))
+        for i in range(FIRST):
+            pair = step * FIRST + i
+            for blk in range(EDGE + 1):
+                values = result[i * PAIRS : (i + 1) * PAIRS, blk * BLK : (blk + 1) * BLK]
+                put(act1, pair, blk, jnp.maximum(values, 0.0) * scale(mask1[blk], 2 * pair - H))
+            put_sides(act1, pair, EDGE + 1)
         return carry
 
-    lax.fori_loop(0, yw // 4, first, 0, unroll=2)
-
-    def layer(source, w_ref, y, count):
-        taps = []
-        for dy in range(3):
-            for dt in range(3):
-                part_in = source[pl.ds(y + dy, count), :, SUB * dt : SUB * dt + NT, :]
-                taps.append(part_in.reshape(count * 2 * NT, BLK))
-        return dot(jnp.concatenate(taps, axis=1), w_ref[...].reshape(9 * BLK, BLK))
+    lax.fori_loop(0, pairs1 // FIRST, first, 0)
+
+    def layer(source, w_ref, pair, count):
+        size = count * EDGE * PAIRS
+        tiles = []
+        for kind in range(3):
+            centre = source[kind, pl.ds(pair + 1, count), :EDGE].reshape(size, BLK)
+            before = source[kind, pl.ds(pair, count), :EDGE, :, 128:].reshape(size, 128)
+            after = source[kind, pl.ds(pair + 2, count), :EDGE, :, :128].reshape(size, 128)
+            tiles += [centre, before, after]
+        return dot(jnp.concatenate(tiles, axis=1), w_ref[...])
 
     block, up_y, down_y, up_t, down_t = plane_shifts(yw)
 
@@ -287,78 +346,90 @@
         scale = -1.0 / (sums[2] + 0.05)
         slope[0, at] = sums[0] * scale
         slope[1, at] = sums[1] * scale
-
-    mask2 = lane_mask(-6)
-    lane_half = iota((NT, 128), 1)
-    steps2, steps3 = (ty + 12) // SECOND, (ty + 10) // THIRD
+    steps2, steps3 = pairs2 // SECOND, pairs2 // THIRD
     blocks2 = -(-(FX // RX + 1) // steps2)
     blocks3 = -(-(FX // RX) // steps3)
+    mask2 = lane_masks(EDGE)
 
     def second(step, carry):
         for i in range(blocks2):
             products(jnp.minimum((step * blocks2 + i) * RX, FX))
-        for begin, count in groups(SECOND):
-            y = step * SECOND + begin
-            result = layer(act1, w2_ref, y, count)
-            for row in range(count):
-                ok = inside_y(y + row - 6)
-                low = result[row * 2 * NT : row * 2 * NT + NT]
-                high = result[row * 2 * NT + NT : (row + 1) * 2 * NT]
-                moved = jnp.where(lane_half >= 96, pltpu.roll(high[:, :128], 96, 1), low[:, 128:])
-                low = jnp.concatenate([low[:, :128], moved], axis=1)
-                put(act2, y + row, 0, jnp.maximum(low, 0.0) * (mask2[0] * ok))
-                put(act2, y + row, 1, jnp.maximum(high, 0.0) * (mask2[1] * ok))
+        for begin in range(0, SECOND, GROUP):
+            count = min(GROUP, SECOND - begin)
+            result = layer(act1, w2_ref, step * SECOND + begin, count)
+            for i in range(count):
+                pair = step * SECOND + begin + i
+                for blk in range(EDGE):
+                    at = (i * EDGE + blk) * PAIRS
+                    values = jnp.maximum(result[at : at + PAIRS], 0.0)
+                    put(act2, pair + 1, blk, values * scale(mask2[blk], 2 * pair - 6))
+                put_sides(act2, pair + 1, EDGE)
         return carry
 
+    for edge in (0, pairs2 + 1):
+        for kind in range(3):
+            act2[kind, edge] = jnp.zeros((EDGE, PAIRS, BLK), BF16)
     lax.fori_loop(0, steps2, second, 0)
 
-    mask3 = lane_mask(-5)
+    act3 = act1.at[0]
 
     def third(step, carry):
         for i in range(blocks3):
             slopes(jnp.minimum((step * blocks3 + i) * RX, FX - RX))
-        for begin, count in groups(THIRD):
-            y = step * THIRD + begin
-            result = layer(act2, w3_ref, y, count)
-            for row in range(count):
-                ok = inside_y(y + row - 5)
-                for blk in range(2):
-                    at = (row * 2 + blk) * NT
-                    values = jnp.maximum(result[at : at + NT], 0.0) * (mask3[blk] * ok)
-                    act3[y + row, :, blk * BLK : (blk + 1) * BLK] = values.astype(BF16)
+        for begin in range(0, THIRD, GROUP):
+            count = min(GROUP, THIRD - begin)
+            result = layer(act2, w3_ref, step * THIRD + begin, count)
+            for i in range(count):
+                pair = step * THIRD + begin + i
+                for blk in range(EDGE):
+                    at = (i * EDGE + blk) * PAIRS
+                    values = jnp.maximum(result[at : at + PAIRS], 0.0)
+                    values = values * scale(mask2[blk], 2 * pair - 6)
+                    act3[pair, blk] = values.astype(BF16)
         return carry
 
     lax.fori_loop(0, steps3, third, 0)
+    for pair in range(pairs2, pairs1):
+        act3[pair] = jnp.zeros((EDGE + 1, PAIRS, BLK), BF16)
 
     def fourth(step, carry):
-        y = step * 3
-        result = dot_nt(w4_ref[...], act3[pl.ds(y, 3)].reshape(3 * NT, 2 * BLK))
-        for row in range(3):
-            part[y + row] = result[:, row * NT : (row + 1) * NT]
+        pair = step * 4
+        cells = [act3[pl.ds(pair, 4), blk].reshape(4 * PAIRS, BLK) for blk in range(EDGE)]
+        result = dot_nt(w4_ref[...], jnp.concatenate(cells, axis=1))
+        for half in range(2):
+            columns = result[:, half * NT : (half + 1) * NT]
+            sums = jnp.concatenate(
+                [
+                    jnp.concatenate(
+                        [columns[(yi * 4 + j) * FX : (yi * 4 + j + 1) * FX] for j in range(4)],
+                        axis=1,
+                    )
+                    for yi in range(4)
+                ],
+                axis=0,
+            )
+            high = sums.astype(BF16)
+            low = (sums - high.astype(F32)).astype(BF16)
+            both = dot(jnp.concatenate([high, low], axis=0), from_pairs)
+            share = both[: 4 * FX] + both[4 * FX :]
+            for i in range(2):
+                part[pair + half * 2 + i] = share[:, i * NT : (i + 1) * NT]
         return carry
 
-    lax.fori_loop(0, (ty + 10) // 3, fourth, 0, unroll=7)
+    lax.fori_loop(0, pairs1 // 4, fourth, 0, unroll=2)
 
     for x in range(FX):
         prob[x * yw : x * yw + H, :] = jnp.zeros((H, NT), F32)
         prob[(x + 1) * yw - H : (x + 1) * yw, :] = jnp.zeros((H, NT), F32)
 
     def order(step, carry):
-        sums = []
-        for row in range(8):
-            y = step * 8 + row
-            total = (
-                part[y, 0 : 3 * FX] + part[y + 1, 3 * FX : 6 * FX] + part[y + 2, 6 * FX : 9 * FX]
-            )
-            sums.append(jnp.concatenate([total[i * FX : (i + 1) * FX] for i in range(3)], axis=1))
-        sums = jnp.concatenate(sums, axis=0)
-        high = sums.astype(BF16)
-        low = (sums - high.astype(F32)).astype(BF16)
-        both = dot(jnp.concatenate([high, low], axis=0), from_tiles)
-        values = both[: 8 * FX] + both[8 * FX :]
-        values = (1.0 / (1.0 + jnp.exp(-values))).astype(BF16).astype(F32)
-        for row in range(8):
-            prob[pl.ds(step * 8 + row + 4, FX, stride=yw), :] = values[row * FX : (row + 1) * FX]
+        for i in range(4):
+            pair = step * 4 + i + 1
+            even = part[pair, FX : 2 * FX] + part[pair - 1, 3 * FX :]
+            odd = part[pair, 2 * FX : 3 * FX] + part[pair + 1, :FX]
+            for row, values in enumerate((even, odd)):
+                values = (1.0 / (1.0 + jnp.exp(-values))).astype(BF16).astype(F32)
+                prob[pl.ds(2 * pair + 2 + row, FX, stride=yw), :] = values
         return carry
 
     lax.fori_loop(0, (ty + 8) // 8, order, 0)
@@ -481,7 +552,8 @@
                 ref[which, row] = wave[to + row, H : H + ty, :].astype(BF16)
 
 
-def last_kernel(ty, mom_ref, face, wave2, out_ref):
+def last_kernel(ty, mom_ref, face, wave2, after_ref, out_ref):
+    del after_ref
     shifts = plane_shifts(ty + 2 * H)
 
     def finish(step, total):
@@ -554,10 +626,10 @@
     w1, w2, w3, w4 = pl.pallas_call(
         prep_kernel,
         out_shape=[
-            jax.ShapeDtypeStruct((3 * 4 * XW, 4 * BLK), BF16),
-            jax.ShapeDtypeStruct((9, BLK, BLK), BF16),
-            jax.ShapeDtypeStruct((9, BLK, BLK), BF16),
-            jax.ShapeDtypeStruct((9 * FX, 2 * BLK), BF16),
+            jax.ShapeDtypeStruct((16 * XW, (EDGE + 1) * BLK), BF16),
+            jax.ShapeDtypeStruct((6 * BLK, BLK), BF16),
+            jax.ShapeDtypeStruct((6 * BLK, BLK), BF16),
+            jax.ShapeDtypeStruct((16 * FX, EDGE * BLK), BF16),
         ],
         in_specs=[pl.BlockSpec(memory_space=pltpu.HBM)] * 4 + [pl.BlockSpec(memory_space=pl.ANY)],
         out_specs=vmem(4),
@@ -591,11 +663,10 @@
         out_specs=vmem(3),
         scratch_shapes=[
             pltpu.VMEM(((XW + 2) * yw, NT), F32),
-            pltpu.VMEM((yw + 2, XW, NT), F32),
-            pltpu.VMEM((yw, 2, PAD, BLK), BF16),
-            pltpu.VMEM((ty + 12, 2, PAD, BLK), BF16),
-            pltpu.VMEM((ty + 10, NT, 2 * BLK), BF16),
-            pltpu.VMEM((ty + 10, 9 * FX, NT), F32),
+            pltpu.VMEM((yw + 2, XW, NT), BF16),
+            pltpu.VMEM((3, yw // 2, EDGE + 1, PAIRS, BLK), BF16),
+            pltpu.VMEM((3, yw // 2, EDGE, PAIRS, BLK), BF16),
+            pltpu.VMEM((yw // 2, 4 * FX, NT), F32),
             pltpu.VMEM((3, FX + 4, yw, NT), F32),
         ],
         compiler_params=pltpu.CompilerParams(vmem_limit_bytes=46 * 2**20),
@@ -628,20 +699,20 @@
         name="solver_waves",
     )(prob, slope)
 
+    arrived = [waves[0]]
+    for place in range(1, n_gy):
+        pairs = [(i, (i + place) % n_gy) for i in range(n_gy)]
+        arrived.append(lax.ppermute(waves[place], "gy", pairs))
+
     everyone = pl.pallas_call(
         functools.partial(last_kernel, ty),
         out_shape=jax.ShapeDtypeStruct((n_gx * n_gy, 8, NT), F32),
-        in_specs=vmem(3),
+        in_specs=vmem(3) + [pl.BlockSpec(memory_space=pl.ANY)],
         out_specs=pl.BlockSpec(memory_space=pltpu.VMEM),
         compiler_params=pltpu.CompilerParams(vmem_limit_bytes=16 * 2**20),
         cost_estimate=pl.CostEstimate(flops=10**9, bytes_accessed=10**8, transcendentals=0),
         name="last_moment",
-    )(moments, face, wave2)
-
-    arrived = [waves[0]]
-    for place in range(1, n_gy):
-        pairs = [(i, (i + place) % n_gy) for i in range(n_gy)]
-        arrived.append(lax.ppermute(waves[place], "gy", pairs))
+    )(moments, face, wave2, arrived[-1])
     moments = lax.all_to_all(everyone, ("gx", "gy"), split_axis=0, concat_axis=0, tiled=True)
     shift_field = pl.pallas_call(
         functools.partial(combine_kernel, n_gy, ty),

time: 85.4 us -> 91.3 us (1.069)
  waiting for transfers between devices: 7.68 us -> 11.9 us
  starting transfers between devices: 26.2 us -> 28.1 us
    ppermute x3, waiting for transfers between devices: 7.59 us -> 11.8 us  [on_device(): arrived.append(lax.ppermute(waves[place], 'gy', pairs))]
    ppermute x3, starting transfers between devices: 5.65 us -> 8.93 us  [on_device(): arrived.append(lax.ppermute(waves[place], 'gy', pairs))]
    all_to_all x1, starting transfers between devices: 10 us -> 8.58 us  [on_device(): lax.all_to_all(everyone, ('gx', 'gy'), split_axis=0, concat_axis=0, tiled...]
    pallas_call x1, Pallas kernels: 38.7 us -> 37.5 us  [on_device(): pl.pallas_call(functools.partial(net_kernel, grid_x, grid_y, ty), out_sha...]
    pallas_call x1, Pallas kernels: 2.16 us -> 3.21 us  [on_device(): pl.pallas_call(prep_kernel, out_shape=[jax.ShapeDtypeStruct((16 * XW, (ED...]
  transfers between devices with their start and end apart: 8 -> 8, of which waited for: 3 -> 4; matrix products, arithmetic and copies ran while one was open for 1% -> 1% of each run, Pallas kernels for 3% -> 4%
where the time goes in v5:
time: 91.3 us; the launch traced here: 90.8 us
  Pallas kernels  45.2 us (50%)
  starting transfers between devices  28.1 us (31%)
  waiting for transfers between devices  11.9 us (13%)
  local copies, waits for them, and re-layouts  4.87 us (5%)
    pallas_call x1, Pallas kernels, on_device(): pl.pallas_call(functools.partial(net_kernel, grid_x, grid_y, ty), out_sha...  37.5 us
    ppermute x3, waiting for transfers between devices, on_device(): arrived.append(lax.ppermute(waves[place], 'gy', pairs))  11.8 us
    ppermute x4, starting transfers between devices, shift(): return lax.ppermute(values, axis, pairs)  10.5 us
    ppermute x3, starting transfers between devices, on_device(): arrived.append(lax.ppermute(waves[place], 'gy', pairs))  8.93 us
    all_to_all x1, starting transfers between devices, on_device(): lax.all_to_all(everyone, ('gx', 'gy'), split_axis=0, concat_axis=0, tiled...  8.58 us
    pallas_call x1, Pallas kernels, on_device(): pl.pallas_call(prep_kernel, out_shape=[jax.ShapeDtypeStruct((16 * XW, (ED...  3.21 us
    unnamed x10, local copies, waits for them, and re-layouts  3.19 us
    pallas_call x1, Pallas kernels, on_device(): pl.pallas_call(functools.partial(waves_kernel, grid_x, grid_y, ty), out_s...  2.39 us
  transfers between devices with their start and end apart: 8, of which 4 were waited for; matrix products, arithmetic and copies ran while one was open for 1% of the time, Pallas kernels for 4%

profile of v5, /device:TPU:0, one launch (start us, length us, event | category | flops | bytes accessed | tf_op | source)
XLA Modules:
  0.0 90.8 jit_solution(10865504688635087923)
XLA Ops:
  0.6 0.9 fusion.1
  1.5 1.3 %collective-permute-start.1 = (bf16[8,32,128]{2,1,0:T(8,128)(2,1)S(1)}, bf16[8,32,128]{2,1,0:T(8,128)(2,1)S(1)}, u32[]{:S(2)}, u32[]{:S(2)}) collective-permute-start(bf16[8,32,128]{2,1,0:T(8,128)(2,1)S(1)} %get-tuple-element.32), channel_id=1, source_target_pairs={{4,0},{8,4},{12,8},{16,12},{20,16},{24,20},{28,24},{5,1},{9,5},{13... | collective-permute-start | bytes 196616 | tf_op jit(solution)/shard_map/ppermute | solution.py:609
  2.8 3.0 %collective-permute-start = (bf16[8,32,128]{2,1,0:T(8,128)(2,1)S(1)}, bf16[8,32,128]{2,1,0:T(8,128)(2,1)S(1)}, u32[]{:S(2)}, u32[]{:S(2)}) collective-permute-start(bf16[8,32,128]{2,1,0:T(8,128)(2,1)S(1)} %get-tuple-element.33), channel_id=1, source_target_pairs={{0,4},{4,8},{8,12},{12,16},{16,20},{20,24},{24,28},{1,5},{5,9},{9,... | collective-permute-start | bytes 196616 | tf_op jit(solution)/shard_map/ppermute | solution.py:609
  5.9 0.8 fusion
  6.6 0.0 collective-permute-done.1.xhigh_ref
  6.7 0.1 collective-permute-done.after_ref.xlow_ref
  6.8 4.9 %collective-permute-start.2 = (bf16[32,8,128]{2,1,0:T(8,128)(2,1)S(1)}, bf16[32,8,128]{2,1,0:T(8,128)(2,1)S(1)}, u32[]{:S(2)}, u32[]{:S(2)}) collective-permute-start(bf16[32,8,128]{2,1,0:T(8,128)(2,1)S(1)} %pad_maximum_fusion), channel_id=1, source_target_pairs={{0,1},{1,2},{2,3},{4,5},{5,6},{6,7},{8,9},{9,10},{10,11},{12,13},{... | collective-permute-start | bytes 196616 | tf_op jit(solution)/shard_map/ppermute | solution.py:609
  11.7 1.3 %collective-permute-start.3 = (bf16[32,8,128]{2,1,0:T(8,128)(2,1)S(1)}, bf16[32,8,128]{2,1,0:T(8,128)(2,1)S(1)}, u32[]{:S(2)}, u32[]{:S(2)}) collective-permute-start(bf16[32,8,128]{2,1,0:T(8,128)(2,1)S(1)} %pad_maximum_fusion.1), channel_id=1, source_target_pairs={{1,0},{2,1},{3,2},{5,4},{6,5},{7,6},{9,8},{10,9},{11,10},{13,12},{... | collective-permute-start | bytes 196616 | tf_op jit(solution)/shard_map/ppermute | solution.py:609
  13.0 0.0 copy-start.1
  13.0 0.9 copy-done.1
  13.9 0.0 copy-start.2
  13.9 0.9 copy-done.2
  14.8 0.0 copy-start.3
  14.8 0.7 copy-done.3
  15.5 0.0 copy-start.4
  15.5 0.7 copy-done.4
  16.2 3.2 %band_weights.1 = (bf16[512,2048]{1,0:T(8,128)(2,1)S(1)}, bf16[1536,256]{1,0:T(8,128)(2,1)S(1)}, bf16[1536,256]{1,0:T(8,128)(2,1)S(1)}, bf16[384,1792]{1,0:T(8,128)(2,1)S(1)}) custom-call(bf16[1,3,3,3,16]{4,3,2,1,0:T(4,128)(2,1)S(1)} %bitcast.10, bf16[432,16]{1,0:T(8,128)(2,1)S(1)} %bitcast.8, bf16[432,16]{1,0:T(8,128)(2,1)S(1)} %bitcast.9, ...), custom_call_target="tpu_custom_call" | custom-call | flops 1000000000 | bytes 10000000 | tf_op jit(solution)/shard_map/band_weights/pallas_call | solution.py:626
  19.4 0.0 collective-permute-done.2.ylow_ref
  19.4 0.0 collective-permute-done.3.yhigh_ref
  19.4 0.0 copy-done
  19.5 37.5 %fault_net.1 = (bf16[16,32,128]{2,1,0:T(8,128)(2,1)}, f32[1152,128]{1,0:T(8,128)S(1)}, f32[2,26,48,128]{3,2,1,0:T(8,128)S(1)}) custom-call(bf16[16,32,128]{2,1,0:T(8,128)(2,1)S(1)} %copy-done, bf16[8,32,128]{2,1,0:T(8,128)(2,1)S(1)} %collective-permute-done.after_ref.xlow_ref, bf16[8,32,128]{2,1,0:T(8,128)(2,1)S(1)} %collective-permute-done.1.xhigh_ref, ...), custom_call_target="tpu_custom_call" | custom-call | flops 30000001024 | bytes 10000000 | tf_op jit(solution)/shard_map/fault_net/pallas_call | solution.py:655
  57.0 2.4 %solver_waves.1 = (f32[8,128]{1,0:T(8,128)S(1)}, f32[2,26,48,128]{3,2,1,0:T(8,128)S(1)}, f32[26,48,128]{2,1,0:T(8,128)S(1)}, bf16[3,4,32,128]{3,2,1,0:T(8,128)(2...) custom-call(f32[1152,128]{1,0:T(8,128)S(1)} %get-tuple-element.21.pr, ...), custom_call_target="tpu_custom_call" | custom-call | flops 100000000 | bytes 10000000 | tf_op jit(solution)/shard_map/solver_waves/pallas_call | solution.py:680
  59.4 4.7 %collective-permute-start.4 = (bf16[3,4,32,128]{3,2,1,0:T(8,128)(2,1)S(1)}, bf16[3,4,32,128]{3,2,1,0:T(8,128)(2,1)S(1)}, u32[]{:S(2)}, u32[]{:S(2)}) collective-permute-start(bf16[3,4,32,128]{3,2,1,0:T(8,128)(2,1)S(1)} %get-tuple-element.26), channel_id=1, source_target_pairs={{0,3},{1,0},{2,1},{3,2},{4,7},{5,4},{6,5},{7,6},{8,11},{9,8},{10,9... | collective-permute-start | bytes 294920 | tf_op jit(solution)/shard_map/ppermute | solution.py:705
  64.1 3.2 %collective-permute-done.4.after_ref.refs_3_ = bf16[3,4,32,128]{3,2,1,0:T(8,128)(2,1)S(1)} collective-permute-done((bf16[3,4,32,128]{3,2,1,0:T(8,128)(2,1)S(1)}, bf16[3,4,32,128]{3,2,1,0:T(8,128)(2,1)S(1)}, u32[]{:S(2)}, u32[]{:S(2)}) %collective-permute-start.4) | collective-permute-done | bytes 98336 | tf_op jit(solution)/shard_map/ppermute | solution.py:705
  67.3 1.1 %last_moment.1 = f32[32,8,128]{2,1,0:T(8,128)} custom-call(f32[8,128]{1,0:T(8,128)S(1)} %get-tuple-element.23.mom_ref, f32[2,26,48,128]{3,2,1,0:T(8,128)S(1)} %get-tuple-element.24.face, f32[26,48,128]{2,1,0:T(8,128)S(1)} %get-tuple-element.25.wave2, bf16[3,4,32,128]{3,2,1,0:T(8,128)(2,1)S(1)} %collective-permute-done.4.after_ref.refs_3_), custom_call_target="tpu_custom_call" | custom-call | flops 1000000000 | bytes 100000000 | tf_op jit(solution)/shard_map/last_moment/pallas_call | solution.py:707
  68.4 8.6 %all-to-all-start = ((f32[32,8,128]{2,1,0:T(8,128)}), f32[32,8,128]{2,1,0:T(8,128)S(1)}, u32[]{:S(2)}, u32[]{:S(2)}) async-start(f32[32,8,128]{2,1,0:T(8,128)} %last_moment.1), calls=%async_computation | async-start | bytes 262144 | tf_op jit(solution)/shard_map/all_to_all | solution.py:716
  77.0 1.8 %collective-permute-start.5 = (bf16[3,4,32,128]{3,2,1,0:T(8,128)(2,1)S(1)}, bf16[3,4,32,128]{3,2,1,0:T(8,128)(2,1)S(1)}, u32[]{:S(2)}, u32[]{:S(2)}) collective-permute-start(bf16[3,4,32,128]{3,2,1,0:T(8,128)(2,1)S(1)} %get-tuple-element.28), channel_id=1, source_target_pairs={{0,1},{1,2},{2,3},{3,0},{4,5},{5,6},{6,7},{7,4},{8,9},{9,10},{10,1... | collective-permute-start | bytes 294920 | tf_op jit(solution)/shard_map/ppermute | solution.py:705
  78.8 2.4 %collective-permute-start.6 = (bf16[3,4,32,128]{3,2,1,0:T(8,128)(2,1)S(1)}, bf16[3,4,32,128]{3,2,1,0:T(8,128)(2,1)S(1)}, u32[]{:S(2)}, u32[]{:S(2)}) collective-permute-start(bf16[3,4,32,128]{3,2,1,0:T(8,128)(2,1)S(1)} %get-tuple-element.29), channel_id=1, source_target_pairs={{0,2},{1,3},{2,0},{3,1},{4,6},{5,7},{6,4},{7,5},{8,10},{9,11},{10,... | collective-permute-start | bytes 294920 | tf_op jit(solution)/shard_map/ppermute | solution.py:705
  81.2 5.2 %collective-permute-done.5.refs_1_ = bf16[3,4,32,128]{3,2,1,0:T(8,128)(2,1)S(1)} collective-permute-done((bf16[3,4,32,128]{3,2,1,0:T(8,128)(2,1)S(1)}, bf16[3,4,32,128]{3,2,1,0:T(8,128)(2,1)S(1)}, u32[]{:S(2)}, u32[]{:S(2)}) %collective-permute-start.5) | collective-permute-done | bytes 98336 | tf_op jit(solution)/shard_map/ppermute | solution.py:705
  86.4 3.5 %collective-permute-done.6.refs_2_ = bf16[3,4,32,128]{3,2,1,0:T(8,128)(2,1)S(1)} collective-permute-done((bf16[3,4,32,128]{3,2,1,0:T(8,128)(2,1)S(1)}, bf16[3,4,32,128]{3,2,1,0:T(8,128)(2,1)S(1)}, u32[]{:S(2)}, u32[]{:S(2)}) %collective-permute-start.6) | collective-permute-done | bytes 98336 | tf_op jit(solution)/shard_map/ppermute | solution.py:705
  89.9 0.0 all-to-all-done.mom_ref
  89.9 0.9 %combine_waves.1 = f32[4,128,128]{2,1,0:T(8,128)} custom-call(f32[32,8,128]{2,1,0:T(8,128)S(1)} %all-to-all-done.mom_ref, bf16[3,4,32,128]{3,2,1,0:T(8,128)(2,1)S(1)} %get-tuple-element.27.refs_0_, bf16[3,4,32,128]{3,2,1,0:T(8,128)(2,1)S(1)} %collective-permute-done.5.refs_1_, bf16[3,4,32,128]{3,2,1,0:T(8,128)(2,1)S(1)} %collective-permute-done.6.refs_2_, ...), custom_call_target="tpu_custom_call" | custom-call | tf_op jit(solution)/shard_map/combine_waves/pallas_call | solution.py:717
  (5 shorter events, 0.0 us)
Async XLA Ops:
  1.5 5.1 %collective-permute-start.1 = (bf16[8,32,128]{2,1,0:T(8,128)(2,1)S(1)}, bf16[8,32,128]{2,1,0:T(8,128)(2,1)S(1)}, u32[]{:S(2)}, u32[]{:S(2)}) collective-permute-start(bf16[8,32,128]{2,1,0:T(8,128)(2,1)S(1)} %get-tuple-element.32), channel_id=1, source_target_pairs={{4,0},{8,4},{12,8},{16,12},{20,16},{24,20},{28,24},{5,1},{9,5},{13... | collective-permute-start | bytes 196616 | tf_op jit(solution)/shard_map/ppermute | solution.py:609
  2.8 3.9 %collective-permute-start = (bf16[8,32,128]{2,1,0:T(8,128)(2,1)S(1)}, bf16[8,32,128]{2,1,0:T(8,128)(2,1)S(1)}, u32[]{:S(2)}, u32[]{:S(2)}) collective-permute-start(bf16[8,32,128]{2,1,0:T(8,128)(2,1)S(1)} %get-tuple-element.33), channel_id=1, source_target_pairs={{0,4},{4,8},{8,12},{12,16},{16,20},{20,24},{24,28},{1,5},{5,9},{9,... | collective-permute-start | bytes 196616 | tf_op jit(solution)/shard_map/ppermute | solution.py:609
  6.8 12.7 %collective-permute-start.2 = (bf16[32,8,128]{2,1,0:T(8,128)(2,1)S(1)}, bf16[32,8,128]{2,1,0:T(8,128)(2,1)S(1)}, u32[]{:S(2)}, u32[]{:S(2)}) collective-permute-start(bf16[32,8,128]{2,1,0:T(8,128)(2,1)S(1)} %pad_maximum_fusion), channel_id=1, source_target_pairs={{0,1},{1,2},{2,3},{4,5},{5,6},{6,7},{8,9},{9,10},{10,11},{12,13},{... | collective-permute-start | bytes 196616 | tf_op jit(solution)/shard_map/ppermute | solution.py:609
  11.7 7.7 %collective-permute-start.3 = (bf16[32,8,128]{2,1,0:T(8,128)(2,1)S(1)}, bf16[32,8,128]{2,1,0:T(8,128)(2,1)S(1)}, u32[]{:S(2)}, u32[]{:S(2)}) collective-permute-start(bf16[32,8,128]{2,1,0:T(8,128)(2,1)S(1)} %pad_maximum_fusion.1), channel_id=1, source_target_pairs={{1,0},{2,1},{3,2},{5,4},{6,5},{7,6},{9,8},{10,9},{11,10},{13,12},{... | collective-permute-start | bytes 196616 | tf_op jit(solution)/shard_map/ppermute | solution.py:609
  13.0 0.9 copy-start.1
  13.9 0.9 copy-start.2
  14.8 0.7 copy-start.3
  15.5 0.7 copy-start.4
  16.2 3.2 %copy-start = (bf16[16,32,128]{2,1,0:T(8,128)(2,1)S(1)}, bf16[16,32,128]{2,1,0:T(8,128)(2,1)}, u32[]{:S(2)}) copy-start(bf16[16,32,128]{2,1,0:T(8,128)(2,1)} %amp_ref.1) | copy-start | bytes 393220
  59.4 7.9 %collective-permute-start.4 = (bf16[3,4,32,128]{3,2,1,0:T(8,128)(2,1)S(1)}, bf16[3,4,32,128]{3,2,1,0:T(8,128)(2,1)S(1)}, u32[]{:S(2)}, u32[]{:S(2)}) collective-permute-start(bf16[3,4,32,128]{3,2,1,0:T(8,128)(2,1)S(1)} %get-tuple-element.26), channel_id=1, source_target_pairs={{0,3},{1,0},{2,1},{3,2},{4,7},{5,4},{6,5},{7,6},{8,11},{9,8},{10,9... | collective-permute-start | bytes 294920 | tf_op jit(solution)/shard_map/ppermute | solution.py:705
  68.4 21.5 %all-to-all-start = ((f32[32,8,128]{2,1,0:T(8,128)}), f32[32,8,128]{2,1,0:T(8,128)S(1)}, u32[]{:S(2)}, u32[]{:S(2)}) async-start(f32[32,8,128]{2,1,0:T(8,128)} %last_moment.1), calls=%async_computation | async-start | bytes 262144 | tf_op jit(solution)/shard_map/all_to_all | solution.py:716
  77.0 9.4 %collective-permute-start.5 = (bf16[3,4,32,128]{3,2,1,0:T(8,128)(2,1)S(1)}, bf16[3,4,32,128]{3,2,1,0:T(8,128)(2,1)S(1)}, u32[]{:S(2)}, u32[]{:S(2)}) collective-permute-start(bf16[3,4,32,128]{3,2,1,0:T(8,128)(2,1)S(1)} %get-tuple-element.28), channel_id=1, source_target_pairs={{0,1},{1,2},{2,3},{3,0},{4,5},{5,6},{6,7},{7,4},{8,9},{9,10},{10,1... | collective-permute-start | bytes 294920 | tf_op jit(solution)/shard_map/ppermute | solution.py:705
  78.8 11.1 %collective-permute-start.6 = (bf16[3,4,32,128]{3,2,1,0:T(8,128)(2,1)S(1)}, bf16[3,4,32,128]{3,2,1,0:T(8,128)(2,1)S(1)}, u32[]{:S(2)}, u32[]{:S(2)}) collective-permute-start(bf16[3,4,32,128]{3,2,1,0:T(8,128)(2,1)S(1)} %get-tuple-element.29), channel_id=1, source_target_pairs={{0,2},{1,3},{2,0},{3,1},{4,6},{5,7},{6,4},{7,5},{8,10},{9,11},{10,... | collective-permute-start | bytes 294920 | tf_op jit(solution)/shard_map/ppermute | solution.py:705

commit v6 on v5

--- a/solution.py
+++ b/solution.py
@@ -141,12 +141,12 @@
 
 def input_cells():
     tiles = []
-    for times in ((0, 1), (-1, 2)):
+    here = [(t, x) for t in (0, 1) for x in range(4)]
+    near = [(2, 2), (2, 3), (-1, 0), (-1, 1), (-1, 2), (-1, 3), (2, 0), (2, 1)]
+    side = [(0, 4), (2, -1), (-1, 4), (0, -1), (1, 4), (-1, -1), (2, 4), (1, -1)]
+    for cells in (here, near, side):
         for rows in ((0, 1), (-1, 2)):
-            tiles.append([(y, t, x) for y in rows for t in times for x in range(4)])
-    for rows in ((0, 1), (-1, 2)):
-        side = [(0, 4), (-1, 4), (-1, -1), (0, -1), (1, 4), (2, 4), (2, -1), (1, -1)]
-        tiles.append([(y, t, x) for y in rows for t, x in side])
+            tiles.append([(y, t, x) for y in rows for t, x in cells])
     return tiles
 
 
@@ -244,23 +244,23 @@
                 at = x0 - 6 + 4 * blk + slot
             else:
                 at = x0 + jnp.where(slot == 0, 22, -7)
-            masks.append((at >= 0) & (at < grid_x))
+            masks.append(jnp.where((at >= 0) & (at < grid_x), 1.0, 0.0))
         return masks
 
     second_row = iota((1, BLK), 1) >= 128
 
-    def scale(mask, y):
+    def row_mask(y):
         at = y0 + y + jnp.where(second_row, 1, 0)
-        return jnp.where(mask & (at >= 0) & (at < grid_y), 1.0, 0.0)
+        return jnp.where((at >= 0) & (at < grid_y), 1.0, 0.0)
 
     sub_row = iota((SUB, 128), 0)
-    early = iota((PAIRS, 128), 1) < 64
-    slot = iota((PAIRS, 128), 1) // CH % 4
+    place = iota((PAIRS, 128), 1) // CH
+    early = (place >= 2) & (place < 6)
 
     def put(act, pair, blk, values):
         act[0, pair, blk] = values.astype(BF16)
         for half in range(2):
-            turned = pltpu.roll(values[:, half * 128 : (half + 1) * 128], 64, 1)
+            turned = pltpu.roll(values[:, half * 128 : (half + 1) * 128], 96, 1)
             head = jnp.where(sub_row == 0, 0.0, pltpu.roll(turned[PAIRS - SUB :], 1, 0))
             tail = jnp.where(sub_row == SUB - 1, 0.0, pltpu.roll(turned[:SUB], SUB - 1, 0))
             before = jnp.concatenate([head, turned[: PAIRS - SUB]], axis=0)
@@ -273,18 +273,9 @@
             left, right = (blk - 1) % blocks, (blk + 1) % blocks
             for half in range(2):
                 at = slice(half * 128, (half + 1) * 128)
-                here = jnp.where(
-                    slot == 0,
-                    act[0, pair, right, :, at].astype(F32),
-                    act[0, pair, left, :, at].astype(F32),
-                )
-                near = jnp.where(
-                    slot == 1,
-                    pltpu.roll(act[1, pair, right, :, at].astype(F32), CH, 1),
-                    pltpu.roll(act[1, pair, left, :, at].astype(F32), 128 - CH, 1),
-                )
-                mixed = jnp.where((slot == 0) | (slot == 3), here, near)
-                act[2, pair, blk, :, at] = mixed.astype(BF16)
+                even = jnp.where(place % 4 == 0, act[0, pair, right, :, at], act[1, pair, right, :, at])
+                odd = jnp.where(place % 4 == 3, act[0, pair, left, :, at], act[1, pair, left, :, at])
+                act[2, pair, blk, :, at] = jnp.where(place % 2 == 0, even, odd)
 
     mask1 = lane_masks(EDGE + 1)
 
@@ -299,9 +290,10 @@
         result = dot(jnp.concatenate(pieces, axis=0), w1_ref[...])
         for i in range(FIRST):
             pair = step * FIRST + i
+            inside = row_mask(2 * pair - H)
             for blk in range(EDGE + 1):
                 values = result[i * PAIRS : (i + 1) * PAIRS, blk * BLK : (blk + 1) * BLK]
-                put(act1, pair, blk, jnp.maximum(values, 0.0) * scale(mask1[blk], 2 * pair - H))
+                put(act1, pair, blk, jnp.maximum(values, 0.0) * (mask1[blk] * inside))
             put_sides(act1, pair, EDGE + 1)
         return carry
 
@@ -359,10 +351,11 @@
             result = layer(act1, w2_ref, step * SECOND + begin, count)
             for i in range(count):
                 pair = step * SECOND + begin + i
+                inside = row_mask(2 * pair - 6)
                 for blk in range(EDGE):
                     at = (i * EDGE + blk) * PAIRS
                     values = jnp.maximum(result[at : at + PAIRS], 0.0)
-                    put(act2, pair + 1, blk, values * scale(mask2[blk], 2 * pair - 6))
+                    put(act2, pair + 1, blk, values * (mask2[blk] * inside))
                 put_sides(act2, pair + 1, EDGE)
         return carry
 
@@ -381,11 +374,11 @@
             result = layer(act2, w3_ref, step * THIRD + begin, count)
             for i in range(count):
                 pair = step * THIRD + begin + i
+                inside = row_mask(2 * pair - 6)
                 for blk in range(EDGE):
                     at = (i * EDGE + blk) * PAIRS
                     values = jnp.maximum(result[at : at + PAIRS], 0.0)
-                    values = values * scale(mask2[blk], 2 * pair - 6)
-                    act3[pair, blk] = values.astype(BF16)
+                    act3[pair, blk] = (values * (mask2[blk] * inside)).astype(BF16)
         return carry
 
     lax.fori_loop(0, steps3, third, 0)
@@ -552,8 +545,7 @@
                 ref[which, row] = wave[to + row, H : H + ty, :].astype(BF16)
 
 
-def last_kernel(ty, mom_ref, face, wave2, after_ref, out_ref):
-    del after_ref
+def last_kernel(ty, mom_ref, face, wave2, out_ref):
     shifts = plane_shifts(ty + 2 * H)
 
     def finish(step, total):
@@ -563,7 +555,9 @@
 
     total = lax.fori_loop(0, TX // RX, finish, jnp.zeros((ty, NT), F32))
     a4 = jnp.sum(total, axis=0, keepdims=True)
-    values = jnp.where(iota((8, NT), 0) == 5, a4, mom_ref[...])
+    sums = jnp.sum(jnp.where(iota((8, NT), 0) == 5, a4, mom_ref[...]), axis=1, keepdims=True)
+    values = jnp.where(iota((8, NT), 0) == iota((8, NT), 1), sums, 0.0)
+    values = jnp.sum(values, axis=0, keepdims=True)
     for device in range(out_ref.shape[0]):
         out_ref[device] = values
 
@@ -571,9 +565,9 @@
 def combine_kernel(n_gy, ty, mom_ref, *refs):
     waves_refs, out_ref = refs[:n_gy], refs[n_gy]
     place_y = lax.axis_index("gy")
-    moments = jnp.sum(jnp.sum(mom_ref[...], axis=0), axis=1, keepdims=True)
+    moments = jnp.sum(mom_ref[...], axis=0)
     b0, a0, a1, a2, a3, a4 = [
-        jnp.broadcast_to(moments[i : i + 1], (1, NT)) for i in range(6)
+        jnp.broadcast_to(moments[:, i : i + 1], (1, NT)) for i in range(6)
     ]
     a0, a1, a2, a3, a4 = [v / b0 for v in (a0, a1, a2, a3, a4)]
     l21 = a1 / a0
@@ -706,13 +700,13 @@
 
     everyone = pl.pallas_call(
         functools.partial(last_kernel, ty),
-        out_shape=jax.ShapeDtypeStruct((n_gx * n_gy, 8, NT), F32),
-        in_specs=vmem(3) + [pl.BlockSpec(memory_space=pl.ANY)],
+        out_shape=jax.ShapeDtypeStruct((n_gx * n_gy, 1, NT), F32),
+        in_specs=vmem(3),
         out_specs=pl.BlockSpec(memory_space=pltpu.VMEM),
         compiler_params=pltpu.CompilerParams(vmem_limit_bytes=16 * 2**20),
         cost_estimate=pl.CostEstimate(flops=10**9, bytes_accessed=10**8, transcendentals=0),
         name="last_moment",
-    )(moments, face, wave2, arrived[-1])
+    )(moments, face, wave2)
     moments = lax.all_to_all(everyone, ("gx", "gy"), split_axis=0, concat_axis=0, tiled=True)
     shift_field = pl.pallas_call(
         functools.partial(combine_kernel, n_gy, ty),

time: 91.3 us -> 80 us (0.88)
  blocking collectives: 0 us -> 13.1 us
  waiting for transfers between devices: 11.9 us -> 0.09 us
  starting transfers between devices: 28.1 us -> 17.2 us
  Pallas kernels: 45.2 us -> 43.5 us
    all_to_all x0 -> x1, blocking collectives: none -> 13.1 us  [on_device(): lax.all_to_all(everyone, ('gx', 'gy'), split_axis=0, concat_axis=0, tiled...]
    ppermute x3, waiting for transfers between devices: 11.8 us -> 0.01 us  [on_device(): arrived.append(lax.ppermute(waves[place], 'gy', pairs))]
    all_to_all x1 -> x0, starting transfers between devices: 8.58 us -> none  [on_device(): lax.all_to_all(everyone, ('gx', 'gy'), split_axis=0, concat_axis=0, tiled...]
    ppermute x3, starting transfers between devices: 8.93 us -> 6.64 us  [on_device(): arrived.append(lax.ppermute(waves[place], 'gy', pairs))]
    pallas_call x1, Pallas kernels: 37.5 us -> 36.4 us  [on_device(): pl.pallas_call(functools.partial(net_kernel, grid_x, grid_y, ty), out_sha...]
  transfers between devices with their start and end apart: 8 -> 7, of which waited for: 4 -> 1; matrix products, arithmetic and copies ran while one was open for 1% -> 1% of each run, Pallas kernels for 4% -> 5%
where the time goes in v6:
time: 80 us; the launch traced here: 79.5 us
  Pallas kernels  43.5 us (54%)
  starting transfers between devices  17.2 us (22%)
  blocking collectives  13.1 us (16%)
  local copies, waits for them, and re-layouts  4.87 us (6%)
    pallas_call x1, Pallas kernels, on_device(): pl.pallas_call(functools.partial(net_kernel, grid_x, grid_y, ty), out_sha...  36.4 us
    all_to_all x1, blocking collectives, on_device(): lax.all_to_all(everyone, ('gx', 'gy'), split_axis=0, concat_axis=0, tiled...  13.1 us
    ppermute x4, starting transfers between devices, shift(): return lax.ppermute(values, axis, pairs)  10.5 us
    ppermute x3, starting transfers between devices, on_device(): arrived.append(lax.ppermute(waves[place], 'gy', pairs))  6.64 us
    pallas_call x1, Pallas kernels, on_device(): pl.pallas_call(prep_kernel, out_shape=[jax.ShapeDtypeStruct((16 * XW, (ED...  3.22 us
    unnamed x10, local copies, waits for them, and re-layouts  3.19 us
    pallas_call x1, Pallas kernels, on_device(): pl.pallas_call(functools.partial(waves_kernel, grid_x, grid_y, ty), out_s...  2.39 us
  transfers between devices with their start and end apart: 7, of which 1 were waited for; matrix products, arithmetic and copies ran while one was open for 1% of the time, Pallas kernels for 5%

profile of v6, /device:TPU:0, one launch (start us, length us, event | category | flops | bytes accessed | tf_op | source)
XLA Modules:
  0.0 79.5 jit_solution(13764306540339859534)
XLA Ops:
  0.6 0.9 %fusion.1 = (bf16[8,32,128]{2,1,0:T(8,128)(2,1)S(1)}, bf16[8,32,128]{2,1,0:T(8,128)(2,1)S(1)}) fusion(bf16[16,32,128]{2,1,0:T(8,128)(2,1)} %amp_ref.1), kind=kLoop, calls=%fused_computation.3 | loop fusion | bytes 262144 | tf_op jit(solution)/shard_map/slice | solution.py:606
  1.5 1.3 %collective-permute-start.1 = (bf16[8,32,128]{2,1,0:T(8,128)(2,1)S(1)}, bf16[8,32,128]{2,1,0:T(8,128)(2,1)S(1)}, u32[]{:S(2)}, u32[]{:S(2)}) collective-permute-start(bf16[8,32,128]{2,1,0:T(8,128)(2,1)S(1)} %get-tuple-element.32), channel_id=1, source_target_pairs={{4,0},{8,4},{12,8},{16,12},{20,16},{24,20},{28,24},{5,1},{9,5},{13... | collective-permute-start | bytes 196616 | tf_op jit(solution)/shard_map/ppermute | solution.py:603
  2.8 3.0 %collective-permute-start = (bf16[8,32,128]{2,1,0:T(8,128)(2,1)S(1)}, bf16[8,32,128]{2,1,0:T(8,128)(2,1)S(1)}, u32[]{:S(2)}, u32[]{:S(2)}) collective-permute-start(bf16[8,32,128]{2,1,0:T(8,128)(2,1)S(1)} %get-tuple-element.33), channel_id=1, source_target_pairs={{0,4},{4,8},{8,12},{12,16},{16,20},{20,24},{24,28},{1,5},{5,9},{9,... | collective-permute-start | bytes 196616 | tf_op jit(solution)/shard_map/ppermute | solution.py:603
  5.9 0.8 fusion
  6.6 0.0 collective-permute-done.1.xhigh_ref
  6.7 0.1 collective-permute-done.after_ref.xlow_ref
  6.8 4.9 %collective-permute-start.2 = (bf16[32,8,128]{2,1,0:T(8,128)(2,1)S(1)}, bf16[32,8,128]{2,1,0:T(8,128)(2,1)S(1)}, u32[]{:S(2)}, u32[]{:S(2)}) collective-permute-start(bf16[32,8,128]{2,1,0:T(8,128)(2,1)S(1)} %pad_maximum_fusion), channel_id=1, source_target_pairs={{0,1},{1,2},{2,3},{4,5},{5,6},{6,7},{8,9},{9,10},{10,11},{12,13},{... | collective-permute-start | bytes 196616 | tf_op jit(solution)/shard_map/ppermute | solution.py:603
  11.7 1.3 %collective-permute-start.3 = (bf16[32,8,128]{2,1,0:T(8,128)(2,1)S(1)}, bf16[32,8,128]{2,1,0:T(8,128)(2,1)S(1)}, u32[]{:S(2)}, u32[]{:S(2)}) collective-permute-start(bf16[32,8,128]{2,1,0:T(8,128)(2,1)S(1)} %pad_maximum_fusion.1), channel_id=1, source_target_pairs={{1,0},{2,1},{3,2},{5,4},{6,5},{7,6},{9,8},{10,9},{11,10},{13,12},{... | collective-permute-start | bytes 196616 | tf_op jit(solution)/shard_map/ppermute | solution.py:603
  13.0 0.0 copy-start.1
  13.0 0.9 %copy-done.1 = bf16[16,16,3,3,3]{1,0,4,3,2:T(8,128)(2,1)S(1)} copy-done((bf16[16,16,3,3,3]{1,0,4,3,2:T(8,128)(2,1)S(1)}, bf16[16,16,3,3,3]{1,0,4,3,2:T(8,128)(2,1)}, u32[]{:S(2)}) %copy-start.1) | copy-done | bytes 13848
  13.9 0.0 copy-start.2
  13.9 0.9 %copy-done.2 = bf16[16,16,3,3,3]{1,0,4,3,2:T(8,128)(2,1)S(1)} copy-done((bf16[16,16,3,3,3]{1,0,4,3,2:T(8,128)(2,1)S(1)}, bf16[16,16,3,3,3]{1,0,4,3,2:T(8,128)(2,1)}, u32[]{:S(2)}) %copy-start.2) | copy-done | bytes 13848
  14.8 0.0 copy-start.3
  14.8 0.7 copy-done.3
  15.5 0.0 copy-start.4
  15.5 0.7 copy-done.4
  16.2 0.0 copy-start
  16.2 3.2 %band_weights.1 = (bf16[512,2048]{1,0:T(8,128)(2,1)S(1)}, bf16[1536,256]{1,0:T(8,128)(2,1)S(1)}, bf16[1536,256]{1,0:T(8,128)(2,1)S(1)}, bf16[384,1792]{1,0:T(8,128)(2,1)S(1)}) custom-call(bf16[1,3,3,3,16]{4,3,2,1,0:T(4,128)(2,1)S(1)} %bitcast.10, bf16[432,16]{1,0:T(8,128)(2,1)S(1)} %bitcast.8, bf16[432,16]{1,0:T(8,128)(2,1)S(1)} %bitcast.9, ...), custom_call_target="tpu_custom_call" | custom-call | flops 1000000000 | bytes 10000000 | tf_op jit(solution)/shard_map/band_weights/pallas_call | solution.py:620
  19.4 0.0 collective-permute-done.2.ylow_ref
  19.5 0.0 collective-permute-done.3.yhigh_ref
  19.5 0.0 copy-done
  19.5 36.4 %fault_net.1 = (bf16[16,32,128]{2,1,0:T(8,128)(2,1)}, f32[1152,128]{1,0:T(8,128)S(1)}, f32[2,26,48,128]{3,2,1,0:T(8,128)S(1)}) custom-call(bf16[16,32,128]{2,1,0:T(8,128)(2,1)S(1)} %copy-done, bf16[8,32,128]{2,1,0:T(8,128)(2,1)S(1)} %collective-permute-done.after_ref.xlow_ref, bf16[8,32,128]{2,1,0:T(8,128)(2,1)S(1)} %collective-permute-done.1.xhigh_ref, ...), custom_call_target="tpu_custom_call" | custom-call | flops 30000001024 | bytes 10000000 | tf_op jit(solution)/shard_map/fault_net/pallas_call | solution.py:649
  55.9 2.4 %solver_waves.1 = (f32[8,128]{1,0:T(8,128)S(1)}, f32[2,26,48,128]{3,2,1,0:T(8,128)S(1)}, f32[26,48,128]{2,1,0:T(8,128)S(1)}, bf16[3,4,32,128]{3,2,1,0:T(8,128)(2...) custom-call(f32[1152,128]{1,0:T(8,128)S(1)} %get-tuple-element.21.pr, ...), custom_call_target="tpu_custom_call" | custom-call | flops 100000000 | bytes 10000000 | tf_op jit(solution)/shard_map/solver_waves/pallas_call | solution.py:674
  58.3 2.7 %collective-permute-start.4 = (bf16[3,4,32,128]{3,2,1,0:T(8,128)(2,1)S(1)}, bf16[3,4,32,128]{3,2,1,0:T(8,128)(2,1)S(1)}, u32[]{:S(2)}, u32[]{:S(2)}) collective-permute-start(bf16[3,4,32,128]{3,2,1,0:T(8,128)(2,1)S(1)} %get-tuple-element.27), channel_id=1, source_target_pairs={{0,1},{1,2},{2,3},{3,0},{4,5},{5,6},{6,7},{7,4},{8,9},{9,10},{10,1... | collective-permute-start | bytes 294920 | tf_op jit(solution)/shard_map/ppermute | solution.py:699
  61.0 2.6 %collective-permute-start.5 = (bf16[3,4,32,128]{3,2,1,0:T(8,128)(2,1)S(1)}, bf16[3,4,32,128]{3,2,1,0:T(8,128)(2,1)S(1)}, u32[]{:S(2)}, u32[]{:S(2)}) collective-permute-start(bf16[3,4,32,128]{3,2,1,0:T(8,128)(2,1)S(1)} %get-tuple-element.28), channel_id=1, source_target_pairs={{0,2},{1,3},{2,0},{3,1},{4,6},{5,7},{6,4},{7,5},{8,10},{9,11},{10,... | collective-permute-start | bytes 294920 | tf_op jit(solution)/shard_map/ppermute | solution.py:699
  63.6 1.3 %collective-permute-start.6 = (bf16[3,4,32,128]{3,2,1,0:T(8,128)(2,1)S(1)}, bf16[3,4,32,128]{3,2,1,0:T(8,128)(2,1)S(1)}, u32[]{:S(2)}, u32[]{:S(2)}) collective-permute-start(bf16[3,4,32,128]{3,2,1,0:T(8,128)(2,1)S(1)} %get-tuple-element.29), channel_id=1, source_target_pairs={{0,3},{1,0},{2,1},{3,2},{4,7},{5,4},{6,5},{7,6},{8,11},{9,8},{10,9... | collective-permute-start | bytes 294920 | tf_op jit(solution)/shard_map/ppermute | solution.py:699
  65.0 0.6 last_moment.1
  65.5 13.1 %all_to_all.5.mom_ref = f32[32,1,128]{2,1,0:T(1,128)S(1)} all-to-all(f32[32,1,128]{2,1,0:T(1,128)S(1)} %last_moment.1), channel_id=1, replica_groups=mesh['gx'=8,'gy'=4] {'gx','gy'}, dimensions={0} | all-to-all | bytes 32768 | tf_op jit(solution)/shard_map/all_to_all | solution.py:710
  78.6 0.0 collective-permute-done.4.refs_1_
  78.6 0.0 collective-permute-done.5.refs_2_
  78.6 0.0 collective-permute-done.6.refs_3_
  78.6 0.9 %combine_waves.1 = f32[4,128,128]{2,1,0:T(8,128)} custom-call(f32[32,1,128]{2,1,0:T(1,128)S(1)} %all_to_all.5.mom_ref, bf16[3,4,32,128]{3,2,1,0:T(8,128)(2,1)S(1)} %get-tuple-element.26.refs_0_, bf16[3,4,32,128]{3,2,1,0:T(8,128)(2,1)S(1)} %collective-permute-done.4.refs_1_, bf16[3,4,32,128]{3,2,1,0:T(8,128)(2,1)S(1)} %collective-permute-done.5.refs_2_, ...), custom_call_target="tpu_custom_call" | custom-call | tf_op jit(solution)/shard_map/combine_waves/pallas_call | solution.py:711
  (4 shorter events, 0.0 us)
Async XLA Ops:
  1.5 5.1 %collective-permute-start.1 = (bf16[8,32,128]{2,1,0:T(8,128)(2,1)S(1)}, bf16[8,32,128]{2,1,0:T(8,128)(2,1)S(1)}, u32[]{:S(2)}, u32[]{:S(2)}) collective-permute-start(bf16[8,32,128]{2,1,0:T(8,128)(2,1)S(1)} %get-tuple-element.32), channel_id=1, source_target_pairs={{4,0},{8,4},{12,8},{16,12},{20,16},{24,20},{28,24},{5,1},{9,5},{13... | collective-permute-start | bytes 196616 | tf_op jit(solution)/shard_map/ppermute | solution.py:603
  2.8 3.9 %collective-permute-start = (bf16[8,32,128]{2,1,0:T(8,128)(2,1)S(1)}, bf16[8,32,128]{2,1,0:T(8,128)(2,1)S(1)}, u32[]{:S(2)}, u32[]{:S(2)}) collective-permute-start(bf16[8,32,128]{2,1,0:T(8,128)(2,1)S(1)} %get-tuple-element.33), channel_id=1, source_target_pairs={{0,4},{4,8},{8,12},{12,16},{16,20},{20,24},{24,28},{1,5},{5,9},{9,... | collective-permute-start | bytes 196616 | tf_op jit(solution)/shard_map/ppermute | solution.py:603
  6.8 12.7 %collective-permute-start.2 = (bf16[32,8,128]{2,1,0:T(8,128)(2,1)S(1)}, bf16[32,8,128]{2,1,0:T(8,128)(2,1)S(1)}, u32[]{:S(2)}, u32[]{:S(2)}) collective-permute-start(bf16[32,8,128]{2,1,0:T(8,128)(2,1)S(1)} %pad_maximum_fusion), channel_id=1, source_target_pairs={{0,1},{1,2},{2,3},{4,5},{5,6},{6,7},{8,9},{9,10},{10,11},{12,13},{... | collective-permute-start | bytes 196616 | tf_op jit(solution)/shard_map/ppermute | solution.py:603
  11.7 7.7 %collective-permute-start.3 = (bf16[32,8,128]{2,1,0:T(8,128)(2,1)S(1)}, bf16[32,8,128]{2,1,0:T(8,128)(2,1)S(1)}, u32[]{:S(2)}, u32[]{:S(2)}) collective-permute-start(bf16[32,8,128]{2,1,0:T(8,128)(2,1)S(1)} %pad_maximum_fusion.1), channel_id=1, source_target_pairs={{1,0},{2,1},{3,2},{5,4},{6,5},{7,6},{9,8},{10,9},{11,10},{13,12},{... | collective-permute-start | bytes 196616 | tf_op jit(solution)/shard_map/ppermute | solution.py:603
  13.0 0.9 %copy-start.1 = (bf16[16,16,3,3,3]{1,0,4,3,2:T(8,128)(2,1)S(1)}, bf16[16,16,3,3,3]{1,0,4,3,2:T(8,128)(2,1)}, u32[]{:S(2)}) copy-start(bf16[16,16,3,3,3]{1,0,4,3,2:T(8,128)(2,1)} %param.7) | copy-start | bytes 41476
  13.9 0.9 %copy-start.2 = (bf16[16,16,3,3,3]{1,0,4,3,2:T(8,128)(2,1)S(1)}, bf16[16,16,3,3,3]{1,0,4,3,2:T(8,128)(2,1)}, u32[]{:S(2)}) copy-start(bf16[16,16,3,3,3]{1,0,4,3,2:T(8,128)(2,1)} %param.8) | copy-start | bytes 41476
  14.8 0.7 copy-start.3
  15.5 0.7 copy-start.4
  16.2 3.3 %copy-start = (bf16[16,32,128]{2,1,0:T(8,128)(2,1)S(1)}, bf16[16,32,128]{2,1,0:T(8,128)(2,1)}, u32[]{:S(2)}) copy-start(bf16[16,32,128]{2,1,0:T(8,128)(2,1)} %amp_ref.1) | copy-start | bytes 393220
  58.3 20.3 %collective-permute-start.4 = (bf16[3,4,32,128]{3,2,1,0:T(8,128)(2,1)S(1)}, bf16[3,4,32,128]{3,2,1,0:T(8,128)(2,1)S(1)}, u32[]{:S(2)}, u32[]{:S(2)}) collective-permute-start(bf16[3,4,32,128]{3,2,1,0:T(8,128)(2,1)S(1)} %get-tuple-element.27), channel_id=1, source_target_pairs={{0,1},{1,2},{2,3},{3,0},{4,5},{5,6},{6,7},{7,4},{8,9},{9,10},{10,1... | collective-permute-start | bytes 294920 | tf_op jit(solution)/shard_map/ppermute | solution.py:699
  61.0 17.6 %collective-permute-start.5 = (bf16[3,4,32,128]{3,2,1,0:T(8,128)(2,1)S(1)}, bf16[3,4,32,128]{3,2,1,0:T(8,128)(2,1)S(1)}, u32[]{:S(2)}, u32[]{:S(2)}) collective-permute-start(bf16[3,4,32,128]{3,2,1,0:T(8,128)(2,1)S(1)} %get-tuple-element.28), channel_id=1, source_target_pairs={{0,2},{1,3},{2,0},{3,1},{4,6},{5,7},{6,4},{7,5},{8,10},{9,11},{10,... | collective-permute-start | bytes 294920 | tf_op jit(solution)/shard_map/ppermute | solution.py:699
  63.6 15.0 %collective-permute-start.6 = (bf16[3,4,32,128]{3,2,1,0:T(8,128)(2,1)S(1)}, bf16[3,4,32,128]{3,2,1,0:T(8,128)(2,1)S(1)}, u32[]{:S(2)}, u32[]{:S(2)}) collective-permute-start(bf16[3,4,32,128]{3,2,1,0:T(8,128)(2,1)S(1)} %get-tuple-element.29), channel_id=1, source_target_pairs={{0,3},{1,0},{2,1},{3,2},{4,7},{5,4},{6,5},{7,6},{8,11},{9,8},{10,9... | collective-permute-start | bytes 294920 | tf_op jit(solution)/shard_map/ppermute | solution.py:699

commit v7 on v6

--- a/solution.py
+++ b/solution.py
@@ -15,8 +15,8 @@
 XW = TX + 2 * H
 FX = TX + 8
 RX = 4
-FIRST, SECOND, THIRD = 4, 11, 11
-GROUP = 2
+FIRST, SECOND, THIRD = 8, 2, 2
+GROUP = 1
 BLK = 256
 EDGE = 7
 SUB = 16
@@ -34,109 +34,94 @@
     return lax.dot_general(a, b, (((1,), (1,)), ((), ())), preferred_element_type=F32)
 
 
-def prep_kernel(
-    first_in,
-    second_in,
-    third_in,
-    last_in,
-    after_ref,
-    w1_ref,
-    w2_ref,
-    w3_ref,
-    w4_ref,
-    first_ref,
-    second_ref,
-    third_ref,
-    last_ref,
-    sems,
-):
+def prep_kernel(inner_ref, outer_ref, after_ref, w1_ref, w2_ref, w3_ref, w4_ref):
     del after_ref
-    pairs = ((second_in, second_ref), (third_in, third_ref), (first_in, first_ref), (last_in, last_ref))
-    copies = [pltpu.make_async_copy(a, b, sems.at[i]) for i, (a, b) in enumerate(pairs)]
-    for copy in copies:
-        copy.start()
-    for copy in copies:
-        copy.wait()
     spread = jnp.where(iota((CH, BLK), 1) % CH == iota((CH, BLK), 0), 1.0, 0.0).astype(BF16)
     unit = jnp.where(iota((BLK, BLK), 1) == iota((BLK, BLK), 0), 1.0, 0.0).astype(BF16)
+    none = jnp.zeros((CH, BLK), BF16)
     cell = iota((CH, BLK), 1) // CH
+    at_cell = [cell == at for at in range(16)]
     inputs = input_cells()
-    for source, ref in ((second_ref, w2_ref), (third_ref, w3_ref)):
-        tiled = jnp.dot(source[...], spread, preferred_element_type=F32)
+    tiled = jnp.dot(inner_ref[...], spread, preferred_element_type=F32).astype(BF16)
+    for layer, ref in enumerate((w2_ref, w3_ref)):
         for tile in range(6):
             bands = []
             for yo in range(2):
                 for to in range(2):
                     for xo in range(4):
-                        band = jnp.zeros((CH, BLK), F32)
+                        band = none
                         for at, (y, t, x) in enumerate(inputs[tile]):
                             dx, dy, dt = x - xo + 1, y - yo + 1, t - to + 1
                             if min(dx, dy, dt) >= 0 and max(dx, dy, dt) <= 2:
-                                tap = tiled[(dx * 9 + dy * 3 + dt) * CH :][:CH]
-                                band = jnp.where(cell == at, tap, band)
-                        bands.append(band.astype(BF16))
+                                tap = tiled[(layer * 27 + dx * 9 + dy * 3 + dt) * CH :][:CH]
+                                band = jnp.where(at_cell[at], tap, band)
+                        bands.append(band)
             turned = dot_nt(unit, jnp.concatenate(bands, axis=0))
             ref[tile * BLK : (tile + 1) * BLK, :] = turned.astype(BF16)
 
-    def taps(ref):
+    def taps(which):
         found = {}
         for dx in range(3):
             for dy in range(3):
-                piece = ref[0, dx, dy].astype(BF16)
-                tiled = jnp.dot(piece, spread, preferred_element_type=F32)
+                tiled = jnp.dot(outer_ref[which, dx, dy], spread, preferred_element_type=F32)
                 for dt in range(3):
                     found[dx, dy, dt] = tiled[dt : dt + 1]
         return found
 
-    first, last = taps(first_ref), taps(last_ref)
+    first, last = taps(0), taps(1)
+    lane_yt = iota((1, BLK), 1) // 64
+    quarter = [lane_yt == at for at in range(4)]
+
+    def by_quarter(found, dx, at):
+        value = jnp.zeros((1, BLK), F32)
+        for y in range(2):
+            for t in range(2):
+                dy, dt = at(y, t)
+                if 0 <= dy <= 2 and 0 <= dt <= 2:
+                    value = jnp.where(quarter[y * 2 + t], found[dx, dy, dt], value)
+        return value
+
+    def rows_of(found, rows, at):
+        return [
+            jnp.broadcast_to(by_quarter(found, dx, at), (rows, BLK)).astype(BF16)
+            for dx in range(3)
+        ]
+
     row_x = iota((XW, BLK), 0)
-    lane = iota((XW, BLK), 1)
-    lane_yt, lane_x = lane // 64, lane // CH % 4
-    offset_x = []
-    for blk in range(EDGE):
-        offset_x.append(row_x - 1 - 4 * blk - lane_x)
-    edge = jnp.where(lane_x == 0, row_x - 29, jnp.where(lane_x == 3, row_x, -1))
-    offset_x.append(edge)
-    masks = [[offset_x[blk] == dx for dx in range(3)] for blk in range(EDGE + 1)]
+    lane_x = iota((XW, BLK), 1) // CH % 4
+    offset_x = [row_x - 1 - 4 * blk - lane_x for blk in range(EDGE)]
+    offset_x.append(jnp.where(lane_x == 0, row_x - 29, jnp.where(lane_x == 3, row_x, -1)))
+    masks = [[offset == dx for dx in range(3)] for offset in offset_x]
+    none = jnp.zeros((XW, BLK), BF16)
     for j in range(4):
         for yi in range(4):
             row = (j * 4 + yi) * XW
-            columns = []
-            for dx in range(3):
-                value = jnp.zeros((1, BLK), F32)
-                for yo in range(2):
-                    for to in range(2):
-                        dy, dt = yi - yo, j - to
-                        if 0 <= dy <= 2 and 0 <= dt <= 2:
-                            value = jnp.where(
-                                lane_yt[:1] == yo * 2 + to, first[dx, dy, dt], value
-                            )
-                columns.append(value)
+            values = rows_of(first, XW, lambda y, t: (yi - y, j - t))
             for blk in range(EDGE + 1):
-                band = jnp.zeros((XW, BLK), F32)
+                band = none
                 for dx in range(3):
-                    band = jnp.where(masks[blk][dx], columns[dx], band)
-                w1_ref[row : row + XW, blk * BLK : (blk + 1) * BLK] = band.astype(BF16)
+                    band = jnp.where(masks[blk][dx], values[dx], band)
+                w1_ref[row : row + XW, blk * BLK : (blk + 1) * BLK] = band
     row_x = iota((FX, BLK), 0)
     lane_x = iota((FX, BLK), 1) // CH % 4
+    masks = [
+        [4 * blk + lane_x - 1 - row_x == dx for dx in range(3)] for blk in range(EDGE)
+    ]
+    none = jnp.zeros((FX, BLK), F32)
+    bands = [[] for blk in range(EDGE)]
+    for yi in range(4):
+        for j in range(4):
+            values = [
+                by_quarter(last, dx, lambda y, t: (y + 2 - yi, t + 2 - j)) for dx in range(3)
+            ]
+            for blk in range(EDGE):
+                band = none
+                for dx in range(3):
+                    band = jnp.where(masks[blk][dx], values[dx], band)
+                bands[blk].append(band)
     for blk in range(EDGE):
-        masks = [4 * blk + lane_x - 1 - row_x == dx for dx in range(3)]
-        bands = []
-        for yi in range(4):
-            for j in range(4):
-                band = jnp.zeros((FX, BLK), F32)
-                for dx in range(3):
-                    value = jnp.zeros((1, BLK), F32)
-                    for y in range(2):
-                        for t in range(2):
-                            dy, dt = y + 2 - yi, t + 2 - j
-                            if 0 <= dy <= 2 and 0 <= dt <= 2:
-                                value = jnp.where(
-                                    lane_yt[:1] == y * 2 + t, last[dx, dy, dt], value
-                                )
-                    band = jnp.where(masks[dx], value, band)
-                bands.append(band)
-        w4_ref[:, blk * BLK : (blk + 1) * BLK] = jnp.concatenate(bands, axis=0).astype(BF16)
+        whole = jnp.concatenate(bands[blk], axis=0).astype(BF16)
+        w4_ref[:, blk * BLK : (blk + 1) * BLK] = whole
 
 
 def input_cells():
@@ -625,23 +610,16 @@
             jax.ShapeDtypeStruct((6 * BLK, BLK), BF16),
             jax.ShapeDtypeStruct((16 * FX, EDGE * BLK), BF16),
         ],
-        in_specs=[pl.BlockSpec(memory_space=pltpu.HBM)] * 4 + [pl.BlockSpec(memory_space=pl.ANY)],
+        in_specs=vmem(2) + [pl.BlockSpec(memory_space=pl.ANY)],
         out_specs=vmem(4),
-        scratch_shapes=[
-            pltpu.VMEM((1, 3, 3, 3, CH), BF16),
-            pltpu.VMEM((27 * CH, CH), BF16),
-            pltpu.VMEM((27 * CH, CH), BF16),
-            pltpu.VMEM((1, 3, 3, 3, CH), BF16),
-            pltpu.SemaphoreType.DMA((4,)),
-        ],
         compiler_params=pltpu.CompilerParams(vmem_limit_bytes=16 * 2**20),
         cost_estimate=pl.CostEstimate(flops=10**9, bytes_accessed=10**7, transcendentals=0),
         name="band_weights",
     )(
-        jnp.transpose(conv_first, (1, 2, 3, 4, 0)),
-        taps_first(conv_second).reshape(27 * CH, CH),
-        taps_first(conv_third).reshape(27 * CH, CH),
-        jnp.transpose(conv_last, (0, 2, 3, 4, 1)),
+        jnp.concatenate([taps_first(conv_second), taps_first(conv_third)]).reshape(54 * CH, CH),
+        jnp.concatenate(
+            [jnp.transpose(conv_first, (1, 2, 3, 4, 0)), jnp.transpose(conv_last, (0, 2, 3, 4, 1))]
+        ),
         xlow,
     )
 

time: 80 us -> 80 us (level)
  waiting for transfers between devices: 0.09 us -> 3.29 us
  local copies, waits for them, and re-layouts: 4.87 us -> 1.68 us
  blocking collectives: 13.1 us -> 10.7 us
  Pallas kernels: 43.5 us -> 45.4 us
  other arithmetic: 0.02 us -> 1.76 us
  starting transfers between devices: 17.2 us -> 16.1 us
    ppermute x4, waiting for transfers between devices: 0.09 us -> 3.28 us  [shift(): return lax.ppermute(values, axis, pairs)]
    unnamed x10 -> x2, local copies, waits for them, and re-layouts: 3.19 us -> 0.01 us
    pallas_call x1, Pallas kernels: 36.4 us -> 39.4 us  [on_device(): pl.pallas_call(functools.partial(net_kernel, grid_x, grid_y, ty), out_sha...]
    all_to_all x1, blocking collectives: 13.1 us -> 10.7 us  [on_device(): lax.all_to_all(everyone, ('gx', 'gy'), split_axis=0, concat_axis=0, tiled...]
    concatenate x0 -> x2, other arithmetic: none -> 1.74 us  [the longest x1 1 us: on_device(): jnp.concatenate([taps_first(conv_second), taps_first(conv_third)])]
    pallas_call x1, Pallas kernels: 3.22 us -> 2.12 us  [on_device(): pl.pallas_call(prep_kernel, out_shape=[jax.ShapeDtypeStruct((16 * XW, (ED...]
    ppermute x3, starting transfers between devices: 6.64 us -> 5.57 us  [on_device(): arrived.append(lax.ppermute(waves[place], 'gy', pairs))]
  transfers between devices with their start and end apart: 7 -> 7, of which waited for: 1 -> 1; matrix products, arithmetic and copies ran while one was open for 1% -> 3% of each run, Pallas kernels for 5% -> 3%
where the time goes in v7:
time: 80 us; the launch traced here: 79.6 us
  Pallas kernels  45.4 us (57%)
  starting transfers between devices  16.1 us (20%)
  blocking collectives  10.7 us (13%)
  waiting for transfers between devices  3.29 us (4%)
  other arithmetic  1.76 us (2%)
  local copies, waits for them, and re-layouts  1.68 us (2%)
    pallas_call x1, Pallas kernels, on_device(): pl.pallas_call(functools.partial(net_kernel, grid_x, grid_y, ty), out_sha...  39.4 us
    all_to_all x1, blocking collectives, on_device(): lax.all_to_all(everyone, ('gx', 'gy'), split_axis=0, concat_axis=0, tiled...  10.7 us
    ppermute x4, starting transfers between devices, shift(): return lax.ppermute(values, axis, pairs)  10.5 us
    ppermute x3, starting transfers between devices, on_device(): arrived.append(lax.ppermute(waves[place], 'gy', pairs))  5.57 us
    ppermute x4, waiting for transfers between devices, shift(): return lax.ppermute(values, axis, pairs)  3.28 us
    pallas_call x1, Pallas kernels, on_device(): pl.pallas_call(functools.partial(waves_kernel, grid_x, grid_y, ty), out_s...  2.39 us
    pallas_call x1, Pallas kernels, on_device(): pl.pallas_call(prep_kernel, out_shape=[jax.ShapeDtypeStruct((16 * XW, (ED...  2.12 us
  transfers between devices with their start and end apart: 7, of which 1 were waited for; matrix products, arithmetic and copies ran while one was open for 3% of the time, Pallas kernels for 3%

profile of v7, /device:TPU:0, one launch (start us, length us, event | category | flops | bytes accessed | tf_op | source)
XLA Modules:
  0.0 79.6 jit_solution(9769808410660742957)
XLA Ops:
  0.6 0.9 %fusion.1 = (bf16[8,32,128]{2,1,0:T(8,128)(2,1)S(1)}, bf16[8,32,128]{2,1,0:T(8,128)(2,1)S(1)}) fusion(bf16[16,32,128]{2,1,0:T(8,128)(2,1)} %amp_ref.1), kind=kLoop, calls=%fused_computation.5 | loop fusion | bytes 262144 | tf_op jit(solution)/shard_map/slice | solution.py:591
  1.5 1.3 %collective-permute-start.1 = (bf16[8,32,128]{2,1,0:T(8,128)(2,1)S(1)}, bf16[8,32,128]{2,1,0:T(8,128)(2,1)S(1)}, u32[]{:S(2)}, u32[]{:S(2)}) collective-permute-start(bf16[8,32,128]{2,1,0:T(8,128)(2,1)S(1)} %get-tuple-element.32), channel_id=1, source_target_pairs={{4,0},{8,4},{12,8},{16,12},{20,16},{24,20},{28,24},{5,1},{9,5},{13... | collective-permute-start | bytes 196616 | tf_op jit(solution)/shard_map/ppermute | solution.py:588
  2.8 3.0 %collective-permute-start = (bf16[8,32,128]{2,1,0:T(8,128)(2,1)S(1)}, bf16[8,32,128]{2,1,0:T(8,128)(2,1)S(1)}, u32[]{:S(2)}, u32[]{:S(2)}) collective-permute-start(bf16[8,32,128]{2,1,0:T(8,128)(2,1)S(1)} %get-tuple-element.33), channel_id=1, source_target_pairs={{0,4},{4,8},{8,12},{12,16},{16,20},{20,24},{24,28},{1,5},{5,9},{9,... | collective-permute-start | bytes 196616 | tf_op jit(solution)/shard_map/ppermute | solution.py:588
  5.9 0.8 fusion
  6.6 1.0 %pad_maximum_fusion = bf16[6,3,3,16,16]{4,3,2,1,0:T(8,128)(2,1)S(1)} fusion(bf16[3,3,3,16,16]{4,3,2,1,0:T(8,128)(2,1)} %bitcast.6, bf16[3,3,3,16,16]{4,3,2,1,0:T(8,128)(2,1)} %bitcast.7), kind=kLoop, calls=%fused_computation | loop fusion | flops 13824 | bytes 55296 | tf_op jit(solution)/shard_map/concatenate | solution.py:619
  7.6 0.7 pad_maximum_fusion.3.outer_ref
  8.4 0.0 collective-permute-done.1.xhigh_ref
  8.4 0.0 collective-permute-done.after_ref.xlow_ref
  8.4 4.9 %collective-permute-start.2 = (bf16[32,8,128]{2,1,0:T(8,128)(2,1)S(1)}, bf16[32,8,128]{2,1,0:T(8,128)(2,1)S(1)}, u32[]{:S(2)}, u32[]{:S(2)}) collective-permute-start(bf16[32,8,128]{2,1,0:T(8,128)(2,1)S(1)} %pad_maximum_fusion.1), channel_id=1, source_target_pairs={{0,1},{1,2},{2,3},{4,5},{5,6},{6,7},{8,9},{9,10},{10,11},{12,13},{... | collective-permute-start | bytes 196616 | tf_op jit(solution)/shard_map/ppermute | solution.py:588
  13.4 1.3 %collective-permute-start.3 = (bf16[32,8,128]{2,1,0:T(8,128)(2,1)S(1)}, bf16[32,8,128]{2,1,0:T(8,128)(2,1)S(1)}, u32[]{:S(2)}, u32[]{:S(2)}) collective-permute-start(bf16[32,8,128]{2,1,0:T(8,128)(2,1)S(1)} %pad_maximum_fusion.2), channel_id=1, source_target_pairs={{1,0},{2,1},{3,2},{5,4},{6,5},{7,6},{9,8},{10,9},{11,10},{13,12},{... | collective-permute-start | bytes 196616 | tf_op jit(solution)/shard_map/ppermute | solution.py:588
  14.7 0.0 copy-start
  14.7 2.1 %band_weights.1 = (bf16[512,2048]{1,0:T(8,128)(2,1)S(1)}, bf16[1536,256]{1,0:T(8,128)(2,1)S(1)}, bf16[1536,256]{1,0:T(8,128)(2,1)S(1)}, bf16[384,1792]{1,0:T(8,128)(2,1)S(1)}) custom-call(bf16[864,16]{1,0:T(8,128)(2,1)S(1)} %bitcast.5, bf16[2,3,3,3,16]{4,3,2,1,0:T(4,128)(2,1)S(1)} %pad_maximum_fusion.3.outer_ref, ...), custom_call_target="tpu_custom_call" | custom-call | flops 1000000000 | bytes 10000000 | tf_op jit(solution)/shard_map/band_weights/pallas_call | solution.py:605
  16.8 0.0 collective-permute-done.2.ylow_ref
  16.9 3.3 %collective-permute-done.3.yhigh_ref = bf16[32,8,128]{2,1,0:T(8,128)(2,1)S(1)} collective-permute-done((bf16[32,8,128]{2,1,0:T(8,128)(2,1)S(1)}, bf16[32,8,128]{2,1,0:T(8,128)(2,1)S(1)}, u32[]{:S(2)}, u32[]{:S(2)}) %collective-permute-start.3) | collective-permute-done | bytes 65568 | tf_op jit(solution)/shard_map/ppermute | solution.py:588
  20.1 0.0 copy-done
  20.1 39.4 %fault_net.1 = (bf16[16,32,128]{2,1,0:T(8,128)(2,1)}, f32[1152,128]{1,0:T(8,128)S(1)}, f32[2,26,48,128]{3,2,1,0:T(8,128)S(1)}) custom-call(bf16[16,32,128]{2,1,0:T(8,128)(2,1)S(1)} %copy-done, bf16[8,32,128]{2,1,0:T(8,128)(2,1)S(1)} %collective-permute-done.after_ref.xlow_ref, bf16[8,32,128]{2,1,0:T(8,128)(2,1)S(1)} %collective-permute-done.1.xhigh_ref, ...), custom_call_target="tpu_custom_call" | custom-call | flops 30000001024 | bytes 10000000 | tf_op jit(solution)/shard_map/fault_net/pallas_call | solution.py:627
  59.5 2.4 %solver_waves.1 = (f32[8,128]{1,0:T(8,128)S(1)}, f32[2,26,48,128]{3,2,1,0:T(8,128)S(1)}, f32[26,48,128]{2,1,0:T(8,128)S(1)}, bf16[3,4,32,128]{3,2,1,0:T(8,128)(2...) custom-call(f32[1152,128]{1,0:T(8,128)S(1)} %get-tuple-element.21.pr, ...), custom_call_target="tpu_custom_call" | custom-call | flops 100000000 | bytes 10000000 | tf_op jit(solution)/shard_map/solver_waves/pallas_call | solution.py:652
  61.9 1.6 %collective-permute-start.4 = (bf16[3,4,32,128]{3,2,1,0:T(8,128)(2,1)S(1)}, bf16[3,4,32,128]{3,2,1,0:T(8,128)(2,1)S(1)}, u32[]{:S(2)}, u32[]{:S(2)}) collective-permute-start(bf16[3,4,32,128]{3,2,1,0:T(8,128)(2,1)S(1)} %get-tuple-element.27), channel_id=1, source_target_pairs={{0,1},{1,2},{2,3},{3,0},{4,5},{5,6},{6,7},{7,4},{8,9},{9,10},{10,1... | collective-permute-start | bytes 294920 | tf_op jit(solution)/shard_map/ppermute | solution.py:677
  63.5 1.1 %collective-permute-start.5 = (bf16[3,4,32,128]{3,2,1,0:T(8,128)(2,1)S(1)}, bf16[3,4,32,128]{3,2,1,0:T(8,128)(2,1)S(1)}, u32[]{:S(2)}, u32[]{:S(2)}) collective-permute-start(bf16[3,4,32,128]{3,2,1,0:T(8,128)(2,1)S(1)} %get-tuple-element.28), channel_id=1, source_target_pairs={{0,2},{1,3},{2,0},{3,1},{4,6},{5,7},{6,4},{7,5},{8,10},{9,11},{10,... | collective-permute-start | bytes 294920 | tf_op jit(solution)/shard_map/ppermute | solution.py:677
  64.6 2.8 %collective-permute-start.6 = (bf16[3,4,32,128]{3,2,1,0:T(8,128)(2,1)S(1)}, bf16[3,4,32,128]{3,2,1,0:T(8,128)(2,1)S(1)}, u32[]{:S(2)}, u32[]{:S(2)}) collective-permute-start(bf16[3,4,32,128]{3,2,1,0:T(8,128)(2,1)S(1)} %get-tuple-element.29), channel_id=1, source_target_pairs={{0,3},{1,0},{2,1},{3,2},{4,7},{5,4},{6,5},{7,6},{8,11},{9,8},{10,9... | collective-permute-start | bytes 294920 | tf_op jit(solution)/shard_map/ppermute | solution.py:677
  67.5 0.6 last_moment.1
  68.0 10.7 %all_to_all.5.mom_ref = f32[32,1,128]{2,1,0:T(1,128)S(1)} all-to-all(f32[32,1,128]{2,1,0:T(1,128)S(1)} %last_moment.1), channel_id=1, replica_groups=mesh['gx'=8,'gy'=4] {'gx','gy'}, dimensions={0} | all-to-all | bytes 32768 | tf_op jit(solution)/shard_map/all_to_all | solution.py:688
  78.7 0.0 collective-permute-done.4.refs_1_
  78.7 0.0 collective-permute-done.5.refs_2_
  78.7 0.0 collective-permute-done.6.refs_3_
  78.7 0.9 %combine_waves.1 = f32[4,128,128]{2,1,0:T(8,128)} custom-call(f32[32,1,128]{2,1,0:T(1,128)S(1)} %all_to_all.5.mom_ref, bf16[3,4,32,128]{3,2,1,0:T(8,128)(2,1)S(1)} %get-tuple-element.26.refs_0_, bf16[3,4,32,128]{3,2,1,0:T(8,128)(2,1)S(1)} %collective-permute-done.4.refs_1_, bf16[3,4,32,128]{3,2,1,0:T(8,128)(2,1)S(1)} %collective-permute-done.5.refs_2_, ...), custom_call_target="tpu_custom_call" | custom-call | tf_op jit(solution)/shard_map/combine_waves/pallas_call | solution.py:689
  (4 shorter events, 0.0 us)
Async XLA Ops:
  1.5 6.9 %collective-permute-start.1 = (bf16[8,32,128]{2,1,0:T(8,128)(2,1)S(1)}, bf16[8,32,128]{2,1,0:T(8,128)(2,1)S(1)}, u32[]{:S(2)}, u32[]{:S(2)}) collective-permute-start(bf16[8,32,128]{2,1,0:T(8,128)(2,1)S(1)} %get-tuple-element.32), channel_id=1, source_target_pairs={{4,0},{8,4},{12,8},{16,12},{20,16},{24,20},{28,24},{5,1},{9,5},{13... | collective-permute-start | bytes 196616 | tf_op jit(solution)/shard_map/ppermute | solution.py:588
  2.8 5.6 %collective-permute-start = (bf16[8,32,128]{2,1,0:T(8,128)(2,1)S(1)}, bf16[8,32,128]{2,1,0:T(8,128)(2,1)S(1)}, u32[]{:S(2)}, u32[]{:S(2)}) collective-permute-start(bf16[8,32,128]{2,1,0:T(8,128)(2,1)S(1)} %get-tuple-element.33), channel_id=1, source_target_pairs={{0,4},{4,8},{8,12},{12,16},{16,20},{20,24},{24,28},{1,5},{5,9},{9,... | collective-permute-start | bytes 196616 | tf_op jit(solution)/shard_map/ppermute | solution.py:588
  8.4 8.4 %collective-permute-start.2 = (bf16[32,8,128]{2,1,0:T(8,128)(2,1)S(1)}, bf16[32,8,128]{2,1,0:T(8,128)(2,1)S(1)}, u32[]{:S(2)}, u32[]{:S(2)}) collective-permute-start(bf16[32,8,128]{2,1,0:T(8,128)(2,1)S(1)} %pad_maximum_fusion.1), channel_id=1, source_target_pairs={{0,1},{1,2},{2,3},{4,5},{5,6},{6,7},{8,9},{9,10},{10,11},{12,13},{... | collective-permute-start | bytes 196616 | tf_op jit(solution)/shard_map/ppermute | solution.py:588
  13.4 6.7 %collective-permute-start.3 = (bf16[32,8,128]{2,1,0:T(8,128)(2,1)S(1)}, bf16[32,8,128]{2,1,0:T(8,128)(2,1)S(1)}, u32[]{:S(2)}, u32[]{:S(2)}) collective-permute-start(bf16[32,8,128]{2,1,0:T(8,128)(2,1)S(1)} %pad_maximum_fusion.2), channel_id=1, source_target_pairs={{1,0},{2,1},{3,2},{5,4},{6,5},{7,6},{9,8},{10,9},{11,10},{13,12},{... | collective-permute-start | bytes 196616 | tf_op jit(solution)/shard_map/ppermute | solution.py:588
  14.7 5.4 %copy-start = (bf16[16,32,128]{2,1,0:T(8,128)(2,1)S(1)}, bf16[16,32,128]{2,1,0:T(8,128)(2,1)}, u32[]{:S(2)}) copy-start(bf16[16,32,128]{2,1,0:T(8,128)(2,1)} %amp_ref.1) | copy-start | bytes 393220
  61.9 16.8 %collective-permute-start.4 = (bf16[3,4,32,128]{3,2,1,0:T(8,128)(2,1)S(1)}, bf16[3,4,32,128]{3,2,1,0:T(8,128)(2,1)S(1)}, u32[]{:S(2)}, u32[]{:S(2)}) collective-permute-start(bf16[3,4,32,128]{3,2,1,0:T(8,128)(2,1)S(1)} %get-tuple-element.27), channel_id=1, source_target_pairs={{0,1},{1,2},{2,3},{3,0},{4,5},{5,6},{6,7},{7,4},{8,9},{9,10},{10,1... | collective-permute-start | bytes 294920 | tf_op jit(solution)/shard_map/ppermute | solution.py:677
  63.5 15.2 %collective-permute-start.5 = (bf16[3,4,32,128]{3,2,1,0:T(8,128)(2,1)S(1)}, bf16[3,4,32,128]{3,2,1,0:T(8,128)(2,1)S(1)}, u32[]{:S(2)}, u32[]{:S(2)}) collective-permute-start(bf16[3,4,32,128]{3,2,1,0:T(8,128)(2,1)S(1)} %get-tuple-element.28), channel_id=1, source_target_pairs={{0,2},{1,3},{2,0},{3,1},{4,6},{5,7},{6,4},{7,5},{8,10},{9,11},{10,... | collective-permute-start | bytes 294920 | tf_op jit(solution)/shard_map/ppermute | solution.py:677
  64.6 14.1 %collective-permute-start.6 = (bf16[3,4,32,128]{3,2,1,0:T(8,128)(2,1)S(1)}, bf16[3,4,32,128]{3,2,1,0:T(8,128)(2,1)S(1)}, u32[]{:S(2)}, u32[]{:S(2)}) collective-permute-start(bf16[3,4,32,128]{3,2,1,0:T(8,128)(2,1)S(1)} %get-tuple-element.29), channel_id=1, source_target_pairs={{0,3},{1,0},{2,1},{3,2},{4,7},{5,4},{6,5},{7,6},{8,11},{9,8},{10,9... | collective-permute-start | bytes 294920 | tf_op jit(solution)/shard_map/ppermute | solution.py:677

commit v8 on v7

--- a/solution.py
+++ b/solution.py
@@ -15,8 +15,9 @@
 XW = TX + 2 * H
 FX = TX + 8
 RX = 4
-FIRST, SECOND, THIRD = 8, 2, 2
-GROUP = 1
+FIRST, SECOND, THIRD = 8, 11, 11
+LIMIT = 6
+GROUP = 2
 BLK = 256
 EDGE = 7
 SUB = 16
@@ -156,7 +157,69 @@
     return block, up_y, down_y, up_t, down_t
 
 
-def net_kernel(
+def dot(a, b):
+    return jnp.dot(a, b, preferred_element_type=F32)
+
+
+def pair_of(row):
+    return row // SUB + (row % SUB) * 4
+
+
+def lane_masks(x0, grid_x, blocks):
+    slot = iota((1, BLK), 1) // CH % 4
+    masks = []
+    for blk in range(blocks):
+        if blk < EDGE:
+            at = x0 - 6 + 4 * blk + slot
+        else:
+            at = x0 + jnp.where(slot == 0, 22, -7)
+        masks.append(jnp.where((at >= 0) & (at < grid_x), 1.0, 0.0))
+    return masks
+
+
+def row_mask(y, grid_y):
+    at = y + jnp.where(iota((1, BLK), 1) >= 128, 1, 0)
+    return jnp.where((at >= 0) & (at < grid_y), 1.0, 0.0)
+
+
+def put(act, pair, blk, values):
+    sub_row = iota((SUB, 128), 0)
+    place = iota((PAIRS, 128), 1) // CH
+    early = (place >= 2) & (place < 6)
+    act[0, pair, blk] = values.astype(BF16)
+    for half in range(2):
+        turned = pltpu.roll(values[:, half * 128 : (half + 1) * 128], 96, 1)
+        head = jnp.where(sub_row == 0, 0.0, pltpu.roll(turned[PAIRS - SUB :], 1, 0))
+        tail = jnp.where(sub_row == SUB - 1, 0.0, pltpu.roll(turned[:SUB], SUB - 1, 0))
+        before = jnp.concatenate([head, turned[: PAIRS - SUB]], axis=0)
+        after = jnp.concatenate([turned[SUB:], tail], axis=0)
+        both = jnp.where(early, before, after)
+        act[1, pair, blk, :, half * 128 : (half + 1) * 128] = both.astype(BF16)
+
+
+def put_sides(act, pair, blocks):
+    place = iota((PAIRS, 128), 1) // CH
+    for blk in range(EDGE):
+        left, right = (blk - 1) % blocks, (blk + 1) % blocks
+        for half in range(2):
+            at = slice(half * 128, (half + 1) * 128)
+            even = jnp.where(place % 4 == 0, act[0, pair, right, :, at], act[1, pair, right, :, at])
+            odd = jnp.where(place % 4 == 3, act[0, pair, left, :, at], act[1, pair, left, :, at])
+            act[2, pair, blk, :, at] = jnp.where(place % 2 == 0, even, odd)
+
+
+def layer(source, w_ref, pair, count):
+    size = count * EDGE * PAIRS
+    tiles = []
+    for kind in range(3):
+        centre = source[kind, pl.ds(pair + 1, count), :EDGE].reshape(size, BLK)
+        before = source[kind, pl.ds(pair, count), :EDGE, :, 128:].reshape(size, 128)
+        after = source[kind, pl.ds(pair + 2, count), :EDGE, :, :128].reshape(size, 128)
+        tiles += [centre, before, after]
+    return dot(jnp.concatenate(tiles, axis=1), w_ref[...])
+
+
+def first_kernel(
     grid_x,
     grid_y,
     ty,
@@ -166,24 +229,13 @@
     ylow_ref,
     yhigh_ref,
     w1_ref,
-    w2_ref,
-    w3_ref,
-    w4_ref,
-    fault_ref,
-    prob,
-    slope,
+    act1,
     raw,
     amp,
-    act1,
-    act2,
-    part,
-    prod,
 ):
     x0 = lax.axis_index("gx") * TX
     y0 = lax.axis_index("gy") * ty
     yw = ty + 2 * H
-    pairs1, pairs2 = yw // 2, ty // 2 + 6
-    dot = functools.partial(jnp.dot, preferred_element_type=F32)
 
     for x in range(XW):
         row = x * yw
@@ -205,64 +257,11 @@
     amp[0] = jnp.zeros((XW, NT), BF16)
     amp[yw + 1] = jnp.zeros((XW, NT), BF16)
 
-    def pair_of(row):
-        return row // SUB + (row % SUB) * 4
-
     at_row = iota((4 * PAIRS, NT), 0)
     to_pairs = jnp.where(
         iota((4 * PAIRS, NT), 1) == 2 * pair_of(at_row % PAIRS) - 1 + at_row // PAIRS, 1.0, 0.0
     ).astype(BF16)
-    at_row = iota((4 * NT, 2 * NT), 0)
-    at_lane = iota((4 * NT, 2 * NT), 1)
-    from_pairs = jnp.where(
-        (at_lane % NT == 2 * pair_of(at_row % PAIRS) - 1 + at_row // NT)
-        & (at_lane // NT == at_row % NT // PAIRS),
-        1.0,
-        0.0,
-    ).astype(BF16)
-
-    def lane_masks(blocks):
-        slot = iota((1, BLK), 1) // CH % 4
-        masks = []
-        for blk in range(blocks):
-            if blk < EDGE:
-                at = x0 - 6 + 4 * blk + slot
-            else:
-                at = x0 + jnp.where(slot == 0, 22, -7)
-            masks.append(jnp.where((at >= 0) & (at < grid_x), 1.0, 0.0))
-        return masks
-
-    second_row = iota((1, BLK), 1) >= 128
-
-    def row_mask(y):
-        at = y0 + y + jnp.where(second_row, 1, 0)
-        return jnp.where((at >= 0) & (at < grid_y), 1.0, 0.0)
-
-    sub_row = iota((SUB, 128), 0)
-    place = iota((PAIRS, 128), 1) // CH
-    early = (place >= 2) & (place < 6)
-
-    def put(act, pair, blk, values):
-        act[0, pair, blk] = values.astype(BF16)
-        for half in range(2):
-            turned = pltpu.roll(values[:, half * 128 : (half + 1) * 128], 96, 1)
-            head = jnp.where(sub_row == 0, 0.0, pltpu.roll(turned[PAIRS - SUB :], 1, 0))
-            tail = jnp.where(sub_row == SUB - 1, 0.0, pltpu.roll(turned[:SUB], SUB - 1, 0))
-            before = jnp.concatenate([head, turned[: PAIRS - SUB]], axis=0)
-            after = jnp.concatenate([turned[SUB:], tail], axis=0)
-            both = jnp.where(early, before, after)
-            act[1, pair, blk, :, half * 128 : (half + 1) * 128] = both.astype(BF16)
-
-    def put_sides(act, pair, blocks):
-        for blk in range(EDGE):
-            left, right = (blk - 1) % blocks, (blk + 1) % blocks
-            for half in range(2):
-                at = slice(half * 128, (half + 1) * 128)
-                even = jnp.where(place % 4 == 0, act[0, pair, right, :, at], act[1, pair, right, :, at])
-                odd = jnp.where(place % 4 == 3, act[0, pair, left, :, at], act[1, pair, left, :, at])
-                act[2, pair, blk, :, at] = jnp.where(place % 2 == 0, even, odd)
-
-    mask1 = lane_masks(EDGE + 1)
+    mask1 = lane_masks(x0, grid_x, EDGE + 1)
 
     def first(step, carry):
         pieces = []
@@ -275,25 +274,21 @@
         result = dot(jnp.concatenate(pieces, axis=0), w1_ref[...])
         for i in range(FIRST):
             pair = step * FIRST + i
-            inside = row_mask(2 * pair - H)
+            inside = row_mask(y0 + 2 * pair - H, grid_y)
             for blk in range(EDGE + 1):
                 values = result[i * PAIRS : (i + 1) * PAIRS, blk * BLK : (blk + 1) * BLK]
                 put(act1, pair, blk, jnp.maximum(values, 0.0) * (mask1[blk] * inside))
             put_sides(act1, pair, EDGE + 1)
         return carry
 
-    lax.fori_loop(0, pairs1 // FIRST, first, 0)
-
-    def layer(source, w_ref, pair, count):
-        size = count * EDGE * PAIRS
-        tiles = []
-        for kind in range(3):
-            centre = source[kind, pl.ds(pair + 1, count), :EDGE].reshape(size, BLK)
-            before = source[kind, pl.ds(pair, count), :EDGE, :, 128:].reshape(size, 128)
-            after = source[kind, pl.ds(pair + 2, count), :EDGE, :, :128].reshape(size, 128)
-            tiles += [centre, before, after]
-        return dot(jnp.concatenate(tiles, axis=1), w_ref[...])
-
+    lax.fori_loop(0, yw // 2 // FIRST, first, 0)
+
+
+def second_kernel(grid_x, grid_y, ty, act1, raw, w2_ref, act2, prod):
+    x0 = lax.axis_index("gx") * TX
+    y0 = lax.axis_index("gy") * ty
+    yw = ty + 2 * H
+    pairs2 = ty // 2 + 6
     block, up_y, down_y, up_t, down_t = plane_shifts(yw)
 
     def smooth_yt(v, edge=0.0):
@@ -314,6 +309,48 @@
         energy = grad_t * grad_t + 0.25 * (grad_x * grad_x + grad_y * grad_y)
         prod[2, at] = smooth_yt(energy, 0.25 * here * here)
 
+    steps2 = pairs2 // SECOND
+    blocks2 = -(-(FX // RX + 1) // steps2)
+    mask2 = lane_masks(x0, grid_x, EDGE)
+
+    def second(step, carry):
+        for i in range(blocks2):
+            products(jnp.minimum((step * blocks2 + i) * RX, FX))
+        for begin in range(0, SECOND, GROUP):
+            count = min(GROUP, SECOND - begin)
+            result = layer(act1, w2_ref, step * SECOND + begin, count)
+            for i in range(count):
+                pair = step * SECOND + begin + i
+                inside = row_mask(y0 + 2 * pair - 6, grid_y)
+                for blk in range(EDGE):
+                    at = (i * EDGE + blk) * PAIRS
+                    values = jnp.maximum(result[at : at + PAIRS], 0.0)
+                    put(act2, pair + 1, blk, values * (mask2[blk] * inside))
+                put_sides(act2, pair + 1, EDGE)
+        return carry
+
+    for edge in (0, pairs2 + 1):
+        for kind in range(3):
+            act2[kind, edge] = jnp.zeros((EDGE, PAIRS, BLK), BF16)
+    lax.fori_loop(0, steps2, second, 0)
+
+
+def third_kernel(
+    grid_x, grid_y, ty, act2, prod, w3_ref, w4_ref, fault_ref, prob, slope, act3, part
+):
+    x0 = lax.axis_index("gx") * TX
+    y0 = lax.axis_index("gy") * ty
+    yw = ty + 2 * H
+    pairs1, pairs2 = yw // 2, ty // 2 + 6
+    at_row = iota((4 * NT, 2 * NT), 0)
+    at_lane = iota((4 * NT, 2 * NT), 1)
+    from_pairs = jnp.where(
+        (at_lane % NT == 2 * pair_of(at_row % PAIRS) - 1 + at_row // NT)
+        & (at_lane // NT == at_row % NT // PAIRS),
+        1.0,
+        0.0,
+    ).astype(BF16)
+
     def slopes(k):
         at = pl.ds(k + 1, RX)
         sums = []
@@ -323,33 +360,10 @@
         scale = -1.0 / (sums[2] + 0.05)
         slope[0, at] = sums[0] * scale
         slope[1, at] = sums[1] * scale
-    steps2, steps3 = pairs2 // SECOND, pairs2 // THIRD
-    blocks2 = -(-(FX // RX + 1) // steps2)
+
+    steps3 = pairs2 // THIRD
     blocks3 = -(-(FX // RX) // steps3)
-    mask2 = lane_masks(EDGE)
-
-    def second(step, carry):
-        for i in range(blocks2):
-            products(jnp.minimum((step * blocks2 + i) * RX, FX))
-        for begin in range(0, SECOND, GROUP):
-            count = min(GROUP, SECOND - begin)
-            result = layer(act1, w2_ref, step * SECOND + begin, count)
-            for i in range(count):
-                pair = step * SECOND + begin + i
-                inside = row_mask(2 * pair - 6)
-                for blk in range(EDGE):
-                    at = (i * EDGE + blk) * PAIRS
-                    values = jnp.maximum(result[at : at + PAIRS], 0.0)
-                    put(act2, pair + 1, blk, values * (mask2[blk] * inside))
-                put_sides(act2, pair + 1, EDGE)
-        return carry
-
-    for edge in (0, pairs2 + 1):
-        for kind in range(3):
-            act2[kind, edge] = jnp.zeros((EDGE, PAIRS, BLK), BF16)
-    lax.fori_loop(0, steps2, second, 0)
-
-    act3 = act1.at[0]
+    mask2 = lane_masks(x0, grid_x, EDGE)
 
     def third(step, carry):
         for i in range(blocks3):
@@ -359,7 +373,7 @@
             result = layer(act2, w3_ref, step * THIRD + begin, count)
             for i in range(count):
                 pair = step * THIRD + begin + i
-                inside = row_mask(2 * pair - 6)
+                inside = row_mask(y0 + 2 * pair - 6, grid_y)
                 for blk in range(EDGE):
                     at = (i * EDGE + blk) * PAIRS
                     values = jnp.maximum(result[at : at + PAIRS], 0.0)
@@ -368,7 +382,7 @@
 
     lax.fori_loop(0, steps3, third, 0)
     for pair in range(pairs2, pairs1):
-        act3[pair] = jnp.zeros((EDGE + 1, PAIRS, BLK), BF16)
+        act3[pair] = jnp.zeros((EDGE, PAIRS, BLK), BF16)
 
     def fourth(step, carry):
         pair = step * 4
@@ -599,6 +613,9 @@
         jnp.concatenate([xlow[:, :H], amplitude[:, :H], xhigh[:, :H]]), "gy", n_gy, -1
     )
 
+    weights = (conv_first, conv_second, conv_third, conv_last)
+    (conv_first, conv_second, conv_third, conv_last), _ = lax.optimization_barrier((weights, xlow))
+
     def taps_first(weight):
         return jnp.transpose(weight, (2, 3, 4, 0, 1))
 
@@ -624,29 +641,52 @@
     )
 
     yw, nf = ty + 2 * H, FX + 2
+    act1, raw = pl.pallas_call(
+        functools.partial(first_kernel, grid_x, grid_y, ty),
+        out_shape=[
+            jax.ShapeDtypeStruct((3, yw // 2, EDGE + 1, PAIRS, BLK), BF16),
+            jax.ShapeDtypeStruct(((XW + 2) * yw, NT), F32),
+        ],
+        in_specs=vmem(6),
+        out_specs=vmem(2),
+        scratch_shapes=[pltpu.VMEM((yw + 2, XW, NT), BF16)],
+        compiler_params=pltpu.CompilerParams(vmem_limit_bytes=LIMIT * 2**20),
+        cost_estimate=pl.CostEstimate(flops=10**10, bytes_accessed=10**7, transcendentals=0),
+        name="layer_one",
+    )(amplitude, xlow, xhigh, ylow, yhigh, w1)
+
+    act2, prod = pl.pallas_call(
+        functools.partial(second_kernel, grid_x, grid_y, ty),
+        out_shape=[
+            jax.ShapeDtypeStruct((3, yw // 2, EDGE, PAIRS, BLK), BF16),
+            jax.ShapeDtypeStruct((3, FX + 4, yw, NT), F32),
+        ],
+        in_specs=vmem(3),
+        out_specs=vmem(2),
+        compiler_params=pltpu.CompilerParams(vmem_limit_bytes=LIMIT * 2**20),
+        cost_estimate=pl.CostEstimate(flops=10**10, bytes_accessed=10**7, transcendentals=0),
+        name="layer_two",
+    )(act1, raw, w2)
+
     fault, prob, slope = pl.pallas_call(
-        functools.partial(net_kernel, grid_x, grid_y, ty),
+        functools.partial(third_kernel, grid_x, grid_y, ty),
         out_shape=[
             jax.ShapeDtypeStruct((TX, ty, NT), BF16),
             jax.ShapeDtypeStruct((FX * yw, NT), F32),
             jax.ShapeDtypeStruct((2, nf, yw, NT), F32),
         ],
-        in_specs=vmem(9),
+        in_specs=vmem(4),
         out_specs=vmem(3),
         scratch_shapes=[
-            pltpu.VMEM(((XW + 2) * yw, NT), F32),
-            pltpu.VMEM((yw + 2, XW, NT), BF16),
-            pltpu.VMEM((3, yw // 2, EDGE + 1, PAIRS, BLK), BF16),
-            pltpu.VMEM((3, yw // 2, EDGE, PAIRS, BLK), BF16),
+            pltpu.VMEM((yw // 2, EDGE, PAIRS, BLK), BF16),
             pltpu.VMEM((yw // 2, 4 * FX, NT), F32),
-            pltpu.VMEM((3, FX + 4, yw, NT), F32),
         ],
-        compiler_params=pltpu.CompilerParams(vmem_limit_bytes=46 * 2**20),
+        compiler_params=pltpu.CompilerParams(vmem_limit_bytes=(LIMIT + 8) * 2**20),
         cost_estimate=pl.CostEstimate(
-            flops=3 * 10**10, bytes_accessed=10**7, transcendentals=10**6
+            flops=10**10, bytes_accessed=10**7, transcendentals=10**6
         ),
-        name="fault_net",
-    )(amplitude, xlow, xhigh, ylow, yhigh, w1, w2, w3, w4)
+        name="layers_three_four",
+    )(act2, prod, w3, w4)
 
     rows = TX // n_gy
     moments, face, wave2, *waves = pl.pallas_call(

time: 80 us -> 76.2 us (0.953)
  Pallas kernels: 45.4 us -> 41.3 us
  blocking collectives: 10.7 us -> 12.8 us
  waiting for transfers between devices: 3.29 us -> 1.45 us
    pallas_call x1 -> x3, Pallas kernels: 39.4 us -> 35.3 us  [the longest x1 16.1 us: on_device(): pl.pallas_call(functools.partial(third_kernel, grid_x, grid_y, ty), out_s...]
    all_to_all x1, blocking collectives: 10.7 us -> 12.8 us  [on_device(): lax.all_to_all(everyone, ('gx', 'gy'), split_axis=0, concat_axis=0, tiled...]
    ppermute x4, waiting for transfers between devices: 3.28 us -> 1.44 us  [shift(): return lax.ppermute(values, axis, pairs)]
  transfers between devices with their start and end apart: 7 -> 7, of which waited for: 1 -> 2; matrix products, arithmetic and copies ran while one was open for 3% -> 3% of each run, Pallas kernels for 3% -> 4%
where the time goes in v8:
time: 76.2 us; the launch traced here: 75.8 us
  Pallas kernels  41.3 us (54%)
  starting transfers between devices  16.1 us (21%)
  blocking collectives  12.8 us (17%)
  other arithmetic  1.79 us (2%)
  local copies, waits for them, and re-layouts  1.68 us (2%)
  waiting for transfers between devices  1.45 us (2%)
    pallas_call x1, Pallas kernels, on_device(): pl.pallas_call(functools.partial(third_kernel, grid_x, grid_y, ty), out_s...  16.1 us
    all_to_all x1, blocking collectives, on_device(): lax.all_to_all(everyone, ('gx', 'gy'), split_axis=0, concat_axis=0, tiled...  12.8 us
    pallas_call x1, Pallas kernels, on_device(): pl.pallas_call(functools.partial(second_kernel, grid_x, grid_y, ty), out_...  10.8 us
    ppermute x4, starting transfers between devices, shift(): return lax.ppermute(values, axis, pairs)  10.5 us
    pallas_call x1, Pallas kernels, on_device(): pl.pallas_call(functools.partial(first_kernel, grid_x, grid_y, ty), out_s...  8.45 us
    ppermute x3, starting transfers between devices, on_device(): arrived.append(lax.ppermute(waves[place], 'gy', pairs))  5.57 us
    pallas_call x1, Pallas kernels, on_device(): pl.pallas_call(functools.partial(waves_kernel, grid_x, grid_y, ty), out_s...  2.39 us
    pallas_call x1, Pallas kernels, on_device(): pl.pallas_call(prep_kernel, out_shape=[jax.ShapeDtypeStruct((16 * XW, (ED...  2.12 us
  transfers between devices with their start and end apart: 7, of which 2 were waited for; matrix products, arithmetic and copies ran while one was open for 3% of the time, Pallas kernels for 4%

profile of v8, /device:TPU:0, one launch (start us, length us, event | category | flops | bytes accessed | tf_op | source)
XLA Modules:
  0.0 75.8 jit_solution(13471573692520045154)
XLA Ops:
  0.6 0.9 %fusion.1 = (bf16[8,32,128]{2,1,0:T(8,128)(2,1)S(1)}, bf16[8,32,128]{2,1,0:T(8,128)(2,1)S(1)}) fusion(bf16[16,32,128]{2,1,0:T(8,128)(2,1)} %amp_ref.1), kind=kLoop, calls=%fused_computation.5 | loop fusion | bytes 262144 | tf_op jit(solution)/shard_map/slice | solution.py:605
  1.5 1.3 %collective-permute-start.1 = (bf16[8,32,128]{2,1,0:T(8,128)(2,1)S(1)}, bf16[8,32,128]{2,1,0:T(8,128)(2,1)S(1)}, u32[]{:S(2)}, u32[]{:S(2)}) collective-permute-start(bf16[8,32,128]{2,1,0:T(8,128)(2,1)S(1)} %get-tuple-element.48), channel_id=1, source_target_pairs={{4,0},{8,4},{12,8},{16,12},{20,16},{24,20},{28,24},{5,1},{9,5},{13... | collective-permute-start | bytes 196616 | tf_op jit(solution)/shard_map/ppermute | solution.py:602
  2.8 3.0 %collective-permute-start = (bf16[8,32,128]{2,1,0:T(8,128)(2,1)S(1)}, bf16[8,32,128]{2,1,0:T(8,128)(2,1)S(1)}, u32[]{:S(2)}, u32[]{:S(2)}) collective-permute-start(bf16[8,32,128]{2,1,0:T(8,128)(2,1)S(1)} %get-tuple-element.49), channel_id=1, source_target_pairs={{0,4},{4,8},{8,12},{12,16},{16,20},{20,24},{24,28},{1,5},{5,9},{9,... | collective-permute-start | bytes 196616 | tf_op jit(solution)/shard_map/ppermute | solution.py:602
  5.9 0.8 %fusion = (bf16[16,8,128]{2,1,0:T(8,128)(2,1)S(1)}, bf16[16,8,128]{2,1,0:T(8,128)(2,1)S(1)}) fusion(bf16[16,32,128]{2,1,0:T(8,128)(2,1)} %amp_ref.1), kind=kLoop, calls=%fused_computation.4 | loop fusion | bytes 131072 | tf_op jit(solution)/shard_map/slice | solution.py:613
  6.6 0.1 collective-permute-done.after_ref.xlow_ref
  6.7 0.0 collective-permute-done.1.xhigh_ref
  6.8 4.9 %collective-permute-start.2 = (bf16[32,8,128]{2,1,0:T(8,128)(2,1)S(1)}, bf16[32,8,128]{2,1,0:T(8,128)(2,1)S(1)}, u32[]{:S(2)}, u32[]{:S(2)}) collective-permute-start(bf16[32,8,128]{2,1,0:T(8,128)(2,1)S(1)} %pad_maximum_fusion.1), channel_id=1, source_target_pairs={{0,1},{1,2},{2,3},{4,5},{5,6},{6,7},{8,9},{9,10},{10,11},{12,13},{... | collective-permute-start | bytes 196616 | tf_op jit(solution)/shard_map/ppermute | solution.py:602
  11.7 1.3 %collective-permute-start.3 = (bf16[32,8,128]{2,1,0:T(8,128)(2,1)S(1)}, bf16[32,8,128]{2,1,0:T(8,128)(2,1)S(1)}, u32[]{:S(2)}, u32[]{:S(2)}) collective-permute-start(bf16[32,8,128]{2,1,0:T(8,128)(2,1)S(1)} %pad_maximum_fusion.2), channel_id=1, source_target_pairs={{1,0},{2,1},{3,2},{5,4},{6,5},{7,6},{9,8},{10,9},{11,10},{13,12},{... | collective-permute-start | bytes 196616 | tf_op jit(solution)/shard_map/ppermute | solution.py:602
  13.0 0.7 pad_maximum_fusion.3.outer_ref
  13.8 0.0 copy-start
  13.8 1.0 %pad_maximum_fusion = bf16[6,3,3,16,16]{4,3,2,1,0:T(8,128)(2,1)S(1)} fusion(bf16[3,3,3,16,16]{4,3,2,1,0:T(8,128)(2,1)} %bitcast.6, bf16[3,3,3,16,16]{4,3,2,1,0:T(8,128)(2,1)} %bitcast.7), kind=kLoop, calls=%fused_computation | loop fusion | flops 13824 | bytes 55296 | tf_op jit(solution)/shard_map/concatenate | solution.py:636
  14.8 2.1 %band_weights.1 = (bf16[512,2048]{1,0:T(8,128)(2,1)S(1)}, bf16[1536,256]{1,0:T(8,128)(2,1)S(1)}, bf16[1536,256]{1,0:T(8,128)(2,1)S(1)}, bf16[384,1792]{1,0:T(8,128)(2,1)S(1)}) custom-call(bf16[864,16]{1,0:T(8,128)(2,1)S(1)} %bitcast.5, bf16[2,3,3,3,16]{4,3,2,1,0:T(4,128)(2,1)S(1)} %pad_maximum_fusion.3.outer_ref, ...), custom_call_target="tpu_custom_call" | custom-call | flops 1000000000 | bytes 10000000 | tf_op jit(solution)/shard_map/band_weights/pallas_call | solution.py:622
  16.9 0.0 collective-permute-done.2.ylow_ref
  17.0 1.3 %collective-permute-done.3.yhigh_ref = bf16[32,8,128]{2,1,0:T(8,128)(2,1)S(1)} collective-permute-done((bf16[32,8,128]{2,1,0:T(8,128)(2,1)S(1)}, bf16[32,8,128]{2,1,0:T(8,128)(2,1)S(1)}, u32[]{:S(2)}, u32[]{:S(2)}) %collective-permute-start.3) | collective-permute-done | bytes 65568 | tf_op jit(solution)/shard_map/ppermute | solution.py:602
  18.3 0.0 copy-done
  18.3 8.5 %layer_one.1 = (bf16[3,24,8,64,256]{4,3,2,1,0:T(8,128)(2,1)S(1)}, f32[1632,128]{1,0:T(8,128)S(1)}) custom-call(bf16[16,32,128]{2,1,0:T(8,128)(2,1)S(1)} %copy-done, bf16[8,32,128]{2,1,0:T(8,128)(2,1)S(1)} %collective-permute-done.after_ref.xlow_ref, bf16[8,32,128]{2,1,0:T(8,128)(2,1)S(1)} %collective-permute-done.1.xhigh_ref, ...), custom_call_target="tpu_custom_call" | custom-call | flops 10000000000 | bytes 10000000 | tf_op jit(solution)/shard_map/layer_one/pallas_call | solution.py:644
  26.8 10.8 %layer_two.1 = (bf16[3,24,7,64,256]{4,3,2,1,0:T(8,128)(2,1)S(1)}, f32[3,28,48,128]{3,2,1,0:T(8,128)S(1)}) custom-call(bf16[3,24,8,64,256]{4,3,2,1,0:T(8,128)(2,1)S(1)} %get-tuple-element.29.act1, f32[1632,128]{1,0:T(8,128)S(1)} %get-tuple-element.30.raw, bf16[1536,256]{1,0:T(8,128)(2,1)S(1)} %get-tuple-element.31.w2_ref), custom_call_target="tpu_custom_call" | custom-call | flops 10000000000 | bytes 10000000 | tf_op jit(solution)/shard_map/layer_two/pallas_call | solution.py:658
  37.6 16.1 %layers_three_four.1 = (bf16[16,32,128]{2,1,0:T(8,128)(2,1)}, f32[1152,128]{1,0:T(8,128)S(1)}, f32[2,26,48,128]{3,2,1,0:T(8,128)S(1)}) custom-call(bf16[3,24,7,64,256]{4,3,2,1,0:T(8,128)(2,1)S(1)} %get-tuple-element.32.act2, f32[3,28,48,128]{3,2,1,0:T(8,128)S(1)} %get-tuple-element.33.prod, bf16[1536,256]{1,0:T(8,128)(2,1)S(1)} %get-tuple-element.34.w3_ref, ...), custom_call_target="tpu_custom_call" | custom-call | flops 10000000000 | bytes 10000000 | tf_op jit(solution)/shard_map/layers_three_four/pallas_call | solution.py:671
  53.6 2.4 %solver_waves.1 = (f32[8,128]{1,0:T(8,128)S(1)}, f32[2,26,48,128]{3,2,1,0:T(8,128)S(1)}, f32[26,48,128]{2,1,0:T(8,128)S(1)}, bf16[3,4,32,128]{3,2,1,0:T(8,128)(2...) custom-call(f32[1152,128]{1,0:T(8,128)S(1)} %get-tuple-element.37.pr, ...), custom_call_target="tpu_custom_call" | custom-call | flops 100000000 | bytes 10000000 | tf_op jit(solution)/shard_map/solver_waves/pallas_call | solution.py:692
  56.0 1.6 %collective-permute-start.4 = (bf16[3,4,32,128]{3,2,1,0:T(8,128)(2,1)S(1)}, bf16[3,4,32,128]{3,2,1,0:T(8,128)(2,1)S(1)}, u32[]{:S(2)}, u32[]{:S(2)}) collective-permute-start(bf16[3,4,32,128]{3,2,1,0:T(8,128)(2,1)S(1)} %get-tuple-element.43), channel_id=1, source_target_pairs={{0,1},{1,2},{2,3},{3,0},{4,5},{5,6},{6,7},{7,4},{8,9},{9,10},{10,1... | collective-permute-start | bytes 294920 | tf_op jit(solution)/shard_map/ppermute | solution.py:717
  57.6 2.3 %collective-permute-start.5 = (bf16[3,4,32,128]{3,2,1,0:T(8,128)(2,1)S(1)}, bf16[3,4,32,128]{3,2,1,0:T(8,128)(2,1)S(1)}, u32[]{:S(2)}, u32[]{:S(2)}) collective-permute-start(bf16[3,4,32,128]{3,2,1,0:T(8,128)(2,1)S(1)} %get-tuple-element.44), channel_id=1, source_target_pairs={{0,2},{1,3},{2,0},{3,1},{4,6},{5,7},{6,4},{7,5},{8,10},{9,11},{10,... | collective-permute-start | bytes 294920 | tf_op jit(solution)/shard_map/ppermute | solution.py:717
  60.0 1.6 %collective-permute-start.6 = (bf16[3,4,32,128]{3,2,1,0:T(8,128)(2,1)S(1)}, bf16[3,4,32,128]{3,2,1,0:T(8,128)(2,1)S(1)}, u32[]{:S(2)}, u32[]{:S(2)}) collective-permute-start(bf16[3,4,32,128]{3,2,1,0:T(8,128)(2,1)S(1)} %get-tuple-element.45), channel_id=1, source_target_pairs={{0,3},{1,0},{2,1},{3,2},{4,7},{5,4},{6,5},{7,6},{8,11},{9,8},{10,9... | collective-permute-start | bytes 294920 | tf_op jit(solution)/shard_map/ppermute | solution.py:717
  61.6 0.6 last_moment.1
  62.1 12.8 %all_to_all.5.mom_ref = f32[32,1,128]{2,1,0:T(1,128)S(1)} all-to-all(f32[32,1,128]{2,1,0:T(1,128)S(1)} %last_moment.1), channel_id=1, replica_groups=mesh['gx'=8,'gy'=4] {'gx','gy'}, dimensions={0} | all-to-all | bytes 32768 | tf_op jit(solution)/shard_map/all_to_all | solution.py:728
  74.9 0.0 collective-permute-done.4.refs_1_
  74.9 0.0 collective-permute-done.5.refs_2_
  74.9 0.0 collective-permute-done.6.refs_3_
  74.9 0.9 %combine_waves.1 = f32[4,128,128]{2,1,0:T(8,128)} custom-call(f32[32,1,128]{2,1,0:T(1,128)S(1)} %all_to_all.5.mom_ref, bf16[3,4,32,128]{3,2,1,0:T(8,128)(2,1)S(1)} %get-tuple-element.42.refs_0_, bf16[3,4,32,128]{3,2,1,0:T(8,128)(2,1)S(1)} %collective-permute-done.4.refs_1_, bf16[3,4,32,128]{3,2,1,0:T(8,128)(2,1)S(1)} %collective-permute-done.5.refs_2_, ...), custom_call_target="tpu_custom_call" | custom-call | tf_op jit(solution)/shard_map/combine_waves/pallas_call | solution.py:729
  (4 shorter events, 0.0 us)
Async XLA Ops:
  1.5 5.2 %collective-permute-start.1 = (bf16[8,32,128]{2,1,0:T(8,128)(2,1)S(1)}, bf16[8,32,128]{2,1,0:T(8,128)(2,1)S(1)}, u32[]{:S(2)}, u32[]{:S(2)}) collective-permute-start(bf16[8,32,128]{2,1,0:T(8,128)(2,1)S(1)} %get-tuple-element.48), channel_id=1, source_target_pairs={{4,0},{8,4},{12,8},{16,12},{20,16},{24,20},{28,24},{5,1},{9,5},{13... | collective-permute-start | bytes 196616 | tf_op jit(solution)/shard_map/ppermute | solution.py:602
  2.8 3.9 %collective-permute-start = (bf16[8,32,128]{2,1,0:T(8,128)(2,1)S(1)}, bf16[8,32,128]{2,1,0:T(8,128)(2,1)S(1)}, u32[]{:S(2)}, u32[]{:S(2)}) collective-permute-start(bf16[8,32,128]{2,1,0:T(8,128)(2,1)S(1)} %get-tuple-element.49), channel_id=1, source_target_pairs={{0,4},{4,8},{8,12},{12,16},{16,20},{20,24},{24,28},{1,5},{5,9},{9,... | collective-permute-start | bytes 196616 | tf_op jit(solution)/shard_map/ppermute | solution.py:602
  6.8 10.2 %collective-permute-start.2 = (bf16[32,8,128]{2,1,0:T(8,128)(2,1)S(1)}, bf16[32,8,128]{2,1,0:T(8,128)(2,1)S(1)}, u32[]{:S(2)}, u32[]{:S(2)}) collective-permute-start(bf16[32,8,128]{2,1,0:T(8,128)(2,1)S(1)} %pad_maximum_fusion.1), channel_id=1, source_target_pairs={{0,1},{1,2},{2,3},{4,5},{5,6},{6,7},{8,9},{9,10},{10,11},{12,13},{... | collective-permute-start | bytes 196616 | tf_op jit(solution)/shard_map/ppermute | solution.py:602
  11.7 6.6 %collective-permute-start.3 = (bf16[32,8,128]{2,1,0:T(8,128)(2,1)S(1)}, bf16[32,8,128]{2,1,0:T(8,128)(2,1)S(1)}, u32[]{:S(2)}, u32[]{:S(2)}) collective-permute-start(bf16[32,8,128]{2,1,0:T(8,128)(2,1)S(1)} %pad_maximum_fusion.2), channel_id=1, source_target_pairs={{1,0},{2,1},{3,2},{5,4},{6,5},{7,6},{9,8},{10,9},{11,10},{13,12},{... | collective-permute-start | bytes 196616 | tf_op jit(solution)/shard_map/ppermute | solution.py:602
  13.8 4.5 %copy-start = (bf16[16,32,128]{2,1,0:T(8,128)(2,1)S(1)}, bf16[16,32,128]{2,1,0:T(8,128)(2,1)}, u32[]{:S(2)}) copy-start(bf16[16,32,128]{2,1,0:T(8,128)(2,1)} %amp_ref.1) | copy-start | bytes 393220
  56.0 18.9 %collective-permute-start.4 = (bf16[3,4,32,128]{3,2,1,0:T(8,128)(2,1)S(1)}, bf16[3,4,32,128]{3,2,1,0:T(8,128)(2,1)S(1)}, u32[]{:S(2)}, u32[]{:S(2)}) collective-permute-start(bf16[3,4,32,128]{3,2,1,0:T(8,128)(2,1)S(1)} %get-tuple-element.43), channel_id=1, source_target_pairs={{0,1},{1,2},{2,3},{3,0},{4,5},{5,6},{6,7},{7,4},{8,9},{9,10},{10,1... | collective-permute-start | bytes 294920 | tf_op jit(solution)/shard_map/ppermute | solution.py:717
  57.6 17.3 %collective-permute-start.5 = (bf16[3,4,32,128]{3,2,1,0:T(8,128)(2,1)S(1)}, bf16[3,4,32,128]{3,2,1,0:T(8,128)(2,1)S(1)}, u32[]{:S(2)}, u32[]{:S(2)}) collective-permute-start(bf16[3,4,32,128]{3,2,1,0:T(8,128)(2,1)S(1)} %get-tuple-element.44), channel_id=1, source_target_pairs={{0,2},{1,3},{2,0},{3,1},{4,6},{5,7},{6,4},{7,5},{8,10},{9,11},{10,... | collective-permute-start | bytes 294920 | tf_op jit(solution)/shard_map/ppermute | solution.py:717
  60.0 14.9 %collective-permute-start.6 = (bf16[3,4,32,128]{3,2,1,0:T(8,128)(2,1)S(1)}, bf16[3,4,32,128]{3,2,1,0:T(8,128)(2,1)S(1)}, u32[]{:S(2)}, u32[]{:S(2)}) collective-permute-start(bf16[3,4,32,128]{3,2,1,0:T(8,128)(2,1)S(1)} %get-tuple-element.45), channel_id=1, source_target_pairs={{0,3},{1,0},{2,1},{3,2},{4,7},{5,4},{6,5},{7,6},{8,11},{9,8},{10,9... | collective-permute-start | bytes 294920 | tf_op jit(solution)/shard_map/ppermute | solution.py:717

commit v9 on v8

--- a/solution.py
+++ b/solution.py
@@ -16,6 +16,7 @@
 FX = TX + 8
 RX = 4
 FIRST, SECOND, THIRD = 8, 11, 11
+Y_SLOTS = (1, 2, 3, 0)
 LIMIT = 6
 GROUP = 2
 BLK = 256
@@ -103,26 +104,21 @@
                 for dx in range(3):
                     band = jnp.where(masks[blk][dx], values[dx], band)
                 w1_ref[row : row + XW, blk * BLK : (blk + 1) * BLK] = band
-    row_x = iota((FX, BLK), 0)
-    lane_x = iota((FX, BLK), 1) // CH % 4
     masks = [
         [4 * blk + lane_x - 1 - row_x == dx for dx in range(3)] for blk in range(EDGE)
     ]
-    none = jnp.zeros((FX, BLK), F32)
     bands = [[] for blk in range(EDGE)]
-    for yi in range(4):
-        for j in range(4):
-            values = [
-                by_quarter(last, dx, lambda y, t: (y + 2 - yi, t + 2 - j)) for dx in range(3)
-            ]
+    for j in range(4):
+        for yi in Y_SLOTS:
+            values = rows_of(last, XW, lambda y, t: (y + 2 - yi, t + 2 - j))
             for blk in range(EDGE):
                 band = none
                 for dx in range(3):
                     band = jnp.where(masks[blk][dx], values[dx], band)
                 bands[blk].append(band)
     for blk in range(EDGE):
-        whole = jnp.concatenate(bands[blk], axis=0).astype(BF16)
-        w4_ref[:, blk * BLK : (blk + 1) * BLK] = whole
+        turned = dot_nt(unit, jnp.concatenate(bands[blk], axis=0))
+        w4_ref[blk * BLK : (blk + 1) * BLK, :] = turned.astype(BF16)
 
 
 def input_cells():
@@ -271,51 +267,32 @@
             pieces.append(
                 jnp.concatenate([turned[j * PAIRS : (j + 1) * PAIRS] for j in range(4)], axis=1)
             )
-        result = dot(jnp.concatenate(pieces, axis=0), w1_ref[...])
+        pieces = jnp.concatenate(pieces, axis=0)
+        for begin in range(0, EDGE + 1, 2):
+            result = dot(pieces, w1_ref[:, begin * BLK : (begin + 2) * BLK])
+            for i in range(FIRST):
+                pair = step * FIRST + i
+                inside = row_mask(y0 + 2 * pair - H, grid_y)
+                for blk in (begin, begin + 1):
+                    lane = (blk - begin) * BLK
+                    values = result[i * PAIRS : (i + 1) * PAIRS, lane : lane + BLK]
+                    put(act1, pair, blk, jnp.maximum(values, 0.0) * (mask1[blk] * inside))
         for i in range(FIRST):
-            pair = step * FIRST + i
-            inside = row_mask(y0 + 2 * pair - H, grid_y)
-            for blk in range(EDGE + 1):
-                values = result[i * PAIRS : (i + 1) * PAIRS, blk * BLK : (blk + 1) * BLK]
-                put(act1, pair, blk, jnp.maximum(values, 0.0) * (mask1[blk] * inside))
-            put_sides(act1, pair, EDGE + 1)
+            put_sides(act1, step * FIRST + i, EDGE + 1)
         return carry
 
     lax.fori_loop(0, yw // 2 // FIRST, first, 0)
 
 
-def second_kernel(grid_x, grid_y, ty, act1, raw, w2_ref, act2, prod):
+def second_kernel(grid_x, grid_y, ty, act1, w2_ref, act2):
     x0 = lax.axis_index("gx") * TX
     y0 = lax.axis_index("gy") * ty
     yw = ty + 2 * H
     pairs2 = ty // 2 + 6
-    block, up_y, down_y, up_t, down_t = plane_shifts(yw)
-
-    def smooth_yt(v, edge=0.0):
-        v = 0.5 * v + 0.25 * (up_t(v, edge) + down_t(v, edge))
-        return 0.5 * v + 0.25 * (up_y(v) + down_y(v))
-
-    def amp_rows(x):
-        return raw[pl.ds(pl.multiple_of(x * yw, 8), RX * yw), :].reshape(block)
-
-    def products(k):
-        here = amp_rows(k + 3)
-        grad_x = 0.5 * (amp_rows(k + 4) - amp_rows(k + 2))
-        grad_y = 0.5 * (up_y(here) - down_y(here))
-        grad_t = 0.5 * (up_t(here) - down_t(here))
-        at = pl.ds(k, RX)
-        prod[0, at] = smooth_yt(grad_x * grad_t)
-        prod[1, at] = smooth_yt(grad_y * grad_t)
-        energy = grad_t * grad_t + 0.25 * (grad_x * grad_x + grad_y * grad_y)
-        prod[2, at] = smooth_yt(energy, 0.25 * here * here)
-
     steps2 = pairs2 // SECOND
-    blocks2 = -(-(FX // RX + 1) // steps2)
     mask2 = lane_masks(x0, grid_x, EDGE)
 
     def second(step, carry):
-        for i in range(blocks2):
-            products(jnp.minimum((step * blocks2 + i) * RX, FX))
         for begin in range(0, SECOND, GROUP):
             count = min(GROUP, SECOND - begin)
             result = layer(act1, w2_ref, step * SECOND + begin, count)
@@ -335,39 +312,38 @@
     lax.fori_loop(0, steps2, second, 0)
 
 
-def third_kernel(
-    grid_x, grid_y, ty, act2, prod, w3_ref, w4_ref, fault_ref, prob, slope, act3, part
-):
+def third_kernel(grid_x, grid_y, ty, act2, raw, w3_ref, act3, prod):
     x0 = lax.axis_index("gx") * TX
     y0 = lax.axis_index("gy") * ty
     yw = ty + 2 * H
     pairs1, pairs2 = yw // 2, ty // 2 + 6
-    at_row = iota((4 * NT, 2 * NT), 0)
-    at_lane = iota((4 * NT, 2 * NT), 1)
-    from_pairs = jnp.where(
-        (at_lane % NT == 2 * pair_of(at_row % PAIRS) - 1 + at_row // NT)
-        & (at_lane // NT == at_row % NT // PAIRS),
-        1.0,
-        0.0,
-    ).astype(BF16)
-
-    def slopes(k):
-        at = pl.ds(k + 1, RX)
-        sums = []
-        for which in range(3):
-            before, here, after = [prod[which, pl.ds(k + i, RX)] for i in range(3)]
-            sums.append(0.5 * here + 0.25 * (before + after))
-        scale = -1.0 / (sums[2] + 0.05)
-        slope[0, at] = sums[0] * scale
-        slope[1, at] = sums[1] * scale
+    block, up_y, down_y, up_t, down_t = plane_shifts(yw)
+
+    def smooth_yt(v, edge=0.0):
+        v = 0.5 * v + 0.25 * (up_t(v, edge) + down_t(v, edge))
+        return 0.5 * v + 0.25 * (up_y(v) + down_y(v))
+
+    def amp_rows(x):
+        return raw[pl.ds(pl.multiple_of(x * yw, 8), RX * yw), :].reshape(block)
+
+    def products(k):
+        here = amp_rows(k + 3)
+        grad_x = 0.5 * (amp_rows(k + 4) - amp_rows(k + 2))
+        grad_y = 0.5 * (up_y(here) - down_y(here))
+        grad_t = 0.5 * (up_t(here) - down_t(here))
+        at = pl.ds(k, RX)
+        prod[0, at] = smooth_yt(grad_x * grad_t)
+        prod[1, at] = smooth_yt(grad_y * grad_t)
+        energy = grad_t * grad_t + 0.25 * (grad_x * grad_x + grad_y * grad_y)
+        prod[2, at] = smooth_yt(energy, 0.25 * here * here)
 
     steps3 = pairs2 // THIRD
-    blocks3 = -(-(FX // RX) // steps3)
+    blocks3 = -(-(FX // RX + 1) // steps3)
     mask2 = lane_masks(x0, grid_x, EDGE)
 
     def third(step, carry):
         for i in range(blocks3):
-            slopes(jnp.minimum((step * blocks3 + i) * RX, FX - RX))
+            products(jnp.minimum((step * blocks3 + i) * RX, FX))
         for begin in range(0, THIRD, GROUP):
             count = min(GROUP, THIRD - begin)
             result = layer(act2, w3_ref, step * THIRD + begin, count)
@@ -384,47 +360,72 @@
     for pair in range(pairs2, pairs1):
         act3[pair] = jnp.zeros((EDGE, PAIRS, BLK), BF16)
 
+
+def fourth_kernel(ty, act3, prod, w4_ref, fault_ref, prob, slope, part):
+    yw = ty + 2 * H
+    pairs1 = yw // 2
+    at_lane = iota((NT, 8 * PAIRS), 1) % (4 * PAIRS)
+    from_pairs = jnp.where(
+        iota((NT, 8 * PAIRS), 0) == 2 * pair_of(at_lane % PAIRS) - 1 + at_lane // PAIRS, 1.0, 0.0
+    ).astype(BF16)
+
+    def slopes(k):
+        at = pl.ds(k + 1, RX)
+        sums = []
+        for which in range(3):
+            before, here, after = [prod[which, pl.ds(k + i, RX)] for i in range(3)]
+            sums.append(0.5 * here + 0.25 * (before + after))
+        scale = -1.0 / (sums[2] + 0.05)
+        slope[0, at] = sums[0] * scale
+        slope[1, at] = sums[1] * scale
+
     def fourth(step, carry):
-        pair = step * 4
-        cells = [act3[pl.ds(pair, 4), blk].reshape(4 * PAIRS, BLK) for blk in range(EDGE)]
-        result = dot_nt(w4_ref[...], jnp.concatenate(cells, axis=1))
-        for half in range(2):
-            columns = result[:, half * NT : (half + 1) * NT]
-            sums = jnp.concatenate(
-                [
-                    jnp.concatenate(
-                        [columns[(yi * 4 + j) * FX : (yi * 4 + j + 1) * FX] for j in range(4)],
-                        axis=1,
-                    )
-                    for yi in range(4)
-                ],
-                axis=0,
-            )
-            high = sums.astype(BF16)
-            low = (sums - high.astype(F32)).astype(BF16)
-            both = dot(jnp.concatenate([high, low], axis=0), from_pairs)
-            share = both[: 4 * FX] + both[4 * FX :]
-            for i in range(2):
-                part[pair + half * 2 + i] = share[:, i * NT : (i + 1) * NT]
+        for i in range(2):
+            slopes(jnp.minimum((step * 2 + i) * RX, FX - RX))
+        pair = step * 8
+        cells = [act3[pl.ds(pair, 8), blk].reshape(8 * PAIRS, BLK) for blk in range(EDGE)]
+        result = dot(jnp.concatenate(cells, axis=1), w4_ref[...])
+        for i in range(0, 8, 2):
+            sides = []
+            for at in (i, i + 1):
+                rows = result[at * PAIRS : (at + 1) * PAIRS]
+                sides.append(
+                    jnp.concatenate([rows[:, j * 128 : (j + 1) * 128] for j in range(4)], axis=0)
+                )
+            both = jnp.concatenate(sides, axis=1)
+            high = both.astype(BF16)
+            low = (both - high.astype(F32)).astype(BF16)
+            share = dot(from_pairs, jnp.concatenate([high, low], axis=0))
+            part[pair + i] = share[:, :128]
+            part[pair + i + 1] = share[:, 128:]
         return carry
 
-    lax.fori_loop(0, pairs1 // 4, fourth, 0, unroll=2)
+    lax.fori_loop(0, pairs1 // 8, fourth, 0)
 
     for x in range(FX):
         prob[x * yw : x * yw + H, :] = jnp.zeros((H, NT), F32)
         prob[(x + 1) * yw - H : (x + 1) * yw, :] = jnp.zeros((H, NT), F32)
+    lane = iota((NT, 128), 1)
 
     def order(step, carry):
-        for i in range(4):
-            pair = step * 4 + i + 1
-            even = part[pair, FX : 2 * FX] + part[pair - 1, 3 * FX :]
-            odd = part[pair, 2 * FX : 3 * FX] + part[pair + 1, :FX]
-            for row, values in enumerate((even, odd)):
-                values = (1.0 / (1.0 + jnp.exp(-values))).astype(BF16).astype(F32)
-                prob[pl.ds(2 * pair + 2 + row, FX, stride=yw), :] = values
+        pair = 2 * step + 1
+        here = part[pair]
+        before = pltpu.roll(part[pair - 1], 64, 1)
+        after = pltpu.roll(part[pair + 1], 64, 1)
+        own = jnp.where(lane < 64, here, after)
+        other = jnp.where(
+            lane < 32,
+            before,
+            jnp.where(lane < 64, after, jnp.where(lane < 96, here, part[pair + 2])),
+        )
+        values = 1.0 / (1.0 + jnp.exp(-(own + other)))
+        values = values.astype(BF16).astype(F32).T
+        for row in range(4):
+            at = pl.ds(2 * pair + 2 + row, FX, stride=yw)
+            prob[at, :] = values[row * XW : row * XW + FX]
         return carry
 
-    lax.fori_loop(0, (ty + 8) // 8, order, 0)
+    lax.fori_loop(0, (ty + 8) // 4, order, 0, unroll=2)
 
     for which in range(2):
         slope[which, FX + 1] = jnp.zeros((yw, NT), F32)
@@ -625,7 +626,7 @@
             jax.ShapeDtypeStruct((16 * XW, (EDGE + 1) * BLK), BF16),
             jax.ShapeDtypeStruct((6 * BLK, BLK), BF16),
             jax.ShapeDtypeStruct((6 * BLK, BLK), BF16),
-            jax.ShapeDtypeStruct((16 * FX, EDGE * BLK), BF16),
+            jax.ShapeDtypeStruct((EDGE * BLK, 16 * XW), BF16),
         ],
         in_specs=vmem(2) + [pl.BlockSpec(memory_space=pl.ANY)],
         out_specs=vmem(4),
@@ -655,38 +656,45 @@
         name="layer_one",
     )(amplitude, xlow, xhigh, ylow, yhigh, w1)
 
-    act2, prod = pl.pallas_call(
+    act2 = pl.pallas_call(
         functools.partial(second_kernel, grid_x, grid_y, ty),
+        out_shape=jax.ShapeDtypeStruct((3, yw // 2, EDGE, PAIRS, BLK), BF16),
+        in_specs=vmem(2),
+        out_specs=pl.BlockSpec(memory_space=pltpu.VMEM),
+        compiler_params=pltpu.CompilerParams(vmem_limit_bytes=LIMIT * 2**20),
+        cost_estimate=pl.CostEstimate(flops=10**10, bytes_accessed=10**7, transcendentals=0),
+        name="layer_two",
+    )(act1, w2)
+
+    act3, prod = pl.pallas_call(
+        functools.partial(third_kernel, grid_x, grid_y, ty),
         out_shape=[
-            jax.ShapeDtypeStruct((3, yw // 2, EDGE, PAIRS, BLK), BF16),
+            jax.ShapeDtypeStruct((yw // 2, EDGE, PAIRS, BLK), BF16),
             jax.ShapeDtypeStruct((3, FX + 4, yw, NT), F32),
         ],
         in_specs=vmem(3),
         out_specs=vmem(2),
         compiler_params=pltpu.CompilerParams(vmem_limit_bytes=LIMIT * 2**20),
         cost_estimate=pl.CostEstimate(flops=10**10, bytes_accessed=10**7, transcendentals=0),
-        name="layer_two",
-    )(act1, raw, w2)
+        name="layer_three",
+    )(act2, raw, w3)
 
     fault, prob, slope = pl.pallas_call(
-        functools.partial(third_kernel, grid_x, grid_y, ty),
+        functools.partial(fourth_kernel, ty),
         out_shape=[
             jax.ShapeDtypeStruct((TX, ty, NT), BF16),
             jax.ShapeDtypeStruct((FX * yw, NT), F32),
             jax.ShapeDtypeStruct((2, nf, yw, NT), F32),
         ],
-        in_specs=vmem(4),
+        in_specs=vmem(3),
         out_specs=vmem(3),
-        scratch_shapes=[
-            pltpu.VMEM((yw // 2, EDGE, PAIRS, BLK), BF16),
-            pltpu.VMEM((yw // 2, 4 * FX, NT), F32),
-        ],
-        compiler_params=pltpu.CompilerParams(vmem_limit_bytes=(LIMIT + 8) * 2**20),
+        scratch_shapes=[pltpu.VMEM((yw // 2, NT, 128), F32)],
+        compiler_params=pltpu.CompilerParams(vmem_limit_bytes=(LIMIT + 4) * 2**20),
         cost_estimate=pl.CostEstimate(
             flops=10**10, bytes_accessed=10**7, transcendentals=10**6
         ),
-        name="layers_three_four",
-    )(act2, prod, w3, w4)
+        name="layer_four",
+    )(act3, prod, w4)
 
     rows = TX // n_gy
     moments, face, wave2, *waves = pl.pallas_call(

time: 76.2 us -> 74.5 us (0.978)
  Pallas kernels: 41.3 us -> 39.4 us
    pallas_call x1, Pallas kernels: 16.1 us -> 8.33 us  [on_device(): pl.pallas_call(functools.partial(third_kernel, grid_x, grid_y, ty), out_s...]
    pallas_call x0 -> x1, Pallas kernels: none -> 6.01 us  [on_device(): pl.pallas_call(functools.partial(fourth_kernel, ty), out_shape=[jax.Shape...]
where the time goes in v9:
time: 74.5 us; the launch traced here: 74.1 us
  Pallas kernels  39.4 us (53%)
  starting transfers between devices  16.3 us (22%)
  blocking collectives  12.8 us (17%)
  other arithmetic  1.76 us (2%)
  local copies, waits for them, and re-layouts  1.68 us (2%)
  waiting for transfers between devices  1.45 us (2%)
  between operations  0.76 us (1%)
    all_to_all x1, blocking collectives, on_device(): lax.all_to_all(everyone, ('gx', 'gy'), split_axis=0, concat_axis=0, tiled...  12.8 us
    ppermute x4, starting transfers between devices, shift(): return lax.ppermute(values, axis, pairs)  10.7 us
    pallas_call x1, Pallas kernels, on_device(): pl.pallas_call(functools.partial(second_kernel, grid_x, grid_y, ty), out_...  10.5 us
    pallas_call x1, Pallas kernels, on_device(): pl.pallas_call(functools.partial(first_kernel, grid_x, grid_y, ty), out_s...  8.47 us
    pallas_call x1, Pallas kernels, on_device(): pl.pallas_call(functools.partial(third_kernel, grid_x, grid_y, ty), out_s...  8.33 us
    pallas_call x1, Pallas kernels, on_device(): pl.pallas_call(functools.partial(fourth_kernel, ty), out_shape=[jax.Shape...  6.01 us
    ppermute x3, starting transfers between devices, on_device(): arrived.append(lax.ppermute(waves[place], 'gy', pairs))  5.58 us
    pallas_call x1, Pallas kernels, on_device(): pl.pallas_call(functools.partial(waves_kernel, grid_x, grid_y, ty), out_s...  2.39 us
  transfers between devices with their start and end apart: 7, of which 2 were waited for; matrix products, arithmetic and copies ran while one was open for 3% of the time, Pallas kernels for 4%

profile of v9, /device:TPU:0, one launch (start us, length us, event | category | flops | bytes accessed | tf_op | source)
XLA Modules:
  0.0 74.1 jit_solution(2605668508621639150)
XLA Ops:
  0.6 0.9 %fusion.1 = (bf16[8,32,128]{2,1,0:T(8,128)(2,1)S(1)}, bf16[8,32,128]{2,1,0:T(8,128)(2,1)S(1)}) fusion(bf16[16,32,128]{2,1,0:T(8,128)(2,1)} %amp_ref.1), kind=kLoop, calls=%fused_computation.5 | loop fusion | bytes 262144 | tf_op jit(solution)/shard_map/slice | solution.py:606
  1.5 1.3 %collective-permute-start.1 = (bf16[8,32,128]{2,1,0:T(8,128)(2,1)S(1)}, bf16[8,32,128]{2,1,0:T(8,128)(2,1)S(1)}, u32[]{:S(2)}, u32[]{:S(2)}) collective-permute-start(bf16[8,32,128]{2,1,0:T(8,128)(2,1)S(1)} %get-tuple-element.48), channel_id=1, source_target_pairs={{4,0},{8,4},{12,8},{16,12},{20,16},{24,20},{28,24},{5,1},{9,5},{13... | collective-permute-start | bytes 196616 | tf_op jit(solution)/shard_map/ppermute | solution.py:603
  2.8 3.0 %collective-permute-start = (bf16[8,32,128]{2,1,0:T(8,128)(2,1)S(1)}, bf16[8,32,128]{2,1,0:T(8,128)(2,1)S(1)}, u32[]{:S(2)}, u32[]{:S(2)}) collective-permute-start(bf16[8,32,128]{2,1,0:T(8,128)(2,1)S(1)} %get-tuple-element.49), channel_id=1, source_target_pairs={{0,4},{4,8},{8,12},{12,16},{16,20},{20,24},{24,28},{1,5},{5,9},{9,... | collective-permute-start | bytes 196616 | tf_op jit(solution)/shard_map/ppermute | solution.py:603
  5.9 0.8 %fusion = (bf16[16,8,128]{2,1,0:T(8,128)(2,1)S(1)}, bf16[16,8,128]{2,1,0:T(8,128)(2,1)S(1)}) fusion(bf16[16,32,128]{2,1,0:T(8,128)(2,1)} %amp_ref.1), kind=kLoop, calls=%fused_computation.4 | loop fusion | bytes 131072 | tf_op jit(solution)/shard_map/slice | solution.py:614
  6.6 0.1 collective-permute-done.after_ref.xlow_ref
  6.7 0.0 collective-permute-done.1.xhigh_ref
  6.8 4.9 %collective-permute-start.2 = (bf16[32,8,128]{2,1,0:T(8,128)(2,1)S(1)}, bf16[32,8,128]{2,1,0:T(8,128)(2,1)S(1)}, u32[]{:S(2)}, u32[]{:S(2)}) collective-permute-start(bf16[32,8,128]{2,1,0:T(8,128)(2,1)S(1)} %pad_maximum_fusion.1), channel_id=1, source_target_pairs={{0,1},{1,2},{2,3},{4,5},{5,6},{6,7},{8,9},{9,10},{10,11},{12,13},{... | collective-permute-start | bytes 196616 | tf_op jit(solution)/shard_map/ppermute | solution.py:603
  11.7 0.0 copy-start
  11.7 1.4 %collective-permute-start.3 = (bf16[32,8,128]{2,1,0:T(8,128)(2,1)S(1)}, bf16[32,8,128]{2,1,0:T(8,128)(2,1)S(1)}, u32[]{:S(2)}, u32[]{:S(2)}) collective-permute-start(bf16[32,8,128]{2,1,0:T(8,128)(2,1)S(1)} %pad_maximum_fusion.2), channel_id=1, source_target_pairs={{1,0},{2,1},{3,2},{5,4},{6,5},{7,6},{9,8},{10,9},{11,10},{13,12},{... | collective-permute-start | bytes 196616 | tf_op jit(solution)/shard_map/ppermute | solution.py:603
  13.2 0.7 pad_maximum_fusion.3.outer_ref
  13.9 1.0 %pad_maximum_fusion = bf16[6,3,3,16,16]{4,3,2,1,0:T(8,128)(2,1)S(1)} fusion(bf16[3,3,3,16,16]{4,3,2,1,0:T(8,128)(2,1)} %bitcast.6, bf16[3,3,3,16,16]{4,3,2,1,0:T(8,128)(2,1)} %bitcast.7), kind=kLoop, calls=%fused_computation | loop fusion | flops 13824 | bytes 55296 | tf_op jit(solution)/shard_map/concatenate | solution.py:637
  14.9 2.2 %band_weights.1 = (bf16[512,2048]{1,0:T(8,128)(2,1)S(1)}, bf16[1536,256]{1,0:T(8,128)(2,1)S(1)}, bf16[1536,256]{1,0:T(8,128)(2,1)S(1)}, bf16[1792,512]{1,0:T(8,128)(2,1)S(1)}) custom-call(bf16[864,16]{1,0:T(8,128)(2,1)S(1)} %bitcast.5, bf16[2,3,3,3,16]{4,3,2,1,0:T(4,128)(2,1)S(1)} %pad_maximum_fusion.3.outer_ref, ...), custom_call_target="tpu_custom_call" | custom-call | flops 1000000000 | bytes 10000000 | tf_op jit(solution)/shard_map/band_weights/pallas_call | solution.py:623
  17.1 0.0 collective-permute-done.2.ylow_ref
  17.1 1.3 %collective-permute-done.3.yhigh_ref = bf16[32,8,128]{2,1,0:T(8,128)(2,1)S(1)} collective-permute-done((bf16[32,8,128]{2,1,0:T(8,128)(2,1)S(1)}, bf16[32,8,128]{2,1,0:T(8,128)(2,1)S(1)}, u32[]{:S(2)}, u32[]{:S(2)}) %collective-permute-start.3) | collective-permute-done | bytes 65568 | tf_op jit(solution)/shard_map/ppermute | solution.py:603
  18.4 0.0 copy-done
  18.4 8.5 %layer_one.1 = (bf16[3,24,8,64,256]{4,3,2,1,0:T(8,128)(2,1)S(1)}, f32[1632,128]{1,0:T(8,128)S(1)}) custom-call(bf16[16,32,128]{2,1,0:T(8,128)(2,1)S(1)} %copy-done, bf16[8,32,128]{2,1,0:T(8,128)(2,1)S(1)} %collective-permute-done.after_ref.xlow_ref, bf16[8,32,128]{2,1,0:T(8,128)(2,1)S(1)} %collective-permute-done.1.xhigh_ref, ...), custom_call_target="tpu_custom_call" | custom-call | flops 10000000000 | bytes 10000000 | tf_op jit(solution)/shard_map/layer_one/pallas_call | solution.py:645
  26.9 10.5 %layer_two.1.act2 = bf16[3,24,7,64,256]{4,3,2,1,0:T(8,128)(2,1)S(1)} custom-call(bf16[3,24,8,64,256]{4,3,2,1,0:T(8,128)(2,1)S(1)} %get-tuple-element.29.act1, bf16[1536,256]{1,0:T(8,128)(2,1)S(1)} %get-tuple-element.30.w2_ref), custom_call_target="tpu_custom_call" | custom-call | flops 10000000000 | bytes 10000000 | tf_op jit(solution)/shard_map/layer_two/pallas_call | solution.py:659
  37.5 8.3 %layer_three.1 = (bf16[24,7,64,256]{3,2,1,0:T(8,128)(2,1)S(1)}, f32[3,28,48,128]{3,2,1,0:T(8,128)S(1)}) custom-call(bf16[3,24,7,64,256]{4,3,2,1,0:T(8,128)(2,1)S(1)} %layer_two.1.act2, f32[1632,128]{1,0:T(8,128)S(1)} %get-tuple-element.31.raw, bf16[1536,256]{1,0:T(8,128)(2,1)S(1)} %get-tuple-element.32.w3_ref), custom_call_target="tpu_custom_call" | custom-call | flops 10000000000 | bytes 10000000 | tf_op jit(solution)/shard_map/layer_three/pallas_call | solution.py:669
  45.8 6.0 %layer_four.1 = (bf16[16,32,128]{2,1,0:T(8,128)(2,1)}, f32[1152,128]{1,0:T(8,128)S(1)}, f32[2,26,48,128]{3,2,1,0:T(8,128)S(1)}) custom-call(bf16[24,7,64,256]{3,2,1,0:T(8,128)(2,1)S(1)} %get-tuple-element.33.act3, f32[3,28,48,128]{3,2,1,0:T(8,128)S(1)} %get-tuple-element.34.prod, bf16[1792,512]{1,0:T(8,128)(2,1)S(1)} %get-tuple-element.35.w4_ref), custom_call_target="tpu_custom_call" | custom-call | flops 10000000000 | bytes 10000000 | tf_op jit(solution)/shard_map/layer_four/pallas_call | solution.py:682
  51.8 2.4 %solver_waves.1 = (f32[8,128]{1,0:T(8,128)S(1)}, f32[2,26,48,128]{3,2,1,0:T(8,128)S(1)}, f32[26,48,128]{2,1,0:T(8,128)S(1)}, bf16[3,4,32,128]{3,2,1,0:T(8,128)(2...) custom-call(f32[1152,128]{1,0:T(8,128)S(1)} %get-tuple-element.37.pr, ...), custom_call_target="tpu_custom_call" | custom-call | flops 100000000 | bytes 10000000 | tf_op jit(solution)/shard_map/solver_waves/pallas_call | solution.py:700
  54.2 1.6 %collective-permute-start.4 = (bf16[3,4,32,128]{3,2,1,0:T(8,128)(2,1)S(1)}, bf16[3,4,32,128]{3,2,1,0:T(8,128)(2,1)S(1)}, u32[]{:S(2)}, u32[]{:S(2)}) collective-permute-start(bf16[3,4,32,128]{3,2,1,0:T(8,128)(2,1)S(1)} %get-tuple-element.43), channel_id=1, source_target_pairs={{0,1},{1,2},{2,3},{3,0},{4,5},{5,6},{6,7},{7,4},{8,9},{9,10},{10,1... | collective-permute-start | bytes 294920 | tf_op jit(solution)/shard_map/ppermute | solution.py:725
  55.8 2.3 %collective-permute-start.5 = (bf16[3,4,32,128]{3,2,1,0:T(8,128)(2,1)S(1)}, bf16[3,4,32,128]{3,2,1,0:T(8,128)(2,1)S(1)}, u32[]{:S(2)}, u32[]{:S(2)}) collective-permute-start(bf16[3,4,32,128]{3,2,1,0:T(8,128)(2,1)S(1)} %get-tuple-element.44), channel_id=1, source_target_pairs={{0,2},{1,3},{2,0},{3,1},{4,6},{5,7},{6,4},{7,5},{8,10},{9,11},{10,... | collective-permute-start | bytes 294920 | tf_op jit(solution)/shard_map/ppermute | solution.py:725
  58.2 1.6 %collective-permute-start.6 = (bf16[3,4,32,128]{3,2,1,0:T(8,128)(2,1)S(1)}, bf16[3,4,32,128]{3,2,1,0:T(8,128)(2,1)S(1)}, u32[]{:S(2)}, u32[]{:S(2)}) collective-permute-start(bf16[3,4,32,128]{3,2,1,0:T(8,128)(2,1)S(1)} %get-tuple-element.45), channel_id=1, source_target_pairs={{0,3},{1,0},{2,1},{3,2},{4,7},{5,4},{6,5},{7,6},{8,11},{9,8},{10,9... | collective-permute-start | bytes 294920 | tf_op jit(solution)/shard_map/ppermute | solution.py:725
  59.8 0.6 last_moment.1
  60.3 12.8 %all_to_all.5.mom_ref = f32[32,1,128]{2,1,0:T(1,128)S(1)} all-to-all(f32[32,1,128]{2,1,0:T(1,128)S(1)} %last_moment.1), channel_id=1, replica_groups=mesh['gx'=8,'gy'=4] {'gx','gy'}, dimensions={0} | all-to-all | bytes 32768 | tf_op jit(solution)/shard_map/all_to_all | solution.py:736
  73.1 0.0 collective-permute-done.4.refs_1_
  73.1 0.0 collective-permute-done.5.refs_2_
  73.1 0.0 collective-permute-done.6.refs_3_
  73.2 0.9 %combine_waves.1 = f32[4,128,128]{2,1,0:T(8,128)} custom-call(f32[32,1,128]{2,1,0:T(1,128)S(1)} %all_to_all.5.mom_ref, bf16[3,4,32,128]{3,2,1,0:T(8,128)(2,1)S(1)} %get-tuple-element.42.refs_0_, bf16[3,4,32,128]{3,2,1,0:T(8,128)(2,1)S(1)} %collective-permute-done.4.refs_1_, bf16[3,4,32,128]{3,2,1,0:T(8,128)(2,1)S(1)} %collective-permute-done.5.refs_2_, ...), custom_call_target="tpu_custom_call" | custom-call | tf_op jit(solution)/shard_map/combine_waves/pallas_call | solution.py:737
  (4 shorter events, 0.0 us)
Async XLA Ops:
  1.5 5.2 %collective-permute-start.1 = (bf16[8,32,128]{2,1,0:T(8,128)(2,1)S(1)}, bf16[8,32,128]{2,1,0:T(8,128)(2,1)S(1)}, u32[]{:S(2)}, u32[]{:S(2)}) collective-permute-start(bf16[8,32,128]{2,1,0:T(8,128)(2,1)S(1)} %get-tuple-element.48), channel_id=1, source_target_pairs={{4,0},{8,4},{12,8},{16,12},{20,16},{24,20},{28,24},{5,1},{9,5},{13... | collective-permute-start | bytes 196616 | tf_op jit(solution)/shard_map/ppermute | solution.py:603
  2.8 3.9 %collective-permute-start = (bf16[8,32,128]{2,1,0:T(8,128)(2,1)S(1)}, bf16[8,32,128]{2,1,0:T(8,128)(2,1)S(1)}, u32[]{:S(2)}, u32[]{:S(2)}) collective-permute-start(bf16[8,32,128]{2,1,0:T(8,128)(2,1)S(1)} %get-tuple-element.49), channel_id=1, source_target_pairs={{0,4},{4,8},{8,12},{12,16},{16,20},{20,24},{24,28},{1,5},{5,9},{9,... | collective-permute-start | bytes 196616 | tf_op jit(solution)/shard_map/ppermute | solution.py:603
  6.8 10.3 %collective-permute-start.2 = (bf16[32,8,128]{2,1,0:T(8,128)(2,1)S(1)}, bf16[32,8,128]{2,1,0:T(8,128)(2,1)S(1)}, u32[]{:S(2)}, u32[]{:S(2)}) collective-permute-start(bf16[32,8,128]{2,1,0:T(8,128)(2,1)S(1)} %pad_maximum_fusion.1), channel_id=1, source_target_pairs={{0,1},{1,2},{2,3},{4,5},{5,6},{6,7},{8,9},{9,10},{10,11},{12,13},{... | collective-permute-start | bytes 196616 | tf_op jit(solution)/shard_map/ppermute | solution.py:603
  11.7 6.7 %copy-start = (bf16[16,32,128]{2,1,0:T(8,128)(2,1)S(1)}, bf16[16,32,128]{2,1,0:T(8,128)(2,1)}, u32[]{:S(2)}) copy-start(bf16[16,32,128]{2,1,0:T(8,128)(2,1)} %amp_ref.1) | copy-start | bytes 393220
  11.7 6.7 %collective-permute-start.3 = (bf16[32,8,128]{2,1,0:T(8,128)(2,1)S(1)}, bf16[32,8,128]{2,1,0:T(8,128)(2,1)S(1)}, u32[]{:S(2)}, u32[]{:S(2)}) collective-permute-start(bf16[32,8,128]{2,1,0:T(8,128)(2,1)S(1)} %pad_maximum_fusion.2), channel_id=1, source_target_pairs={{1,0},{2,1},{3,2},{5,4},{6,5},{7,6},{9,8},{10,9},{11,10},{13,12},{... | collective-permute-start | bytes 196616 | tf_op jit(solution)/shard_map/ppermute | solution.py:603
  54.2 18.9 %collective-permute-start.4 = (bf16[3,4,32,128]{3,2,1,0:T(8,128)(2,1)S(1)}, bf16[3,4,32,128]{3,2,1,0:T(8,128)(2,1)S(1)}, u32[]{:S(2)}, u32[]{:S(2)}) collective-permute-start(bf16[3,4,32,128]{3,2,1,0:T(8,128)(2,1)S(1)} %get-tuple-element.43), channel_id=1, source_target_pairs={{0,1},{1,2},{2,3},{3,0},{4,5},{5,6},{6,7},{7,4},{8,9},{9,10},{10,1... | collective-permute-start | bytes 294920 | tf_op jit(solution)/shard_map/ppermute | solution.py:725
  55.8 17.3 %collective-permute-start.5 = (bf16[3,4,32,128]{3,2,1,0:T(8,128)(2,1)S(1)}, bf16[3,4,32,128]{3,2,1,0:T(8,128)(2,1)S(1)}, u32[]{:S(2)}, u32[]{:S(2)}) collective-permute-start(bf16[3,4,32,128]{3,2,1,0:T(8,128)(2,1)S(1)} %get-tuple-element.44), channel_id=1, source_target_pairs={{0,2},{1,3},{2,0},{3,1},{4,6},{5,7},{6,4},{7,5},{8,10},{9,11},{10,... | collective-permute-start | bytes 294920 | tf_op jit(solution)/shard_map/ppermute | solution.py:725
  58.2 15.0 %collective-permute-start.6 = (bf16[3,4,32,128]{3,2,1,0:T(8,128)(2,1)S(1)}, bf16[3,4,32,128]{3,2,1,0:T(8,128)(2,1)S(1)}, u32[]{:S(2)}, u32[]{:S(2)}) collective-permute-start(bf16[3,4,32,128]{3,2,1,0:T(8,128)(2,1)S(1)} %get-tuple-element.45), channel_id=1, source_target_pairs={{0,3},{1,0},{2,1},{3,2},{4,7},{5,4},{6,5},{7,6},{8,11},{9,8},{10,9... | collective-permute-start | bytes 294920 | tf_op jit(solution)/shard_map/ppermute | solution.py:725

commit v10 on v9

--- a/solution.py
+++ b/solution.py
@@ -121,6 +121,14 @@
         w4_ref[blk * BLK : (blk + 1) * BLK, :] = turned.astype(BF16)
 
 
+def slices_kernel(amp_ref, first_x, last_x, first_y, last_y):
+    ty = amp_ref.shape[1]
+    first_x[...] = amp_ref[:H]
+    last_x[...] = amp_ref[TX - H :]
+    first_y[...] = amp_ref[:, :H]
+    last_y[...] = amp_ref[:, ty - H :]
+
+
 def input_cells():
     tiles = []
     here = [(t, x) for t in (0, 1) for x in range(4)]
@@ -178,30 +186,37 @@
     return jnp.where((at >= 0) & (at < grid_y), 1.0, 0.0)
 
 
+def lanes16():
+    return iota((PAIRS, 128), 1).astype(jnp.int16)
+
+
 def put(act, pair, blk, values):
     sub_row = iota((SUB, 128), 0)
-    place = iota((PAIRS, 128), 1) // CH
-    early = (place >= 2) & (place < 6)
-    act[0, pair, blk] = values.astype(BF16)
+    lane = lanes16()
+    early = (lane >= 32) & (lane < 96)
+    values = values.astype(BF16)
+    act[0, pair, blk] = values
     for half in range(2):
         turned = pltpu.roll(values[:, half * 128 : (half + 1) * 128], 96, 1)
-        head = jnp.where(sub_row == 0, 0.0, pltpu.roll(turned[PAIRS - SUB :], 1, 0))
-        tail = jnp.where(sub_row == SUB - 1, 0.0, pltpu.roll(turned[:SUB], SUB - 1, 0))
+        head = pltpu.roll(turned[PAIRS - SUB :].astype(F32), 1, 0)
+        head = jnp.where(sub_row == 0, 0.0, head).astype(BF16)
+        tail = pltpu.roll(turned[:SUB].astype(F32), SUB - 1, 0)
+        tail = jnp.where(sub_row == SUB - 1, 0.0, tail).astype(BF16)
         before = jnp.concatenate([head, turned[: PAIRS - SUB]], axis=0)
         after = jnp.concatenate([turned[SUB:], tail], axis=0)
-        both = jnp.where(early, before, after)
-        act[1, pair, blk, :, half * 128 : (half + 1) * 128] = both.astype(BF16)
+        act[1, pair, blk, :, half * 128 : (half + 1) * 128] = jnp.where(early, before, after)
 
 
 def put_sides(act, pair, blocks):
-    place = iota((PAIRS, 128), 1) // CH
+    lane = lanes16()
+    slot0, slot3, even_slot = (lane & 48) == 0, (lane & 48) == 48, (lane & 16) == 0
     for blk in range(EDGE):
         left, right = (blk - 1) % blocks, (blk + 1) % blocks
         for half in range(2):
             at = slice(half * 128, (half + 1) * 128)
-            even = jnp.where(place % 4 == 0, act[0, pair, right, :, at], act[1, pair, right, :, at])
-            odd = jnp.where(place % 4 == 3, act[0, pair, left, :, at], act[1, pair, left, :, at])
-            act[2, pair, blk, :, at] = jnp.where(place % 2 == 0, even, odd)
+            even = jnp.where(slot0, act[0, pair, right, :, at], act[1, pair, right, :, at])
+            odd = jnp.where(slot3, act[0, pair, left, :, at], act[1, pair, left, :, at])
+            act[2, pair, blk, :, at] = jnp.where(even_slot, even, odd)
 
 
 def layer(source, w_ref, pair, count):
@@ -281,7 +296,7 @@
             put_sides(act1, step * FIRST + i, EDGE + 1)
         return carry
 
-    lax.fori_loop(0, yw // 2 // FIRST, first, 0)
+    lax.fori_loop(0, yw // 2 // FIRST, first, 0, unroll=True)
 
 
 def second_kernel(grid_x, grid_y, ty, act1, w2_ref, act2):
@@ -400,7 +415,7 @@
             part[pair + i + 1] = share[:, 128:]
         return carry
 
-    lax.fori_loop(0, pairs1 // 8, fourth, 0)
+    lax.fori_loop(0, pairs1 // 8, fourth, 0, unroll=True)
 
     for x in range(FX):
         prob[x * yw : x * yw + H, :] = jnp.zeros((H, NT), F32)
@@ -425,7 +440,7 @@
             prob[at, :] = values[row * XW : row * XW + FX]
         return carry
 
-    lax.fori_loop(0, (ty + 8) // 4, order, 0, unroll=2)
+    lax.fori_loop(0, (ty + 8) // 4, order, 0, unroll=5)
 
     for which in range(2):
         slope[which, FX + 1] = jnp.zeros((yw, NT), F32)
@@ -602,17 +617,20 @@
         pairs = [(i, i + step) for i in range(count) if 0 <= i + step < count]
         return lax.ppermute(values, axis, pairs)
 
-    xlow = shift(amplitude[TX - H :], "gx", n_gx, 1)
-    xhigh = shift(amplitude[:H], "gx", n_gx, -1)
+    first_x, last_x, first_y, last_y = pl.pallas_call(
+        slices_kernel,
+        out_shape=[jax.ShapeDtypeStruct((H, ty, NT), BF16)] * 2
+        + [jax.ShapeDtypeStruct((TX, H, NT), BF16)] * 2,
+        in_specs=vmem(1),
+        out_specs=vmem(4),
+        name="halo_slices",
+    )(amplitude)
+    xlow = shift(last_x, "gx", n_gx, 1)
+    xhigh = shift(first_x, "gx", n_gx, -1)
     ylow = shift(
-        jnp.concatenate([xlow[:, ty - H :], amplitude[:, ty - H :], xhigh[:, ty - H :]]),
-        "gy",
-        n_gy,
-        1,
+        jnp.concatenate([xlow[:, ty - H :], last_y, xhigh[:, ty - H :]]), "gy", n_gy, 1
     )
-    yhigh = shift(
-        jnp.concatenate([xlow[:, :H], amplitude[:, :H], xhigh[:, :H]]), "gy", n_gy, -1
-    )
+    yhigh = shift(jnp.concatenate([xlow[:, :H], first_y, xhigh[:, :H]]), "gy", n_gy, -1)
 
     weights = (conv_first, conv_second, conv_third, conv_last)
     (conv_first, conv_second, conv_third, conv_last), _ = lax.optimization_barrier((weights, xlow))

time: 74.5 us -> 74.2 us (level)
  waiting for transfers between devices: 1.45 us -> 5.06 us
  starting transfers between devices: 16.3 us -> 14.3 us
  local copies, waits for them, and re-layouts: 1.68 us -> 0.02 us
  other arithmetic: 1.76 us -> 3.27 us
  blocking collectives: 12.8 us -> 11.3 us
    ppermute x4, waiting for transfers between devices: 1.44 us -> 5.06 us  [shift(): return lax.ppermute(values, axis, pairs)]
    ppermute x4, starting transfers between devices: 10.7 us -> 8.55 us  [shift(): return lax.ppermute(values, axis, pairs)]
    slice x2 -> x0, local copies, waits for them, and re-layouts: 1.67 us -> none  [the longest x1 0.88 us: on_device(): xhigh = shift(amplitude[:H], 'gx', n_gx, -1)]
    pallas_call x0 -> x1, Pallas kernels: none -> 1.58 us  [on_device(): pl.pallas_call(slices_kernel, out_shape=[jax.ShapeDtypeStruct((H, ty, NT)...]
    concatenate x2, other arithmetic: 0.02 us -> 1.54 us  [the longest x1 0.77 us: on_device(): jnp.concatenate([xlow[:, :H], first_y, xhigh[:, :H]])]
    all_to_all x1, blocking collectives: 12.8 us -> 11.3 us  [on_device(): lax.all_to_all(everyone, ('gx', 'gy'), split_axis=0, concat_axis=0, tiled...]
    pallas_call x1, Pallas kernels: 8.47 us -> 7.41 us  [on_device(): pl.pallas_call(functools.partial(first_kernel, grid_x, grid_y, ty), out_s...]
where the time goes in v10:
time: 74.2 us; the launch traced here: 73.7 us
  Pallas kernels  39 us (53%)
  starting transfers between devices  14.3 us (19%)
  blocking collectives  11.3 us (15%)
  waiting for transfers between devices  5.06 us (7%)
  other arithmetic  3.27 us (4%)
  between operations  0.76 us (1%)
    all_to_all x1, blocking collectives, on_device(): lax.all_to_all(everyone, ('gx', 'gy'), split_axis=0, concat_axis=0, tiled...  11.3 us
    pallas_call x1, Pallas kernels, on_device(): pl.pallas_call(functools.partial(second_kernel, grid_x, grid_y, ty), out_...  9.91 us
    pallas_call x1, Pallas kernels, on_device(): pl.pallas_call(functools.partial(third_kernel, grid_x, grid_y, ty), out_s...  8.55 us
    ppermute x4, starting transfers between devices, shift(): return lax.ppermute(values, axis, pairs)  8.55 us
    pallas_call x1, Pallas kernels, on_device(): pl.pallas_call(functools.partial(first_kernel, grid_x, grid_y, ty), out_s...  7.41 us
    ppermute x3, starting transfers between devices, on_device(): arrived.append(lax.ppermute(waves[place], 'gy', pairs))  5.74 us
    pallas_call x1, Pallas kernels, on_device(): pl.pallas_call(functools.partial(fourth_kernel, ty), out_shape=[jax.Shape...  5.52 us
    ppermute x4, waiting for transfers between devices, shift(): return lax.ppermute(values, axis, pairs)  5.06 us
  transfers between devices with their start and end apart: 7, of which 2 were waited for; matrix products, arithmetic and copies ran while one was open for 3% of the time, Pallas kernels for 4%

profile of v10, /device:TPU:0, one launch (start us, length us, event | category | flops | bytes accessed | tf_op | source)
XLA Modules:
  0.0 73.7 jit_solution(9169908224489441184)
XLA Ops:
  0.6 1.6 %halo_slices.1 = (bf16[8,32,128]{2,1,0:T(8,128)(2,1)}, bf16[8,32,128]{2,1,0:T(8,128)(2,1)}, bf16[16,8,128]{2,1,0:T(8,128)(2,1)}, bf16[16,8,128]{2,1,0:T(8,128)(2,1)}) custom-call(bf16[16,32,128]{2,1,0:T(8,128)(2,1)} %amp_ref.3), custom_call_target="tpu_custom_call" | custom-call | tf_op jit(solution)/shard_map/halo_slices/pallas_call | solution.py:620
  2.2 2.3 %collective-permute-start = (bf16[8,32,128]{2,1,0:T(8,128)(2,1)}, bf16[8,32,128]{2,1,0:T(8,128)(2,1)S(1)}, u32[]{:S(2)}, u32[]{:S(2)}) collective-permute-start(bf16[8,32,128]{2,1,0:T(8,128)(2,1)} %get-tuple-element.28), channel_id=1, source_target_pairs={{0,4},{4,8},{8,12},{12,16},{16,20},{20,24},{24,28},{1,5},{5,9},{9,... | collective-permute-start | bytes 196616 | tf_op jit(solution)/shard_map/ppermute | solution.py:618
  4.6 1.3 %collective-permute-start.1 = (bf16[8,32,128]{2,1,0:T(8,128)(2,1)}, bf16[8,32,128]{2,1,0:T(8,128)(2,1)S(1)}, u32[]{:S(2)}, u32[]{:S(2)}) collective-permute-start(bf16[8,32,128]{2,1,0:T(8,128)(2,1)} %get-tuple-element.29), channel_id=1, source_target_pairs={{4,0},{8,4},{12,8},{16,12},{20,16},{24,20},{28,24},{5,1},{9,5},{13... | collective-permute-start | bytes 196616 | tf_op jit(solution)/shard_map/ppermute | solution.py:618
  5.9 0.0 collective-permute-done.after_ref.xlow_ref
  5.9 4.1 %collective-permute-done.1.xhigh_ref = bf16[8,32,128]{2,1,0:T(8,128)(2,1)S(1)} collective-permute-done((bf16[8,32,128]{2,1,0:T(8,128)(2,1)}, bf16[8,32,128]{2,1,0:T(8,128)(2,1)S(1)}, u32[]{:S(2)}, u32[]{:S(2)}) %collective-permute-start.1) | collective-permute-done | bytes 65568 | tf_op jit(solution)/shard_map/ppermute | solution.py:618
  10.0 0.8 %pad_maximum_fusion.1 = bf16[32,8,128]{2,1,0:T(8,128)(2,1)S(1)} fusion(bf16[8,8,128]{2,1,0:T(8,128)(2,1)S(1)} %get-tuple-element.57, bf16[16,8,128]{2,1,0:T(8,128)(2,1)} %get-tuple-element.30, bf16[8,8,128]{2,1,0:T(8,128)(2,1)S(1)} %get-tuple-element.55), kind=kLoop, calls=%fused_computation.1 | loop fusion | flops 65536 | bytes 131072 | tf_op jit(solution)/shard_map/concatenate | solution.py:631
  10.8 3.5 %collective-permute-start.2 = (bf16[32,8,128]{2,1,0:T(8,128)(2,1)S(1)}, bf16[32,8,128]{2,1,0:T(8,128)(2,1)S(1)}, u32[]{:S(2)}, u32[]{:S(2)}) collective-permute-start(bf16[32,8,128]{2,1,0:T(8,128)(2,1)S(1)} %pad_maximum_fusion.1), channel_id=1, source_target_pairs={{0,1},{1,2},{2,3},{4,5},{5,6},{6,7},{8,9},{9,10},{10,11},{12,13},{... | collective-permute-start | bytes 196616 | tf_op jit(solution)/shard_map/ppermute | solution.py:618
  14.3 0.8 %pad_maximum_fusion.2 = bf16[32,8,128]{2,1,0:T(8,128)(2,1)S(1)} fusion(bf16[8,8,128]{2,1,0:T(8,128)(2,1)S(1)} %get-tuple-element.56, bf16[16,8,128]{2,1,0:T(8,128)(2,1)} %get-tuple-element.31, bf16[8,8,128]{2,1,0:T(8,128)(2,1)S(1)} %get-tuple-element.54), kind=kLoop, calls=%fused_computation.2 | loop fusion | flops 65536 | bytes 131072 | tf_op jit(solution)/shard_map/concatenate | solution.py:633
  15.1 0.0 copy-start
  15.1 1.4 %collective-permute-start.3 = (bf16[32,8,128]{2,1,0:T(8,128)(2,1)S(1)}, bf16[32,8,128]{2,1,0:T(8,128)(2,1)S(1)}, u32[]{:S(2)}, u32[]{:S(2)}) collective-permute-start(bf16[32,8,128]{2,1,0:T(8,128)(2,1)S(1)} %pad_maximum_fusion.2), channel_id=1, source_target_pairs={{1,0},{2,1},{3,2},{5,4},{6,5},{7,6},{9,8},{10,9},{11,10},{13,12},{... | collective-permute-start | bytes 196616 | tf_op jit(solution)/shard_map/ppermute | solution.py:618
  16.5 0.7 %pad_maximum_fusion.3.outer_ref = bf16[2,3,3,3,16]{4,3,2,1,0:T(4,128)(2,1)S(1)} fusion(bf16[1,3,3,3,16]{4,3,2,1,0:T(4,128)(2,1)} %bitcast.8, bf16[1,3,3,3,16]{4,3,2,1,0:T(4,128)(2,1)} %bitcast.9), kind=kLoop, calls=%fused_computation.3 | loop fusion | flops 864 | bytes 3456 | tf_op jit(solution)/shard_map/concatenate | solution.py:656
  17.3 1.0 %pad_maximum_fusion = bf16[6,3,3,16,16]{4,3,2,1,0:T(8,128)(2,1)S(1)} fusion(bf16[3,3,3,16,16]{4,3,2,1,0:T(8,128)(2,1)} %bitcast.6, bf16[3,3,3,16,16]{4,3,2,1,0:T(8,128)(2,1)} %bitcast.7), kind=kLoop, calls=%fused_computation | loop fusion | flops 13824 | bytes 55296 | tf_op jit(solution)/shard_map/concatenate | solution.py:655
  18.3 2.2 %band_weights.1 = (bf16[512,2048]{1,0:T(8,128)(2,1)S(1)}, bf16[1536,256]{1,0:T(8,128)(2,1)S(1)}, bf16[1536,256]{1,0:T(8,128)(2,1)S(1)}, bf16[1792,512]{1,0:T(8,128)(2,1)S(1)}) custom-call(bf16[864,16]{1,0:T(8,128)(2,1)S(1)} %bitcast.5, bf16[2,3,3,3,16]{4,3,2,1,0:T(4,128)(2,1)S(1)} %pad_maximum_fusion.3.outer_ref, ...), custom_call_target="tpu_custom_call" | custom-call | flops 1000000000 | bytes 10000000 | tf_op jit(solution)/shard_map/band_weights/pallas_call | solution.py:641
  20.4 0.0 collective-permute-done.2.ylow_ref
  20.5 0.9 %collective-permute-done.3.yhigh_ref = bf16[32,8,128]{2,1,0:T(8,128)(2,1)S(1)} collective-permute-done((bf16[32,8,128]{2,1,0:T(8,128)(2,1)S(1)}, bf16[32,8,128]{2,1,0:T(8,128)(2,1)S(1)}, u32[]{:S(2)}, u32[]{:S(2)}) %collective-permute-start.3) | collective-permute-done | bytes 65568 | tf_op jit(solution)/shard_map/ppermute | solution.py:618
  21.4 0.0 copy-done
  21.4 7.4 %layer_one.1 = (bf16[3,24,8,64,256]{4,3,2,1,0:T(8,128)(2,1)S(1)}, f32[1632,128]{1,0:T(8,128)S(1)}) custom-call(bf16[16,32,128]{2,1,0:T(8,128)(2,1)S(1)} %copy-done, bf16[8,32,128]{2,1,0:T(8,128)(2,1)S(1)} %collective-permute-done.after_ref.xlow_ref, bf16[8,32,128]{2,1,0:T(8,128)(2,1)S(1)} %collective-permute-done.1.xhigh_ref, ...), custom_call_target="tpu_custom_call" | custom-call | flops 10000000000 | bytes 10000000 | tf_op jit(solution)/shard_map/layer_one/pallas_call | solution.py:663
  28.8 9.9 %layer_two.1.act2 = bf16[3,24,7,64,256]{4,3,2,1,0:T(8,128)(2,1)S(1)} custom-call(bf16[3,24,8,64,256]{4,3,2,1,0:T(8,128)(2,1)S(1)} %get-tuple-element.37.act1, bf16[1536,256]{1,0:T(8,128)(2,1)S(1)} %get-tuple-element.38.w2_ref), custom_call_target="tpu_custom_call" | custom-call | flops 10000000000 | bytes 10000000 | tf_op jit(solution)/shard_map/layer_two/pallas_call | solution.py:677
  38.7 8.6 %layer_three.1 = (bf16[24,7,64,256]{3,2,1,0:T(8,128)(2,1)S(1)}, f32[3,28,48,128]{3,2,1,0:T(8,128)S(1)}) custom-call(bf16[3,24,7,64,256]{4,3,2,1,0:T(8,128)(2,1)S(1)} %layer_two.1.act2, f32[1632,128]{1,0:T(8,128)S(1)} %get-tuple-element.39.raw, bf16[1536,256]{1,0:T(8,128)(2,1)S(1)} %get-tuple-element.40.w3_ref), custom_call_target="tpu_custom_call" | custom-call | flops 10000000000 | bytes 10000000 | tf_op jit(solution)/shard_map/layer_three/pallas_call | solution.py:687
  47.3 5.5 %layer_four.1 = (bf16[16,32,128]{2,1,0:T(8,128)(2,1)}, f32[1152,128]{1,0:T(8,128)S(1)}, f32[2,26,48,128]{3,2,1,0:T(8,128)S(1)}) custom-call(bf16[24,7,64,256]{3,2,1,0:T(8,128)(2,1)S(1)} %get-tuple-element.41.act3, f32[3,28,48,128]{3,2,1,0:T(8,128)S(1)} %get-tuple-element.42.prod, bf16[1792,512]{1,0:T(8,128)(2,1)S(1)} %get-tuple-element.43.w4_ref), custom_call_target="tpu_custom_call" | custom-call | flops 10000000000 | bytes 10000000 | tf_op jit(solution)/shard_map/layer_four/pallas_call | solution.py:700
  52.8 2.4 %solver_waves.1 = (f32[8,128]{1,0:T(8,128)S(1)}, f32[2,26,48,128]{3,2,1,0:T(8,128)S(1)}, f32[26,48,128]{2,1,0:T(8,128)S(1)}, bf16[3,4,32,128]{3,2,1,0:T(8,128)(2...) custom-call(f32[1152,128]{1,0:T(8,128)S(1)} %get-tuple-element.45.pr, ...), custom_call_target="tpu_custom_call" | custom-call | flops 100000000 | bytes 10000000 | tf_op jit(solution)/shard_map/solver_waves/pallas_call | solution.py:718
  55.2 1.8 %collective-permute-start.4 = (bf16[3,4,32,128]{3,2,1,0:T(8,128)(2,1)S(1)}, bf16[3,4,32,128]{3,2,1,0:T(8,128)(2,1)S(1)}, u32[]{:S(2)}, u32[]{:S(2)}) collective-permute-start(bf16[3,4,32,128]{3,2,1,0:T(8,128)(2,1)S(1)} %get-tuple-element.51), channel_id=1, source_target_pairs={{0,1},{1,2},{2,3},{3,0},{4,5},{5,6},{6,7},{7,4},{8,9},{9,10},{10,1... | collective-permute-start | bytes 294920 | tf_op jit(solution)/shard_map/ppermute | solution.py:743
  57.0 2.6 %collective-permute-start.5 = (bf16[3,4,32,128]{3,2,1,0:T(8,128)(2,1)S(1)}, bf16[3,4,32,128]{3,2,1,0:T(8,128)(2,1)S(1)}, u32[]{:S(2)}, u32[]{:S(2)}) collective-permute-start(bf16[3,4,32,128]{3,2,1,0:T(8,128)(2,1)S(1)} %get-tuple-element.52), channel_id=1, source_target_pairs={{0,2},{1,3},{2,0},{3,1},{4,6},{5,7},{6,4},{7,5},{8,10},{9,11},{10,... | collective-permute-start | bytes 294920 | tf_op jit(solution)/shard_map/ppermute | solution.py:743
  59.6 1.3 %collective-permute-start.6 = (bf16[3,4,32,128]{3,2,1,0:T(8,128)(2,1)S(1)}, bf16[3,4,32,128]{3,2,1,0:T(8,128)(2,1)S(1)}, u32[]{:S(2)}, u32[]{:S(2)}) collective-permute-start(bf16[3,4,32,128]{3,2,1,0:T(8,128)(2,1)S(1)} %get-tuple-element.53), channel_id=1, source_target_pairs={{0,3},{1,0},{2,1},{3,2},{4,7},{5,4},{6,5},{7,6},{8,11},{9,8},{10,9... | collective-permute-start | bytes 294920 | tf_op jit(solution)/shard_map/ppermute | solution.py:743
  60.9 0.6 last_moment.1
  61.5 11.3 %all_to_all.5.mom_ref = f32[32,1,128]{2,1,0:T(1,128)S(1)} all-to-all(f32[32,1,128]{2,1,0:T(1,128)S(1)} %last_moment.1), channel_id=1, replica_groups=mesh['gx'=8,'gy'=4] {'gx','gy'}, dimensions={0} | all-to-all | bytes 32768 | tf_op jit(solution)/shard_map/all_to_all | solution.py:754
  72.8 0.0 collective-permute-done.4.refs_1_
  72.8 0.0 collective-permute-done.5.refs_2_
  72.8 0.0 collective-permute-done.6.refs_3_
  72.8 0.9 %combine_waves.1 = f32[4,128,128]{2,1,0:T(8,128)} custom-call(f32[32,1,128]{2,1,0:T(1,128)S(1)} %all_to_all.5.mom_ref, bf16[3,4,32,128]{3,2,1,0:T(8,128)(2,1)S(1)} %get-tuple-element.50.refs_0_, bf16[3,4,32,128]{3,2,1,0:T(8,128)(2,1)S(1)} %collective-permute-done.4.refs_1_, bf16[3,4,32,128]{3,2,1,0:T(8,128)(2,1)S(1)} %collective-permute-done.5.refs_2_, ...), custom_call_target="tpu_custom_call" | custom-call | tf_op jit(solution)/shard_map/combine_waves/pallas_call | solution.py:755
  (2 shorter events, 0.0 us)
Async XLA Ops:
  2.2 3.7 %collective-permute-start = (bf16[8,32,128]{2,1,0:T(8,128)(2,1)}, bf16[8,32,128]{2,1,0:T(8,128)(2,1)S(1)}, u32[]{:S(2)}, u32[]{:S(2)}) collective-permute-start(bf16[8,32,128]{2,1,0:T(8,128)(2,1)} %get-tuple-element.28), channel_id=1, source_target_pairs={{0,4},{4,8},{8,12},{12,16},{16,20},{20,24},{24,28},{1,5},{5,9},{9,... | collective-permute-start | bytes 196616 | tf_op jit(solution)/shard_map/ppermute | solution.py:618
  4.6 5.5 %collective-permute-start.1 = (bf16[8,32,128]{2,1,0:T(8,128)(2,1)}, bf16[8,32,128]{2,1,0:T(8,128)(2,1)S(1)}, u32[]{:S(2)}, u32[]{:S(2)}) collective-permute-start(bf16[8,32,128]{2,1,0:T(8,128)(2,1)} %get-tuple-element.29), channel_id=1, source_target_pairs={{4,0},{8,4},{12,8},{16,12},{20,16},{24,20},{28,24},{5,1},{9,5},{13... | collective-permute-start | bytes 196616 | tf_op jit(solution)/shard_map/ppermute | solution.py:618
  10.8 9.6 %collective-permute-start.2 = (bf16[32,8,128]{2,1,0:T(8,128)(2,1)S(1)}, bf16[32,8,128]{2,1,0:T(8,128)(2,1)S(1)}, u32[]{:S(2)}, u32[]{:S(2)}) collective-permute-start(bf16[32,8,128]{2,1,0:T(8,128)(2,1)S(1)} %pad_maximum_fusion.1), channel_id=1, source_target_pairs={{0,1},{1,2},{2,3},{4,5},{5,6},{6,7},{8,9},{9,10},{10,11},{12,13},{... | collective-permute-start | bytes 196616 | tf_op jit(solution)/shard_map/ppermute | solution.py:618
  15.1 6.3 %copy-start = (bf16[16,32,128]{2,1,0:T(8,128)(2,1)S(1)}, bf16[16,32,128]{2,1,0:T(8,128)(2,1)}, u32[]{:S(2)}) copy-start(bf16[16,32,128]{2,1,0:T(8,128)(2,1)} %amp_ref.3) | copy-start | bytes 393220
  15.1 6.3 %collective-permute-start.3 = (bf16[32,8,128]{2,1,0:T(8,128)(2,1)S(1)}, bf16[32,8,128]{2,1,0:T(8,128)(2,1)S(1)}, u32[]{:S(2)}, u32[]{:S(2)}) collective-permute-start(bf16[32,8,128]{2,1,0:T(8,128)(2,1)S(1)} %pad_maximum_fusion.2), channel_id=1, source_target_pairs={{1,0},{2,1},{3,2},{5,4},{6,5},{7,6},{9,8},{10,9},{11,10},{13,12},{... | collective-permute-start | bytes 196616 | tf_op jit(solution)/shard_map/ppermute | solution.py:618
  55.2 17.6 %collective-permute-start.4 = (bf16[3,4,32,128]{3,2,1,0:T(8,128)(2,1)S(1)}, bf16[3,4,32,128]{3,2,1,0:T(8,128)(2,1)S(1)}, u32[]{:S(2)}, u32[]{:S(2)}) collective-permute-start(bf16[3,4,32,128]{3,2,1,0:T(8,128)(2,1)S(1)} %get-tuple-element.51), channel_id=1, source_target_pairs={{0,1},{1,2},{2,3},{3,0},{4,5},{5,6},{6,7},{7,4},{8,9},{9,10},{10,1... | collective-permute-start | bytes 294920 | tf_op jit(solution)/shard_map/ppermute | solution.py:743
  57.0 15.8 %collective-permute-start.5 = (bf16[3,4,32,128]{3,2,1,0:T(8,128)(2,1)S(1)}, bf16[3,4,32,128]{3,2,1,0:T(8,128)(2,1)S(1)}, u32[]{:S(2)}, u32[]{:S(2)}) collective-permute-start(bf16[3,4,32,128]{3,2,1,0:T(8,128)(2,1)S(1)} %get-tuple-element.52), channel_id=1, source_target_pairs={{0,2},{1,3},{2,0},{3,1},{4,6},{5,7},{6,4},{7,5},{8,10},{9,11},{10,... | collective-permute-start | bytes 294920 | tf_op jit(solution)/shard_map/ppermute | solution.py:743
  59.6 13.2 %collective-permute-start.6 = (bf16[3,4,32,128]{3,2,1,0:T(8,128)(2,1)S(1)}, bf16[3,4,32,128]{3,2,1,0:T(8,128)(2,1)S(1)}, u32[]{:S(2)}, u32[]{:S(2)}) collective-permute-start(bf16[3,4,32,128]{3,2,1,0:T(8,128)(2,1)S(1)} %get-tuple-element.53), channel_id=1, source_target_pairs={{0,3},{1,0},{2,1},{3,2},{4,7},{5,4},{6,5},{7,6},{8,11},{9,8},{10,9... | collective-permute-start | bytes 294920 | tf_op jit(solution)/shard_map/ppermute | solution.py:743

commit v11 on v10

--- a/solution.py
+++ b/solution.py
@@ -276,12 +276,13 @@
 
     def first(step, carry):
         pieces = []
-        for i in range(FIRST):
-            rows = amp[pl.ds((step * FIRST + i) * 2, 4)].reshape(4 * XW, NT)
-            turned = dot_nt(to_pairs, rows).astype(BF16)
-            pieces.append(
-                jnp.concatenate([turned[j * PAIRS : (j + 1) * PAIRS] for j in range(4)], axis=1)
-            )
+        for i in range(0, FIRST, 2):
+            y = (step * FIRST + i) * 2
+            rows = [amp[pl.ds(y + 2 * k, 4)].reshape(4 * XW, NT) for k in range(2)]
+            turned = dot_nt(to_pairs, jnp.concatenate(rows, axis=0)).astype(BF16)
+            for k in range(2):
+                parts = [turned[j * PAIRS : (j + 1) * PAIRS, k * 128 : (k + 1) * 128] for j in range(4)]
+                pieces.append(jnp.concatenate(parts, axis=1))
         pieces = jnp.concatenate(pieces, axis=0)
         for begin in range(0, EDGE + 1, 2):
             result = dot(pieces, w1_ref[:, begin * BLK : (begin + 2) * BLK])
@@ -575,6 +576,12 @@
     values = jnp.sum(values, axis=0, keepdims=True)
     for device in range(out_ref.shape[0]):
         out_ref[device] = values
+
+
+def sum_kernel(mom_ref, out_ref):
+    total = jnp.sum(mom_ref[...], axis=0)
+    for device in range(out_ref.shape[0]):
+        out_ref[device] = total
 
 
 def combine_kernel(n_gy, ty, mom_ref, *refs):
@@ -623,6 +630,7 @@
         + [jax.ShapeDtypeStruct((TX, H, NT), BF16)] * 2,
         in_specs=vmem(1),
         out_specs=vmem(4),
+        compiler_params=pltpu.CompilerParams(vmem_limit_bytes=4 * 2**20),
         name="halo_slices",
     )(amplitude)
     xlow = shift(last_x, "gx", n_gx, 1)
@@ -744,14 +752,23 @@
 
     everyone = pl.pallas_call(
         functools.partial(last_kernel, ty),
-        out_shape=jax.ShapeDtypeStruct((n_gx * n_gy, 1, NT), F32),
+        out_shape=jax.ShapeDtypeStruct((n_gx, 1, NT), F32),
         in_specs=vmem(3),
         out_specs=pl.BlockSpec(memory_space=pltpu.VMEM),
         compiler_params=pltpu.CompilerParams(vmem_limit_bytes=16 * 2**20),
         cost_estimate=pl.CostEstimate(flops=10**9, bytes_accessed=10**8, transcendentals=0),
         name="last_moment",
     )(moments, face, wave2)
-    moments = lax.all_to_all(everyone, ("gx", "gy"), split_axis=0, concat_axis=0, tiled=True)
+    moments = lax.all_to_all(everyone, "gx", split_axis=0, concat_axis=0, tiled=True)
+    moments = pl.pallas_call(
+        sum_kernel,
+        out_shape=jax.ShapeDtypeStruct((n_gy, 1, NT), F32),
+        in_specs=vmem(1),
+        out_specs=pl.BlockSpec(memory_space=pltpu.VMEM),
+        compiler_params=pltpu.CompilerParams(vmem_limit_bytes=4 * 2**20),
+        name="sum_moments",
+    )(moments)
+    moments = lax.all_to_all(moments, "gy", split_axis=0, concat_axis=0, tiled=True)
     shift_field = pl.pallas_call(
         functools.partial(combine_kernel, n_gy, ty),
         out_shape=jax.ShapeDtypeStruct((rows, grid_y, NT), F32),

time: 74.2 us -> 77.6 us (1.046)
  blocking collectives: 11.3 us -> 17.4 us
  Pallas kernels: 39 us -> 37.2 us
  other arithmetic: 3.27 us -> 1.76 us
  local copies, waits for them, and re-layouts: 0.02 us -> 0.91 us
    all_to_all x1 -> x2, blocking collectives: 11.3 us -> 17.4 us  [the longest x1 9.49 us: on_device(): lax.all_to_all(everyone, 'gx', split_axis=0, concat_axis=0, tiled=True)]
    pallas_call x1, Pallas kernels: 1.58 us -> 0.02 us  [on_device(): pl.pallas_call(slices_kernel, out_shape=[jax.ShapeDtypeStruct((H, ty, NT)...]
    unnamed x2 -> x4, local copies, waits for them, and re-layouts: 0.01 us -> 0.91 us
  transfers between devices with their start and end apart: 7 -> 7, of which waited for: 2 -> 2; matrix products, arithmetic and copies ran while one was open for 3% -> 2% of each run, Pallas kernels for 4% -> 4%
where the time goes in v11:
time: 77.6 us; the launch traced here: 77.2 us
  Pallas kernels  37.2 us (48%)
  blocking collectives  17.4 us (22%)
  starting transfers between devices  14.3 us (18%)
  waiting for transfers between devices  4.86 us (6%)
  other arithmetic  1.76 us (2%)
  local copies, waits for them, and re-layouts  0.91 us (1%)
    pallas_call x1, Pallas kernels, on_device(): pl.pallas_call(functools.partial(second_kernel, grid_x, grid_y, ty), out_...  9.91 us
    all_to_all x1, blocking collectives, on_device(): lax.all_to_all(everyone, 'gx', split_axis=0, concat_axis=0, tiled=True)  9.49 us
    ppermute x4, starting transfers between devices, shift(): return lax.ppermute(values, axis, pairs)  8.56 us
    pallas_call x1, Pallas kernels, on_device(): pl.pallas_call(functools.partial(third_kernel, grid_x, grid_y, ty), out_s...  8.52 us
    all_to_all x1, blocking collectives, on_device(): lax.all_to_all(moments, 'gy', split_axis=0, concat_axis=0, tiled=True)  7.88 us
    pallas_call x1, Pallas kernels, on_device(): pl.pallas_call(functools.partial(first_kernel, grid_x, grid_y, ty), out_s...  7.26 us
    ppermute x3, starting transfers between devices, on_device(): arrived.append(lax.ppermute(waves[place], 'gy', pairs))  5.72 us
    pallas_call x1, Pallas kernels, on_device(): pl.pallas_call(functools.partial(fourth_kernel, ty), out_shape=[jax.Shape...  5.53 us
  transfers between devices with their start and end apart: 7, of which 2 were waited for; matrix products, arithmetic and copies ran while one was open for 2% of the time, Pallas kernels for 4%

profile of v11, /device:TPU:0, one launch (start us, length us, event | category | flops | bytes accessed | tf_op | source)
XLA Modules:
  0.0 77.2 jit_solution(2440777767428694517)
XLA Ops:
  0.6 0.0 copy-start
  0.6 0.9 %copy-done = bf16[16,32,128]{2,1,0:T(8,128)(2,1)S(1)} copy-done((bf16[16,32,128]{2,1,0:T(8,128)(2,1)S(1)}, bf16[16,32,128]{2,1,0:T(8,128)(2,1)}, u32[]{:S(2)}) %copy-start) | copy-done | bytes 131096
  1.6 2.4 %collective-permute-start = (bf16[8,32,128]{2,1,0:T(8,128)(2,1)S(1)}, bf16[8,32,128]{2,1,0:T(8,128)(2,1)S(1)}, u32[]{:S(2)}, u32[]{:S(2)}) collective-permute-start(bf16[8,32,128]{2,1,0:T(8,128)(2,1)S(1)} %get-tuple-element.28), channel_id=1, source_target_pairs={{0,4},{4,8},{8,12},{12,16},{16,20},{20,24},{24,28},{1,5},{5,9},{9,... | collective-permute-start | bytes 196616 | tf_op jit(solution)/shard_map/ppermute | solution.py:625
  3.9 1.3 %collective-permute-start.1 = (bf16[8,32,128]{2,1,0:T(8,128)(2,1)S(1)}, bf16[8,32,128]{2,1,0:T(8,128)(2,1)S(1)}, u32[]{:S(2)}, u32[]{:S(2)}) collective-permute-start(bf16[8,32,128]{2,1,0:T(8,128)(2,1)S(1)} %get-tuple-element.29), channel_id=1, source_target_pairs={{4,0},{8,4},{12,8},{16,12},{20,16},{24,20},{28,24},{5,1},{9,5},{13... | collective-permute-start | bytes 196616 | tf_op jit(solution)/shard_map/ppermute | solution.py:625
  5.2 0.0 collective-permute-done.after_ref.xlow_ref
  5.3 3.9 %collective-permute-done.1.xhigh_ref = bf16[8,32,128]{2,1,0:T(8,128)(2,1)S(1)} collective-permute-done((bf16[8,32,128]{2,1,0:T(8,128)(2,1)S(1)}, bf16[8,32,128]{2,1,0:T(8,128)(2,1)S(1)}, u32[]{:S(2)}, u32[]{:S(2)}) %collective-permute-start.1) | collective-permute-done | bytes 65568 | tf_op jit(solution)/shard_map/ppermute | solution.py:625
  9.2 3.5 %collective-permute-start.2 = (bf16[32,8,128]{2,1,0:T(8,128)(2,1)S(1)}, bf16[32,8,128]{2,1,0:T(8,128)(2,1)S(1)}, u32[]{:S(2)}, u32[]{:S(2)}) collective-permute-start(bf16[32,8,128]{2,1,0:T(8,128)(2,1)S(1)} %pad_maximum_fusion.1), channel_id=1, source_target_pairs={{0,1},{1,2},{2,3},{4,5},{5,6},{6,7},{8,9},{9,10},{10,11},{12,13},{... | collective-permute-start | bytes 196616 | tf_op jit(solution)/shard_map/ppermute | solution.py:625
  12.7 0.0 copy-start.1
  12.7 1.4 %collective-permute-start.3 = (bf16[32,8,128]{2,1,0:T(8,128)(2,1)S(1)}, bf16[32,8,128]{2,1,0:T(8,128)(2,1)S(1)}, u32[]{:S(2)}, u32[]{:S(2)}) collective-permute-start(bf16[32,8,128]{2,1,0:T(8,128)(2,1)S(1)} %pad_maximum_fusion.2), channel_id=1, source_target_pairs={{1,0},{2,1},{3,2},{5,4},{6,5},{7,6},{9,8},{10,9},{11,10},{13,12},{... | collective-permute-start | bytes 196616 | tf_op jit(solution)/shard_map/ppermute | solution.py:625
  14.2 0.7 pad_maximum_fusion.3.outer_ref
  14.9 1.0 %pad_maximum_fusion = bf16[6,3,3,16,16]{4,3,2,1,0:T(8,128)(2,1)S(1)} fusion(bf16[3,3,3,16,16]{4,3,2,1,0:T(8,128)(2,1)} %bitcast.6, bf16[3,3,3,16,16]{4,3,2,1,0:T(8,128)(2,1)} %bitcast.7), kind=kLoop, calls=%fused_computation | loop fusion | flops 13824 | bytes 55296 | tf_op jit(solution)/shard_map/concatenate | solution.py:663
  15.9 2.2 %band_weights.1 = (bf16[512,2048]{1,0:T(8,128)(2,1)S(1)}, bf16[1536,256]{1,0:T(8,128)(2,1)S(1)}, bf16[1536,256]{1,0:T(8,128)(2,1)S(1)}, bf16[1792,512]{1,0:T(8,128)(2,1)S(1)}) custom-call(bf16[864,16]{1,0:T(8,128)(2,1)S(1)} %bitcast.5, bf16[2,3,3,3,16]{4,3,2,1,0:T(4,128)(2,1)S(1)} %pad_maximum_fusion.3.outer_ref, ...), custom_call_target="tpu_custom_call" | custom-call | flops 1000000000 | bytes 10000000 | tf_op jit(solution)/shard_map/band_weights/pallas_call | solution.py:649
  18.1 0.0 collective-permute-done.2.ylow_ref
  18.1 0.9 %collective-permute-done.3.yhigh_ref = bf16[32,8,128]{2,1,0:T(8,128)(2,1)S(1)} collective-permute-done((bf16[32,8,128]{2,1,0:T(8,128)(2,1)S(1)}, bf16[32,8,128]{2,1,0:T(8,128)(2,1)S(1)}, u32[]{:S(2)}, u32[]{:S(2)}) %collective-permute-start.3) | collective-permute-done | bytes 65568 | tf_op jit(solution)/shard_map/ppermute | solution.py:625
  19.0 0.0 copy-done.1
  19.0 7.3 %layer_one.1 = (bf16[3,24,8,64,256]{4,3,2,1,0:T(8,128)(2,1)S(1)}, f32[1632,128]{1,0:T(8,128)S(1)}) custom-call(bf16[16,32,128]{2,1,0:T(8,128)(2,1)S(1)} %copy-done.1, bf16[8,32,128]{2,1,0:T(8,128)(2,1)S(1)} %collective-permute-done.after_ref.xlow_ref, bf16[8,32,128]{2,1,0:T(8,128)(2,1)S(1)} %collective-permute-done.1.xhigh_ref, ...), custom_call_target="tpu_custom_call" | custom-call | flops 10000000000 | bytes 10000000 | tf_op jit(solution)/shard_map/layer_one/pallas_call | solution.py:671
  26.3 9.9 %layer_two.1.act2 = bf16[3,24,7,64,256]{4,3,2,1,0:T(8,128)(2,1)S(1)} custom-call(bf16[3,24,8,64,256]{4,3,2,1,0:T(8,128)(2,1)S(1)} %get-tuple-element.37.act1, bf16[1536,256]{1,0:T(8,128)(2,1)S(1)} %get-tuple-element.38.w2_ref), custom_call_target="tpu_custom_call" | custom-call | flops 10000000000 | bytes 10000000 | tf_op jit(solution)/shard_map/layer_two/pallas_call | solution.py:685
  36.2 8.5 %layer_three.1 = (bf16[24,7,64,256]{3,2,1,0:T(8,128)(2,1)S(1)}, f32[3,28,48,128]{3,2,1,0:T(8,128)S(1)}) custom-call(bf16[3,24,7,64,256]{4,3,2,1,0:T(8,128)(2,1)S(1)} %layer_two.1.act2, f32[1632,128]{1,0:T(8,128)S(1)} %get-tuple-element.39.raw, bf16[1536,256]{1,0:T(8,128)(2,1)S(1)} %get-tuple-element.40.w3_ref), custom_call_target="tpu_custom_call" | custom-call | flops 10000000000 | bytes 10000000 | tf_op jit(solution)/shard_map/layer_three/pallas_call | solution.py:695
  44.7 5.5 %layer_four.1 = (bf16[16,32,128]{2,1,0:T(8,128)(2,1)}, f32[1152,128]{1,0:T(8,128)S(1)}, f32[2,26,48,128]{3,2,1,0:T(8,128)S(1)}) custom-call(bf16[24,7,64,256]{3,2,1,0:T(8,128)(2,1)S(1)} %get-tuple-element.41.act3, f32[3,28,48,128]{3,2,1,0:T(8,128)S(1)} %get-tuple-element.42.prod, bf16[1792,512]{1,0:T(8,128)(2,1)S(1)} %get-tuple-element.43.w4_ref), custom_call_target="tpu_custom_call" | custom-call | flops 10000000000 | bytes 10000000 | tf_op jit(solution)/shard_map/layer_four/pallas_call | solution.py:708
  50.2 2.4 %solver_waves.1 = (f32[8,128]{1,0:T(8,128)S(1)}, f32[2,26,48,128]{3,2,1,0:T(8,128)S(1)}, f32[26,48,128]{2,1,0:T(8,128)S(1)}, bf16[3,4,32,128]{3,2,1,0:T(8,128)(2...) custom-call(f32[1152,128]{1,0:T(8,128)S(1)} %get-tuple-element.45.pr, ...), custom_call_target="tpu_custom_call" | custom-call | flops 100000000 | bytes 10000000 | tf_op jit(solution)/shard_map/solver_waves/pallas_call | solution.py:726
  52.6 1.8 %collective-permute-start.4 = (bf16[3,4,32,128]{3,2,1,0:T(8,128)(2,1)S(1)}, bf16[3,4,32,128]{3,2,1,0:T(8,128)(2,1)S(1)}, u32[]{:S(2)}, u32[]{:S(2)}) collective-permute-start(bf16[3,4,32,128]{3,2,1,0:T(8,128)(2,1)S(1)} %get-tuple-element.51), channel_id=1, source_target_pairs={{0,1},{1,2},{2,3},{3,0},{4,5},{5,6},{6,7},{7,4},{8,9},{9,10},{10,1... | collective-permute-start | bytes 294920 | tf_op jit(solution)/shard_map/ppermute | solution.py:751
  54.4 2.6 %collective-permute-start.5 = (bf16[3,4,32,128]{3,2,1,0:T(8,128)(2,1)S(1)}, bf16[3,4,32,128]{3,2,1,0:T(8,128)(2,1)S(1)}, u32[]{:S(2)}, u32[]{:S(2)}) collective-permute-start(bf16[3,4,32,128]{3,2,1,0:T(8,128)(2,1)S(1)} %get-tuple-element.52), channel_id=1, source_target_pairs={{0,2},{1,3},{2,0},{3,1},{4,6},{5,7},{6,4},{7,5},{8,10},{9,11},{10,... | collective-permute-start | bytes 294920 | tf_op jit(solution)/shard_map/ppermute | solution.py:751
  57.0 1.3 %collective-permute-start.6 = (bf16[3,4,32,128]{3,2,1,0:T(8,128)(2,1)S(1)}, bf16[3,4,32,128]{3,2,1,0:T(8,128)(2,1)S(1)}, u32[]{:S(2)}, u32[]{:S(2)}) collective-permute-start(bf16[3,4,32,128]{3,2,1,0:T(8,128)(2,1)S(1)} %get-tuple-element.53), channel_id=1, source_target_pairs={{0,3},{1,0},{2,1},{3,2},{4,7},{5,4},{6,5},{7,6},{8,11},{9,8},{10,9... | collective-permute-start | bytes 294920 | tf_op jit(solution)/shard_map/ppermute | solution.py:751
  58.4 0.6 last_moment.1
  58.9 9.5 %all_to_all.10.mom_ref = f32[8,1,128]{2,1,0:T(1,128)S(1)} all-to-all(f32[8,1,128]{2,1,0:T(1,128)S(1)} %last_moment.1), channel_id=1, replica_groups=mesh['gx'=8,'gy'=4] {'gx'}, dimensions={0} | all-to-all | bytes 8192 | tf_op jit(solution)/shard_map/all_to_all | solution.py:762
  68.4 7.9 %all_to_all.11.mom_ref = f32[4,1,128]{2,1,0:T(1,128)S(1)} all-to-all(f32[4,1,128]{2,1,0:T(1,128)S(1)} %sum_moments.1), channel_id=1, replica_groups=mesh['gx'=8,'gy'=4] {'gy'}, dimensions={0} | all-to-all | bytes 4096 | tf_op jit(solution)/shard_map/all_to_all | solution.py:771
  76.3 0.0 collective-permute-done.4.refs_1_
  76.3 0.0 collective-permute-done.5.refs_2_
  76.3 0.0 collective-permute-done.6.refs_3_
  76.3 0.9 %combine_waves.1 = f32[4,128,128]{2,1,0:T(8,128)} custom-call(f32[4,1,128]{2,1,0:T(1,128)S(1)} %all_to_all.11.mom_ref, bf16[3,4,32,128]{3,2,1,0:T(8,128)(2,1)S(1)} %get-tuple-element.50.refs_0_, bf16[3,4,32,128]{3,2,1,0:T(8,128)(2,1)S(1)} %collective-permute-done.4.refs_1_, bf16[3,4,32,128]{3,2,1,0:T(8,128)(2,1)S(1)} %collective-permute-done.5.refs_2_, ...), custom_call_target="tpu_custom_call" | custom-call | tf_op jit(solution)/shard_map/combine_waves/pallas_call | solution.py:772
  (6 shorter events, 0.1 us)
Async XLA Ops:
  0.6 0.9 %copy-start = (bf16[16,32,128]{2,1,0:T(8,128)(2,1)S(1)}, bf16[16,32,128]{2,1,0:T(8,128)(2,1)}, u32[]{:S(2)}) copy-start(bf16[16,32,128]{2,1,0:T(8,128)(2,1)} %amp_ref.3) | copy-start | bytes 393220
  1.6 3.7 %collective-permute-start = (bf16[8,32,128]{2,1,0:T(8,128)(2,1)S(1)}, bf16[8,32,128]{2,1,0:T(8,128)(2,1)S(1)}, u32[]{:S(2)}, u32[]{:S(2)}) collective-permute-start(bf16[8,32,128]{2,1,0:T(8,128)(2,1)S(1)} %get-tuple-element.28), channel_id=1, source_target_pairs={{0,4},{4,8},{8,12},{12,16},{16,20},{20,24},{24,28},{1,5},{5,9},{9,... | collective-permute-start | bytes 196616 | tf_op jit(solution)/shard_map/ppermute | solution.py:625
  3.9 5.3 %collective-permute-start.1 = (bf16[8,32,128]{2,1,0:T(8,128)(2,1)S(1)}, bf16[8,32,128]{2,1,0:T(8,128)(2,1)S(1)}, u32[]{:S(2)}, u32[]{:S(2)}) collective-permute-start(bf16[8,32,128]{2,1,0:T(8,128)(2,1)S(1)} %get-tuple-element.29), channel_id=1, source_target_pairs={{4,0},{8,4},{12,8},{16,12},{20,16},{24,20},{28,24},{5,1},{9,5},{13... | collective-permute-start | bytes 196616 | tf_op jit(solution)/shard_map/ppermute | solution.py:625
  9.2 8.9 %collective-permute-start.2 = (bf16[32,8,128]{2,1,0:T(8,128)(2,1)S(1)}, bf16[32,8,128]{2,1,0:T(8,128)(2,1)S(1)}, u32[]{:S(2)}, u32[]{:S(2)}) collective-permute-start(bf16[32,8,128]{2,1,0:T(8,128)(2,1)S(1)} %pad_maximum_fusion.1), channel_id=1, source_target_pairs={{0,1},{1,2},{2,3},{4,5},{5,6},{6,7},{8,9},{9,10},{10,11},{12,13},{... | collective-permute-start | bytes 196616 | tf_op jit(solution)/shard_map/ppermute | solution.py:625
  12.7 6.3 %copy-start.1 = (bf16[16,32,128]{2,1,0:T(8,128)(2,1)S(1)}, bf16[16,32,128]{2,1,0:T(8,128)(2,1)}, u32[]{:S(2)}) copy-start(bf16[16,32,128]{2,1,0:T(8,128)(2,1)} %amp_ref.3) | copy-start | bytes 393220
  12.7 6.3 %collective-permute-start.3 = (bf16[32,8,128]{2,1,0:T(8,128)(2,1)S(1)}, bf16[32,8,128]{2,1,0:T(8,128)(2,1)S(1)}, u32[]{:S(2)}, u32[]{:S(2)}) collective-permute-start(bf16[32,8,128]{2,1,0:T(8,128)(2,1)S(1)} %pad_maximum_fusion.2), channel_id=1, source_target_pairs={{1,0},{2,1},{3,2},{5,4},{6,5},{7,6},{9,8},{10,9},{11,10},{13,12},{... | collective-permute-start | bytes 196616 | tf_op jit(solution)/shard_map/ppermute | solution.py:625
  52.6 23.7 %collective-permute-start.4 = (bf16[3,4,32,128]{3,2,1,0:T(8,128)(2,1)S(1)}, bf16[3,4,32,128]{3,2,1,0:T(8,128)(2,1)S(1)}, u32[]{:S(2)}, u32[]{:S(2)}) collective-permute-start(bf16[3,4,32,128]{3,2,1,0:T(8,128)(2,1)S(1)} %get-tuple-element.51), channel_id=1, source_target_pairs={{0,1},{1,2},{2,3},{3,0},{4,5},{5,6},{6,7},{7,4},{8,9},{9,10},{10,1... | collective-permute-start | bytes 294920 | tf_op jit(solution)/shard_map/ppermute | solution.py:751
  54.4 21.9 %collective-permute-start.5 = (bf16[3,4,32,128]{3,2,1,0:T(8,128)(2,1)S(1)}, bf16[3,4,32,128]{3,2,1,0:T(8,128)(2,1)S(1)}, u32[]{:S(2)}, u32[]{:S(2)}) collective-permute-start(bf16[3,4,32,128]{3,2,1,0:T(8,128)(2,1)S(1)} %get-tuple-element.52), channel_id=1, source_target_pairs={{0,2},{1,3},{2,0},{3,1},{4,6},{5,7},{6,4},{7,5},{8,10},{9,11},{10,... | collective-permute-start | bytes 294920 | tf_op jit(solution)/shard_map/ppermute | solution.py:751
  57.0 19.3 %collective-permute-start.6 = (bf16[3,4,32,128]{3,2,1,0:T(8,128)(2,1)S(1)}, bf16[3,4,32,128]{3,2,1,0:T(8,128)(2,1)S(1)}, u32[]{:S(2)}, u32[]{:S(2)}) collective-permute-start(bf16[3,4,32,128]{3,2,1,0:T(8,128)(2,1)S(1)} %get-tuple-element.53), channel_id=1, source_target_pairs={{0,3},{1,0},{2,1},{3,2},{4,7},{5,4},{6,5},{7,6},{8,11},{9,8},{10,9... | collective-permute-start | bytes 294920 | tf_op jit(solution)/shard_map/ppermute | solution.py:751

commit v12 on v10

--- a/solution.py
+++ b/solution.py
@@ -15,7 +15,8 @@
 XW = TX + 2 * H
 FX = TX + 8
 RX = 4
-FIRST, SECOND, THIRD = 8, 11, 11
+FIRST = 4
+RING = 12
 Y_SLOTS = (1, 2, 3, 0)
 LIMIT = 6
 GROUP = 2
@@ -220,17 +221,22 @@
 
 
 def layer(source, w_ref, pair, count):
-    size = count * EDGE * PAIRS
+    def rows(kind, offset, at):
+        found = []
+        for i in range(count):
+            place = (pair + offset + i) % RING
+            found.append(source[kind, place, :EDGE, :, at].reshape(EDGE * PAIRS, -1))
+        return jnp.concatenate(found, axis=0)
+
     tiles = []
     for kind in range(3):
-        centre = source[kind, pl.ds(pair + 1, count), :EDGE].reshape(size, BLK)
-        before = source[kind, pl.ds(pair, count), :EDGE, :, 128:].reshape(size, 128)
-        after = source[kind, pl.ds(pair + 2, count), :EDGE, :, :128].reshape(size, 128)
-        tiles += [centre, before, after]
+        tiles.append(rows(kind, 1, slice(0, BLK)))
+        tiles.append(rows(kind, 0, slice(128, BLK)))
+        tiles.append(rows(kind, 2, slice(0, 128)))
     return dot(jnp.concatenate(tiles, axis=1), w_ref[...])
 
 
-def first_kernel(
+def net_kernel(
     grid_x,
     grid_y,
     ty,
@@ -240,14 +246,19 @@
     ylow_ref,
     yhigh_ref,
     w1_ref,
-    act1,
+    w2_ref,
+    w3_ref,
+    act3,
+    prod,
     raw,
     amp,
+    act1,
+    act2,
 ):
     x0 = lax.axis_index("gx") * TX
     y0 = lax.axis_index("gy") * ty
     yw = ty + 2 * H
-
+    pairs1, pairs2 = yw // 2, ty // 2 + 6
     for x in range(XW):
         row = x * yw
         if x < H:
@@ -272,16 +283,17 @@
     to_pairs = jnp.where(
         iota((4 * PAIRS, NT), 1) == 2 * pair_of(at_row % PAIRS) - 1 + at_row // PAIRS, 1.0, 0.0
     ).astype(BF16)
-    mask1 = lane_masks(x0, grid_x, EDGE + 1)
-
-    def first(step, carry):
+    mask = lane_masks(x0, grid_x, EDGE + 1)
+
+    def first(step):
         pieces = []
-        for i in range(FIRST):
-            rows = amp[pl.ds((step * FIRST + i) * 2, 4)].reshape(4 * XW, NT)
-            turned = dot_nt(to_pairs, rows).astype(BF16)
-            pieces.append(
-                jnp.concatenate([turned[j * PAIRS : (j + 1) * PAIRS] for j in range(4)], axis=1)
-            )
+        for i in range(0, FIRST, 2):
+            y = (step * FIRST + i) * 2
+            rows = [amp[pl.ds(y + 2 * k, 4)].reshape(4 * XW, NT) for k in range(2)]
+            turned = dot_nt(to_pairs, jnp.concatenate(rows, axis=0)).astype(BF16)
+            for k in range(2):
+                parts = [turned[j * PAIRS : (j + 1) * PAIRS, k * 128 : (k + 1) * 128] for j in range(4)]
+                pieces.append(jnp.concatenate(parts, axis=1))
         pieces = jnp.concatenate(pieces, axis=0)
         for begin in range(0, EDGE + 1, 2):
             result = dot(pieces, w1_ref[:, begin * BLK : (begin + 2) * BLK])
@@ -291,47 +303,33 @@
                 for blk in (begin, begin + 1):
                     lane = (blk - begin) * BLK
                     values = result[i * PAIRS : (i + 1) * PAIRS, lane : lane + BLK]
-                    put(act1, pair, blk, jnp.maximum(values, 0.0) * (mask1[blk] * inside))
+                    put(act1, pair % RING, blk, jnp.maximum(values, 0.0) * (mask[blk] * inside))
         for i in range(FIRST):
-            put_sides(act1, step * FIRST + i, EDGE + 1)
-        return carry
-
-    lax.fori_loop(0, yw // 2 // FIRST, first, 0, unroll=True)
-
-
-def second_kernel(grid_x, grid_y, ty, act1, w2_ref, act2):
-    x0 = lax.axis_index("gx") * TX
-    y0 = lax.axis_index("gy") * ty
-    yw = ty + 2 * H
-    pairs2 = ty // 2 + 6
-    steps2 = pairs2 // SECOND
-    mask2 = lane_masks(x0, grid_x, EDGE)
-
-    def second(step, carry):
-        for begin in range(0, SECOND, GROUP):
-            count = min(GROUP, SECOND - begin)
-            result = layer(act1, w2_ref, step * SECOND + begin, count)
-            for i in range(count):
-                pair = step * SECOND + begin + i
-                inside = row_mask(y0 + 2 * pair - 6, grid_y)
-                for blk in range(EDGE):
-                    at = (i * EDGE + blk) * PAIRS
-                    values = jnp.maximum(result[at : at + PAIRS], 0.0)
-                    put(act2, pair + 1, blk, values * (mask2[blk] * inside))
-                put_sides(act2, pair + 1, EDGE)
-        return carry
-
-    for edge in (0, pairs2 + 1):
-        for kind in range(3):
-            act2[kind, edge] = jnp.zeros((EDGE, PAIRS, BLK), BF16)
-    lax.fori_loop(0, steps2, second, 0)
-
-
-def third_kernel(grid_x, grid_y, ty, act2, raw, w3_ref, act3, prod):
-    x0 = lax.axis_index("gx") * TX
-    y0 = lax.axis_index("gy") * ty
-    yw = ty + 2 * H
-    pairs1, pairs2 = yw // 2, ty // 2 + 6
+            put_sides(act1, (step * FIRST + i) % RING, EDGE + 1)
+
+    def second(begin, end):
+        count = end - begin
+        result = layer(act1, w2_ref, begin, count)
+        for i in range(count):
+            pair = begin + i
+            inside = row_mask(y0 + 2 * pair - 6, grid_y)
+            for blk in range(EDGE):
+                at = (i * EDGE + blk) * PAIRS
+                values = jnp.maximum(result[at : at + PAIRS], 0.0)
+                put(act2, (pair + 1) % RING, blk, values * (mask[blk] * inside))
+            put_sides(act2, (pair + 1) % RING, EDGE)
+
+    def third(begin, end):
+        count = end - begin
+        result = layer(act2, w3_ref, begin, count)
+        for i in range(count):
+            pair = begin + i
+            inside = row_mask(y0 + 2 * pair - 6, grid_y)
+            for blk in range(EDGE):
+                at = (i * EDGE + blk) * PAIRS
+                values = jnp.maximum(result[at : at + PAIRS], 0.0)
+                act3[pair, blk] = (values * (mask[blk] * inside)).astype(BF16)
+
     block, up_y, down_y, up_t, down_t = plane_shifts(yw)
 
     def smooth_yt(v, edge=0.0):
@@ -352,28 +350,36 @@
         energy = grad_t * grad_t + 0.25 * (grad_x * grad_x + grad_y * grad_y)
         prod[2, at] = smooth_yt(energy, 0.25 * here * here)
 
-    steps3 = pairs2 // THIRD
-    blocks3 = -(-(FX // RX + 1) // steps3)
-    mask2 = lane_masks(x0, grid_x, EDGE)
-
-    def third(step, carry):
-        for i in range(blocks3):
-            products(jnp.minimum((step * blocks3 + i) * RX, FX))
-        for begin in range(0, THIRD, GROUP):
-            count = min(GROUP, THIRD - begin)
-            result = layer(act2, w3_ref, step * THIRD + begin, count)
-            for i in range(count):
-                pair = step * THIRD + begin + i
-                inside = row_mask(y0 + 2 * pair - 6, grid_y)
-                for blk in range(EDGE):
-                    at = (i * EDGE + blk) * PAIRS
-                    values = jnp.maximum(result[at : at + PAIRS], 0.0)
-                    act3[pair, blk] = (values * (mask2[blk] * inside)).astype(BF16)
-        return carry
-
-    lax.fori_loop(0, steps3, third, 0)
+    def outside(edge):
+        for kind in range(3):
+            act2[kind, edge % RING] = jnp.zeros((EDGE, PAIRS, BLK), BF16)
+
+    outside(0)
     for pair in range(pairs2, pairs1):
         act3[pair] = jnp.zeros((EDGE, PAIRS, BLK), BF16)
+
+    chunks = pairs1 // FIRST
+    done2 = done3 = done_slopes = 0
+    for stage in range(chunks + 2):
+        end2 = min(pairs2, stage * FIRST - 2) if stage else 0
+        end3 = pairs2 if stage == chunks + 1 else max(0, done2 - 1)
+        if stage == chunks:
+            outside(pairs2 + 1)
+        work = []
+        for end, done, run in ((end3, done3, third), (end2, done2, second)):
+            steps = range(done, end, GROUP)
+            work.append([functools.partial(run, at, min(at + GROUP, end)) for at in steps])
+        if stage < chunks:
+            work.append([functools.partial(first, stage)])
+        if stage and done_slopes <= FX:
+            work.append([functools.partial(products, done_slopes)])
+            done_slopes += RX
+        for turn_of in range(max(len(w) for w in work)):
+            for w in work:
+                if turn_of < len(w):
+                    w[turn_of]()
+        done2, done3 = max(done2, end2), max(done3, end3)
+    assert done2 == done3 == pairs2 and done_slopes > FX
 
 
 def fourth_kernel(ty, act3, prod, w4_ref, fault_ref, prob, slope, part):
@@ -623,17 +629,18 @@
         + [jax.ShapeDtypeStruct((TX, H, NT), BF16)] * 2,
         in_specs=vmem(1),
         out_specs=vmem(4),
+        compiler_params=pltpu.CompilerParams(vmem_limit_bytes=4 * 2**20),
         name="halo_slices",
     )(amplitude)
+    xhigh = shift(first_x, "gx", n_gx, -1)
     xlow = shift(last_x, "gx", n_gx, 1)
-    xhigh = shift(first_x, "gx", n_gx, -1)
     ylow = shift(
         jnp.concatenate([xlow[:, ty - H :], last_y, xhigh[:, ty - H :]]), "gy", n_gy, 1
     )
     yhigh = shift(jnp.concatenate([xlow[:, :H], first_y, xhigh[:, :H]]), "gy", n_gy, -1)
 
     weights = (conv_first, conv_second, conv_third, conv_last)
-    (conv_first, conv_second, conv_third, conv_last), _ = lax.optimization_barrier((weights, xlow))
+    (conv_first, conv_second, conv_third, conv_last), _ = lax.optimization_barrier((weights, xhigh))
 
     def taps_first(weight):
         return jnp.transpose(weight, (2, 3, 4, 0, 1))
@@ -656,46 +663,28 @@
         jnp.concatenate(
             [jnp.transpose(conv_first, (1, 2, 3, 4, 0)), jnp.transpose(conv_last, (0, 2, 3, 4, 1))]
         ),
-        xlow,
+        xhigh,
     )
 
     yw, nf = ty + 2 * H, FX + 2
-    act1, raw = pl.pallas_call(
-        functools.partial(first_kernel, grid_x, grid_y, ty),
-        out_shape=[
-            jax.ShapeDtypeStruct((3, yw // 2, EDGE + 1, PAIRS, BLK), BF16),
-            jax.ShapeDtypeStruct(((XW + 2) * yw, NT), F32),
-        ],
-        in_specs=vmem(6),
-        out_specs=vmem(2),
-        scratch_shapes=[pltpu.VMEM((yw + 2, XW, NT), BF16)],
-        compiler_params=pltpu.CompilerParams(vmem_limit_bytes=LIMIT * 2**20),
-        cost_estimate=pl.CostEstimate(flops=10**10, bytes_accessed=10**7, transcendentals=0),
-        name="layer_one",
-    )(amplitude, xlow, xhigh, ylow, yhigh, w1)
-
-    act2 = pl.pallas_call(
-        functools.partial(second_kernel, grid_x, grid_y, ty),
-        out_shape=jax.ShapeDtypeStruct((3, yw // 2, EDGE, PAIRS, BLK), BF16),
-        in_specs=vmem(2),
-        out_specs=pl.BlockSpec(memory_space=pltpu.VMEM),
-        compiler_params=pltpu.CompilerParams(vmem_limit_bytes=LIMIT * 2**20),
-        cost_estimate=pl.CostEstimate(flops=10**10, bytes_accessed=10**7, transcendentals=0),
-        name="layer_two",
-    )(act1, w2)
-
     act3, prod = pl.pallas_call(
-        functools.partial(third_kernel, grid_x, grid_y, ty),
+        functools.partial(net_kernel, grid_x, grid_y, ty),
         out_shape=[
             jax.ShapeDtypeStruct((yw // 2, EDGE, PAIRS, BLK), BF16),
             jax.ShapeDtypeStruct((3, FX + 4, yw, NT), F32),
         ],
-        in_specs=vmem(3),
+        in_specs=vmem(8),
         out_specs=vmem(2),
-        compiler_params=pltpu.CompilerParams(vmem_limit_bytes=LIMIT * 2**20),
-        cost_estimate=pl.CostEstimate(flops=10**10, bytes_accessed=10**7, transcendentals=0),
-        name="layer_three",
-    )(act2, raw, w3)
+        scratch_shapes=[
+            pltpu.VMEM(((XW + 2) * yw, NT), F32),
+            pltpu.VMEM((yw + 2, XW, NT), BF16),
+            pltpu.VMEM((3, RING, EDGE + 1, PAIRS, BLK), BF16),
+            pltpu.VMEM((3, RING, EDGE, PAIRS, BLK), BF16),
+        ],
+        compiler_params=pltpu.CompilerParams(vmem_limit_bytes=28 * 2**20),
+        cost_estimate=pl.CostEstimate(flops=3 * 10**10, bytes_accessed=10**7, transcendentals=0),
+        name="layers_one_to_three",
+    )(amplitude, xlow, xhigh, ylow, yhigh, w1, w2, w3)
 
     fault, prob, slope = pl.pallas_call(
         functools.partial(fourth_kernel, ty),

time: 74.2 us -> 68.7 us (0.926)
  Pallas kernels: 39 us -> 33.8 us
  waiting for transfers between devices: 5.06 us -> 2.14 us
  starting transfers between devices: 14.3 us -> 16.1 us
  blocking collectives: 11.3 us -> 12.8 us
  other arithmetic: 3.27 us -> 1.8 us
  local copies, waits for them, and re-layouts: 0.02 us -> 0.91 us
    pallas_call x3 -> x1, Pallas kernels: 25.9 us -> 22.2 us  [on_device(): pl.pallas_call(functools.partial(net_kernel, grid_x, grid_y, ty), out_sha...]
    ppermute x4, waiting for transfers between devices: 5.06 us -> 2.14 us  [shift(): return lax.ppermute(values, axis, pairs)]
    ppermute x4, starting transfers between devices: 8.55 us -> 10.5 us  [shift(): return lax.ppermute(values, axis, pairs)]
    pallas_call x1, Pallas kernels: 1.58 us -> 0.02 us  [on_device(): pl.pallas_call(slices_kernel, out_shape=[jax.ShapeDtypeStruct((H, ty, NT)...]
    all_to_all x1, blocking collectives: 11.3 us -> 12.8 us  [on_device(): lax.all_to_all(everyone, ('gx', 'gy'), split_axis=0, concat_axis=0, tiled...]
    unnamed x2 -> x4, local copies, waits for them, and re-layouts: 0.01 us -> 0.91 us
    concatenate x1, other arithmetic: 0.77 us -> 0.01 us  [on_device(): jnp.concatenate([xlow[:, :H], first_y, xhigh[:, :H]])]
    concatenate x1, other arithmetic: 0.77 us -> 0.01 us  [on_device(): jnp.concatenate([xlow[:, ty - H:], last_y, xhigh[:, ty - H:]])]
where the time goes in v12:
time: 68.7 us; the launch traced here: 68.3 us
  Pallas kernels  33.8 us (49%)
  starting transfers between devices  16.1 us (23%)
  blocking collectives  12.8 us (19%)
  waiting for transfers between devices  2.14 us (3%)
  other arithmetic  1.8 us (3%)
  local copies, waits for them, and re-layouts  0.91 us (1%)
  between operations  0.75 us (1%)
    pallas_call x1, Pallas kernels, on_device(): pl.pallas_call(functools.partial(net_kernel, grid_x, grid_y, ty), out_sha...  22.2 us
    all_to_all x1, blocking collectives, on_device(): lax.all_to_all(everyone, ('gx', 'gy'), split_axis=0, concat_axis=0, tiled...  12.8 us
    ppermute x4, starting transfers between devices, shift(): return lax.ppermute(values, axis, pairs)  10.5 us
    ppermute x3, starting transfers between devices, on_device(): arrived.append(lax.ppermute(waves[place], 'gy', pairs))  5.57 us
    pallas_call x1, Pallas kernels, on_device(): pl.pallas_call(functools.partial(fourth_kernel, ty), out_shape=[jax.Shape...  5.52 us
    pallas_call x1, Pallas kernels, on_device(): pl.pallas_call(functools.partial(waves_kernel, grid_x, grid_y, ty), out_s...  2.39 us
    pallas_call x1, Pallas kernels, on_device(): pl.pallas_call(prep_kernel, out_shape=[jax.ShapeDtypeStruct((16 * XW, (ED...  2.19 us
    ppermute x4, waiting for transfers between devices, shift(): return lax.ppermute(values, axis, pairs)  2.14 us
  transfers between devices with their start and end apart: 7, of which 2 were waited for; matrix products, arithmetic and copies ran while one was open for 3% of the time, Pallas kernels for 4%

profile of v12, /device:TPU:0, one launch (start us, length us, event | category | flops | bytes accessed | tf_op | source)
XLA Modules:
  0.0 68.3 jit_solution(16976976098079602899)
XLA Ops:
  0.6 0.0 copy-start
  0.6 0.9 %copy-done = bf16[16,32,128]{2,1,0:T(8,128)(2,1)S(1)} copy-done((bf16[16,32,128]{2,1,0:T(8,128)(2,1)S(1)}, bf16[16,32,128]{2,1,0:T(8,128)(2,1)}, u32[]{:S(2)}) %copy-start) | copy-done | bytes 131096
  1.6 1.3 %collective-permute-start.1 = (bf16[8,32,128]{2,1,0:T(8,128)(2,1)S(1)}, bf16[8,32,128]{2,1,0:T(8,128)(2,1)S(1)}, u32[]{:S(2)}, u32[]{:S(2)}) collective-permute-start(bf16[8,32,128]{2,1,0:T(8,128)(2,1)S(1)} %get-tuple-element.27), channel_id=1, source_target_pairs={{4,0},{8,4},{12,8},{16,12},{20,16},{24,20},{28,24},{5,1},{9,5},{13... | collective-permute-start | bytes 196616 | tf_op jit(solution)/shard_map/ppermute | solution.py:624
  2.9 3.0 %collective-permute-start = (bf16[8,32,128]{2,1,0:T(8,128)(2,1)S(1)}, bf16[8,32,128]{2,1,0:T(8,128)(2,1)S(1)}, u32[]{:S(2)}, u32[]{:S(2)}) collective-permute-start(bf16[8,32,128]{2,1,0:T(8,128)(2,1)S(1)} %get-tuple-element.26), channel_id=1, source_target_pairs={{0,4},{4,8},{8,12},{12,16},{16,20},{20,24},{24,28},{1,5},{5,9},{9,... | collective-permute-start | bytes 196616 | tf_op jit(solution)/shard_map/ppermute | solution.py:624
  5.9 0.0 collective-permute-done.1.after_ref.xhigh_ref
  5.9 0.9 %collective-permute-done.xlow_ref = bf16[8,32,128]{2,1,0:T(8,128)(2,1)S(1)} collective-permute-done((bf16[8,32,128]{2,1,0:T(8,128)(2,1)S(1)}, bf16[8,32,128]{2,1,0:T(8,128)(2,1)S(1)}, u32[]{:S(2)}, u32[]{:S(2)}) %collective-permute-start) | collective-permute-done | bytes 65568 | tf_op jit(solution)/shard_map/ppermute | solution.py:624
  6.8 4.9 %collective-permute-start.2 = (bf16[32,8,128]{2,1,0:T(8,128)(2,1)S(1)}, bf16[32,8,128]{2,1,0:T(8,128)(2,1)S(1)}, u32[]{:S(2)}, u32[]{:S(2)}) collective-permute-start(bf16[32,8,128]{2,1,0:T(8,128)(2,1)S(1)} %pad_maximum_fusion.1), channel_id=1, source_target_pairs={{0,1},{1,2},{2,3},{4,5},{5,6},{6,7},{8,9},{9,10},{10,11},{12,13},{... | collective-permute-start | bytes 196616 | tf_op jit(solution)/shard_map/ppermute | solution.py:624
  11.8 1.3 %collective-permute-start.3 = (bf16[32,8,128]{2,1,0:T(8,128)(2,1)S(1)}, bf16[32,8,128]{2,1,0:T(8,128)(2,1)S(1)}, u32[]{:S(2)}, u32[]{:S(2)}) collective-permute-start(bf16[32,8,128]{2,1,0:T(8,128)(2,1)S(1)} %pad_maximum_fusion.2), channel_id=1, source_target_pairs={{1,0},{2,1},{3,2},{5,4},{6,5},{7,6},{9,8},{10,9},{11,10},{13,12},{... | collective-permute-start | bytes 196616 | tf_op jit(solution)/shard_map/ppermute | solution.py:624
  13.1 0.7 %pad_maximum_fusion.3.outer_ref = bf16[2,3,3,3,16]{4,3,2,1,0:T(4,128)(2,1)S(1)} fusion(bf16[1,3,3,3,16]{4,3,2,1,0:T(4,128)(2,1)} %bitcast.8, bf16[1,3,3,3,16]{4,3,2,1,0:T(4,128)(2,1)} %bitcast.9), kind=kLoop, calls=%fused_computation.3 | loop fusion | flops 864 | bytes 3456 | tf_op jit(solution)/shard_map/concatenate | solution.py:663
  13.8 0.0 copy-start.1
  13.8 1.0 %pad_maximum_fusion = bf16[6,3,3,16,16]{4,3,2,1,0:T(8,128)(2,1)S(1)} fusion(bf16[3,3,3,16,16]{4,3,2,1,0:T(8,128)(2,1)} %bitcast.6, bf16[3,3,3,16,16]{4,3,2,1,0:T(8,128)(2,1)} %bitcast.7), kind=kLoop, calls=%fused_computation | loop fusion | flops 13824 | bytes 55296 | tf_op jit(solution)/shard_map/concatenate | solution.py:662
  14.8 2.2 %band_weights.1 = (bf16[512,2048]{1,0:T(8,128)(2,1)S(1)}, bf16[1536,256]{1,0:T(8,128)(2,1)S(1)}, bf16[1536,256]{1,0:T(8,128)(2,1)S(1)}, bf16[1792,512]{1,0:T(8,128)(2,1)S(1)}) custom-call(bf16[864,16]{1,0:T(8,128)(2,1)S(1)} %bitcast.5, bf16[2,3,3,3,16]{4,3,2,1,0:T(4,128)(2,1)S(1)} %pad_maximum_fusion.3.outer_ref, ...), custom_call_target="tpu_custom_call" | custom-call | flops 1000000000 | bytes 10000000 | tf_op jit(solution)/shard_map/band_weights/pallas_call | solution.py:648
  17.0 0.0 collective-permute-done.2.ylow_ref
  17.1 1.3 %collective-permute-done.3.yhigh_ref = bf16[32,8,128]{2,1,0:T(8,128)(2,1)S(1)} collective-permute-done((bf16[32,8,128]{2,1,0:T(8,128)(2,1)S(1)}, bf16[32,8,128]{2,1,0:T(8,128)(2,1)S(1)}, u32[]{:S(2)}, u32[]{:S(2)}) %collective-permute-start.3) | collective-permute-done | bytes 65568 | tf_op jit(solution)/shard_map/ppermute | solution.py:624
  18.3 0.0 copy-done.1
  18.3 22.2 %layers_one_to_three.1 = (bf16[24,7,64,256]{3,2,1,0:T(8,128)(2,1)S(1)}, f32[3,28,48,128]{3,2,1,0:T(8,128)S(1)}) custom-call(bf16[16,32,128]{2,1,0:T(8,128)(2,1)S(1)} %copy-done.1, bf16[8,32,128]{2,1,0:T(8,128)(2,1)S(1)} %collective-permute-done.xlow_ref, bf16[8,32,128]{2,1,0:T(8,128)(2,1)S(1)} %collective-permute-done.1.after_ref.xhigh_ref, ...), custom_call_target="tpu_custom_call" | custom-call | flops 30000001024 | bytes 10000000 | tf_op jit(solution)/shard_map/layers_one_to_three/pallas_call | solution.py:670
  40.5 5.5 %layer_four.1 = (bf16[16,32,128]{2,1,0:T(8,128)(2,1)}, f32[1152,128]{1,0:T(8,128)S(1)}, f32[2,26,48,128]{3,2,1,0:T(8,128)S(1)}) custom-call(bf16[24,7,64,256]{3,2,1,0:T(8,128)(2,1)S(1)} %get-tuple-element.37.act3, f32[3,28,48,128]{3,2,1,0:T(8,128)S(1)} %get-tuple-element.38.prod, bf16[1792,512]{1,0:T(8,128)(2,1)S(1)} %get-tuple-element.39.w4_ref), custom_call_target="tpu_custom_call" | custom-call | flops 10000000000 | bytes 10000000 | tf_op jit(solution)/shard_map/layer_four/pallas_call | solution.py:689
  46.0 2.4 %solver_waves.1 = (f32[8,128]{1,0:T(8,128)S(1)}, f32[2,26,48,128]{3,2,1,0:T(8,128)S(1)}, f32[26,48,128]{2,1,0:T(8,128)S(1)}, bf16[3,4,32,128]{3,2,1,0:T(8,128)(2...) custom-call(f32[1152,128]{1,0:T(8,128)S(1)} %get-tuple-element.41.pr, ...), custom_call_target="tpu_custom_call" | custom-call | flops 100000000 | bytes 10000000 | tf_op jit(solution)/shard_map/solver_waves/pallas_call | solution.py:707
  48.4 1.6 %collective-permute-start.4 = (bf16[3,4,32,128]{3,2,1,0:T(8,128)(2,1)S(1)}, bf16[3,4,32,128]{3,2,1,0:T(8,128)(2,1)S(1)}, u32[]{:S(2)}, u32[]{:S(2)}) collective-permute-start(bf16[3,4,32,128]{3,2,1,0:T(8,128)(2,1)S(1)} %get-tuple-element.47), channel_id=1, source_target_pairs={{0,1},{1,2},{2,3},{3,0},{4,5},{5,6},{6,7},{7,4},{8,9},{9,10},{10,1... | collective-permute-start | bytes 294920 | tf_op jit(solution)/shard_map/ppermute | solution.py:732
  50.1 2.4 %collective-permute-start.5 = (bf16[3,4,32,128]{3,2,1,0:T(8,128)(2,1)S(1)}, bf16[3,4,32,128]{3,2,1,0:T(8,128)(2,1)S(1)}, u32[]{:S(2)}, u32[]{:S(2)}) collective-permute-start(bf16[3,4,32,128]{3,2,1,0:T(8,128)(2,1)S(1)} %get-tuple-element.48), channel_id=1, source_target_pairs={{0,2},{1,3},{2,0},{3,1},{4,6},{5,7},{6,4},{7,5},{8,10},{9,11},{10,... | collective-permute-start | bytes 294920 | tf_op jit(solution)/shard_map/ppermute | solution.py:732
  52.5 1.6 %collective-permute-start.6 = (bf16[3,4,32,128]{3,2,1,0:T(8,128)(2,1)S(1)}, bf16[3,4,32,128]{3,2,1,0:T(8,128)(2,1)S(1)}, u32[]{:S(2)}, u32[]{:S(2)}) collective-permute-start(bf16[3,4,32,128]{3,2,1,0:T(8,128)(2,1)S(1)} %get-tuple-element.49), channel_id=1, source_target_pairs={{0,3},{1,0},{2,1},{3,2},{4,7},{5,4},{6,5},{7,6},{8,11},{9,8},{10,9... | collective-permute-start | bytes 294920 | tf_op jit(solution)/shard_map/ppermute | solution.py:732
  54.0 0.6 last_moment.1
  54.6 12.8 %all_to_all.5.mom_ref = f32[32,1,128]{2,1,0:T(1,128)S(1)} all-to-all(f32[32,1,128]{2,1,0:T(1,128)S(1)} %last_moment.1), channel_id=1, replica_groups=mesh['gx'=8,'gy'=4] {'gx','gy'}, dimensions={0} | all-to-all | bytes 32768 | tf_op jit(solution)/shard_map/all_to_all | solution.py:743
  67.4 0.0 collective-permute-done.4.refs_1_
  67.4 0.0 collective-permute-done.5.refs_2_
  67.4 0.0 collective-permute-done.6.refs_3_
  67.4 0.9 %combine_waves.1 = f32[4,128,128]{2,1,0:T(8,128)} custom-call(f32[32,1,128]{2,1,0:T(1,128)S(1)} %all_to_all.5.mom_ref, bf16[3,4,32,128]{3,2,1,0:T(8,128)(2,1)S(1)} %get-tuple-element.46.refs_0_, bf16[3,4,32,128]{3,2,1,0:T(8,128)(2,1)S(1)} %collective-permute-done.4.refs_1_, bf16[3,4,32,128]{3,2,1,0:T(8,128)(2,1)S(1)} %collective-permute-done.5.refs_2_, ...), custom_call_target="tpu_custom_call" | custom-call | tf_op jit(solution)/shard_map/combine_waves/pallas_call | solution.py:744
  (5 shorter events, 0.1 us)
Async XLA Ops:
  0.6 0.9 %copy-start = (bf16[16,32,128]{2,1,0:T(8,128)(2,1)S(1)}, bf16[16,32,128]{2,1,0:T(8,128)(2,1)}, u32[]{:S(2)}) copy-start(bf16[16,32,128]{2,1,0:T(8,128)(2,1)} %amp_ref.3) | copy-start | bytes 393220
  1.6 4.3 %collective-permute-start.1 = (bf16[8,32,128]{2,1,0:T(8,128)(2,1)S(1)}, bf16[8,32,128]{2,1,0:T(8,128)(2,1)S(1)}, u32[]{:S(2)}, u32[]{:S(2)}) collective-permute-start(bf16[8,32,128]{2,1,0:T(8,128)(2,1)S(1)} %get-tuple-element.27), channel_id=1, source_target_pairs={{4,0},{8,4},{12,8},{16,12},{20,16},{24,20},{28,24},{5,1},{9,5},{13... | collective-permute-start | bytes 196616 | tf_op jit(solution)/shard_map/ppermute | solution.py:624
  2.9 3.9 %collective-permute-start = (bf16[8,32,128]{2,1,0:T(8,128)(2,1)S(1)}, bf16[8,32,128]{2,1,0:T(8,128)(2,1)S(1)}, u32[]{:S(2)}, u32[]{:S(2)}) collective-permute-start(bf16[8,32,128]{2,1,0:T(8,128)(2,1)S(1)} %get-tuple-element.26), channel_id=1, source_target_pairs={{0,4},{4,8},{8,12},{12,16},{16,20},{20,24},{24,28},{1,5},{5,9},{9,... | collective-permute-start | bytes 196616 | tf_op jit(solution)/shard_map/ppermute | solution.py:624
  6.8 10.2 %collective-permute-start.2 = (bf16[32,8,128]{2,1,0:T(8,128)(2,1)S(1)}, bf16[32,8,128]{2,1,0:T(8,128)(2,1)S(1)}, u32[]{:S(2)}, u32[]{:S(2)}) collective-permute-start(bf16[32,8,128]{2,1,0:T(8,128)(2,1)S(1)} %pad_maximum_fusion.1), channel_id=1, source_target_pairs={{0,1},{1,2},{2,3},{4,5},{5,6},{6,7},{8,9},{9,10},{10,11},{12,13},{... | collective-permute-start | bytes 196616 | tf_op jit(solution)/shard_map/ppermute | solution.py:624
  11.8 6.6 %collective-permute-start.3 = (bf16[32,8,128]{2,1,0:T(8,128)(2,1)S(1)}, bf16[32,8,128]{2,1,0:T(8,128)(2,1)S(1)}, u32[]{:S(2)}, u32[]{:S(2)}) collective-permute-start(bf16[32,8,128]{2,1,0:T(8,128)(2,1)S(1)} %pad_maximum_fusion.2), channel_id=1, source_target_pairs={{1,0},{2,1},{3,2},{5,4},{6,5},{7,6},{9,8},{10,9},{11,10},{13,12},{... | collective-permute-start | bytes 196616 | tf_op jit(solution)/shard_map/ppermute | solution.py:624
  13.8 4.5 %copy-start.1 = (bf16[16,32,128]{2,1,0:T(8,128)(2,1)S(1)}, bf16[16,32,128]{2,1,0:T(8,128)(2,1)}, u32[]{:S(2)}) copy-start(bf16[16,32,128]{2,1,0:T(8,128)(2,1)} %amp_ref.3) | copy-start | bytes 393220
  48.4 19.0 %collective-permute-start.4 = (bf16[3,4,32,128]{3,2,1,0:T(8,128)(2,1)S(1)}, bf16[3,4,32,128]{3,2,1,0:T(8,128)(2,1)S(1)}, u32[]{:S(2)}, u32[]{:S(2)}) collective-permute-start(bf16[3,4,32,128]{3,2,1,0:T(8,128)(2,1)S(1)} %get-tuple-element.47), channel_id=1, source_target_pairs={{0,1},{1,2},{2,3},{3,0},{4,5},{5,6},{6,7},{7,4},{8,9},{9,10},{10,1... | collective-permute-start | bytes 294920 | tf_op jit(solution)/shard_map/ppermute | solution.py:732
  50.1 17.3 %collective-permute-start.5 = (bf16[3,4,32,128]{3,2,1,0:T(8,128)(2,1)S(1)}, bf16[3,4,32,128]{3,2,1,0:T(8,128)(2,1)S(1)}, u32[]{:S(2)}, u32[]{:S(2)}) collective-permute-start(bf16[3,4,32,128]{3,2,1,0:T(8,128)(2,1)S(1)} %get-tuple-element.48), channel_id=1, source_target_pairs={{0,2},{1,3},{2,0},{3,1},{4,6},{5,7},{6,4},{7,5},{8,10},{9,11},{10,... | collective-permute-start | bytes 294920 | tf_op jit(solution)/shard_map/ppermute | solution.py:732
  52.5 15.0 %collective-permute-start.6 = (bf16[3,4,32,128]{3,2,1,0:T(8,128)(2,1)S(1)}, bf16[3,4,32,128]{3,2,1,0:T(8,128)(2,1)S(1)}, u32[]{:S(2)}, u32[]{:S(2)}) collective-permute-start(bf16[3,4,32,128]{3,2,1,0:T(8,128)(2,1)S(1)} %get-tuple-element.49), channel_id=1, source_target_pairs={{0,3},{1,0},{2,1},{3,2},{4,7},{5,4},{6,5},{7,6},{8,11},{9,8},{10,9... | collective-permute-start | bytes 294920 | tf_op jit(solution)/shard_map/ppermute | solution.py:732

commit v13 on v12

--- a/solution.py
+++ b/solution.py
@@ -18,7 +18,6 @@
 FIRST = 4
 RING = 12
 Y_SLOTS = (1, 2, 3, 0)
-LIMIT = 6
 GROUP = 2
 BLK = 256
 EDGE = 7
@@ -248,12 +247,17 @@
     w1_ref,
     w2_ref,
     w3_ref,
-    act3,
-    prod,
+    w4_ref,
+    fault_ref,
+    prob,
+    slope,
     raw,
     amp,
     act1,
     act2,
+    act3,
+    prod,
+    part,
 ):
     x0 = lax.axis_index("gx") * TX
     y0 = lax.axis_index("gy") * ty
@@ -350,41 +354,6 @@
         energy = grad_t * grad_t + 0.25 * (grad_x * grad_x + grad_y * grad_y)
         prod[2, at] = smooth_yt(energy, 0.25 * here * here)
 
-    def outside(edge):
-        for kind in range(3):
-            act2[kind, edge % RING] = jnp.zeros((EDGE, PAIRS, BLK), BF16)
-
-    outside(0)
-    for pair in range(pairs2, pairs1):
-        act3[pair] = jnp.zeros((EDGE, PAIRS, BLK), BF16)
-
-    chunks = pairs1 // FIRST
-    done2 = done3 = done_slopes = 0
-    for stage in range(chunks + 2):
-        end2 = min(pairs2, stage * FIRST - 2) if stage else 0
-        end3 = pairs2 if stage == chunks + 1 else max(0, done2 - 1)
-        if stage == chunks:
-            outside(pairs2 + 1)
-        work = []
-        for end, done, run in ((end3, done3, third), (end2, done2, second)):
-            steps = range(done, end, GROUP)
-            work.append([functools.partial(run, at, min(at + GROUP, end)) for at in steps])
-        if stage < chunks:
-            work.append([functools.partial(first, stage)])
-        if stage and done_slopes <= FX:
-            work.append([functools.partial(products, done_slopes)])
-            done_slopes += RX
-        for turn_of in range(max(len(w) for w in work)):
-            for w in work:
-                if turn_of < len(w):
-                    w[turn_of]()
-        done2, done3 = max(done2, end2), max(done3, end3)
-    assert done2 == done3 == pairs2 and done_slopes > FX
-
-
-def fourth_kernel(ty, act3, prod, w4_ref, fault_ref, prob, slope, part):
-    yw = ty + 2 * H
-    pairs1 = yw // 2
     at_lane = iota((NT, 8 * PAIRS), 1) % (4 * PAIRS)
     from_pairs = jnp.where(
         iota((NT, 8 * PAIRS), 0) == 2 * pair_of(at_lane % PAIRS) - 1 + at_lane // PAIRS, 1.0, 0.0
@@ -400,15 +369,14 @@
         slope[0, at] = sums[0] * scale
         slope[1, at] = sums[1] * scale
 
-    def fourth(step, carry):
-        for i in range(2):
-            slopes(jnp.minimum((step * 2 + i) * RX, FX - RX))
-        pair = step * 8
-        cells = [act3[pl.ds(pair, 8), blk].reshape(8 * PAIRS, BLK) for blk in range(EDGE)]
+    def fourth(begin, end):
+        cells = [
+            act3[begin:end, blk].reshape((end - begin) * PAIRS, BLK) for blk in range(EDGE)
+        ]
         result = dot(jnp.concatenate(cells, axis=1), w4_ref[...])
-        for i in range(0, 8, 2):
+        for pair in range(begin, end, 2):
             sides = []
-            for at in (i, i + 1):
+            for at in (pair - begin, pair - begin + 1):
                 rows = result[at * PAIRS : (at + 1) * PAIRS]
                 sides.append(
                     jnp.concatenate([rows[:, j * 128 : (j + 1) * 128] for j in range(4)], axis=0)
@@ -417,19 +385,12 @@
             high = both.astype(BF16)
             low = (both - high.astype(F32)).astype(BF16)
             share = dot(from_pairs, jnp.concatenate([high, low], axis=0))
-            part[pair + i] = share[:, :128]
-            part[pair + i + 1] = share[:, 128:]
-        return carry
-
-    lax.fori_loop(0, pairs1 // 8, fourth, 0, unroll=True)
-
-    for x in range(FX):
-        prob[x * yw : x * yw + H, :] = jnp.zeros((H, NT), F32)
-        prob[(x + 1) * yw - H : (x + 1) * yw, :] = jnp.zeros((H, NT), F32)
+            part[pair] = share[:, :128]
+            part[pair + 1] = share[:, 128:]
+
     lane = iota((NT, 128), 1)
 
-    def order(step, carry):
-        pair = 2 * step + 1
+    def order(pair):
         here = part[pair]
         before = pltpu.roll(part[pair - 1], 64, 1)
         after = pltpu.roll(part[pair + 1], 64, 1)
@@ -444,12 +405,58 @@
         for row in range(4):
             at = pl.ds(2 * pair + 2 + row, FX, stride=yw)
             prob[at, :] = values[row * XW : row * XW + FX]
-        return carry
-
-    lax.fori_loop(0, (ty + 8) // 4, order, 0, unroll=5)
-
+
+    def outside(edge):
+        for kind in range(3):
+            act2[kind, edge % RING] = jnp.zeros((EDGE, PAIRS, BLK), BF16)
+
+    outside(0)
+    for pair in range(pairs2, pairs1):
+        act3[pair] = jnp.zeros((EDGE, PAIRS, BLK), BF16)
+
+    for x in range(FX):
+        prob[x * yw : x * yw + H, :] = jnp.zeros((H, NT), F32)
+        prob[(x + 1) * yw - H : (x + 1) * yw, :] = jnp.zeros((H, NT), F32)
     for which in range(2):
         slope[which, FX + 1] = jnp.zeros((yw, NT), F32)
+
+    chunks = pairs1 // FIRST
+    done2 = done3 = done4 = 0
+    next_products = next_slopes = 0
+    next_order = 1
+    last_order = pairs1 - 5
+    for stage in range(chunks + 4):
+        if stage == chunks:
+            outside(pairs2 + 1)
+        end2 = max(0, min(pairs2, stage * FIRST - 2))
+        end3 = pairs2 if done2 == pairs2 else max(0, done2 - 1)
+        end4 = pairs1 if done3 == pairs2 else done3 // 4 * 4
+        work = []
+        for end, done, run in ((end3, done3, third), (end2, done2, second)):
+            steps = range(done, end, GROUP)
+            work.append([functools.partial(run, at, min(at + GROUP, end)) for at in steps])
+        if stage < chunks:
+            work.append([functools.partial(first, stage)])
+        if end4 > done4:
+            work.append([functools.partial(fourth, done4, end4)])
+        ready = []
+        while next_order <= last_order and next_order + 2 < done4:
+            ready.append(functools.partial(order, next_order))
+            next_order += 2
+        work.append(ready)
+        if stage and next_slopes < FX and next_slopes + RX < next_products:
+            work.append([functools.partial(slopes, next_slopes)])
+            next_slopes += RX
+        if stage and next_products <= FX:
+            work.append([functools.partial(products, next_products)])
+            next_products += RX
+        for turn_of in range(max(len(w) for w in work)):
+            for w in work:
+                if turn_of < len(w):
+                    w[turn_of]()
+        done2, done3, done4 = end2, end3, end4
+    assert done4 == pairs1 and next_order > last_order and next_slopes == FX
+
     for x in range(TX):
         fault_ref[x] = prob[(x + 4) * yw + H : (x + 4) * yw + H + ty, :].astype(BF16)
 
@@ -667,41 +674,30 @@
     )
 
     yw, nf = ty + 2 * H, FX + 2
-    act3, prod = pl.pallas_call(
+    fault, prob, slope = pl.pallas_call(
         functools.partial(net_kernel, grid_x, grid_y, ty),
         out_shape=[
-            jax.ShapeDtypeStruct((yw // 2, EDGE, PAIRS, BLK), BF16),
-            jax.ShapeDtypeStruct((3, FX + 4, yw, NT), F32),
+            jax.ShapeDtypeStruct((TX, ty, NT), BF16),
+            jax.ShapeDtypeStruct((FX * yw, NT), F32),
+            jax.ShapeDtypeStruct((2, nf, yw, NT), F32),
         ],
-        in_specs=vmem(8),
-        out_specs=vmem(2),
+        in_specs=vmem(9),
+        out_specs=vmem(3),
         scratch_shapes=[
             pltpu.VMEM(((XW + 2) * yw, NT), F32),
             pltpu.VMEM((yw + 2, XW, NT), BF16),
             pltpu.VMEM((3, RING, EDGE + 1, PAIRS, BLK), BF16),
             pltpu.VMEM((3, RING, EDGE, PAIRS, BLK), BF16),
+            pltpu.VMEM((yw // 2, EDGE, PAIRS, BLK), BF16),
+            pltpu.VMEM((3, FX + 4, yw, NT), F32),
+            pltpu.VMEM((yw // 2, NT, 128), F32),
         ],
-        compiler_params=pltpu.CompilerParams(vmem_limit_bytes=28 * 2**20),
-        cost_estimate=pl.CostEstimate(flops=3 * 10**10, bytes_accessed=10**7, transcendentals=0),
-        name="layers_one_to_three",
-    )(amplitude, xlow, xhigh, ylow, yhigh, w1, w2, w3)
-
-    fault, prob, slope = pl.pallas_call(
-        functools.partial(fourth_kernel, ty),
-        out_shape=[
-            jax.ShapeDtypeStruct((TX, ty, NT), BF16),
-            jax.ShapeDtypeStruct((FX * yw, NT), F32),
-            jax.ShapeDtypeStruct((2, nf, yw, NT), F32),
-        ],
-        in_specs=vmem(3),
-        out_specs=vmem(3),
-        scratch_shapes=[pltpu.VMEM((yw // 2, NT, 128), F32)],
-        compiler_params=pltpu.CompilerParams(vmem_limit_bytes=(LIMIT + 4) * 2**20),
+        compiler_params=pltpu.CompilerParams(vmem_limit_bytes=40 * 2**20),
         cost_estimate=pl.CostEstimate(
-            flops=10**10, bytes_accessed=10**7, transcendentals=10**6
+            flops=3 * 10**10, bytes_accessed=10**7, transcendentals=10**6
         ),
-        name="layer_four",
-    )(act3, prod, w4)
+        name="fault_net",
+    )(amplitude, xlow, xhigh, ylow, yhigh, w1, w2, w3, w4)
 
     rows = TX // n_gy
     moments, face, wave2, *waves = pl.pallas_call(

time: 68.7 us -> 68.2 us (level)
    pallas_call x1 -> x0, Pallas kernels: 5.52 us -> none  [on_device(): pl.pallas_call(functools.partial(fourth_kernel, ty), out_shape=[jax.Shape...]
    pallas_call x1, Pallas kernels: 22.2 us -> 27.3 us  [on_device(): pl.pallas_call(functools.partial(net_kernel, grid_x, grid_y, ty), out_sha...]
where the time goes in v13:
time: 68.2 us; the launch traced here: 67.8 us
  Pallas kernels  33.3 us (49%)
  starting transfers between devices  16.1 us (24%)
  blocking collectives  12.8 us (19%)
  waiting for transfers between devices  2.2 us (3%)
  other arithmetic  1.76 us (3%)
  local copies, waits for them, and re-layouts  0.91 us (1%)
  between operations  0.75 us (1%)
    pallas_call x1, Pallas kernels, on_device(): pl.pallas_call(functools.partial(net_kernel, grid_x, grid_y, ty), out_sha...  27.3 us
    all_to_all x1, blocking collectives, on_device(): lax.all_to_all(everyone, ('gx', 'gy'), split_axis=0, concat_axis=0, tiled...  12.8 us
    ppermute x4, starting transfers between devices, shift(): return lax.ppermute(values, axis, pairs)  10.5 us
    ppermute x3, starting transfers between devices, on_device(): arrived.append(lax.ppermute(waves[place], 'gy', pairs))  5.55 us
    pallas_call x1, Pallas kernels, on_device(): pl.pallas_call(functools.partial(waves_kernel, grid_x, grid_y, ty), out_s...  2.39 us
    ppermute x4, waiting for transfers between devices, shift(): return lax.ppermute(values, axis, pairs)  2.19 us
    pallas_call x1, Pallas kernels, on_device(): pl.pallas_call(prep_kernel, out_shape=[jax.ShapeDtypeStruct((16 * XW, (ED...  2.17 us
  transfers between devices with their start and end apart: 7, of which 2 were waited for; matrix products, arithmetic and copies ran while one was open for 3% of the time, Pallas kernels for 4%

profile of v13, /device:TPU:0, one launch (start us, length us, event | category | flops | bytes accessed | tf_op | source)
XLA Modules:
  0.0 67.8 jit_solution(7056697012095826718)
XLA Ops:
  0.6 0.0 copy-start
  0.6 0.9 %copy-done = bf16[16,32,128]{2,1,0:T(8,128)(2,1)S(1)} copy-done((bf16[16,32,128]{2,1,0:T(8,128)(2,1)S(1)}, bf16[16,32,128]{2,1,0:T(8,128)(2,1)}, u32[]{:S(2)}) %copy-start) | copy-done | bytes 131096
  1.6 1.3 %collective-permute-start.1 = (bf16[8,32,128]{2,1,0:T(8,128)(2,1)S(1)}, bf16[8,32,128]{2,1,0:T(8,128)(2,1)S(1)}, u32[]{:S(2)}, u32[]{:S(2)}) collective-permute-start(bf16[8,32,128]{2,1,0:T(8,128)(2,1)S(1)} %get-tuple-element.25), channel_id=1, source_target_pairs={{4,0},{8,4},{12,8},{16,12},{20,16},{24,20},{28,24},{5,1},{9,5},{13... | collective-permute-start | bytes 196616 | tf_op jit(solution)/shard_map/ppermute | solution.py:631
  2.9 3.0 %collective-permute-start = (bf16[8,32,128]{2,1,0:T(8,128)(2,1)S(1)}, bf16[8,32,128]{2,1,0:T(8,128)(2,1)S(1)}, u32[]{:S(2)}, u32[]{:S(2)}) collective-permute-start(bf16[8,32,128]{2,1,0:T(8,128)(2,1)S(1)} %get-tuple-element.24), channel_id=1, source_target_pairs={{0,4},{4,8},{8,12},{12,16},{16,20},{20,24},{24,28},{1,5},{5,9},{9,... | collective-permute-start | bytes 196616 | tf_op jit(solution)/shard_map/ppermute | solution.py:631
  5.9 0.0 collective-permute-done.1.after_ref.xhigh_ref
  5.9 0.9 %collective-permute-done.xlow_ref = bf16[8,32,128]{2,1,0:T(8,128)(2,1)S(1)} collective-permute-done((bf16[8,32,128]{2,1,0:T(8,128)(2,1)S(1)}, bf16[8,32,128]{2,1,0:T(8,128)(2,1)S(1)}, u32[]{:S(2)}, u32[]{:S(2)}) %collective-permute-start) | collective-permute-done | bytes 65568 | tf_op jit(solution)/shard_map/ppermute | solution.py:631
  6.8 4.9 %collective-permute-start.2 = (bf16[32,8,128]{2,1,0:T(8,128)(2,1)S(1)}, bf16[32,8,128]{2,1,0:T(8,128)(2,1)S(1)}, u32[]{:S(2)}, u32[]{:S(2)}) collective-permute-start(bf16[32,8,128]{2,1,0:T(8,128)(2,1)S(1)} %pad_maximum_fusion.1), channel_id=1, source_target_pairs={{0,1},{1,2},{2,3},{4,5},{5,6},{6,7},{8,9},{9,10},{10,11},{12,13},{... | collective-permute-start | bytes 196616 | tf_op jit(solution)/shard_map/ppermute | solution.py:631
  11.8 1.3 %collective-permute-start.3 = (bf16[32,8,128]{2,1,0:T(8,128)(2,1)S(1)}, bf16[32,8,128]{2,1,0:T(8,128)(2,1)S(1)}, u32[]{:S(2)}, u32[]{:S(2)}) collective-permute-start(bf16[32,8,128]{2,1,0:T(8,128)(2,1)S(1)} %pad_maximum_fusion.2), channel_id=1, source_target_pairs={{1,0},{2,1},{3,2},{5,4},{6,5},{7,6},{9,8},{10,9},{11,10},{13,12},{... | collective-permute-start | bytes 196616 | tf_op jit(solution)/shard_map/ppermute | solution.py:631
  13.1 0.7 %pad_maximum_fusion.3.outer_ref = bf16[2,3,3,3,16]{4,3,2,1,0:T(4,128)(2,1)S(1)} fusion(bf16[1,3,3,3,16]{4,3,2,1,0:T(4,128)(2,1)} %bitcast.8, bf16[1,3,3,3,16]{4,3,2,1,0:T(4,128)(2,1)} %bitcast.9), kind=kLoop, calls=%fused_computation.3 | loop fusion | flops 864 | bytes 3456 | tf_op jit(solution)/shard_map/concatenate | solution.py:670
  13.8 1.0 %pad_maximum_fusion = bf16[6,3,3,16,16]{4,3,2,1,0:T(8,128)(2,1)S(1)} fusion(bf16[3,3,3,16,16]{4,3,2,1,0:T(8,128)(2,1)} %bitcast.6, bf16[3,3,3,16,16]{4,3,2,1,0:T(8,128)(2,1)} %bitcast.7), kind=kLoop, calls=%fused_computation | loop fusion | flops 13824 | bytes 55296 | tf_op jit(solution)/shard_map/concatenate | solution.py:669
  14.8 0.0 copy-start.1
  14.8 2.2 %band_weights.1 = (bf16[512,2048]{1,0:T(8,128)(2,1)S(1)}, bf16[1536,256]{1,0:T(8,128)(2,1)S(1)}, bf16[1536,256]{1,0:T(8,128)(2,1)S(1)}, bf16[1792,512]{1,0:T(8,128)(2,1)S(1)}) custom-call(bf16[864,16]{1,0:T(8,128)(2,1)S(1)} %bitcast.5, bf16[2,3,3,3,16]{4,3,2,1,0:T(4,128)(2,1)S(1)} %pad_maximum_fusion.3.outer_ref, ...), custom_call_target="tpu_custom_call" | custom-call | flops 1000000000 | bytes 10000000 | tf_op jit(solution)/shard_map/band_weights/pallas_call | solution.py:655
  17.0 0.0 collective-permute-done.2.ylow_ref
  17.0 1.3 %collective-permute-done.3.yhigh_ref = bf16[32,8,128]{2,1,0:T(8,128)(2,1)S(1)} collective-permute-done((bf16[32,8,128]{2,1,0:T(8,128)(2,1)S(1)}, bf16[32,8,128]{2,1,0:T(8,128)(2,1)S(1)}, u32[]{:S(2)}, u32[]{:S(2)}) %collective-permute-start.3) | collective-permute-done | bytes 65568 | tf_op jit(solution)/shard_map/ppermute | solution.py:631
  18.3 0.0 copy-done.1
  18.3 27.3 %fault_net.1 = (bf16[16,32,128]{2,1,0:T(8,128)(2,1)}, f32[1152,128]{1,0:T(8,128)S(1)}, f32[2,26,48,128]{3,2,1,0:T(8,128)S(1)}) custom-call(bf16[16,32,128]{2,1,0:T(8,128)(2,1)S(1)} %copy-done.1, bf16[8,32,128]{2,1,0:T(8,128)(2,1)S(1)} %collective-permute-done.xlow_ref, bf16[8,32,128]{2,1,0:T(8,128)(2,1)S(1)} %collective-permute-done.1.after_ref.xhigh_ref, ...), custom_call_target="tpu_custom_call" | custom-call | flops 30000001024 | bytes 10000000 | tf_op jit(solution)/shard_map/fault_net/pallas_call | solution.py:677
  45.6 2.4 %solver_waves.1 = (f32[8,128]{1,0:T(8,128)S(1)}, f32[2,26,48,128]{3,2,1,0:T(8,128)S(1)}, f32[26,48,128]{2,1,0:T(8,128)S(1)}, bf16[3,4,32,128]{3,2,1,0:T(8,128)(2...) custom-call(f32[1152,128]{1,0:T(8,128)S(1)} %get-tuple-element.37.pr, ...), custom_call_target="tpu_custom_call" | custom-call | flops 100000000 | bytes 10000000 | tf_op jit(solution)/shard_map/solver_waves/pallas_call | solution.py:703
  48.0 1.6 %collective-permute-start.4 = (bf16[3,4,32,128]{3,2,1,0:T(8,128)(2,1)S(1)}, bf16[3,4,32,128]{3,2,1,0:T(8,128)(2,1)S(1)}, u32[]{:S(2)}, u32[]{:S(2)}) collective-permute-start(bf16[3,4,32,128]{3,2,1,0:T(8,128)(2,1)S(1)} %get-tuple-element.43), channel_id=1, source_target_pairs={{0,1},{1,2},{2,3},{3,0},{4,5},{5,6},{6,7},{7,4},{8,9},{9,10},{10,1... | collective-permute-start | bytes 294920 | tf_op jit(solution)/shard_map/ppermute | solution.py:728
  49.6 2.4 %collective-permute-start.5 = (bf16[3,4,32,128]{3,2,1,0:T(8,128)(2,1)S(1)}, bf16[3,4,32,128]{3,2,1,0:T(8,128)(2,1)S(1)}, u32[]{:S(2)}, u32[]{:S(2)}) collective-permute-start(bf16[3,4,32,128]{3,2,1,0:T(8,128)(2,1)S(1)} %get-tuple-element.44), channel_id=1, source_target_pairs={{0,2},{1,3},{2,0},{3,1},{4,6},{5,7},{6,4},{7,5},{8,10},{9,11},{10,... | collective-permute-start | bytes 294920 | tf_op jit(solution)/shard_map/ppermute | solution.py:728
  52.0 1.6 %collective-permute-start.6 = (bf16[3,4,32,128]{3,2,1,0:T(8,128)(2,1)S(1)}, bf16[3,4,32,128]{3,2,1,0:T(8,128)(2,1)S(1)}, u32[]{:S(2)}, u32[]{:S(2)}) collective-permute-start(bf16[3,4,32,128]{3,2,1,0:T(8,128)(2,1)S(1)} %get-tuple-element.45), channel_id=1, source_target_pairs={{0,3},{1,0},{2,1},{3,2},{4,7},{5,4},{6,5},{7,6},{8,11},{9,8},{10,9... | collective-permute-start | bytes 294920 | tf_op jit(solution)/shard_map/ppermute | solution.py:728
  53.5 0.6 last_moment.1
  54.1 12.8 %all_to_all.5.mom_ref = f32[32,1,128]{2,1,0:T(1,128)S(1)} all-to-all(f32[32,1,128]{2,1,0:T(1,128)S(1)} %last_moment.1), channel_id=1, replica_groups=mesh['gx'=8,'gy'=4] {'gx','gy'}, dimensions={0} | all-to-all | bytes 32768 | tf_op jit(solution)/shard_map/all_to_all | solution.py:739
  66.9 0.0 collective-permute-done.4.refs_1_
  66.9 0.0 collective-permute-done.5.refs_2_
  66.9 0.0 collective-permute-done.6.refs_3_
  66.9 0.9 %combine_waves.1 = f32[4,128,128]{2,1,0:T(8,128)} custom-call(f32[32,1,128]{2,1,0:T(1,128)S(1)} %all_to_all.5.mom_ref, bf16[3,4,32,128]{3,2,1,0:T(8,128)(2,1)S(1)} %get-tuple-element.42.refs_0_, bf16[3,4,32,128]{3,2,1,0:T(8,128)(2,1)S(1)} %collective-permute-done.4.refs_1_, bf16[3,4,32,128]{3,2,1,0:T(8,128)(2,1)S(1)} %collective-permute-done.5.refs_2_, ...), custom_call_target="tpu_custom_call" | custom-call | tf_op jit(solution)/shard_map/combine_waves/pallas_call | solution.py:740
  (5 shorter events, 0.1 us)
Async XLA Ops:
  0.6 0.9 %copy-start = (bf16[16,32,128]{2,1,0:T(8,128)(2,1)S(1)}, bf16[16,32,128]{2,1,0:T(8,128)(2,1)}, u32[]{:S(2)}) copy-start(bf16[16,32,128]{2,1,0:T(8,128)(2,1)} %amp_ref.3) | copy-start | bytes 393220
  1.6 4.3 %collective-permute-start.1 = (bf16[8,32,128]{2,1,0:T(8,128)(2,1)S(1)}, bf16[8,32,128]{2,1,0:T(8,128)(2,1)S(1)}, u32[]{:S(2)}, u32[]{:S(2)}) collective-permute-start(bf16[8,32,128]{2,1,0:T(8,128)(2,1)S(1)} %get-tuple-element.25), channel_id=1, source_target_pairs={{4,0},{8,4},{12,8},{16,12},{20,16},{24,20},{28,24},{5,1},{9,5},{13... | collective-permute-start | bytes 196616 | tf_op jit(solution)/shard_map/ppermute | solution.py:631
  2.9 3.9 %collective-permute-start = (bf16[8,32,128]{2,1,0:T(8,128)(2,1)S(1)}, bf16[8,32,128]{2,1,0:T(8,128)(2,1)S(1)}, u32[]{:S(2)}, u32[]{:S(2)}) collective-permute-start(bf16[8,32,128]{2,1,0:T(8,128)(2,1)S(1)} %get-tuple-element.24), channel_id=1, source_target_pairs={{0,4},{4,8},{8,12},{12,16},{16,20},{20,24},{24,28},{1,5},{5,9},{9,... | collective-permute-start | bytes 196616 | tf_op jit(solution)/shard_map/ppermute | solution.py:631
  6.8 10.2 %collective-permute-start.2 = (bf16[32,8,128]{2,1,0:T(8,128)(2,1)S(1)}, bf16[32,8,128]{2,1,0:T(8,128)(2,1)S(1)}, u32[]{:S(2)}, u32[]{:S(2)}) collective-permute-start(bf16[32,8,128]{2,1,0:T(8,128)(2,1)S(1)} %pad_maximum_fusion.1), channel_id=1, source_target_pairs={{0,1},{1,2},{2,3},{4,5},{5,6},{6,7},{8,9},{9,10},{10,11},{12,13},{... | collective-permute-start | bytes 196616 | tf_op jit(solution)/shard_map/ppermute | solution.py:631
  11.8 6.6 %collective-permute-start.3 = (bf16[32,8,128]{2,1,0:T(8,128)(2,1)S(1)}, bf16[32,8,128]{2,1,0:T(8,128)(2,1)S(1)}, u32[]{:S(2)}, u32[]{:S(2)}) collective-permute-start(bf16[32,8,128]{2,1,0:T(8,128)(2,1)S(1)} %pad_maximum_fusion.2), channel_id=1, source_target_pairs={{1,0},{2,1},{3,2},{5,4},{6,5},{7,6},{9,8},{10,9},{11,10},{13,12},{... | collective-permute-start | bytes 196616 | tf_op jit(solution)/shard_map/ppermute | solution.py:631
  14.8 3.5 %copy-start.1 = (bf16[16,32,128]{2,1,0:T(8,128)(2,1)S(1)}, bf16[16,32,128]{2,1,0:T(8,128)(2,1)}, u32[]{:S(2)}) copy-start(bf16[16,32,128]{2,1,0:T(8,128)(2,1)} %amp_ref.3) | copy-start | bytes 393220
  48.0 18.9 %collective-permute-start.4 = (bf16[3,4,32,128]{3,2,1,0:T(8,128)(2,1)S(1)}, bf16[3,4,32,128]{3,2,1,0:T(8,128)(2,1)S(1)}, u32[]{:S(2)}, u32[]{:S(2)}) collective-permute-start(bf16[3,4,32,128]{3,2,1,0:T(8,128)(2,1)S(1)} %get-tuple-element.43), channel_id=1, source_target_pairs={{0,1},{1,2},{2,3},{3,0},{4,5},{5,6},{6,7},{7,4},{8,9},{9,10},{10,1... | collective-permute-start | bytes 294920 | tf_op jit(solution)/shard_map/ppermute | solution.py:728
  49.6 17.3 %collective-permute-start.5 = (bf16[3,4,32,128]{3,2,1,0:T(8,128)(2,1)S(1)}, bf16[3,4,32,128]{3,2,1,0:T(8,128)(2,1)S(1)}, u32[]{:S(2)}, u32[]{:S(2)}) collective-permute-start(bf16[3,4,32,128]{3,2,1,0:T(8,128)(2,1)S(1)} %get-tuple-element.44), channel_id=1, source_target_pairs={{0,2},{1,3},{2,0},{3,1},{4,6},{5,7},{6,4},{7,5},{8,10},{9,11},{10,... | collective-permute-start | bytes 294920 | tf_op jit(solution)/shard_map/ppermute | solution.py:728
  52.0 14.9 %collective-permute-start.6 = (bf16[3,4,32,128]{3,2,1,0:T(8,128)(2,1)S(1)}, bf16[3,4,32,128]{3,2,1,0:T(8,128)(2,1)S(1)}, u32[]{:S(2)}, u32[]{:S(2)}) collective-permute-start(bf16[3,4,32,128]{3,2,1,0:T(8,128)(2,1)S(1)} %get-tuple-element.45), channel_id=1, source_target_pairs={{0,3},{1,0},{2,1},{3,2},{4,7},{5,4},{6,5},{7,6},{8,11},{9,8},{10,9... | collective-permute-start | bytes 294920 | tf_op jit(solution)/shard_map/ppermute | solution.py:728

commit v14 on v13

--- a/solution.py
+++ b/solution.py
@@ -15,10 +15,10 @@
 XW = TX + 2 * H
 FX = TX + 8
 RX = 4
-FIRST = 4
-RING = 12
+FIRST, STEP = 8, 4
+RING1, RING2 = 16, 12
 Y_SLOTS = (1, 2, 3, 0)
-GROUP = 2
+GROUP = 5
 BLK = 256
 EDGE = 7
 SUB = 16
@@ -223,7 +223,7 @@
     def rows(kind, offset, at):
         found = []
         for i in range(count):
-            place = (pair + offset + i) % RING
+            place = (pair + offset + i) % source.shape[1]
             found.append(source[kind, place, :EDGE, :, at].reshape(EDGE * PAIRS, -1))
         return jnp.concatenate(found, axis=0)
 
@@ -307,9 +307,9 @@
                 for blk in (begin, begin + 1):
                     lane = (blk - begin) * BLK
                     values = result[i * PAIRS : (i + 1) * PAIRS, lane : lane + BLK]
-                    put(act1, pair % RING, blk, jnp.maximum(values, 0.0) * (mask[blk] * inside))
+                    put(act1, pair % RING1, blk, jnp.maximum(values, 0.0) * (mask[blk] * inside))
         for i in range(FIRST):
-            put_sides(act1, (step * FIRST + i) % RING, EDGE + 1)
+            put_sides(act1, (step * FIRST + i) % RING1, EDGE + 1)
 
     def second(begin, end):
         count = end - begin
@@ -320,8 +320,8 @@
             for blk in range(EDGE):
                 at = (i * EDGE + blk) * PAIRS
                 values = jnp.maximum(result[at : at + PAIRS], 0.0)
-                put(act2, (pair + 1) % RING, blk, values * (mask[blk] * inside))
-            put_sides(act2, (pair + 1) % RING, EDGE)
+                put(act2, (pair + 1) % RING2, blk, values * (mask[blk] * inside))
+            put_sides(act2, (pair + 1) % RING2, EDGE)
 
     def third(begin, end):
         count = end - begin
@@ -408,7 +408,7 @@
 
     def outside(edge):
         for kind in range(3):
-            act2[kind, edge % RING] = jnp.zeros((EDGE, PAIRS, BLK), BF16)
+            act2[kind, edge % RING2] = jnp.zeros((EDGE, PAIRS, BLK), BF16)
 
     outside(0)
     for pair in range(pairs2, pairs1):
@@ -420,23 +420,24 @@
     for which in range(2):
         slope[which, FX + 1] = jnp.zeros((yw, NT), F32)
 
-    chunks = pairs1 // FIRST
-    done2 = done3 = done4 = 0
+    done1 = done2 = done3 = done4 = 0
     next_products = next_slopes = 0
     next_order = 1
     last_order = pairs1 - 5
-    for stage in range(chunks + 4):
-        if stage == chunks:
+    stage = 0
+    while done4 < pairs1 or next_order <= last_order:
+        if done2 == pairs2 - STEP:
             outside(pairs2 + 1)
-        end2 = max(0, min(pairs2, stage * FIRST - 2))
-        end3 = pairs2 if done2 == pairs2 else max(0, done2 - 1)
-        end4 = pairs1 if done3 == pairs2 else done3 // 4 * 4
+        end1 = min(pairs1, done1 + FIRST) if stage % 2 == 0 else done1
+        end2 = max(0, min(pairs2, done2 + STEP, done1 - 2))
+        end3 = pairs2 if done2 == pairs2 else max(0, min(done3 + STEP, done2 - 1))
+        end4 = pairs1 if done3 == pairs2 else done3 // 8 * 8
         work = []
         for end, done, run in ((end3, done3, third), (end2, done2, second)):
             steps = range(done, end, GROUP)
             work.append([functools.partial(run, at, min(at + GROUP, end)) for at in steps])
-        if stage < chunks:
-            work.append([functools.partial(first, stage)])
+        if end1 > done1:
+            work.append([functools.partial(first, done1 // FIRST)])
         if end4 > done4:
             work.append([functools.partial(fourth, done4, end4)])
         ready = []
@@ -454,8 +455,9 @@
             for w in work:
                 if turn_of < len(w):
                     w[turn_of]()
-        done2, done3, done4 = end2, end3, end4
-    assert done4 == pairs1 and next_order > last_order and next_slopes == FX
+        done1, done2, done3, done4 = end1, end2, end3, end4
+        stage += 1
+    assert done3 == pairs2 and next_slopes == FX
 
     for x in range(TX):
         fault_ref[x] = prob[(x + 4) * yw + H : (x + 4) * yw + H + ty, :].astype(BF16)
@@ -686,8 +688,8 @@
         scratch_shapes=[
             pltpu.VMEM(((XW + 2) * yw, NT), F32),
             pltpu.VMEM((yw + 2, XW, NT), BF16),
-            pltpu.VMEM((3, RING, EDGE + 1, PAIRS, BLK), BF16),
-            pltpu.VMEM((3, RING, EDGE, PAIRS, BLK), BF16),
+            pltpu.VMEM((3, RING1, EDGE + 1, PAIRS, BLK), BF16),
+            pltpu.VMEM((3, RING2, EDGE, PAIRS, BLK), BF16),
             pltpu.VMEM((yw // 2, EDGE, PAIRS, BLK), BF16),
             pltpu.VMEM((3, FX + 4, yw, NT), F32),
             pltpu.VMEM((yw // 2, NT, 128), F32),

time: 68.2 us -> 73.1 us (1.072)
  Pallas kernels: 33.3 us -> 38.2 us
    pallas_call x1, Pallas kernels: 27.3 us -> 32.1 us  [on_device(): pl.pallas_call(functools.partial(net_kernel, grid_x, grid_y, ty), out_sha...]
  transfers between devices with their start and end apart: 7 -> 7, of which waited for: 2 -> 2; matrix products, arithmetic and copies ran while one was open for 3% -> 2% of each run, Pallas kernels for 4% -> 4%
where the time goes in v14:
time: 73.1 us; the launch traced here: 72.7 us
  Pallas kernels  38.2 us (52%)
  starting transfers between devices  16.1 us (22%)
  blocking collectives  12.8 us (18%)
  waiting for transfers between devices  2.2 us (3%)
  other arithmetic  1.76 us (2%)
  local copies, waits for them, and re-layouts  0.91 us (1%)
  between operations  0.75 us (1%)
    pallas_call x1, Pallas kernels, on_device(): pl.pallas_call(functools.partial(net_kernel, grid_x, grid_y, ty), out_sha...  32.1 us
    all_to_all x1, blocking collectives, on_device(): lax.all_to_all(everyone, ('gx', 'gy'), split_axis=0, concat_axis=0, tiled...  12.8 us
    ppermute x4, starting transfers between devices, shift(): return lax.ppermute(values, axis, pairs)  10.5 us
    ppermute x3, starting transfers between devices, on_device(): arrived.append(lax.ppermute(waves[place], 'gy', pairs))  5.57 us
    pallas_call x1, Pallas kernels, on_device(): pl.pallas_call(functools.partial(waves_kernel, grid_x, grid_y, ty), out_s...  2.39 us
    ppermute x4, waiting for transfers between devices, shift(): return lax.ppermute(values, axis, pairs)  2.19 us
    pallas_call x1, Pallas kernels, on_device(): pl.pallas_call(prep_kernel, out_shape=[jax.ShapeDtypeStruct((16 * XW, (ED...  2.17 us
  transfers between devices with their start and end apart: 7, of which 2 were waited for; matrix products, arithmetic and copies ran while one was open for 2% of the time, Pallas kernels for 4%

profile of v14, /device:TPU:0, one launch (start us, length us, event | category | flops | bytes accessed | tf_op | source)
XLA Modules:
  0.0 72.7 jit_solution(14433760204968995233)
XLA Ops:
  0.6 0.0 copy-start
  0.6 0.9 %copy-done = bf16[16,32,128]{2,1,0:T(8,128)(2,1)S(1)} copy-done((bf16[16,32,128]{2,1,0:T(8,128)(2,1)S(1)}, bf16[16,32,128]{2,1,0:T(8,128)(2,1)}, u32[]{:S(2)}) %copy-start) | copy-done | bytes 131096
  1.6 1.3 %collective-permute-start.1 = (bf16[8,32,128]{2,1,0:T(8,128)(2,1)S(1)}, bf16[8,32,128]{2,1,0:T(8,128)(2,1)S(1)}, u32[]{:S(2)}, u32[]{:S(2)}) collective-permute-start(bf16[8,32,128]{2,1,0:T(8,128)(2,1)S(1)} %get-tuple-element.25), channel_id=1, source_target_pairs={{4,0},{8,4},{12,8},{16,12},{20,16},{24,20},{28,24},{5,1},{9,5},{13... | collective-permute-start | bytes 196616 | tf_op jit(solution)/shard_map/ppermute | solution.py:633
  2.9 3.0 %collective-permute-start = (bf16[8,32,128]{2,1,0:T(8,128)(2,1)S(1)}, bf16[8,32,128]{2,1,0:T(8,128)(2,1)S(1)}, u32[]{:S(2)}, u32[]{:S(2)}) collective-permute-start(bf16[8,32,128]{2,1,0:T(8,128)(2,1)S(1)} %get-tuple-element.24), channel_id=1, source_target_pairs={{0,4},{4,8},{8,12},{12,16},{16,20},{20,24},{24,28},{1,5},{5,9},{9,... | collective-permute-start | bytes 196616 | tf_op jit(solution)/shard_map/ppermute | solution.py:633
  5.9 0.0 collective-permute-done.1.after_ref.xhigh_ref
  5.9 0.9 %collective-permute-done.xlow_ref = bf16[8,32,128]{2,1,0:T(8,128)(2,1)S(1)} collective-permute-done((bf16[8,32,128]{2,1,0:T(8,128)(2,1)S(1)}, bf16[8,32,128]{2,1,0:T(8,128)(2,1)S(1)}, u32[]{:S(2)}, u32[]{:S(2)}) %collective-permute-start) | collective-permute-done | bytes 65568 | tf_op jit(solution)/shard_map/ppermute | solution.py:633
  6.8 4.9 %collective-permute-start.2 = (bf16[32,8,128]{2,1,0:T(8,128)(2,1)S(1)}, bf16[32,8,128]{2,1,0:T(8,128)(2,1)S(1)}, u32[]{:S(2)}, u32[]{:S(2)}) collective-permute-start(bf16[32,8,128]{2,1,0:T(8,128)(2,1)S(1)} %pad_maximum_fusion.1), channel_id=1, source_target_pairs={{0,1},{1,2},{2,3},{4,5},{5,6},{6,7},{8,9},{9,10},{10,11},{12,13},{... | collective-permute-start | bytes 196616 | tf_op jit(solution)/shard_map/ppermute | solution.py:633
  11.8 1.3 %collective-permute-start.3 = (bf16[32,8,128]{2,1,0:T(8,128)(2,1)S(1)}, bf16[32,8,128]{2,1,0:T(8,128)(2,1)S(1)}, u32[]{:S(2)}, u32[]{:S(2)}) collective-permute-start(bf16[32,8,128]{2,1,0:T(8,128)(2,1)S(1)} %pad_maximum_fusion.2), channel_id=1, source_target_pairs={{1,0},{2,1},{3,2},{5,4},{6,5},{7,6},{9,8},{10,9},{11,10},{13,12},{... | collective-permute-start | bytes 196616 | tf_op jit(solution)/shard_map/ppermute | solution.py:633
  13.1 0.7 %pad_maximum_fusion.3.outer_ref = bf16[2,3,3,3,16]{4,3,2,1,0:T(4,128)(2,1)S(1)} fusion(bf16[1,3,3,3,16]{4,3,2,1,0:T(4,128)(2,1)} %bitcast.8, bf16[1,3,3,3,16]{4,3,2,1,0:T(4,128)(2,1)} %bitcast.9), kind=kLoop, calls=%fused_computation.3 | loop fusion | flops 864 | bytes 3456 | tf_op jit(solution)/shard_map/concatenate | solution.py:672
  13.8 1.0 %pad_maximum_fusion = bf16[6,3,3,16,16]{4,3,2,1,0:T(8,128)(2,1)S(1)} fusion(bf16[3,3,3,16,16]{4,3,2,1,0:T(8,128)(2,1)} %bitcast.6, bf16[3,3,3,16,16]{4,3,2,1,0:T(8,128)(2,1)} %bitcast.7), kind=kLoop, calls=%fused_computation | loop fusion | flops 13824 | bytes 55296 | tf_op jit(solution)/shard_map/concatenate | solution.py:671
  14.8 0.0 copy-start.1
  14.8 2.2 %band_weights.1 = (bf16[512,2048]{1,0:T(8,128)(2,1)S(1)}, bf16[1536,256]{1,0:T(8,128)(2,1)S(1)}, bf16[1536,256]{1,0:T(8,128)(2,1)S(1)}, bf16[1792,512]{1,0:T(8,128)(2,1)S(1)}) custom-call(bf16[864,16]{1,0:T(8,128)(2,1)S(1)} %bitcast.5, bf16[2,3,3,3,16]{4,3,2,1,0:T(4,128)(2,1)S(1)} %pad_maximum_fusion.3.outer_ref, ...), custom_call_target="tpu_custom_call" | custom-call | flops 1000000000 | bytes 10000000 | tf_op jit(solution)/shard_map/band_weights/pallas_call | solution.py:657
  17.0 0.0 collective-permute-done.2.ylow_ref
  17.0 1.3 %collective-permute-done.3.yhigh_ref = bf16[32,8,128]{2,1,0:T(8,128)(2,1)S(1)} collective-permute-done((bf16[32,8,128]{2,1,0:T(8,128)(2,1)S(1)}, bf16[32,8,128]{2,1,0:T(8,128)(2,1)S(1)}, u32[]{:S(2)}, u32[]{:S(2)}) %collective-permute-start.3) | collective-permute-done | bytes 65568 | tf_op jit(solution)/shard_map/ppermute | solution.py:633
  18.3 0.0 copy-done.1
  18.3 32.1 %fault_net.1 = (bf16[16,32,128]{2,1,0:T(8,128)(2,1)}, f32[1152,128]{1,0:T(8,128)S(1)}, f32[2,26,48,128]{3,2,1,0:T(8,128)S(1)}) custom-call(bf16[16,32,128]{2,1,0:T(8,128)(2,1)S(1)} %copy-done.1, bf16[8,32,128]{2,1,0:T(8,128)(2,1)S(1)} %collective-permute-done.xlow_ref, bf16[8,32,128]{2,1,0:T(8,128)(2,1)S(1)} %collective-permute-done.1.after_ref.xhigh_ref, ...), custom_call_target="tpu_custom_call" | custom-call | flops 30000001024 | bytes 10000000 | tf_op jit(solution)/shard_map/fault_net/pallas_call | solution.py:679
  50.4 2.4 %solver_waves.1 = (f32[8,128]{1,0:T(8,128)S(1)}, f32[2,26,48,128]{3,2,1,0:T(8,128)S(1)}, f32[26,48,128]{2,1,0:T(8,128)S(1)}, bf16[3,4,32,128]{3,2,1,0:T(8,128)(2...) custom-call(f32[1152,128]{1,0:T(8,128)S(1)} %get-tuple-element.37.pr, ...), custom_call_target="tpu_custom_call" | custom-call | flops 100000000 | bytes 10000000 | tf_op jit(solution)/shard_map/solver_waves/pallas_call | solution.py:705
  52.8 1.6 %collective-permute-start.4 = (bf16[3,4,32,128]{3,2,1,0:T(8,128)(2,1)S(1)}, bf16[3,4,32,128]{3,2,1,0:T(8,128)(2,1)S(1)}, u32[]{:S(2)}, u32[]{:S(2)}) collective-permute-start(bf16[3,4,32,128]{3,2,1,0:T(8,128)(2,1)S(1)} %get-tuple-element.43), channel_id=1, source_target_pairs={{0,1},{1,2},{2,3},{3,0},{4,5},{5,6},{6,7},{7,4},{8,9},{9,10},{10,1... | collective-permute-start | bytes 294920 | tf_op jit(solution)/shard_map/ppermute | solution.py:730
  54.5 2.4 %collective-permute-start.5 = (bf16[3,4,32,128]{3,2,1,0:T(8,128)(2,1)S(1)}, bf16[3,4,32,128]{3,2,1,0:T(8,128)(2,1)S(1)}, u32[]{:S(2)}, u32[]{:S(2)}) collective-permute-start(bf16[3,4,32,128]{3,2,1,0:T(8,128)(2,1)S(1)} %get-tuple-element.44), channel_id=1, source_target_pairs={{0,2},{1,3},{2,0},{3,1},{4,6},{5,7},{6,4},{7,5},{8,10},{9,11},{10,... | collective-permute-start | bytes 294920 | tf_op jit(solution)/shard_map/ppermute | solution.py:730
  56.8 1.6 %collective-permute-start.6 = (bf16[3,4,32,128]{3,2,1,0:T(8,128)(2,1)S(1)}, bf16[3,4,32,128]{3,2,1,0:T(8,128)(2,1)S(1)}, u32[]{:S(2)}, u32[]{:S(2)}) collective-permute-start(bf16[3,4,32,128]{3,2,1,0:T(8,128)(2,1)S(1)} %get-tuple-element.45), channel_id=1, source_target_pairs={{0,3},{1,0},{2,1},{3,2},{4,7},{5,4},{6,5},{7,6},{8,11},{9,8},{10,9... | collective-permute-start | bytes 294920 | tf_op jit(solution)/shard_map/ppermute | solution.py:730
  58.4 0.6 last_moment.1
  59.0 12.8 %all_to_all.5.mom_ref = f32[32,1,128]{2,1,0:T(1,128)S(1)} all-to-all(f32[32,1,128]{2,1,0:T(1,128)S(1)} %last_moment.1), channel_id=1, replica_groups=mesh['gx'=8,'gy'=4] {'gx','gy'}, dimensions={0} | all-to-all | bytes 32768 | tf_op jit(solution)/shard_map/all_to_all | solution.py:741
  71.8 0.0 collective-permute-done.4.refs_1_
  71.8 0.0 collective-permute-done.5.refs_2_
  71.8 0.0 collective-permute-done.6.refs_3_
  71.8 0.9 %combine_waves.1 = f32[4,128,128]{2,1,0:T(8,128)} custom-call(f32[32,1,128]{2,1,0:T(1,128)S(1)} %all_to_all.5.mom_ref, bf16[3,4,32,128]{3,2,1,0:T(8,128)(2,1)S(1)} %get-tuple-element.42.refs_0_, bf16[3,4,32,128]{3,2,1,0:T(8,128)(2,1)S(1)} %collective-permute-done.4.refs_1_, bf16[3,4,32,128]{3,2,1,0:T(8,128)(2,1)S(1)} %collective-permute-done.5.refs_2_, ...), custom_call_target="tpu_custom_call" | custom-call | tf_op jit(solution)/shard_map/combine_waves/pallas_call | solution.py:742
  (5 shorter events, 0.1 us)
Async XLA Ops:
  0.6 0.9 %copy-start = (bf16[16,32,128]{2,1,0:T(8,128)(2,1)S(1)}, bf16[16,32,128]{2,1,0:T(8,128)(2,1)}, u32[]{:S(2)}) copy-start(bf16[16,32,128]{2,1,0:T(8,128)(2,1)} %amp_ref.3) | copy-start | bytes 393220
  1.6 4.3 %collective-permute-start.1 = (bf16[8,32,128]{2,1,0:T(8,128)(2,1)S(1)}, bf16[8,32,128]{2,1,0:T(8,128)(2,1)S(1)}, u32[]{:S(2)}, u32[]{:S(2)}) collective-permute-start(bf16[8,32,128]{2,1,0:T(8,128)(2,1)S(1)} %get-tuple-element.25), channel_id=1, source_target_pairs={{4,0},{8,4},{12,8},{16,12},{20,16},{24,20},{28,24},{5,1},{9,5},{13... | collective-permute-start | bytes 196616 | tf_op jit(solution)/shard_map/ppermute | solution.py:633
  2.9 3.9 %collective-permute-start = (bf16[8,32,128]{2,1,0:T(8,128)(2,1)S(1)}, bf16[8,32,128]{2,1,0:T(8,128)(2,1)S(1)}, u32[]{:S(2)}, u32[]{:S(2)}) collective-permute-start(bf16[8,32,128]{2,1,0:T(8,128)(2,1)S(1)} %get-tuple-element.24), channel_id=1, source_target_pairs={{0,4},{4,8},{8,12},{12,16},{16,20},{20,24},{24,28},{1,5},{5,9},{9,... | collective-permute-start | bytes 196616 | tf_op jit(solution)/shard_map/ppermute | solution.py:633
  6.8 10.2 %collective-permute-start.2 = (bf16[32,8,128]{2,1,0:T(8,128)(2,1)S(1)}, bf16[32,8,128]{2,1,0:T(8,128)(2,1)S(1)}, u32[]{:S(2)}, u32[]{:S(2)}) collective-permute-start(bf16[32,8,128]{2,1,0:T(8,128)(2,1)S(1)} %pad_maximum_fusion.1), channel_id=1, source_target_pairs={{0,1},{1,2},{2,3},{4,5},{5,6},{6,7},{8,9},{9,10},{10,11},{12,13},{... | collective-permute-start | bytes 196616 | tf_op jit(solution)/shard_map/ppermute | solution.py:633
  11.8 6.6 %collective-permute-start.3 = (bf16[32,8,128]{2,1,0:T(8,128)(2,1)S(1)}, bf16[32,8,128]{2,1,0:T(8,128)(2,1)S(1)}, u32[]{:S(2)}, u32[]{:S(2)}) collective-permute-start(bf16[32,8,128]{2,1,0:T(8,128)(2,1)S(1)} %pad_maximum_fusion.2), channel_id=1, source_target_pairs={{1,0},{2,1},{3,2},{5,4},{6,5},{7,6},{9,8},{10,9},{11,10},{13,12},{... | collective-permute-start | bytes 196616 | tf_op jit(solution)/shard_map/ppermute | solution.py:633
  14.8 3.5 %copy-start.1 = (bf16[16,32,128]{2,1,0:T(8,128)(2,1)S(1)}, bf16[16,32,128]{2,1,0:T(8,128)(2,1)}, u32[]{:S(2)}) copy-start(bf16[16,32,128]{2,1,0:T(8,128)(2,1)} %amp_ref.3) | copy-start | bytes 393220
  52.8 18.9 %collective-permute-start.4 = (bf16[3,4,32,128]{3,2,1,0:T(8,128)(2,1)S(1)}, bf16[3,4,32,128]{3,2,1,0:T(8,128)(2,1)S(1)}, u32[]{:S(2)}, u32[]{:S(2)}) collective-permute-start(bf16[3,4,32,128]{3,2,1,0:T(8,128)(2,1)S(1)} %get-tuple-element.43), channel_id=1, source_target_pairs={{0,1},{1,2},{2,3},{3,0},{4,5},{5,6},{6,7},{7,4},{8,9},{9,10},{10,1... | collective-permute-start | bytes 294920 | tf_op jit(solution)/shard_map/ppermute | solution.py:730
  54.5 17.3 %collective-permute-start.5 = (bf16[3,4,32,128]{3,2,1,0:T(8,128)(2,1)S(1)}, bf16[3,4,32,128]{3,2,1,0:T(8,128)(2,1)S(1)}, u32[]{:S(2)}, u32[]{:S(2)}) collective-permute-start(bf16[3,4,32,128]{3,2,1,0:T(8,128)(2,1)S(1)} %get-tuple-element.44), channel_id=1, source_target_pairs={{0,2},{1,3},{2,0},{3,1},{4,6},{5,7},{6,4},{7,5},{8,10},{9,11},{10,... | collective-permute-start | bytes 294920 | tf_op jit(solution)/shard_map/ppermute | solution.py:730
  56.8 15.0 %collective-permute-start.6 = (bf16[3,4,32,128]{3,2,1,0:T(8,128)(2,1)S(1)}, bf16[3,4,32,128]{3,2,1,0:T(8,128)(2,1)S(1)}, u32[]{:S(2)}, u32[]{:S(2)}) collective-permute-start(bf16[3,4,32,128]{3,2,1,0:T(8,128)(2,1)S(1)} %get-tuple-element.45), channel_id=1, source_target_pairs={{0,3},{1,0},{2,1},{3,2},{4,7},{5,4},{6,5},{7,6},{8,11},{9,8},{10,9... | collective-permute-start | bytes 294920 | tf_op jit(solution)/shard_map/ppermute | solution.py:730

commit v15 on v13

--- a/solution.py
+++ b/solution.py
@@ -18,7 +18,7 @@
 FIRST = 4
 RING = 12
 Y_SLOTS = (1, 2, 3, 0)
-GROUP = 2
+GROUP = 1
 BLK = 256
 EDGE = 7
 SUB = 16

time: 68.2 us -> 68.7 us (level)
  no operation moved by 1% of the time
where the time goes in v15:
time: 68.7 us; the launch traced here: 68.3 us
  Pallas kernels  33.8 us (49%)
  starting transfers between devices  16.1 us (23%)
  blocking collectives  12.8 us (19%)
  waiting for transfers between devices  2.2 us (3%)
  other arithmetic  1.76 us (3%)
  local copies, waits for them, and re-layouts  0.91 us (1%)
  between operations  0.75 us (1%)
    pallas_call x1, Pallas kernels, on_device(): pl.pallas_call(functools.partial(net_kernel, grid_x, grid_y, ty), out_sha...  27.8 us
    all_to_all x1, blocking collectives, on_device(): lax.all_to_all(everyone, ('gx', 'gy'), split_axis=0, concat_axis=0, tiled...  12.8 us
    ppermute x4, starting transfers between devices, shift(): return lax.ppermute(values, axis, pairs)  10.5 us
    ppermute x3, starting transfers between devices, on_device(): arrived.append(lax.ppermute(waves[place], 'gy', pairs))  5.56 us
    pallas_call x1, Pallas kernels, on_device(): pl.pallas_call(functools.partial(waves_kernel, grid_x, grid_y, ty), out_s...  2.39 us
    ppermute x4, waiting for transfers between devices, shift(): return lax.ppermute(values, axis, pairs)  2.19 us
    pallas_call x1, Pallas kernels, on_device(): pl.pallas_call(prep_kernel, out_shape=[jax.ShapeDtypeStruct((16 * XW, (ED...  2.17 us
  transfers between devices with their start and end apart: 7, of which 2 were waited for; matrix products, arithmetic and copies ran while one was open for 3% of the time, Pallas kernels for 4%

profile of v15, /device:TPU:0, one launch (start us, length us, event | category | flops | bytes accessed | tf_op | source)
XLA Modules:
  0.0 68.3 jit_solution(13075104013816288362)
XLA Ops:
  0.6 0.0 copy-start
  0.6 0.9 %copy-done = bf16[16,32,128]{2,1,0:T(8,128)(2,1)S(1)} copy-done((bf16[16,32,128]{2,1,0:T(8,128)(2,1)S(1)}, bf16[16,32,128]{2,1,0:T(8,128)(2,1)}, u32[]{:S(2)}) %copy-start) | copy-done | bytes 131096
  1.6 1.3 %collective-permute-start.1 = (bf16[8,32,128]{2,1,0:T(8,128)(2,1)S(1)}, bf16[8,32,128]{2,1,0:T(8,128)(2,1)S(1)}, u32[]{:S(2)}, u32[]{:S(2)}) collective-permute-start(bf16[8,32,128]{2,1,0:T(8,128)(2,1)S(1)} %get-tuple-element.25), channel_id=1, source_target_pairs={{4,0},{8,4},{12,8},{16,12},{20,16},{24,20},{28,24},{5,1},{9,5},{13... | collective-permute-start | bytes 196616 | tf_op jit(solution)/shard_map/ppermute | solution.py:631
  2.9 3.0 %collective-permute-start = (bf16[8,32,128]{2,1,0:T(8,128)(2,1)S(1)}, bf16[8,32,128]{2,1,0:T(8,128)(2,1)S(1)}, u32[]{:S(2)}, u32[]{:S(2)}) collective-permute-start(bf16[8,32,128]{2,1,0:T(8,128)(2,1)S(1)} %get-tuple-element.24), channel_id=1, source_target_pairs={{0,4},{4,8},{8,12},{12,16},{16,20},{20,24},{24,28},{1,5},{5,9},{9,... | collective-permute-start | bytes 196616 | tf_op jit(solution)/shard_map/ppermute | solution.py:631
  5.9 0.0 collective-permute-done.1.after_ref.xhigh_ref
  5.9 0.9 %collective-permute-done.xlow_ref = bf16[8,32,128]{2,1,0:T(8,128)(2,1)S(1)} collective-permute-done((bf16[8,32,128]{2,1,0:T(8,128)(2,1)S(1)}, bf16[8,32,128]{2,1,0:T(8,128)(2,1)S(1)}, u32[]{:S(2)}, u32[]{:S(2)}) %collective-permute-start) | collective-permute-done | bytes 65568 | tf_op jit(solution)/shard_map/ppermute | solution.py:631
  6.8 4.9 %collective-permute-start.2 = (bf16[32,8,128]{2,1,0:T(8,128)(2,1)S(1)}, bf16[32,8,128]{2,1,0:T(8,128)(2,1)S(1)}, u32[]{:S(2)}, u32[]{:S(2)}) collective-permute-start(bf16[32,8,128]{2,1,0:T(8,128)(2,1)S(1)} %pad_maximum_fusion.1), channel_id=1, source_target_pairs={{0,1},{1,2},{2,3},{4,5},{5,6},{6,7},{8,9},{9,10},{10,11},{12,13},{... | collective-permute-start | bytes 196616 | tf_op jit(solution)/shard_map/ppermute | solution.py:631
  11.8 1.3 %collective-permute-start.3 = (bf16[32,8,128]{2,1,0:T(8,128)(2,1)S(1)}, bf16[32,8,128]{2,1,0:T(8,128)(2,1)S(1)}, u32[]{:S(2)}, u32[]{:S(2)}) collective-permute-start(bf16[32,8,128]{2,1,0:T(8,128)(2,1)S(1)} %pad_maximum_fusion.2), channel_id=1, source_target_pairs={{1,0},{2,1},{3,2},{5,4},{6,5},{7,6},{9,8},{10,9},{11,10},{13,12},{... | collective-permute-start | bytes 196616 | tf_op jit(solution)/shard_map/ppermute | solution.py:631
  13.1 0.7 %pad_maximum_fusion.3.outer_ref = bf16[2,3,3,3,16]{4,3,2,1,0:T(4,128)(2,1)S(1)} fusion(bf16[1,3,3,3,16]{4,3,2,1,0:T(4,128)(2,1)} %bitcast.8, bf16[1,3,3,3,16]{4,3,2,1,0:T(4,128)(2,1)} %bitcast.9), kind=kLoop, calls=%fused_computation.3 | loop fusion | flops 864 | bytes 3456 | tf_op jit(solution)/shard_map/concatenate | solution.py:670
  13.8 1.0 %pad_maximum_fusion = bf16[6,3,3,16,16]{4,3,2,1,0:T(8,128)(2,1)S(1)} fusion(bf16[3,3,3,16,16]{4,3,2,1,0:T(8,128)(2,1)} %bitcast.6, bf16[3,3,3,16,16]{4,3,2,1,0:T(8,128)(2,1)} %bitcast.7), kind=kLoop, calls=%fused_computation | loop fusion | flops 13824 | bytes 55296 | tf_op jit(solution)/shard_map/concatenate | solution.py:669
  14.8 0.0 copy-start.1
  14.8 2.2 %band_weights.1 = (bf16[512,2048]{1,0:T(8,128)(2,1)S(1)}, bf16[1536,256]{1,0:T(8,128)(2,1)S(1)}, bf16[1536,256]{1,0:T(8,128)(2,1)S(1)}, bf16[1792,512]{1,0:T(8,128)(2,1)S(1)}) custom-call(bf16[864,16]{1,0:T(8,128)(2,1)S(1)} %bitcast.5, bf16[2,3,3,3,16]{4,3,2,1,0:T(4,128)(2,1)S(1)} %pad_maximum_fusion.3.outer_ref, ...), custom_call_target="tpu_custom_call" | custom-call | flops 1000000000 | bytes 10000000 | tf_op jit(solution)/shard_map/band_weights/pallas_call | solution.py:655
  17.0 0.0 collective-permute-done.2.ylow_ref
  17.0 1.3 %collective-permute-done.3.yhigh_ref = bf16[32,8,128]{2,1,0:T(8,128)(2,1)S(1)} collective-permute-done((bf16[32,8,128]{2,1,0:T(8,128)(2,1)S(1)}, bf16[32,8,128]{2,1,0:T(8,128)(2,1)S(1)}, u32[]{:S(2)}, u32[]{:S(2)}) %collective-permute-start.3) | collective-permute-done | bytes 65568 | tf_op jit(solution)/shard_map/ppermute | solution.py:631
  18.3 0.0 copy-done.1
  18.3 27.8 %fault_net.1 = (bf16[16,32,128]{2,1,0:T(8,128)(2,1)}, f32[1152,128]{1,0:T(8,128)S(1)}, f32[2,26,48,128]{3,2,1,0:T(8,128)S(1)}) custom-call(bf16[16,32,128]{2,1,0:T(8,128)(2,1)S(1)} %copy-done.1, bf16[8,32,128]{2,1,0:T(8,128)(2,1)S(1)} %collective-permute-done.xlow_ref, bf16[8,32,128]{2,1,0:T(8,128)(2,1)S(1)} %collective-permute-done.1.after_ref.xhigh_ref, ...), custom_call_target="tpu_custom_call" | custom-call | flops 30000001024 | bytes 10000000 | tf_op jit(solution)/shard_map/fault_net/pallas_call | solution.py:677
  46.1 2.4 %solver_waves.1 = (f32[8,128]{1,0:T(8,128)S(1)}, f32[2,26,48,128]{3,2,1,0:T(8,128)S(1)}, f32[26,48,128]{2,1,0:T(8,128)S(1)}, bf16[3,4,32,128]{3,2,1,0:T(8,128)(2...) custom-call(f32[1152,128]{1,0:T(8,128)S(1)} %get-tuple-element.37.pr, ...), custom_call_target="tpu_custom_call" | custom-call | flops 100000000 | bytes 10000000 | tf_op jit(solution)/shard_map/solver_waves/pallas_call | solution.py:703
  48.5 1.6 %collective-permute-start.4 = (bf16[3,4,32,128]{3,2,1,0:T(8,128)(2,1)S(1)}, bf16[3,4,32,128]{3,2,1,0:T(8,128)(2,1)S(1)}, u32[]{:S(2)}, u32[]{:S(2)}) collective-permute-start(bf16[3,4,32,128]{3,2,1,0:T(8,128)(2,1)S(1)} %get-tuple-element.43), channel_id=1, source_target_pairs={{0,1},{1,2},{2,3},{3,0},{4,5},{5,6},{6,7},{7,4},{8,9},{9,10},{10,1... | collective-permute-start | bytes 294920 | tf_op jit(solution)/shard_map/ppermute | solution.py:728
  50.1 2.4 %collective-permute-start.5 = (bf16[3,4,32,128]{3,2,1,0:T(8,128)(2,1)S(1)}, bf16[3,4,32,128]{3,2,1,0:T(8,128)(2,1)S(1)}, u32[]{:S(2)}, u32[]{:S(2)}) collective-permute-start(bf16[3,4,32,128]{3,2,1,0:T(8,128)(2,1)S(1)} %get-tuple-element.44), channel_id=1, source_target_pairs={{0,2},{1,3},{2,0},{3,1},{4,6},{5,7},{6,4},{7,5},{8,10},{9,11},{10,... | collective-permute-start | bytes 294920 | tf_op jit(solution)/shard_map/ppermute | solution.py:728
  52.5 1.6 %collective-permute-start.6 = (bf16[3,4,32,128]{3,2,1,0:T(8,128)(2,1)S(1)}, bf16[3,4,32,128]{3,2,1,0:T(8,128)(2,1)S(1)}, u32[]{:S(2)}, u32[]{:S(2)}) collective-permute-start(bf16[3,4,32,128]{3,2,1,0:T(8,128)(2,1)S(1)} %get-tuple-element.45), channel_id=1, source_target_pairs={{0,3},{1,0},{2,1},{3,2},{4,7},{5,4},{6,5},{7,6},{8,11},{9,8},{10,9... | collective-permute-start | bytes 294920 | tf_op jit(solution)/shard_map/ppermute | solution.py:728
  54.0 0.6 last_moment.1
  54.6 12.8 %all_to_all.5.mom_ref = f32[32,1,128]{2,1,0:T(1,128)S(1)} all-to-all(f32[32,1,128]{2,1,0:T(1,128)S(1)} %last_moment.1), channel_id=1, replica_groups=mesh['gx'=8,'gy'=4] {'gx','gy'}, dimensions={0} | all-to-all | bytes 32768 | tf_op jit(solution)/shard_map/all_to_all | solution.py:739
  67.4 0.0 collective-permute-done.4.refs_1_
  67.4 0.0 collective-permute-done.5.refs_2_
  67.4 0.0 collective-permute-done.6.refs_3_
  67.4 0.9 %combine_waves.1 = f32[4,128,128]{2,1,0:T(8,128)} custom-call(f32[32,1,128]{2,1,0:T(1,128)S(1)} %all_to_all.5.mom_ref, bf16[3,4,32,128]{3,2,1,0:T(8,128)(2,1)S(1)} %get-tuple-element.42.refs_0_, bf16[3,4,32,128]{3,2,1,0:T(8,128)(2,1)S(1)} %collective-permute-done.4.refs_1_, bf16[3,4,32,128]{3,2,1,0:T(8,128)(2,1)S(1)} %collective-permute-done.5.refs_2_, ...), custom_call_target="tpu_custom_call" | custom-call | tf_op jit(solution)/shard_map/combine_waves/pallas_call | solution.py:740
  (5 shorter events, 0.1 us)
Async XLA Ops:
  0.6 0.9 %copy-start = (bf16[16,32,128]{2,1,0:T(8,128)(2,1)S(1)}, bf16[16,32,128]{2,1,0:T(8,128)(2,1)}, u32[]{:S(2)}) copy-start(bf16[16,32,128]{2,1,0:T(8,128)(2,1)} %amp_ref.3) | copy-start | bytes 393220
  1.6 4.3 %collective-permute-start.1 = (bf16[8,32,128]{2,1,0:T(8,128)(2,1)S(1)}, bf16[8,32,128]{2,1,0:T(8,128)(2,1)S(1)}, u32[]{:S(2)}, u32[]{:S(2)}) collective-permute-start(bf16[8,32,128]{2,1,0:T(8,128)(2,1)S(1)} %get-tuple-element.25), channel_id=1, source_target_pairs={{4,0},{8,4},{12,8},{16,12},{20,16},{24,20},{28,24},{5,1},{9,5},{13... | collective-permute-start | bytes 196616 | tf_op jit(solution)/shard_map/ppermute | solution.py:631
  2.9 3.9 %collective-permute-start = (bf16[8,32,128]{2,1,0:T(8,128)(2,1)S(1)}, bf16[8,32,128]{2,1,0:T(8,128)(2,1)S(1)}, u32[]{:S(2)}, u32[]{:S(2)}) collective-permute-start(bf16[8,32,128]{2,1,0:T(8,128)(2,1)S(1)} %get-tuple-element.24), channel_id=1, source_target_pairs={{0,4},{4,8},{8,12},{12,16},{16,20},{20,24},{24,28},{1,5},{5,9},{9,... | collective-permute-start | bytes 196616 | tf_op jit(solution)/shard_map/ppermute | solution.py:631
  6.8 10.2 %collective-permute-start.2 = (bf16[32,8,128]{2,1,0:T(8,128)(2,1)S(1)}, bf16[32,8,128]{2,1,0:T(8,128)(2,1)S(1)}, u32[]{:S(2)}, u32[]{:S(2)}) collective-permute-start(bf16[32,8,128]{2,1,0:T(8,128)(2,1)S(1)} %pad_maximum_fusion.1), channel_id=1, source_target_pairs={{0,1},{1,2},{2,3},{4,5},{5,6},{6,7},{8,9},{9,10},{10,11},{12,13},{... | collective-permute-start | bytes 196616 | tf_op jit(solution)/shard_map/ppermute | solution.py:631
  11.8 6.6 %collective-permute-start.3 = (bf16[32,8,128]{2,1,0:T(8,128)(2,1)S(1)}, bf16[32,8,128]{2,1,0:T(8,128)(2,1)S(1)}, u32[]{:S(2)}, u32[]{:S(2)}) collective-permute-start(bf16[32,8,128]{2,1,0:T(8,128)(2,1)S(1)} %pad_maximum_fusion.2), channel_id=1, source_target_pairs={{1,0},{2,1},{3,2},{5,4},{6,5},{7,6},{9,8},{10,9},{11,10},{13,12},{... | collective-permute-start | bytes 196616 | tf_op jit(solution)/shard_map/ppermute | solution.py:631
  14.8 3.5 %copy-start.1 = (bf16[16,32,128]{2,1,0:T(8,128)(2,1)S(1)}, bf16[16,32,128]{2,1,0:T(8,128)(2,1)}, u32[]{:S(2)}) copy-start(bf16[16,32,128]{2,1,0:T(8,128)(2,1)} %amp_ref.3) | copy-start | bytes 393220
  48.5 18.9 %collective-permute-start.4 = (bf16[3,4,32,128]{3,2,1,0:T(8,128)(2,1)S(1)}, bf16[3,4,32,128]{3,2,1,0:T(8,128)(2,1)S(1)}, u32[]{:S(2)}, u32[]{:S(2)}) collective-permute-start(bf16[3,4,32,128]{3,2,1,0:T(8,128)(2,1)S(1)} %get-tuple-element.43), channel_id=1, source_target_pairs={{0,1},{1,2},{2,3},{3,0},{4,5},{5,6},{6,7},{7,4},{8,9},{9,10},{10,1... | collective-permute-start | bytes 294920 | tf_op jit(solution)/shard_map/ppermute | solution.py:728
  50.1 17.3 %collective-permute-start.5 = (bf16[3,4,32,128]{3,2,1,0:T(8,128)(2,1)S(1)}, bf16[3,4,32,128]{3,2,1,0:T(8,128)(2,1)S(1)}, u32[]{:S(2)}, u32[]{:S(2)}) collective-permute-start(bf16[3,4,32,128]{3,2,1,0:T(8,128)(2,1)S(1)} %get-tuple-element.44), channel_id=1, source_target_pairs={{0,2},{1,3},{2,0},{3,1},{4,6},{5,7},{6,4},{7,5},{8,10},{9,11},{10,... | collective-permute-start | bytes 294920 | tf_op jit(solution)/shard_map/ppermute | solution.py:728
  52.5 14.9 %collective-permute-start.6 = (bf16[3,4,32,128]{3,2,1,0:T(8,128)(2,1)S(1)}, bf16[3,4,32,128]{3,2,1,0:T(8,128)(2,1)S(1)}, u32[]{:S(2)}, u32[]{:S(2)}) collective-permute-start(bf16[3,4,32,128]{3,2,1,0:T(8,128)(2,1)S(1)} %get-tuple-element.45), channel_id=1, source_target_pairs={{0,3},{1,0},{2,1},{3,2},{4,7},{5,4},{6,5},{7,6},{8,11},{9,8},{10,9... | collective-permute-start | bytes 294920 | tf_op jit(solution)/shard_map/ppermute | solution.py:728
